TPU v7x, 32 devices: a whole 2x2x4 slice. The times are simulated.
32 devices in a mesh: dp: 8 (over z, core), ctx: 4 (over y, x).
Axes of the slice: x: 2, y: 2, z: 4, core: 2. Of those that a mesh axis runs over, the one named last changes fastest.
Arguments:
- queries: bfloat16 [8, 512, 4096], P('dp', 'ctx'), may hold values from -8 to 8
- key_rows: bfloat16 [8, 512, 512], P('dp', 'ctx'), may hold values from -8 to 8
- values: bfloat16 [8, 512, 512], P('dp', 'ctx'), may hold values from -6 to 6
- outputs: bfloat16 [8, 512, 4096], P('dp', 'ctx'), may hold values from -4 to 4
- out_grads: bfloat16 [8, 512, 4096], P('dp', 'ctx'), may hold values from -6 to 6
- depths: int32 [8, 512], P('dp', 'ctx'), may hold values from 0 to 63, as said below
- subtree_end: int32 [8, 512], P('dp', 'ctx'), may hold values from 64 to 512, as said below
- file_lengths: int32 [8, 8], P('dp'), may hold values from 1 to 384, 512 in all within a row
- slopes: float32 [32], replicated, may hold values from 0.02 to 0.5
- ancestor_gain: float32 [32], replicated, may hold values from 0.5 to 3
Outputs:
- query_grads: bfloat16 [8, 512, 4096], P('dp', 'ctx')
- key_grads: bfloat16 [8, 512, 512], P('dp', 'ctx')
- value_grads: bfloat16 [8, 512, 512], P('dp', 'ctx')
- bias_grads: float32 [32, 2], P('ctx')
Inputs may be any that keep to these rules, and one draw needn't show every extreme that they name: `depths`: token t has depth t for t < 64; afterwards the depth changes by at most one from a token to the next. `subtree_end`: the first later position of the same sequence whose depth is not above the token's depth, or 512 where there is none.
All inputs are finite; a program needn't handle non-finite values.
Results may differ from a plain program's by a relative error of at most 0.012.
Values may be sent and summed in bfloat16 or wider, within the bound.
No kernel may reach another device: no remote copies, remote signals or barrier semaphores. Data moves between devices by JAX's collectives and lax.ppermute only.
A program may use at most 64 MiB of HBM per device.

v0:
```python
import functools

import jax
import jax.numpy as jnp
from jax import lax
from jax.experimental import pallas as pl
from jax.experimental.pallas import tpu as pltpu
from jax.sharding import PartitionSpec as P

WIDTH = 128
LOG2E = 1.4426950408889634
MASKED = -1e30
META_ROWS = 16
END_UNIT = 64

VMEM_LIMIT = 40 * 1024 * 1024


def dot_nt(a, b):
    return lax.dot_general(a, b, (((1,), (1,)), ((), ())), preferred_element_type=jnp.float32)


def dot_nn(a, b):
    return lax.dot_general(a, b, (((1,), (0,)), ((), ())), preferred_element_type=jnp.float32)


def fold_rows(block):
    return jnp.sum(block.reshape(block.shape[0] // 8, 8, block.shape[1]), axis=0)


def as_column(row):
    size = row.shape[1]
    return jnp.transpose(jnp.broadcast_to(row, (size, size)))


def pack_kernel(key_ref, value_ref, depth_ref, end_ref, message_ref):
    tokens = key_ref.shape[0]
    groups = key_ref.shape[1] // WIDTH
    for kind, ref in enumerate((key_ref, value_ref)):
        for group in range(groups):
            at = (kind * groups + group) * tokens
            message_ref[at : at + tokens, :] = ref[:, group * WIDTH : (group + 1) * WIDTH]
    depth = depth_ref[...]
    end = end_ref[...]
    end_high = end // END_UNIT
    end_low = end - end_high * END_UNIT
    row = lax.broadcasted_iota(jnp.int32, (META_ROWS, tokens), 0)
    meta = jnp.where(row == 0, depth, jnp.where(row == 1, end_high, end_low))
    meta = meta.astype(jnp.float32).astype(jnp.bfloat16)
    message_ref[2 * groups * tokens : 2 * groups * tokens + META_ROWS, :] = meta


def main_kernel(
    blocks,
    heads_per_group,
    groups,
    lengths_ref,
    slope_ref,
    gain_ref,
    depth_ref,
    end_ref,
    query_hbm,
    output_hbm,
    grad_hbm,
    key_ref,
    value_ref,
    *refs,
):
    tokens = query_hbm.shape[0]
    remote = refs[0 : blocks - 1]
    query_grad_hbm = refs[blocks - 1]
    part_refs = refs[blocks : 2 * blocks]
    bias_hbm = refs[2 * blocks]
    (
        query_ref,
        output_ref,
        grad_ref,
        query_grad_ref,
        keys_ref,
        keys_across_ref,
        value_ext_ref,
        distance_ref,
        ancestor_ref,
        slope_rows,
        gain_rows,
        key_acc,
        value_acc,
        weight_ref,
        probs_ref,
        dscore_ref,
        bias_ref,
        load_sems,
        store_sems,
        bias_sem,
    ) = refs[2 * blocks + 1 :]
    factor = WIDTH**-0.5
    group_columns = heads_per_group * WIDTH
    pairs = heads_per_group // 2

    def load(group, index):
        wide = pl.ds(pl.multiple_of(group * group_columns, group_columns), group_columns)
        source = (query_hbm, output_hbm, grad_hbm)[index]
        to = (query_ref, output_ref, grad_ref)[index]
        return pltpu.make_async_copy(
            source.at[:, wide], to.at[group], load_sems.at[3 * group + index]
        )

    def store(group):
        wide = pl.ds(pl.multiple_of(group * group_columns, group_columns), group_columns)
        return pltpu.make_async_copy(
            query_grad_ref.at[group], query_grad_hbm.at[:, wide], store_sems.at[group]
        )

    for group in range(groups):
        for index in range(3):
            load(group, index).start()

    here = lax.axis_index("ctx")
    query_pos = here * tokens + lax.broadcasted_iota(jnp.int32, (tokens, tokens), 1)
    start = jnp.zeros((tokens, tokens), jnp.int32)
    bound = jnp.int32(0)
    for index in range(lengths_ref.shape[1]):
        bound = bound + lengths_ref[0, index]
        start = jnp.where(query_pos >= bound, bound, start)
    query_depth = jnp.broadcast_to(depth_ref[...].astype(jnp.float32), (tokens, tokens))
    block_rows = [slice(s * tokens, (s + 1) * tokens) for s in range(blocks)]
    for s, rows in enumerate(block_rows):
        key_pos = (here ^ s) * tokens + lax.broadcasted_iota(jnp.int32, (tokens, tokens), 0)
        if s == 0:
            key_depth = as_column(depth_ref[...].astype(jnp.float32))
            key_end = as_column(end_ref[...].astype(jnp.float32))
        else:
            below = slice(2 * groups * tokens, 2 * groups * tokens + META_ROWS)
            meta = remote[s - 1][below, :].astype(jnp.float32)
            key_depth = as_column(meta[0:1])
            key_end = as_column(meta[1:2] * END_UNIT + meta[2:3])
        inside = query_pos.astype(jnp.float32) < key_end
        allowed = (key_pos <= query_pos) & (key_pos >= start)
        distance_ref[rows, :] = jnp.abs(query_depth - key_depth)
        ancestor_ref[rows, :] = jnp.where(allowed, jnp.where(inside, 1.0, 0.0), MASKED)

    for group in range(groups):
        for s, rows in enumerate(block_rows):
            if s == 0:
                key = key_ref[:, group * WIDTH : (group + 1) * WIDTH]
                value = value_ref[:, group * WIDTH : (group + 1) * WIDTH]
            else:
                key = remote[s - 1][group * tokens : (group + 1) * tokens, :]
                at = (groups + group) * tokens
                value = remote[s - 1][at : at + tokens, :]
            keys_ref[group, rows, :] = key
            keys_across_ref[group, :, rows] = jnp.transpose(key)
            value_ext_ref[group, rows, 0:WIDTH] = value
            value_ext_ref[group, rows, WIDTH:] = jnp.full(value.shape, -1.0, jnp.bfloat16)
    key_acc[...] = jnp.zeros_like(key_acc)
    value_acc[...] = jnp.zeros_like(value_acc)

    def stacked(ref, step):
        group, pair = step // pairs, step % pairs
        at = pl.multiple_of(pair * 2 * WIDTH, 2 * WIDTH)
        both = ref[group, :, pl.ds(at, 2 * WIDTH)]
        return jnp.concatenate([both[:, 0:WIDTH], both[:, WIDTH:]], axis=0)

    def weigh(step, slot, raw, half):
        gain = gain_ref[2 * step + half] * LOG2E
        slope = slope_ref[2 * step + half] * LOG2E
        lanes = slice(half * tokens, (half + 1) * tokens)
        tops, totals = [], []
        for rows in block_rows:
            score = raw[rows, lanes] * (factor * LOG2E) + (
                gain * ancestor_ref[rows, :] - slope * distance_ref[rows, :]
            )
            top = jnp.max(score, axis=0, keepdims=True)
            weight = jnp.exp2(score - top)
            weight_ref[slot, rows, lanes] = weight
            tops.append(top)
            totals.append(jnp.sum(weight, axis=0, keepdims=True))
        top = functools.reduce(jnp.maximum, tops)
        shrink = [jnp.exp2(t - top) for t in tops]
        inverse = 1.0 / sum(a * b for a, b in zip(totals, shrink))
        return [s * inverse for s in shrink]

    def differentiate(step, slot, centred, scales, half):
        lanes = slice(half * tokens, (half + 1) * tokens)
        slope_sum, gain_sum = 0.0, 0.0
        for rows, scale in zip(block_rows, scales):
            probs = weight_ref[slot, rows, lanes] * scale
            dscore = probs * centred[rows, lanes]
            probs_ref[slot, rows, lanes] = probs.astype(jnp.bfloat16)
            dscore_ref[slot, rows, lanes] = dscore.astype(jnp.bfloat16)
            slope_sum = slope_sum + fold_rows(dscore * distance_ref[rows, :])
            gain_sum = gain_sum + fold_rows(dscore * ancestor_ref[rows, :])
        at = pl.ds(2 * step + half, 1)
        slope_rows[at, :] = -jnp.sum(slope_sum, axis=0, keepdims=True)
        gain_rows[at, :] = jnp.sum(gain_sum, axis=0, keepdims=True)

    def query_part(step, slot):
        group, pair = step // pairs, step % pairs
        across = dot_nn(keys_across_ref[group], dscore_ref[slot]) * factor
        rows = jnp.transpose(across.astype(jnp.bfloat16))
        at = pl.multiple_of(pair * 2 * WIDTH, 2 * WIDTH)
        both = jnp.concatenate([rows[0:tokens], rows[tokens:]], axis=1)
        query_grad_ref[group, :, pl.ds(at, 2 * WIDTH)] = both

    def advance(step, slot, now, before):
        other = 1 - slot
        if now:
            group = step // pairs
            query_pair = stacked(query_ref, step)
            grad_pair = stacked(grad_ref, step)
            grad_ext = jnp.concatenate(
                [grad_pair, grad_pair * stacked(output_ref, step)], axis=1
            )
            raw = dot_nt(keys_ref[group], query_pair)
        if before:
            last = step - 1
            last_group = last // pairs
            key_acc[last_group] += dot_nn(dscore_ref[other], stacked(query_ref, last))
        if now:
            scales = [weigh(step, slot, raw, 0)]
            centred = dot_nt(value_ext_ref[group], grad_ext)
            scales.append(weigh(step, slot, raw, 1))
        if before:
            value_acc[last_group] += dot_nn(probs_ref[other], stacked(grad_ref, last))
        if now:
            differentiate(step, slot, centred, scales[0], 0)
        if before:
            query_part(last, other)
        if now:
            differentiate(step, slot, centred, scales[1], 1)

    steps = groups * pairs
    for index in range(3):
        load(0, index).wait()
    advance(0, 0, True, False)

    @pl.loop(1, steps)
    def _(step):
        @pl.when(step % pairs == 0)
        def _():
            for index in range(3):
                load(step // pairs, index).wait()

        advance(step, step % 2, True, True)

        @pl.when(step % pairs == 0)
        def _():
            store(step // pairs - 1).start()

    advance(steps, steps % 2, False, True)
    store(groups - 1).start()

    for s, rows in enumerate(block_rows):
        for group in range(groups):
            at = group * tokens
            part_refs[s][at : at + tokens, :] = (key_acc[group, rows, :] * factor).astype(
                jnp.bfloat16
            )
            at = (groups + group) * tokens
            part_refs[s][at : at + tokens, :] = value_acc[group, rows, :].astype(jnp.bfloat16)
    slope_sum = jnp.sum(slope_rows[...], axis=1, keepdims=True)
    gain_sum = jnp.sum(gain_rows[...], axis=1, keepdims=True)
    shape = slope_rows.shape
    lane = lax.broadcasted_iota(jnp.int32, shape, 1)
    row = lax.broadcasted_iota(jnp.int32, shape, 0)
    replicas, parts, rows_here, local = bias_ref.shape
    local_heads = shape[0] // parts
    kind = lax.broadcasted_iota(jnp.int32, (rows_here, local), 0)
    for part in range(parts):
        mine = (lane == row - part * local_heads) & (lane < local_heads)
        slope_line = jnp.sum(jnp.where(mine, slope_sum, 0.0), axis=0, keepdims=True)
        gain_line = jnp.sum(jnp.where(mine, gain_sum, 0.0), axis=0, keepdims=True)
        tile = jnp.where(kind == 0, slope_line, jnp.where(kind == 1, gain_line, 0.0))
        bias_ref[:, part] = jnp.broadcast_to(tile[None], (replicas, rows_here, local))
    bias_copy = pltpu.make_async_copy(bias_ref, bias_hbm, bias_sem)
    bias_copy.start()
    for group in range(groups):
        store(group).wait()
    bias_copy.wait()


def final_kernel(blocks, *refs):
    parts = refs[0:blocks]
    bias_parts, key_out, value_out, bias_out = refs[blocks:]
    tokens = key_out.shape[0]
    groups = key_out.shape[1] // WIDTH
    for kind, out in enumerate((key_out, value_out)):
        for group in range(groups):
            at = (kind * groups + group) * tokens
            total = parts[0][at : at + tokens, :].astype(jnp.float32)
            for s in range(1, blocks):
                total = total + parts[s][at : at + tokens, :].astype(jnp.float32)
            out[:, group * WIDTH : (group + 1) * WIDTH] = total.astype(jnp.bfloat16)
    bias_out[...] = jnp.sum(bias_parts[...], axis=0)[0:2, 0 : bias_out.shape[1]]


def body(
    queries,
    key_rows,
    values,
    outputs,
    out_grads,
    depths,
    subtree_end,
    file_lengths,
    slopes,
    ancestor_gain,
):
    blocks = lax.axis_size("ctx")
    replicas = lax.axis_size("dp")
    tokens, width_all = queries.shape[1:]
    kv_width = key_rows.shape[2]
    heads_all = width_all // WIDTH
    groups = kv_width // WIDTH
    heads_per_group = heads_all // groups
    group_columns = heads_per_group * WIDTH
    local_heads = heads_all // blocks
    keys_seen = blocks * tokens
    bf16, f32 = jnp.bfloat16, jnp.float32
    vmem = pl.BlockSpec(memory_space=pltpu.VMEM)
    smem = pl.BlockSpec(memory_space=pltpu.SMEM)
    hbm = pl.BlockSpec(memory_space=pltpu.HBM)
    params = pltpu.CompilerParams(vmem_limit_bytes=VMEM_LIMIT)

    def hold(array):
        return pltpu.with_memory_space_constraint(array, pltpu.HBM)

    key_held, value_held = hold(key_rows[0]), hold(values[0])
    depth_held, end_held = hold(depths), hold(subtree_end)
    message_rows = 2 * groups * tokens
    message = pl.pallas_call(
        pack_kernel,
        out_shape=jax.ShapeDtypeStruct((message_rows + META_ROWS, WIDTH), bf16),
        in_specs=[vmem] * 4,
        out_specs=vmem,
        compiler_params=params,
        name="pack",
    )(key_held, value_held, depth_held, end_held)
    arrived = [
        lax.ppermute(message, "ctx", [(i, i ^ s) for i in range(blocks) if i < i ^ s])
        for s in range(1, blocks)
    ]

    bias_shape = (replicas, blocks, 8, WIDTH)
    matmul_flops = 2 * tokens * keys_seen * WIDTH * heads_all
    results = pl.pallas_call(
        functools.partial(main_kernel, blocks, heads_per_group, groups),
        out_shape=[jax.ShapeDtypeStruct((tokens, width_all), bf16)]
        + [jax.ShapeDtypeStruct((message_rows, WIDTH), bf16)] * blocks
        + [jax.ShapeDtypeStruct(bias_shape, f32)],
        in_specs=[smem] * 3 + [vmem] * 2 + [hbm] * 3 + [vmem] * (1 + blocks),
        out_specs=[hbm] + [vmem] * blocks + [hbm],
        scratch_shapes=[
            pltpu.VMEM((groups, tokens, group_columns), bf16),
            pltpu.VMEM((groups, tokens, group_columns), bf16),
            pltpu.VMEM((groups, tokens, group_columns), bf16),
            pltpu.VMEM((groups, tokens, group_columns), bf16),
            pltpu.VMEM((groups, keys_seen, WIDTH), bf16),
            pltpu.VMEM((groups, WIDTH, keys_seen), bf16),
            pltpu.VMEM((groups, keys_seen, 2 * WIDTH), bf16),
            pltpu.VMEM((keys_seen, tokens), f32),
            pltpu.VMEM((keys_seen, tokens), f32),
            pltpu.VMEM((heads_all, tokens), f32),
            pltpu.VMEM((heads_all, tokens), f32),
            pltpu.VMEM((groups, keys_seen, WIDTH), f32),
            pltpu.VMEM((groups, keys_seen, WIDTH), f32),
            pltpu.VMEM((2, keys_seen, 2 * tokens), f32),
            pltpu.VMEM((2, keys_seen, 2 * tokens), bf16),
            pltpu.VMEM((2, keys_seen, 2 * tokens), bf16),
            pltpu.VMEM(bias_shape, f32),
            pltpu.SemaphoreType.DMA((3 * groups,)),
            pltpu.SemaphoreType.DMA((groups,)),
            pltpu.SemaphoreType.DMA,
        ],
        compiler_params=params,
        cost_estimate=pl.CostEstimate(
            flops=5 * matmul_flops,
            bytes_accessed=10 * tokens * width_all,
            transcendentals=tokens * keys_seen * heads_all,
        ),
        name="attend",
    )(
        hold(file_lengths),
        hold(slopes),
        hold(ancestor_gain),
        depth_held,
        end_held,
        hold(queries[0]),
        hold(outputs[0]),
        hold(out_grads[0]),
        key_held,
        value_held,
        *arrived,
    )
    query_grads = results[0]
    parts = list(results[1 : 1 + blocks])
    bias_parts = results[1 + blocks].reshape(replicas * blocks, 8, WIDTH)
    for s in range(1, blocks):
        back = [(i, i ^ s) for i in range(blocks) if i > i ^ s]
        parts[s] = lax.ppermute(parts[s], "ctx", back)
    bias_parts = lax.all_to_all(bias_parts, ("dp", "ctx"), split_axis=0, concat_axis=0, tiled=True)

    key_grads, value_grads, bias_grads = pl.pallas_call(
        functools.partial(final_kernel, blocks),
        out_shape=[
            jax.ShapeDtypeStruct((tokens, kv_width), bf16),
            jax.ShapeDtypeStruct((tokens, kv_width), bf16),
            jax.ShapeDtypeStruct((2, local_heads), f32),
        ],
        in_specs=[vmem] * (blocks + 1),
        out_specs=[vmem] * 3,
        compiler_params=params,
        name="combine",
    )(*parts, bias_parts)
    return (query_grads[None], key_grads[None], value_grads[None], bias_grads.T)


def solution(mesh):
    in_specs = (
        P("dp", "ctx", None),
        P("dp", "ctx", None),
        P("dp", "ctx", None),
        P("dp", "ctx", None),
        P("dp", "ctx", None),
        P("dp", "ctx"),
        P("dp", "ctx"),
        P("dp", None),
        P(),
        P(),
    )
    out_specs = (P("dp", "ctx", None), P("dp", "ctx", None), P("dp", "ctx", None), P("ctx", None))
    return jax.shard_map(body, mesh=mesh, in_specs=in_specs, out_specs=out_specs, check_vma=False)
```

profile of v0, /device:TPU:0, one launch (start us, length us, event | category | flops | bytes accessed | tf_op | source)
XLA Modules:
  0.0 58.1 jit_solution(10697270283648825939)
XLA Ops:
  0.6 1.0 %pack.1 = bf16[1040,128]{1,0:T(8,128)(2,1)S(1)} custom-call(bf16[128,512]{1,0:T(8,128)(2,1)} %bitcast.11, bf16[128,512]{1,0:T(8,128)(2,1)} %bitcast.13, s32[1,128]{1,0:T(1,128)} %depth_ref.3, s32[1,128]{1,0:T(1,128)} %end_ref.3), custom_call_target="tpu_custom_call" | custom-call | tf_op jit(solution)/shard_map/pack/pallas_call | solution.py:331
  1.7 5.8 %collective-permute-start.2 = (bf16[1040,128]{1,0:T(8,128)(2,1)S(1)}, bf16[1040,128]{1,0:T(8,128)(2,1)S(1)}, u32[]{:S(2)}, u32[]{:S(2)}) collective-permute-start(bf16[1040,128]{1,0:T(8,128)(2,1)S(1)} %pack.1), channel_id=1, source_target_pairs={{0,3},{1,2},{4,7},{5,6},{8,11},{9,10},{12,15},{13,14},{16,19},{17,... | collective-permute-start | bytes 798728 | tf_op jit(solution)/shard_map/ppermute | solution.py:340
  7.5 1.3 %collective-permute-start.1 = (bf16[1040,128]{1,0:T(8,128)(2,1)S(1)}, bf16[1040,128]{1,0:T(8,128)(2,1)S(1)}, u32[]{:S(2)}, u32[]{:S(2)}) collective-permute-start(bf16[1040,128]{1,0:T(8,128)(2,1)S(1)} %pack.1), channel_id=1, source_target_pairs={{0,2},{1,3},{4,6},{5,7},{8,10},{9,11},{12,14},{13,15},{16,18},{17,... | collective-permute-start | bytes 798728 | tf_op jit(solution)/shard_map/ppermute | solution.py:340
  8.8 2.5 %collective-permute-start = (bf16[1040,128]{1,0:T(8,128)(2,1)S(1)}, bf16[1040,128]{1,0:T(8,128)(2,1)S(1)}, u32[]{:S(2)}, u32[]{:S(2)}) collective-permute-start(bf16[1040,128]{1,0:T(8,128)(2,1)S(1)} %pack.1), channel_id=1, source_target_pairs={{0,1},{2,3},{4,5},{6,7},{8,9},{10,11},{12,13},{14,15},{16,17},{18,... | collective-permute-start | bytes 798728 | tf_op jit(solution)/shard_map/ppermute | solution.py:340
  11.3 3.0 %collective-permute-done.2.refs_2_ = bf16[1040,128]{1,0:T(8,128)(2,1)S(1)} collective-permute-done((bf16[1040,128]{1,0:T(8,128)(2,1)S(1)}, bf16[1040,128]{1,0:T(8,128)(2,1)S(1)}, u32[]{:S(2)}, u32[]{:S(2)}) %collective-permute-start.2) | collective-permute-done | bytes 266272 | tf_op jit(solution)/shard_map/ppermute | solution.py:340
  14.3 4.5 %collective-permute-done.1.refs_1_ = bf16[1040,128]{1,0:T(8,128)(2,1)S(1)} collective-permute-done((bf16[1040,128]{1,0:T(8,128)(2,1)S(1)}, bf16[1040,128]{1,0:T(8,128)(2,1)S(1)}, u32[]{:S(2)}, u32[]{:S(2)}) %collective-permute-start.1) | collective-permute-done | bytes 266272 | tf_op jit(solution)/shard_map/ppermute | solution.py:340
  18.8 0.1 collective-permute-done.refs_0_
  18.9 18.2 %attend.1 = (bf16[128,4096]{1,0:T(8,128)(2,1)}, bf16[1024,128]{1,0:T(8,128)(2,1)S(1)}, bf16[1024,128]{1,0:T(8,128)(2,1)S(1)}, bf16[1024,128]{1,0:T(8,128)(2,1)S(...) custom-call(s32[1,8]{1,0:T(1,128)} %lengths_ref.1, f32[32]{0:T(128)} %slope_ref.1, f32[32]{0:T(128)} %gain_ref.1, ...), custom_call_target="tpu_custom_call" | custom-call | flops 2684354560 | bytes 5242880 | tf_op jit(solution)/shard_map/attend/pallas_call | solution.py:346
  37.0 1.3 %collective-permute-start.3 = (bf16[1024,128]{1,0:T(8,128)(2,1)S(1)}, bf16[1024,128]{1,0:T(8,128)(2,1)S(1)}, u32[]{:S(2)}, u32[]{:S(2)}) collective-permute-start(bf16[1024,128]{1,0:T(8,128)(2,1)S(1)} %get-tuple-element.15), channel_id=1, source_target_pairs={{1,0},{3,2},{5,4},{7,6},{9,8},{11,10},{13,12},{15,14},{17,16},{19,... | collective-permute-start | bytes 786440 | tf_op jit(solution)/shard_map/ppermute | solution.py:400
  38.3 1.3 %collective-permute-start.4 = (bf16[1024,128]{1,0:T(8,128)(2,1)S(1)}, bf16[1024,128]{1,0:T(8,128)(2,1)S(1)}, u32[]{:S(2)}, u32[]{:S(2)}) collective-permute-start(bf16[1024,128]{1,0:T(8,128)(2,1)S(1)} %get-tuple-element.16), channel_id=1, source_target_pairs={{2,0},{3,1},{6,4},{7,5},{10,8},{11,9},{14,12},{15,13},{18,16},{19,... | collective-permute-start | bytes 786440 | tf_op jit(solution)/shard_map/ppermute | solution.py:400
  39.6 1.3 %collective-permute-start.5 = (bf16[1024,128]{1,0:T(8,128)(2,1)S(1)}, bf16[1024,128]{1,0:T(8,128)(2,1)S(1)}, u32[]{:S(2)}, u32[]{:S(2)}) collective-permute-start(bf16[1024,128]{1,0:T(8,128)(2,1)S(1)} %get-tuple-element.17), channel_id=1, source_target_pairs={{2,1},{3,0},{6,5},{7,4},{10,9},{11,8},{14,13},{15,12},{18,17},{19,... | collective-permute-start | bytes 786440 | tf_op jit(solution)/shard_map/ppermute | solution.py:400
  40.9 16.4 %all_to_all.5.refs_4_ = f32[32,8,128]{2,1,0:T(8,128)S(1)} all-to-all(f32[32,8,128]{2,1,0:T(8,128)S(1)} %bitcast.10), channel_id=1, replica_groups=mesh['dp'=8,'ctx'=4] {'dp','ctx'}, dimensions={0} | all-to-all | bytes 262144 | tf_op jit(solution)/shard_map/all_to_all | solution.py:401
  57.3 0.0 collective-permute-done.3.refs_1_
  57.3 0.0 collective-permute-done.4.refs_2_
  57.3 0.0 collective-permute-done.5.refs_3_
  57.3 0.8 %combine.1 = (bf16[128,512]{1,0:T(8,128)(2,1)}, bf16[128,512]{1,0:T(8,128)(2,1)}, f32[2,8]{1,0:T(2,128)}) custom-call(bf16[1024,128]{1,0:T(8,128)(2,1)S(1)} %get-tuple-element.14.refs_0_, bf16[1024,128]{1,0:T(8,128)(2,1)S(1)} %collective-permute-done.3.refs_1_, bf16[1024,128]{1,0:T(8,128)(2,1)S(1)} %collective-permute-done.4.refs_2_, ...), custom_call_target="tpu_custom_call" | custom-call | tf_op jit(solution)/shard_map/combine/pallas_call | solution.py:403
Async XLA Ops:
  1.7 12.6 %collective-permute-start.2 = (bf16[1040,128]{1,0:T(8,128)(2,1)S(1)}, bf16[1040,128]{1,0:T(8,128)(2,1)S(1)}, u32[]{:S(2)}, u32[]{:S(2)}) collective-permute-start(bf16[1040,128]{1,0:T(8,128)(2,1)S(1)} %pack.1), channel_id=1, source_target_pairs={{0,3},{1,2},{4,7},{5,6},{8,11},{9,10},{12,15},{13,14},{16,19},{17,... | collective-permute-start | bytes 798728 | tf_op jit(solution)/shard_map/ppermute | solution.py:340
  7.5 11.3 %collective-permute-start.1 = (bf16[1040,128]{1,0:T(8,128)(2,1)S(1)}, bf16[1040,128]{1,0:T(8,128)(2,1)S(1)}, u32[]{:S(2)}, u32[]{:S(2)}) collective-permute-start(bf16[1040,128]{1,0:T(8,128)(2,1)S(1)} %pack.1), channel_id=1, source_target_pairs={{0,2},{1,3},{4,6},{5,7},{8,10},{9,11},{12,14},{13,15},{16,18},{17,... | collective-permute-start | bytes 798728 | tf_op jit(solution)/shard_map/ppermute | solution.py:340
  8.8 10.1 %collective-permute-start = (bf16[1040,128]{1,0:T(8,128)(2,1)S(1)}, bf16[1040,128]{1,0:T(8,128)(2,1)S(1)}, u32[]{:S(2)}, u32[]{:S(2)}) collective-permute-start(bf16[1040,128]{1,0:T(8,128)(2,1)S(1)} %pack.1), channel_id=1, source_target_pairs={{0,1},{2,3},{4,5},{6,7},{8,9},{10,11},{12,13},{14,15},{16,17},{18,... | collective-permute-start | bytes 798728 | tf_op jit(solution)/shard_map/ppermute | solution.py:340
  37.0 20.3 %collective-permute-start.3 = (bf16[1024,128]{1,0:T(8,128)(2,1)S(1)}, bf16[1024,128]{1,0:T(8,128)(2,1)S(1)}, u32[]{:S(2)}, u32[]{:S(2)}) collective-permute-start(bf16[1024,128]{1,0:T(8,128)(2,1)S(1)} %get-tuple-element.15), channel_id=1, source_target_pairs={{1,0},{3,2},{5,4},{7,6},{9,8},{11,10},{13,12},{15,14},{17,16},{19,... | collective-permute-start | bytes 786440 | tf_op jit(solution)/shard_map/ppermute | solution.py:400
  38.3 19.0 %collective-permute-start.4 = (bf16[1024,128]{1,0:T(8,128)(2,1)S(1)}, bf16[1024,128]{1,0:T(8,128)(2,1)S(1)}, u32[]{:S(2)}, u32[]{:S(2)}) collective-permute-start(bf16[1024,128]{1,0:T(8,128)(2,1)S(1)} %get-tuple-element.16), channel_id=1, source_target_pairs={{2,0},{3,1},{6,4},{7,5},{10,8},{11,9},{14,12},{15,13},{18,16},{19,... | collective-permute-start | bytes 786440 | tf_op jit(solution)/shard_map/ppermute | solution.py:400
  39.6 17.7 %collective-permute-start.5 = (bf16[1024,128]{1,0:T(8,128)(2,1)S(1)}, bf16[1024,128]{1,0:T(8,128)(2,1)S(1)}, u32[]{:S(2)}, u32[]{:S(2)}) collective-permute-start(bf16[1024,128]{1,0:T(8,128)(2,1)S(1)} %get-tuple-element.17), channel_id=1, source_target_pairs={{2,1},{3,0},{6,5},{7,4},{10,9},{11,8},{14,13},{15,12},{18,17},{19,... | collective-permute-start | bytes 786440 | tf_op jit(solution)/shard_map/ppermute | solution.py:400
where the time goes:
time: 58.4 us; the launch traced here: 58.1 us
  Pallas kernels  20 us (34%)
  blocking collectives  16.4 us (28%)
  starting transfers between devices  13.5 us (23%)
  waiting for transfers between devices  7.58 us (13%)
  between operations  0.69 us (1%)
    pallas_call x1, Pallas kernels, body(): pl.pallas_call(functools.partial(main_kernel, blocks, heads_per_group, gr...  18.2 us
    all_to_all x1, blocking collectives, body(): lax.all_to_all(bias_parts, ('dp', 'ctx'), split_axis=0, concat_axis=0, ti...  16.4 us
    ppermute x3, starting transfers between devices, body(): lax.ppermute(message, 'ctx', [(i, i ^ s) for i in range(blocks) if i < i...  9.59 us
    ppermute x3, waiting for transfers between devices, body(): lax.ppermute(message, 'ctx', [(i, i ^ s) for i in range(blocks) if i < i...  7.57 us
    ppermute x3, starting transfers between devices, body(): parts[s] = lax.ppermute(parts[s], 'ctx', back)  3.88 us
  transfers between devices with their start and end apart: 6, of which 3 were waited for; matrix products, arithmetic and copies ran while one was open for 0% of the time, Pallas kernels for 0%

commit v1 on v0

--- a/solution.py
+++ b/solution.py
@@ -12,8 +12,6 @@
 MASKED = -1e30
 META_ROWS = 16
 END_UNIT = 64
-
-VMEM_LIMIT = 40 * 1024 * 1024
 
 
 def dot_nt(a, b):
@@ -83,8 +81,6 @@
         ancestor_ref,
         slope_rows,
         gain_rows,
-        key_acc,
-        value_acc,
         weight_ref,
         probs_ref,
         dscore_ref,
@@ -152,27 +148,24 @@
             keys_across_ref[group, :, rows] = jnp.transpose(key)
             value_ext_ref[group, rows, 0:WIDTH] = value
             value_ext_ref[group, rows, WIDTH:] = jnp.full(value.shape, -1.0, jnp.bfloat16)
-    key_acc[...] = jnp.zeros_like(key_acc)
-    value_acc[...] = jnp.zeros_like(value_acc)
-
-    def stacked(ref, step):
-        group, pair = step // pairs, step % pairs
-        at = pl.multiple_of(pair * 2 * WIDTH, 2 * WIDTH)
-        both = ref[group, :, pl.ds(at, 2 * WIDTH)]
-        return jnp.concatenate([both[:, 0:WIDTH], both[:, WIDTH:]], axis=0)
-
-    def weigh(step, slot, raw, half):
-        gain = gain_ref[2 * step + half] * LOG2E
-        slope = slope_ref[2 * step + half] * LOG2E
+
+    def stacked(ref, group, first, count):
+        heads = [slice((first + i) * WIDTH, (first + i + 1) * WIDTH) for i in range(count)]
+        return jnp.concatenate([ref[group, :, h] for h in heads], axis=0)
+
+    def weigh(group, pair, raw, half):
+        head = group * heads_per_group + 2 * pair + half
+        gain = gain_ref[head] * LOG2E
+        slope = slope_ref[head] * LOG2E
         lanes = slice(half * tokens, (half + 1) * tokens)
         tops, totals = [], []
-        for rows in block_rows:
-            score = raw[rows, lanes] * (factor * LOG2E) + (
+        for s, rows in enumerate(block_rows):
+            score = raw[s][:, lanes] * (factor * LOG2E) + (
                 gain * ancestor_ref[rows, :] - slope * distance_ref[rows, :]
             )
             top = jnp.max(score, axis=0, keepdims=True)
             weight = jnp.exp2(score - top)
-            weight_ref[slot, rows, lanes] = weight
+            weight_ref[pair % 2, rows, lanes] = weight
             tops.append(top)
             totals.append(jnp.sum(weight, axis=0, keepdims=True))
         top = functools.reduce(jnp.maximum, tops)
@@ -180,84 +173,85 @@
         inverse = 1.0 / sum(a * b for a, b in zip(totals, shrink))
         return [s * inverse for s in shrink]
 
-    def differentiate(step, slot, centred, scales, half):
+    def differentiate(group, pair, slot, centred, scales, half):
         lanes = slice(half * tokens, (half + 1) * tokens)
+        to = slice((2 * pair + half) * tokens, (2 * pair + half + 1) * tokens)
         slope_sum, gain_sum = 0.0, 0.0
-        for rows, scale in zip(block_rows, scales):
-            probs = weight_ref[slot, rows, lanes] * scale
-            dscore = probs * centred[rows, lanes]
-            probs_ref[slot, rows, lanes] = probs.astype(jnp.bfloat16)
-            dscore_ref[slot, rows, lanes] = dscore.astype(jnp.bfloat16)
+        for s, rows in enumerate(block_rows):
+            probs = weight_ref[pair % 2, rows, lanes] * scales[s]
+            dscore = probs * centred[s][:, lanes]
+            probs_ref[slot, rows, to] = probs.astype(jnp.bfloat16)
+            dscore_ref[slot, rows, to] = dscore.astype(jnp.bfloat16)
             slope_sum = slope_sum + fold_rows(dscore * distance_ref[rows, :])
             gain_sum = gain_sum + fold_rows(dscore * ancestor_ref[rows, :])
-        at = pl.ds(2 * step + half, 1)
+        at = pl.ds(group * heads_per_group + 2 * pair + half, 1)
         slope_rows[at, :] = -jnp.sum(slope_sum, axis=0, keepdims=True)
         gain_rows[at, :] = jnp.sum(gain_sum, axis=0, keepdims=True)
 
-    def query_part(step, slot):
-        group, pair = step // pairs, step % pairs
-        across = dot_nn(keys_across_ref[group], dscore_ref[slot]) * factor
+    def put_part(group, kind, whole):
+        at = pl.multiple_of((kind * groups + group) * tokens, tokens)
+        for s, rows in enumerate(block_rows):
+            part_refs[s][pl.ds(at, tokens), :] = whole[rows].astype(jnp.bfloat16)
+
+    def key_part(group, slot):
+        heads = stacked(query_ref, group, 0, heads_per_group)
+        put_part(group, 0, dot_nn(dscore_ref[slot], heads) * factor)
+
+    def value_part(group, slot):
+        heads = stacked(grad_ref, group, 0, heads_per_group)
+        put_part(group, 1, dot_nn(probs_ref[slot], heads))
+
+    def query_part(group, slot, pair):
+        lanes = slice(2 * pair * tokens, (2 * pair + 2) * tokens)
+        across = dot_nn(keys_across_ref[group], dscore_ref[slot, :, lanes]) * factor
         rows = jnp.transpose(across.astype(jnp.bfloat16))
-        at = pl.multiple_of(pair * 2 * WIDTH, 2 * WIDTH)
-        both = jnp.concatenate([rows[0:tokens], rows[tokens:]], axis=1)
-        query_grad_ref[group, :, pl.ds(at, 2 * WIDTH)] = both
-
-    def advance(step, slot, now, before):
-        other = 1 - slot
-        if now:
-            group = step // pairs
-            query_pair = stacked(query_ref, step)
-            grad_pair = stacked(grad_ref, step)
-            grad_ext = jnp.concatenate(
-                [grad_pair, grad_pair * stacked(output_ref, step)], axis=1
-            )
-            raw = dot_nt(keys_ref[group], query_pair)
-        if before:
-            last = step - 1
-            last_group = last // pairs
-            key_acc[last_group] += dot_nn(dscore_ref[other], stacked(query_ref, last))
-        if now:
-            scales = [weigh(step, slot, raw, 0)]
-            centred = dot_nt(value_ext_ref[group], grad_ext)
-            scales.append(weigh(step, slot, raw, 1))
-        if before:
-            value_acc[last_group] += dot_nn(probs_ref[other], stacked(grad_ref, last))
-        if now:
-            differentiate(step, slot, centred, scales[0], 0)
-        if before:
-            query_part(last, other)
-        if now:
-            differentiate(step, slot, centred, scales[1], 1)
-
-    steps = groups * pairs
-    for index in range(3):
-        load(0, index).wait()
-    advance(0, 0, True, False)
-
-    @pl.loop(1, steps)
-    def _(step):
-        @pl.when(step % pairs == 0)
+        for half in range(2):
+            at = (2 * pair + half) * WIDTH
+            query_grad_ref[group, :, at : at + WIDTH] = rows[half * tokens : (half + 1) * tokens]
+
+    def products(ref, group, other):
+        whole = dot_nt(ref[group], other)
+        return [whole[rows] for rows in block_rows]
+
+    def advance(group, slot, before, before_slot):
+        for pair in range(pairs):
+            if group is not None:
+                query_pair = stacked(query_ref, group, 2 * pair, 2)
+                grad_pair = stacked(grad_ref, group, 2 * pair, 2)
+                output_pair = stacked(output_ref, group, 2 * pair, 2)
+                grad_ext = jnp.concatenate([grad_pair, grad_pair * output_pair], axis=1)
+                raw = products(keys_ref, group, query_pair)
+                scales = [weigh(group, pair, raw, half) for half in range(2)]
+            if pair == 0:
+                key_part(before, before_slot)
+            if pair == 1:
+                value_part(before, before_slot)
+            if group is not None:
+                centred = products(value_ext_ref, group, grad_ext)
+                for half in range(2):
+                    differentiate(group, pair, slot, centred, scales[half], half)
+            query_part(before, before_slot, pair)
+
+    @pl.loop(0, groups // 2)
+    def _(turn):
+        first, second = 2 * turn, 2 * turn + 1
+        for index in range(3):
+            load(first, index).wait()
+        before = jnp.maximum(first - 1, 0)
+        advance(first, 0, before, 1)
+
+        @pl.when(turn > 0)
         def _():
-            for index in range(3):
-                load(step // pairs, index).wait()
-
-        advance(step, step % 2, True, True)
-
-        @pl.when(step % pairs == 0)
-        def _():
-            store(step // pairs - 1).start()
-
-    advance(steps, steps % 2, False, True)
+            store(before).start()
+
+        for index in range(3):
+            load(second, index).wait()
+        advance(second, 1, first, 0)
+        store(first).start()
+
+    advance(None, None, groups - 1, 1)
     store(groups - 1).start()
 
-    for s, rows in enumerate(block_rows):
-        for group in range(groups):
-            at = group * tokens
-            part_refs[s][at : at + tokens, :] = (key_acc[group, rows, :] * factor).astype(
-                jnp.bfloat16
-            )
-            at = (groups + group) * tokens
-            part_refs[s][at : at + tokens, :] = value_acc[group, rows, :].astype(jnp.bfloat16)
     slope_sum = jnp.sum(slope_rows[...], axis=1, keepdims=True)
     gain_sum = jnp.sum(gain_rows[...], axis=1, keepdims=True)
     shape = slope_rows.shape
@@ -279,9 +273,9 @@
     bias_copy.wait()
 
 
-def final_kernel(blocks, *refs):
+def combine_kernel(blocks, *refs):
     parts = refs[0:blocks]
-    bias_parts, key_out, value_out, bias_out = refs[blocks:]
+    key_out, value_out = refs[blocks:]
     tokens = key_out.shape[0]
     groups = key_out.shape[1] // WIDTH
     for kind, out in enumerate((key_out, value_out)):
@@ -291,7 +285,10 @@
             for s in range(1, blocks):
                 total = total + parts[s][at : at + tokens, :].astype(jnp.float32)
             out[:, group * WIDTH : (group + 1) * WIDTH] = total.astype(jnp.bfloat16)
-    bias_out[...] = jnp.sum(bias_parts[...], axis=0)[0:2, 0 : bias_out.shape[1]]
+
+
+def bias_kernel(parts_ref, out_ref):
+    out_ref[...] = jnp.sum(parts_ref[...], axis=0)[0:2, 0 : out_ref.shape[1]]
 
 
 def body(
@@ -320,7 +317,7 @@
     vmem = pl.BlockSpec(memory_space=pltpu.VMEM)
     smem = pl.BlockSpec(memory_space=pltpu.SMEM)
     hbm = pl.BlockSpec(memory_space=pltpu.HBM)
-    params = pltpu.CompilerParams(vmem_limit_bytes=VMEM_LIMIT)
+    params = pltpu.CompilerParams(vmem_limit_bytes=(40 if blocks <= 4 else 56) * 1024 * 1024)
 
     def hold(array):
         return pltpu.with_memory_space_constraint(array, pltpu.HBM)
@@ -362,11 +359,9 @@
             pltpu.VMEM((keys_seen, tokens), f32),
             pltpu.VMEM((heads_all, tokens), f32),
             pltpu.VMEM((heads_all, tokens), f32),
-            pltpu.VMEM((groups, keys_seen, WIDTH), f32),
-            pltpu.VMEM((groups, keys_seen, WIDTH), f32),
             pltpu.VMEM((2, keys_seen, 2 * tokens), f32),
-            pltpu.VMEM((2, keys_seen, 2 * tokens), bf16),
-            pltpu.VMEM((2, keys_seen, 2 * tokens), bf16),
+            pltpu.VMEM((2, keys_seen, group_columns), bf16),
+            pltpu.VMEM((2, keys_seen, group_columns), bf16),
             pltpu.VMEM(bias_shape, f32),
             pltpu.SemaphoreType.DMA((3 * groups,)),
             pltpu.SemaphoreType.DMA((groups,)),
@@ -400,18 +395,27 @@
         parts[s] = lax.ppermute(parts[s], "ctx", back)
     bias_parts = lax.all_to_all(bias_parts, ("dp", "ctx"), split_axis=0, concat_axis=0, tiled=True)
 
-    key_grads, value_grads, bias_grads = pl.pallas_call(
-        functools.partial(final_kernel, blocks),
-        out_shape=[
-            jax.ShapeDtypeStruct((tokens, kv_width), bf16),
-            jax.ShapeDtypeStruct((tokens, kv_width), bf16),
-            jax.ShapeDtypeStruct((2, local_heads), f32),
-        ],
-        in_specs=[vmem] * (blocks + 1),
-        out_specs=[vmem] * 3,
+    key_grads, value_grads = pl.pallas_call(
+        functools.partial(combine_kernel, blocks),
+        out_shape=[jax.ShapeDtypeStruct((tokens, kv_width), bf16)] * 2,
+        in_specs=[vmem] * blocks,
+        out_specs=[vmem] * 2,
         compiler_params=params,
+        cost_estimate=pl.CostEstimate(
+            flops=2 * message_rows * WIDTH * blocks,
+            bytes_accessed=2 * message_rows * WIDTH * (blocks + 1),
+            transcendentals=0,
+        ),
         name="combine",
-    )(*parts, bias_parts)
+    )(*parts)
+    bias_grads = pl.pallas_call(
+        bias_kernel,
+        out_shape=jax.ShapeDtypeStruct((2, local_heads), f32),
+        in_specs=[vmem],
+        out_specs=vmem,
+        compiler_params=params,
+        name="bias",
+    )(bias_parts)
     return (query_grads[None], key_grads[None], value_grads[None], bias_grads.T)
 
 

time: 58.4 us -> 52.6 us (0.901)
  Pallas kernels: 20 us -> 14.2 us
    pallas_call x1, Pallas kernels: 18.2 us -> 11.8 us  [body(): pl.pallas_call(functools.partial(main_kernel, blocks, heads_per_group, gr...]
    pallas_call x1 -> x2, Pallas kernels: 0.81 us -> 1.4 us  [the longest x1 0.81 us: body(): pl.pallas_call(functools.partial(combine_kernel, blocks), out_shape=[jax....]
  transfers between devices with their start and end apart: 6 -> 6, of which waited for: 3 -> 3; matrix products, arithmetic and copies ran while one was open for 0% -> 0% of each run, Pallas kernels for 0% -> 1%
where the time goes in v1:
time: 52.6 us; the launch traced here: 52.3 us
  blocking collectives  16.4 us (31%)
  Pallas kernels  14.2 us (27%)
  starting transfers between devices  13.5 us (26%)
  waiting for transfers between devices  7.58 us (14%)
  between operations  0.69 us (1%)
    all_to_all x1, blocking collectives, body(): lax.all_to_all(bias_parts, ('dp', 'ctx'), split_axis=0, concat_axis=0, ti...  16.4 us
    pallas_call x1, Pallas kernels, body(): pl.pallas_call(functools.partial(main_kernel, blocks, heads_per_group, gr...  11.8 us
    ppermute x3, starting transfers between devices, body(): lax.ppermute(message, 'ctx', [(i, i ^ s) for i in range(blocks) if i < i...  9.59 us
    ppermute x3, waiting for transfers between devices, body(): lax.ppermute(message, 'ctx', [(i, i ^ s) for i in range(blocks) if i < i...  7.57 us
    ppermute x3, starting transfers between devices, body(): parts[s] = lax.ppermute(parts[s], 'ctx', back)  3.88 us
  transfers between devices with their start and end apart: 6, of which 3 were waited for; matrix products, arithmetic and copies ran while one was open for 0% of the time, Pallas kernels for 1%

profile of v1, /device:TPU:0, one launch (start us, length us, event | category | flops | bytes accessed | tf_op | source)
XLA Modules:
  0.0 52.3 jit_solution(457312237444026395)
XLA Ops:
  0.6 1.0 %pack.1 = bf16[1040,128]{1,0:T(8,128)(2,1)S(1)} custom-call(bf16[128,512]{1,0:T(8,128)(2,1)} %bitcast.11, bf16[128,512]{1,0:T(8,128)(2,1)} %bitcast.13, s32[1,128]{1,0:T(1,128)} %depth_ref.3, s32[1,128]{1,0:T(1,128)} %end_ref.3), custom_call_target="tpu_custom_call" | custom-call | tf_op jit(solution)/shard_map/pack/pallas_call | solution.py:328
  1.7 5.8 %collective-permute-start.2 = (bf16[1040,128]{1,0:T(8,128)(2,1)S(1)}, bf16[1040,128]{1,0:T(8,128)(2,1)S(1)}, u32[]{:S(2)}, u32[]{:S(2)}) collective-permute-start(bf16[1040,128]{1,0:T(8,128)(2,1)S(1)} %pack.1), channel_id=1, source_target_pairs={{0,3},{1,2},{4,7},{5,6},{8,11},{9,10},{12,15},{13,14},{16,19},{17,... | collective-permute-start | bytes 798728 | tf_op jit(solution)/shard_map/ppermute | solution.py:337
  7.5 1.3 %collective-permute-start.1 = (bf16[1040,128]{1,0:T(8,128)(2,1)S(1)}, bf16[1040,128]{1,0:T(8,128)(2,1)S(1)}, u32[]{:S(2)}, u32[]{:S(2)}) collective-permute-start(bf16[1040,128]{1,0:T(8,128)(2,1)S(1)} %pack.1), channel_id=1, source_target_pairs={{0,2},{1,3},{4,6},{5,7},{8,10},{9,11},{12,14},{13,15},{16,18},{17,... | collective-permute-start | bytes 798728 | tf_op jit(solution)/shard_map/ppermute | solution.py:337
  8.8 2.5 %collective-permute-start = (bf16[1040,128]{1,0:T(8,128)(2,1)S(1)}, bf16[1040,128]{1,0:T(8,128)(2,1)S(1)}, u32[]{:S(2)}, u32[]{:S(2)}) collective-permute-start(bf16[1040,128]{1,0:T(8,128)(2,1)S(1)} %pack.1), channel_id=1, source_target_pairs={{0,1},{2,3},{4,5},{6,7},{8,9},{10,11},{12,13},{14,15},{16,17},{18,... | collective-permute-start | bytes 798728 | tf_op jit(solution)/shard_map/ppermute | solution.py:337
  11.3 3.0 %collective-permute-done.2.refs_2_ = bf16[1040,128]{1,0:T(8,128)(2,1)S(1)} collective-permute-done((bf16[1040,128]{1,0:T(8,128)(2,1)S(1)}, bf16[1040,128]{1,0:T(8,128)(2,1)S(1)}, u32[]{:S(2)}, u32[]{:S(2)}) %collective-permute-start.2) | collective-permute-done | bytes 266272 | tf_op jit(solution)/shard_map/ppermute | solution.py:337
  14.3 4.5 %collective-permute-done.1.refs_1_ = bf16[1040,128]{1,0:T(8,128)(2,1)S(1)} collective-permute-done((bf16[1040,128]{1,0:T(8,128)(2,1)S(1)}, bf16[1040,128]{1,0:T(8,128)(2,1)S(1)}, u32[]{:S(2)}, u32[]{:S(2)}) %collective-permute-start.1) | collective-permute-done | bytes 266272 | tf_op jit(solution)/shard_map/ppermute | solution.py:337
  18.8 0.1 collective-permute-done.refs_0_
  18.9 11.8 %attend.1 = (bf16[128,4096]{1,0:T(8,128)(2,1)}, bf16[1024,128]{1,0:T(8,128)(2,1)S(1)}, bf16[1024,128]{1,0:T(8,128)(2,1)S(1)}, bf16[1024,128]{1,0:T(8,128)(2,1)S(...) custom-call(s32[1,8]{1,0:T(1,128)} %lengths_ref.1, f32[32]{0:T(128)} %slope_ref.1, f32[32]{0:T(128)} %gain_ref.1, ...), custom_call_target="tpu_custom_call" | custom-call | flops 2684354560 | bytes 5242880 | tf_op jit(solution)/shard_map/attend/pallas_call | solution.py:343
  30.6 1.3 %collective-permute-start.3 = (bf16[1024,128]{1,0:T(8,128)(2,1)S(1)}, bf16[1024,128]{1,0:T(8,128)(2,1)S(1)}, u32[]{:S(2)}, u32[]{:S(2)}) collective-permute-start(bf16[1024,128]{1,0:T(8,128)(2,1)S(1)} %get-tuple-element.14), channel_id=1, source_target_pairs={{1,0},{3,2},{5,4},{7,6},{9,8},{11,10},{13,12},{15,14},{17,16},{19,... | collective-permute-start | bytes 786440 | tf_op jit(solution)/shard_map/ppermute | solution.py:395
  31.9 1.3 %collective-permute-start.4 = (bf16[1024,128]{1,0:T(8,128)(2,1)S(1)}, bf16[1024,128]{1,0:T(8,128)(2,1)S(1)}, u32[]{:S(2)}, u32[]{:S(2)}) collective-permute-start(bf16[1024,128]{1,0:T(8,128)(2,1)S(1)} %get-tuple-element.15), channel_id=1, source_target_pairs={{2,0},{3,1},{6,4},{7,5},{10,8},{11,9},{14,12},{15,13},{18,16},{19,... | collective-permute-start | bytes 786440 | tf_op jit(solution)/shard_map/ppermute | solution.py:395
  33.2 1.3 %collective-permute-start.5 = (bf16[1024,128]{1,0:T(8,128)(2,1)S(1)}, bf16[1024,128]{1,0:T(8,128)(2,1)S(1)}, u32[]{:S(2)}, u32[]{:S(2)}) collective-permute-start(bf16[1024,128]{1,0:T(8,128)(2,1)S(1)} %get-tuple-element.16), channel_id=1, source_target_pairs={{2,1},{3,0},{6,5},{7,4},{10,9},{11,8},{14,13},{15,12},{18,17},{19,... | collective-permute-start | bytes 786440 | tf_op jit(solution)/shard_map/ppermute | solution.py:395
  34.5 16.4 %all_to_all.5.parts_ref = f32[32,8,128]{2,1,0:T(8,128)S(1)} all-to-all(f32[32,8,128]{2,1,0:T(8,128)S(1)} %bitcast.10), channel_id=1, replica_groups=mesh['dp'=8,'ctx'=4] {'dp','ctx'}, dimensions={0} | all-to-all | bytes 262144 | tf_op jit(solution)/shard_map/all_to_all | solution.py:396
  50.9 0.6 %bias.1 = f32[2,8]{1,0:T(2,128)} custom-call(f32[32,8,128]{2,1,0:T(8,128)S(1)} %all_to_all.5.parts_ref), custom_call_target="tpu_custom_call" | custom-call | tf_op jit(solution)/shard_map/bias/pallas_call | solution.py:411
  51.5 0.0 collective-permute-done.3.refs_1_
  51.5 0.0 collective-permute-done.4.refs_2_
  51.5 0.0 collective-permute-done.5.refs_3_
  51.5 0.8 %combine.1 = (bf16[128,512]{1,0:T(8,128)(2,1)}, bf16[128,512]{1,0:T(8,128)(2,1)}) custom-call(bf16[1024,128]{1,0:T(8,128)(2,1)S(1)} %get-tuple-element.13.refs_0_, bf16[1024,128]{1,0:T(8,128)(2,1)S(1)} %collective-permute-done.3.refs_1_, bf16[1024,128]{1,0:T(8,128)(2,1)S(1)} %collective-permute-done.4.refs_2_, ...), custom_call_target="tpu_custom_call" | custom-call | flops 1048576 | bytes 1310720 | tf_op jit(solution)/shard_map/combine/pallas_call | solution.py:398
Async XLA Ops:
  1.7 12.6 %collective-permute-start.2 = (bf16[1040,128]{1,0:T(8,128)(2,1)S(1)}, bf16[1040,128]{1,0:T(8,128)(2,1)S(1)}, u32[]{:S(2)}, u32[]{:S(2)}) collective-permute-start(bf16[1040,128]{1,0:T(8,128)(2,1)S(1)} %pack.1), channel_id=1, source_target_pairs={{0,3},{1,2},{4,7},{5,6},{8,11},{9,10},{12,15},{13,14},{16,19},{17,... | collective-permute-start | bytes 798728 | tf_op jit(solution)/shard_map/ppermute | solution.py:337
  7.5 11.3 %collective-permute-start.1 = (bf16[1040,128]{1,0:T(8,128)(2,1)S(1)}, bf16[1040,128]{1,0:T(8,128)(2,1)S(1)}, u32[]{:S(2)}, u32[]{:S(2)}) collective-permute-start(bf16[1040,128]{1,0:T(8,128)(2,1)S(1)} %pack.1), channel_id=1, source_target_pairs={{0,2},{1,3},{4,6},{5,7},{8,10},{9,11},{12,14},{13,15},{16,18},{17,... | collective-permute-start | bytes 798728 | tf_op jit(solution)/shard_map/ppermute | solution.py:337
  8.8 10.1 %collective-permute-start = (bf16[1040,128]{1,0:T(8,128)(2,1)S(1)}, bf16[1040,128]{1,0:T(8,128)(2,1)S(1)}, u32[]{:S(2)}, u32[]{:S(2)}) collective-permute-start(bf16[1040,128]{1,0:T(8,128)(2,1)S(1)} %pack.1), channel_id=1, source_target_pairs={{0,1},{2,3},{4,5},{6,7},{8,9},{10,11},{12,13},{14,15},{16,17},{18,... | collective-permute-start | bytes 798728 | tf_op jit(solution)/shard_map/ppermute | solution.py:337
  30.6 20.9 %collective-permute-start.3 = (bf16[1024,128]{1,0:T(8,128)(2,1)S(1)}, bf16[1024,128]{1,0:T(8,128)(2,1)S(1)}, u32[]{:S(2)}, u32[]{:S(2)}) collective-permute-start(bf16[1024,128]{1,0:T(8,128)(2,1)S(1)} %get-tuple-element.14), channel_id=1, source_target_pairs={{1,0},{3,2},{5,4},{7,6},{9,8},{11,10},{13,12},{15,14},{17,16},{19,... | collective-permute-start | bytes 786440 | tf_op jit(solution)/shard_map/ppermute | solution.py:395
  31.9 19.6 %collective-permute-start.4 = (bf16[1024,128]{1,0:T(8,128)(2,1)S(1)}, bf16[1024,128]{1,0:T(8,128)(2,1)S(1)}, u32[]{:S(2)}, u32[]{:S(2)}) collective-permute-start(bf16[1024,128]{1,0:T(8,128)(2,1)S(1)} %get-tuple-element.15), channel_id=1, source_target_pairs={{2,0},{3,1},{6,4},{7,5},{10,8},{11,9},{14,12},{15,13},{18,16},{19,... | collective-permute-start | bytes 786440 | tf_op jit(solution)/shard_map/ppermute | solution.py:395
  33.2 18.3 %collective-permute-start.5 = (bf16[1024,128]{1,0:T(8,128)(2,1)S(1)}, bf16[1024,128]{1,0:T(8,128)(2,1)S(1)}, u32[]{:S(2)}, u32[]{:S(2)}) collective-permute-start(bf16[1024,128]{1,0:T(8,128)(2,1)S(1)} %get-tuple-element.16), channel_id=1, source_target_pairs={{2,1},{3,0},{6,5},{7,4},{10,9},{11,8},{14,13},{15,12},{18,17},{19,... | collective-permute-start | bytes 786440 | tf_op jit(solution)/shard_map/ppermute | solution.py:395

commit v2 on v1

v2 whole, which is shorter than its diff:
```python
import functools

import jax
import jax.numpy as jnp
from jax import lax
from jax.experimental import pallas as pl
from jax.experimental.pallas import tpu as pltpu
from jax.sharding import PartitionSpec as P

WIDTH = 128
LOG2E = 1.4426950408889634
MASKED = -1e30
META_ROWS = 16
END_UNIT = 64
CHUNKS = 2


def dot_nt(a, b):
    return lax.dot_general(a, b, (((1,), (1,)), ((), ())), preferred_element_type=jnp.float32)


def dot_nn(a, b):
    return lax.dot_general(a, b, (((1,), (0,)), ((), ())), preferred_element_type=jnp.float32)


def fold_rows(block):
    return jnp.sum(block.reshape(block.shape[0] // 8, 8, block.shape[1]), axis=0)


def as_column(row):
    size = row.shape[1]
    return jnp.transpose(jnp.broadcast_to(row, (size, size)))


def pack_kernel(key_ref, value_ref, depth_ref, end_ref, *message_refs):
    tokens = key_ref.shape[0]
    groups = key_ref.shape[1] // WIDTH // len(message_refs)
    for chunk, message_ref in enumerate(message_refs):
        for kind, ref in enumerate((key_ref, value_ref)):
            for group in range(groups):
                at = (kind * groups + group) * tokens
                source = slice((chunk * groups + group) * WIDTH, (chunk * groups + group + 1) * WIDTH)
                message_ref[at : at + tokens, :] = ref[:, source]
    depth = depth_ref[...]
    end = end_ref[...]
    end_high = end // END_UNIT
    end_low = end - end_high * END_UNIT
    row = lax.broadcasted_iota(jnp.int32, (META_ROWS, tokens), 0)
    meta = jnp.where(row == 0, depth, jnp.where(row == 1, end_high, end_low))
    meta = meta.astype(jnp.float32).astype(jnp.bfloat16)
    message_refs[0][2 * groups * tokens : 2 * groups * tokens + META_ROWS, :] = meta


def fill_tables(
    blocks, groups, lengths_ref, depth_ref, end_ref, remote, distance_ref, ancestor_ref
):
    tokens = depth_ref.shape[1]
    here = lax.axis_index("ctx")
    query_pos = here * tokens + lax.broadcasted_iota(jnp.int32, (tokens, tokens), 1)
    start = jnp.zeros((tokens, tokens), jnp.int32)
    bound = jnp.int32(0)
    for index in range(lengths_ref.shape[1]):
        bound = bound + lengths_ref[0, index]
        start = jnp.where(query_pos >= bound, bound, start)
    query_depth = jnp.broadcast_to(depth_ref[...].astype(jnp.float32), (tokens, tokens))
    for s in range(blocks):
        rows = slice(s * tokens, (s + 1) * tokens)
        key_pos = (here ^ s) * tokens + lax.broadcasted_iota(jnp.int32, (tokens, tokens), 0)
        if s == 0:
            key_depth = as_column(depth_ref[...].astype(jnp.float32))
            key_end = as_column(end_ref[...].astype(jnp.float32))
        else:
            below = slice(2 * groups * tokens, 2 * groups * tokens + META_ROWS)
            meta = remote[s - 1][below, :].astype(jnp.float32)
            key_depth = as_column(meta[0:1])
            key_end = as_column(meta[1:2] * END_UNIT + meta[2:3])
        inside = query_pos.astype(jnp.float32) < key_end
        allowed = (key_pos <= query_pos) & (key_pos >= start)
        distance_ref[rows, :] = jnp.abs(query_depth - key_depth)
        ancestor_ref[rows, :] = jnp.where(allowed, jnp.where(inside, 1.0, 0.0), MASKED)


def main_kernel(blocks, heads_per_group, groups, chunk, last_chunk, *refs):
    refs = list(refs)
    take = lambda count: [refs.pop(0) for _ in range(count)]
    slope_ref, gain_ref, query_hbm, output_hbm, grad_hbm, key_ref, value_ref = take(7)
    remote = take(blocks - 1)
    if chunk == 0:
        lengths_ref, depth_ref, end_ref = take(3)
    else:
        distance_ref, ancestor_ref, sums_before = take(3)
        parts_before = take(blocks)
        take(1)
    (query_grad_hbm,) = take(1)
    part_refs = take(blocks)
    if chunk == 0:
        distance_ref, ancestor_ref = take(2)
    if last_chunk:
        (bias_ref,) = take(1)
        sums_ref = refs.pop()
    else:
        (sums_ref,) = take(1)
    (
        query_ref,
        output_ref,
        grad_ref,
        query_grad_ref,
        weight_ref,
        probs_ref,
        dscore_ref,
        load_sems,
        store_sems,
    ) = refs
    tokens = query_hbm.shape[0]
    factor = WIDTH**-0.5
    group_columns = heads_per_group * WIDTH
    pairs = heads_per_group // 2
    first_group = chunk * groups
    block_rows = [slice(s * tokens, (s + 1) * tokens) for s in range(blocks)]

    def load(group, index):
        wide = pl.ds((first_group + group) * group_columns, group_columns)
        source = (query_hbm, output_hbm, grad_hbm)[index]
        to = (query_ref, output_ref, grad_ref)[index]
        return pltpu.make_async_copy(
            source.at[:, wide], to.at[group], load_sems.at[3 * group + index]
        )

    def store(group):
        wide = pl.ds((first_group + group) * group_columns, group_columns)
        return pltpu.make_async_copy(
            query_grad_ref.at[group], query_grad_hbm.at[:, wide], store_sems.at[group]
        )

    for group in range(groups):
        for index in range(3):
            load(group, index).start()

    if chunk == 0:
        fill_tables(
            blocks, groups, lengths_ref, depth_ref, end_ref, remote, distance_ref, ancestor_ref
        )
    else:
        before = groups * chunk
        for s in range(blocks):
            for kind in range(2):
                part_refs[s][
                    kind * (before + groups) * tokens : (kind * (before + groups) + before) * tokens, :
                ] = parts_before[s][kind * before * tokens : (kind + 1) * before * tokens, :]

    def own_and_remote(ref, kind, group):
        own = ref[:, (first_group + group) * WIDTH : (first_group + group + 1) * WIDTH]
        at = (kind * groups + group) * tokens
        return jnp.concatenate([own] + [r[at : at + tokens, :] for r in remote], axis=0)

    def stacked(ref, group, first, count):
        heads = [slice((first + i) * WIDTH, (first + i + 1) * WIDTH) for i in range(count)]
        return jnp.concatenate([ref[group, :, h] for h in heads], axis=0)

    def weigh(group, pair, raw, half):
        head = (first_group + group) * heads_per_group + 2 * pair + half
        gain = gain_ref[head] * LOG2E
        slope = slope_ref[head] * LOG2E
        lanes = slice(half * tokens, (half + 1) * tokens)
        tops, totals = [], []
        for s, rows in enumerate(block_rows):
            score = raw[s][:, lanes] * (factor * LOG2E) + (
                gain * ancestor_ref[rows, :] - slope * distance_ref[rows, :]
            )
            top = jnp.max(score, axis=0, keepdims=True)
            weight = jnp.exp2(score - top)
            weight_ref[pair % 2, rows, lanes] = weight
            tops.append(top)
            totals.append(jnp.sum(weight, axis=0, keepdims=True))
        top = functools.reduce(jnp.maximum, tops)
        shrink = [jnp.exp2(t - top) for t in tops]
        inverse = 1.0 / sum(a * b for a, b in zip(totals, shrink))
        return [s * inverse for s in shrink]

    def differentiate(group, pair, slot, centred, scales, half):
        lanes = slice(half * tokens, (half + 1) * tokens)
        to = slice((2 * pair + half) * tokens, (2 * pair + half + 1) * tokens)
        slope_sum, gain_sum = 0.0, 0.0
        for s, rows in enumerate(block_rows):
            probs = weight_ref[pair % 2, rows, lanes] * scales[s]
            dscore = probs * centred[s][:, lanes]
            probs_ref[slot, rows, to] = probs.astype(jnp.bfloat16)
            dscore_ref[slot, rows, to] = dscore.astype(jnp.bfloat16)
            slope_sum = slope_sum + fold_rows(dscore * distance_ref[rows, :])
            gain_sum = gain_sum + fold_rows(dscore * ancestor_ref[rows, :])
        at = (first_group + group) * heads_per_group + 2 * pair + half
        sums_ref[0, at : at + 1, :] = -jnp.sum(slope_sum, axis=0, keepdims=True)
        sums_ref[1, at : at + 1, :] = jnp.sum(gain_sum, axis=0, keepdims=True)

    def put_part(group, kind, whole):
        at = (kind * (first_group + groups) + first_group + group) * tokens
        for s, rows in enumerate(block_rows):
            part_refs[s][at : at + tokens, :] = whole[rows].astype(jnp.bfloat16)

    def key_part(group, slot):
        heads = stacked(query_ref, group, 0, heads_per_group)
        put_part(group, 0, dot_nn(dscore_ref[slot], heads) * factor)

    def value_part(group, slot):
        heads = stacked(grad_ref, group, 0, heads_per_group)
        put_part(group, 1, dot_nn(probs_ref[slot], heads))

    def query_part(keys_across, group, slot, pair):
        lanes = slice(2 * pair * tokens, (2 * pair + 2) * tokens)
        across = dot_nn(keys_across, dscore_ref[slot, :, lanes]) * factor
        rows = jnp.transpose(across.astype(jnp.bfloat16))
        for half in range(2):
            at = (2 * pair + half) * WIDTH
            query_grad_ref[group, :, at : at + WIDTH] = rows[half * tokens : (half + 1) * tokens]

    def products(left, right):
        whole = dot_nt(left, right)
        return [whole[rows] for rows in block_rows]

    def advance(group, before):
        if group is not None:
            slot = group % 2
            keys = own_and_remote(key_ref, 0, group)
            values = own_and_remote(value_ref, 1, group)
            minus = jnp.full(values.shape, -1.0, jnp.bfloat16)
            value_ext = jnp.concatenate([values, minus], axis=1)
        if before is not None:
            before_slot = before % 2
            keys_across = jnp.transpose(own_and_remote(key_ref, 0, before))
        for pair in range(pairs):
            if group is not None:
                query_pair = stacked(query_ref, group, 2 * pair, 2)
                grad_pair = stacked(grad_ref, group, 2 * pair, 2)
                output_pair = stacked(output_ref, group, 2 * pair, 2)
                grad_ext = jnp.concatenate([grad_pair, grad_pair * output_pair], axis=1)
                raw = products(keys, query_pair)
                scales = [weigh(group, pair, raw, half) for half in range(2)]
            if before is not None and pair == 0:
                key_part(before, before_slot)
            if before is not None and pair == 1:
                value_part(before, before_slot)
            if group is not None:
                centred = products(value_ext, grad_ext)
                for half in range(2):
                    differentiate(group, pair, slot, centred, scales[half], half)
            if before is not None:
                query_part(keys_across, before, before_slot, pair)

    for group in range(groups):
        for index in range(3):
            load(group, index).wait()
        advance(group, group - 1 if group else None)
        if group:
            store(group - 1).start()
    advance(None, groups - 1)
    store(groups - 1).start()

    if last_chunk:
        heads = heads_per_group * first_group
        rows = [
            jnp.concatenate([sums_before[kind, 0:heads, :], sums_ref[kind, heads:, :]], axis=0)
            for kind in range(2)
        ]
        sums = [jnp.sum(r, axis=1, keepdims=True) for r in rows]
        shape = rows[0].shape
        diagonal = lax.broadcasted_iota(jnp.int32, shape, 0) == lax.broadcasted_iota(
            jnp.int32, shape, 1
        )
        lines = [
            jnp.sum(jnp.where(diagonal, column, 0.0), axis=0, keepdims=True) for column in sums
        ]
        row = lax.broadcasted_iota(jnp.int32, bias_ref.shape[1:], 0)
        tile = jnp.where(row == 0, lines[0], jnp.where(row == 1, lines[1], 0.0))
        bias_ref[...] = jnp.broadcast_to(tile[None], bias_ref.shape)
    for group in range(groups):
        store(group).wait()


def combine_kernel(blocks, *refs):
    parts = refs[0:blocks]
    key_out, value_out = refs[blocks:]
    tokens = key_out.shape[0]
    groups = key_out.shape[1] // WIDTH
    for kind, out in enumerate((key_out, value_out)):
        for group in range(groups):
            at = (kind * groups + group) * tokens
            total = parts[0][at : at + tokens, :].astype(jnp.float32)
            for s in range(1, blocks):
                total = total + parts[s][at : at + tokens, :].astype(jnp.float32)
            out[:, group * WIDTH : (group + 1) * WIDTH] = total.astype(jnp.bfloat16)


def spread_kernel(sums_ref, spread_ref):
    total = jnp.sum(sums_ref[...], axis=0)
    share = spread_ref.shape[2]
    for block in range(spread_ref.shape[0]):
        spread_ref[block] = total[:, block * share : (block + 1) * share]


def bias_kernel(parts_ref, out_ref):
    out_ref[...] = jnp.sum(parts_ref[...], axis=0)[0:2]


def body(
    queries,
    key_rows,
    values,
    outputs,
    out_grads,
    depths,
    subtree_end,
    file_lengths,
    slopes,
    ancestor_gain,
):
    blocks = lax.axis_size("ctx")
    replicas = lax.axis_size("dp")
    tokens, width_all = queries.shape[1:]
    kv_width = key_rows.shape[2]
    heads_all = width_all // WIDTH
    kv_heads = kv_width // WIDTH
    heads_per_group = heads_all // kv_heads
    group_columns = heads_per_group * WIDTH
    local_heads = heads_all // blocks
    keys_seen = blocks * tokens
    groups = kv_heads // CHUNKS
    bf16, f32 = jnp.bfloat16, jnp.float32
    vmem = pl.BlockSpec(memory_space=pltpu.VMEM)
    smem = pl.BlockSpec(memory_space=pltpu.SMEM)
    hbm = pl.BlockSpec(memory_space=pltpu.HBM)
    params = pltpu.CompilerParams(vmem_limit_bytes=(36 if blocks <= 4 else 48) * 1024 * 1024)

    def hold(array):
        return pltpu.with_memory_space_constraint(array, pltpu.HBM)

    def struct(shape, dtype):
        return jax.ShapeDtypeStruct(shape, dtype)

    key_held, value_held = hold(key_rows[0]), hold(values[0])
    depth_held, end_held = hold(depths), hold(subtree_end)
    chunk_rows = 2 * groups * tokens
    messages = pl.pallas_call(
        pack_kernel,
        out_shape=[
            struct((chunk_rows + (0 if chunk else META_ROWS), WIDTH), bf16)
            for chunk in range(CHUNKS)
        ],
        in_specs=[vmem] * 4,
        out_specs=[vmem] * CHUNKS,
        compiler_params=params,
        name="pack",
    )(key_held, value_held, depth_held, end_held)
    arrived = [
        [
            lax.ppermute(message, "ctx", [(i, i ^ s) for i in range(blocks) if i < i ^ s])
            for s in range(1, blocks)
        ]
        for message in messages
    ]

    matmul_flops = 2 * tokens * keys_seen * WIDTH * heads_all
    table = struct((keys_seen, tokens), f32)
    sums = struct((2, heads_all, tokens), f32)
    for chunk in range(CHUNKS):
        last_chunk = chunk == CHUNKS - 1
        operands = [
            hold(slopes),
            hold(ancestor_gain),
            hold(queries[0]),
            hold(outputs[0]),
            hold(out_grads[0]),
            key_held,
            value_held,
            *arrived[chunk],
        ]
        specs = [smem] * 2 + [hbm] * 3 + [vmem] * (1 + blocks)
        part = struct(((chunk + 1) * chunk_rows, WIDTH), bf16)
        out_shape = [struct((tokens, width_all), bf16)] + [part] * blocks
        aliases = {}
        if chunk == 0:
            operands = operands + [hold(file_lengths), depth_held, end_held]
            specs = specs + [smem, vmem, vmem]
            out_shape = out_shape + [table, table]
        else:
            operands = operands + [*tables, sums_before, *parts, query_grads]
            specs = specs + [vmem] * (3 + blocks) + [hbm]
            aliases = {len(operands) - 1: 0}
        out_shape = out_shape + [struct((replicas, 8, WIDTH), f32) if last_chunk else sums]
        scratch = [
            pltpu.VMEM((groups, tokens, group_columns), bf16),
            pltpu.VMEM((groups, tokens, group_columns), bf16),
            pltpu.VMEM((groups, tokens, group_columns), bf16),
            pltpu.VMEM((groups, tokens, group_columns), bf16),
            pltpu.VMEM((2, keys_seen, 2 * tokens), f32),
            pltpu.VMEM((2, keys_seen, group_columns), bf16),
            pltpu.VMEM((2, keys_seen, group_columns), bf16),
            pltpu.SemaphoreType.DMA((3 * groups,)),
            pltpu.SemaphoreType.DMA((groups,)),
        ]
        if last_chunk:
            scratch = scratch + [pltpu.VMEM(sums.shape, f32)]
        results = pl.pallas_call(
            functools.partial(main_kernel, blocks, heads_per_group, groups, chunk, last_chunk),
            out_shape=out_shape,
            in_specs=specs,
            out_specs=[hbm] + [vmem] * (len(out_shape) - 1),
            scratch_shapes=scratch,
            input_output_aliases=aliases,
            compiler_params=params,
            cost_estimate=pl.CostEstimate(
                flops=5 * matmul_flops // CHUNKS,
                bytes_accessed=10 * tokens * width_all // CHUNKS,
                transcendentals=tokens * keys_seen * heads_all // CHUNKS,
            ),
            name=f"attend_{chunk}",
        )(*operands)
        query_grads = results[0]
        parts = list(results[1 : 1 + blocks])
        if chunk == 0:
            tables = results[1 + blocks : 3 + blocks]
        sums_before = results[-1]

    for s in range(1, blocks):
        back = [(i, i ^ s) for i in range(blocks) if i > i ^ s]
        parts[s] = lax.ppermute(parts[s], "ctx", back)
    sums_of_all = lax.all_to_all(sums_before, "dp", split_axis=0, concat_axis=0, tiled=True)
    spread = pl.pallas_call(
        spread_kernel,
        out_shape=struct((blocks, 8, local_heads), f32),
        in_specs=[vmem],
        out_specs=vmem,
        compiler_params=params,
        name="spread",
    )(sums_of_all)
    bias_parts = lax.all_to_all(spread, "ctx", split_axis=0, concat_axis=0, tiled=True)
    bias_grads = pl.pallas_call(
        bias_kernel,
        out_shape=struct((2, local_heads), f32),
        in_specs=[vmem],
        out_specs=vmem,
        compiler_params=params,
        name="bias",
    )(bias_parts)
    key_grads, value_grads = pl.pallas_call(
        functools.partial(combine_kernel, blocks),
        out_shape=[struct((tokens, kv_width), bf16)] * 2,
        in_specs=[vmem] * blocks,
        out_specs=[vmem] * 2,
        compiler_params=params,
        name="combine",
    )(*parts)
    return (query_grads[None], key_grads[None], value_grads[None], bias_grads.T)


def solution(mesh):
    in_specs = (
        P("dp", "ctx", None),
        P("dp", "ctx", None),
        P("dp", "ctx", None),
        P("dp", "ctx", None),
        P("dp", "ctx", None),
        P("dp", "ctx"),
        P("dp", "ctx"),
        P("dp", None),
        P(),
        P(),
    )
    out_specs = (P("dp", "ctx", None), P("dp", "ctx", None), P("dp", "ctx", None), P("ctx", None))
    return jax.shard_map(body, mesh=mesh, in_specs=in_specs, out_specs=out_specs, check_vma=False)
```

time: 52.6 us -> 58.7 us (1.12)
  waiting for transfers between devices: 7.58 us -> 0.02 us
  starting transfers between devices: 13.5 us -> 19.4 us
  blocking collectives: 16.4 us -> 21 us
  Pallas kernels: 14.2 us -> 17.1 us
    ppermute x3 -> x6, waiting for transfers between devices: 7.57 us -> 0.02 us  [body(): lax.ppermute(message, 'ctx', [(i, i ^ s) for i in range(blocks) if i < i...]
    ppermute x3 -> x6, starting transfers between devices: 9.59 us -> 15.5 us  [body(): lax.ppermute(message, 'ctx', [(i, i ^ s) for i in range(blocks) if i < i...]
    all_to_all x1 -> x2, blocking collectives: 16.4 us -> 21 us  [the longest x1 10.5 us: body(): lax.all_to_all(spread, 'ctx', split_axis=0, concat_axis=0, tiled=True)]
    pallas_call x1 -> x2, Pallas kernels: 11.8 us -> 14.7 us  [body(): pl.pallas_call(functools.partial(main_kernel, blocks, heads_per_group, gr...]
    pallas_call x3 -> x4, Pallas kernels: 2.44 us -> 2.47 us  [the longest x1 1.03 us: body(): pl.pallas_call(pack_kernel, out_shape=[struct((chunk_rows + (0 if chunk e...]
  transfers between devices with their start and end apart: 6 -> 9, of which waited for: 3 -> 0; matrix products, arithmetic and copies ran while one was open for 0% -> 0% of each run, Pallas kernels for 1% -> 14%
where the time goes in v2:
time: 58.7 us; the launch traced here: 58.3 us
  blocking collectives  21 us (36%)
  starting transfers between devices  19.4 us (33%)
  Pallas kernels  17.1 us (29%)
  between operations  0.77 us (1%)
    ppermute x6, starting transfers between devices, body(): lax.ppermute(message, 'ctx', [(i, i ^ s) for i in range(blocks) if i < i...  15.5 us
    pallas_call x2, Pallas kernels, body(): pl.pallas_call(functools.partial(main_kernel, blocks, heads_per_group, gr...  14.7 us
    all_to_all x1, blocking collectives, body(): lax.all_to_all(spread, 'ctx', split_axis=0, concat_axis=0, tiled=True)  10.5 us
    all_to_all x1, blocking collectives, body(): lax.all_to_all(sums_before, 'dp', split_axis=0, concat_axis=0, tiled=True)  10.4 us
    ppermute x3, starting transfers between devices, body(): parts[s] = lax.ppermute(parts[s], 'ctx', back)  3.88 us
  transfers between devices with their start and end apart: 9, of which 0 were waited for; matrix products, arithmetic and copies ran while one was open for 0% of the time, Pallas kernels for 14%

profile of v2, /device:TPU:0, one launch (start us, length us, event | category | flops | bytes accessed | tf_op | source)
XLA Modules:
  0.0 58.3 jit_solution(7794169973861906741)
XLA Ops:
  0.6 1.0 %pack.1 = (bf16[528,128]{1,0:T(8,128)(2,1)S(1)}, bf16[512,128]{1,0:T(8,128)(2,1)S(1)}) custom-call(bf16[128,512]{1,0:T(8,128)(2,1)} %bitcast.16, bf16[128,512]{1,0:T(8,128)(2,1)} %bitcast.19, s32[1,128]{1,0:T(1,128)} %refs_11_.1, s32[1,128]{1,0:T(1,128)} %refs_12_.1), custom_call_target="tpu_custom_call" | custom-call | tf_op jit(solution)/shard_map/pack/pallas_call | solution.py:342
  1.7 5.8 %collective-permute-start.5 = (bf16[528,128]{1,0:T(8,128)(2,1)S(1)}, bf16[528,128]{1,0:T(8,128)(2,1)S(1)}, u32[]{:S(2)}, u32[]{:S(2)}) collective-permute-start(bf16[528,128]{1,0:T(8,128)(2,1)S(1)} %get-tuple-element.23), channel_id=1, source_target_pairs={{0,3},{1,2},{4,7},{5,6},{8,11},{9,10},{12,15},{13,14},{16,19},{17,... | collective-permute-start | bytes 405512 | tf_op jit(solution)/shard_map/ppermute | solution.py:355
  7.5 1.3 %collective-permute-start.4 = (bf16[528,128]{1,0:T(8,128)(2,1)S(1)}, bf16[528,128]{1,0:T(8,128)(2,1)S(1)}, u32[]{:S(2)}, u32[]{:S(2)}) collective-permute-start(bf16[528,128]{1,0:T(8,128)(2,1)S(1)} %get-tuple-element.23), channel_id=1, source_target_pairs={{0,2},{1,3},{4,6},{5,7},{8,10},{9,11},{12,14},{13,15},{16,18},{17,... | collective-permute-start | bytes 405512 | tf_op jit(solution)/shard_map/ppermute | solution.py:355
  8.8 2.5 %collective-permute-start.3 = (bf16[528,128]{1,0:T(8,128)(2,1)S(1)}, bf16[528,128]{1,0:T(8,128)(2,1)S(1)}, u32[]{:S(2)}, u32[]{:S(2)}) collective-permute-start(bf16[528,128]{1,0:T(8,128)(2,1)S(1)} %get-tuple-element.23), channel_id=1, source_target_pairs={{0,1},{2,3},{4,5},{6,7},{8,9},{10,11},{12,13},{14,15},{16,17},{18,... | collective-permute-start | bytes 405512 | tf_op jit(solution)/shard_map/ppermute | solution.py:355
  11.3 1.3 %collective-permute-start.2 = (bf16[512,128]{1,0:T(8,128)(2,1)S(1)}, bf16[512,128]{1,0:T(8,128)(2,1)S(1)}, u32[]{:S(2)}, u32[]{:S(2)}) collective-permute-start(bf16[512,128]{1,0:T(8,128)(2,1)S(1)} %get-tuple-element.22), channel_id=1, source_target_pairs={{0,3},{1,2},{4,7},{5,6},{8,11},{9,10},{12,15},{13,14},{16,19},{17,... | collective-permute-start | bytes 393224 | tf_op jit(solution)/shard_map/ppermute | solution.py:355
  12.6 1.3 %collective-permute-start.1 = (bf16[512,128]{1,0:T(8,128)(2,1)S(1)}, bf16[512,128]{1,0:T(8,128)(2,1)S(1)}, u32[]{:S(2)}, u32[]{:S(2)}) collective-permute-start(bf16[512,128]{1,0:T(8,128)(2,1)S(1)} %get-tuple-element.22), channel_id=1, source_target_pairs={{0,2},{1,3},{4,6},{5,7},{8,10},{9,11},{12,14},{13,15},{16,18},{17,... | collective-permute-start | bytes 393224 | tf_op jit(solution)/shard_map/ppermute | solution.py:355
  13.9 0.0 collective-permute-done.5.refs_9_
  13.9 3.4 %collective-permute-start = (bf16[512,128]{1,0:T(8,128)(2,1)S(1)}, bf16[512,128]{1,0:T(8,128)(2,1)S(1)}, u32[]{:S(2)}, u32[]{:S(2)}) collective-permute-start(bf16[512,128]{1,0:T(8,128)(2,1)S(1)} %get-tuple-element.22), channel_id=1, source_target_pairs={{0,1},{2,3},{4,5},{6,7},{8,9},{10,11},{12,13},{14,15},{16,17},{18,... | collective-permute-start | bytes 393224 | tf_op jit(solution)/shard_map/ppermute | solution.py:355
  17.3 0.0 collective-permute-done.4.refs_8_
  17.3 0.0 collective-permute-done.3.refs_7_
  17.3 7.4 %attend_0.1 = (bf16[128,4096]{1,0:T(8,128)(2,1)}, bf16[512,128]{1,0:T(8,128)(2,1)S(1)}, bf16[512,128]{1,0:T(8,128)(2,1)S(1)}, bf16[512,128]{1,0:T(8,128)(2,1)S(1...) custom-call(f32[32]{0:T(128)} %refs_0_.3, ...), custom_call_target="tpu_custom_call" | custom-call | flops 1342177280 | bytes 2621440 | tf_op jit(solution)/shard_map/attend_0/pallas_call | solution.py:402
  24.7 0.0 collective-permute-done.2.refs_9_
  24.7 0.0 collective-permute-done.1.refs_8_
  24.7 0.0 collective-permute-done.refs_7_
  24.7 7.3 %attend_1.1 = (bf16[128,4096]{1,0:T(8,128)(2,1)}, bf16[1024,128]{1,0:T(8,128)(2,1)S(1)}, bf16[1024,128]{1,0:T(8,128)(2,1)S(1)}, bf16[1024,128]{1,0:T(8,128)(2,1)...) custom-call(f32[32]{0:T(128)} %refs_0_.3, f32[32]{0:T(128)} %refs_1_.3, ...), custom_call_target="tpu_custom_call", output_to_operand_aliasing={{0}: (17, {})} | custom-call | flops 1342177280 | bytes 2621440 | tf_op jit(solution)/shard_map/attend_1/pallas_call | solution.py:402
  32.0 1.3 %collective-permute-start.6 = (bf16[1024,128]{1,0:T(8,128)(2,1)S(1)}, bf16[1024,128]{1,0:T(8,128)(2,1)S(1)}, u32[]{:S(2)}, u32[]{:S(2)}) collective-permute-start(bf16[1024,128]{1,0:T(8,128)(2,1)S(1)} %get-tuple-element.34), channel_id=1, source_target_pairs={{1,0},{3,2},{5,4},{7,6},{9,8},{11,10},{13,12},{15,14},{17,16},{19,... | collective-permute-start | bytes 786440 | tf_op jit(solution)/shard_map/ppermute | solution.py:425
  33.3 1.3 %collective-permute-start.7 = (bf16[1024,128]{1,0:T(8,128)(2,1)S(1)}, bf16[1024,128]{1,0:T(8,128)(2,1)S(1)}, u32[]{:S(2)}, u32[]{:S(2)}) collective-permute-start(bf16[1024,128]{1,0:T(8,128)(2,1)S(1)} %get-tuple-element.35), channel_id=1, source_target_pairs={{2,0},{3,1},{6,4},{7,5},{10,8},{11,9},{14,12},{15,13},{18,16},{19,... | collective-permute-start | bytes 786440 | tf_op jit(solution)/shard_map/ppermute | solution.py:425
  34.6 1.3 %collective-permute-start.8 = (bf16[1024,128]{1,0:T(8,128)(2,1)S(1)}, bf16[1024,128]{1,0:T(8,128)(2,1)S(1)}, u32[]{:S(2)}, u32[]{:S(2)}) collective-permute-start(bf16[1024,128]{1,0:T(8,128)(2,1)S(1)} %get-tuple-element.36), channel_id=1, source_target_pairs={{2,1},{3,0},{6,5},{7,4},{10,9},{11,8},{14,13},{15,12},{18,17},{19,... | collective-permute-start | bytes 786440 | tf_op jit(solution)/shard_map/ppermute | solution.py:425
  35.9 10.4 %all_to_all.10.sums_ref = f32[8,8,128]{2,1,0:T(8,128)S(1)} all-to-all(f32[8,8,128]{2,1,0:T(8,128)S(1)} %get-tuple-element.39), channel_id=1, replica_groups=mesh['dp'=8,'ctx'=4] {'dp'}, dimensions={0} | all-to-all | bytes 65536 | tf_op jit(solution)/shard_map/all_to_all | solution.py:426
  46.3 0.1 spread.1
  46.4 10.5 %all_to_all.11.parts_ref = f32[4,8,8]{2,1,0:T(8,128)S(1)} all-to-all(f32[4,8,8]{2,1,0:T(8,128)S(1)} %spread.1), channel_id=1, replica_groups=mesh['dp'=8,'ctx'=4] {'ctx'}, dimensions={0} | all-to-all | bytes 2048 | tf_op jit(solution)/shard_map/all_to_all | solution.py:435
  56.9 0.6 bias.1
  57.5 0.0 collective-permute-done.6.refs_1_
  57.5 0.8 %combine.1 = (bf16[128,512]{1,0:T(8,128)(2,1)}, bf16[128,512]{1,0:T(8,128)(2,1)}) custom-call(bf16[1024,128]{1,0:T(8,128)(2,1)S(1)} %get-tuple-element.33.refs_0_, bf16[1024,128]{1,0:T(8,128)(2,1)S(1)} %collective-permute-done.6.refs_1_, bf16[1024,128]{1,0:T(8,128)(2,1)S(1)} %collective-permute-done.7.refs_2_, ...), custom_call_target="tpu_custom_call" | custom-call | tf_op jit(solution)/shard_map/combine/pallas_call | solution.py:444
  (2 shorter events, 0.0 us)
Async XLA Ops:
  1.7 12.2 %collective-permute-start.5 = (bf16[528,128]{1,0:T(8,128)(2,1)S(1)}, bf16[528,128]{1,0:T(8,128)(2,1)S(1)}, u32[]{:S(2)}, u32[]{:S(2)}) collective-permute-start(bf16[528,128]{1,0:T(8,128)(2,1)S(1)} %get-tuple-element.23), channel_id=1, source_target_pairs={{0,3},{1,2},{4,7},{5,6},{8,11},{9,10},{12,15},{13,14},{16,19},{17,... | collective-permute-start | bytes 405512 | tf_op jit(solution)/shard_map/ppermute | solution.py:355
  7.5 9.8 %collective-permute-start.4 = (bf16[528,128]{1,0:T(8,128)(2,1)S(1)}, bf16[528,128]{1,0:T(8,128)(2,1)S(1)}, u32[]{:S(2)}, u32[]{:S(2)}) collective-permute-start(bf16[528,128]{1,0:T(8,128)(2,1)S(1)} %get-tuple-element.23), channel_id=1, source_target_pairs={{0,2},{1,3},{4,6},{5,7},{8,10},{9,11},{12,14},{13,15},{16,18},{17,... | collective-permute-start | bytes 405512 | tf_op jit(solution)/shard_map/ppermute | solution.py:355
  8.8 8.5 %collective-permute-start.3 = (bf16[528,128]{1,0:T(8,128)(2,1)S(1)}, bf16[528,128]{1,0:T(8,128)(2,1)S(1)}, u32[]{:S(2)}, u32[]{:S(2)}) collective-permute-start(bf16[528,128]{1,0:T(8,128)(2,1)S(1)} %get-tuple-element.23), channel_id=1, source_target_pairs={{0,1},{2,3},{4,5},{6,7},{8,9},{10,11},{12,13},{14,15},{16,17},{18,... | collective-permute-start | bytes 405512 | tf_op jit(solution)/shard_map/ppermute | solution.py:355
  11.3 13.4 %collective-permute-start.2 = (bf16[512,128]{1,0:T(8,128)(2,1)S(1)}, bf16[512,128]{1,0:T(8,128)(2,1)S(1)}, u32[]{:S(2)}, u32[]{:S(2)}) collective-permute-start(bf16[512,128]{1,0:T(8,128)(2,1)S(1)} %get-tuple-element.22), channel_id=1, source_target_pairs={{0,3},{1,2},{4,7},{5,6},{8,11},{9,10},{12,15},{13,14},{16,19},{17,... | collective-permute-start | bytes 393224 | tf_op jit(solution)/shard_map/ppermute | solution.py:355
  12.6 12.1 %collective-permute-start.1 = (bf16[512,128]{1,0:T(8,128)(2,1)S(1)}, bf16[512,128]{1,0:T(8,128)(2,1)S(1)}, u32[]{:S(2)}, u32[]{:S(2)}) collective-permute-start(bf16[512,128]{1,0:T(8,128)(2,1)S(1)} %get-tuple-element.22), channel_id=1, source_target_pairs={{0,2},{1,3},{4,6},{5,7},{8,10},{9,11},{12,14},{13,15},{16,18},{17,... | collective-permute-start | bytes 393224 | tf_op jit(solution)/shard_map/ppermute | solution.py:355
  13.9 10.8 %collective-permute-start = (bf16[512,128]{1,0:T(8,128)(2,1)S(1)}, bf16[512,128]{1,0:T(8,128)(2,1)S(1)}, u32[]{:S(2)}, u32[]{:S(2)}) collective-permute-start(bf16[512,128]{1,0:T(8,128)(2,1)S(1)} %get-tuple-element.22), channel_id=1, source_target_pairs={{0,1},{2,3},{4,5},{6,7},{8,9},{10,11},{12,13},{14,15},{16,17},{18,... | collective-permute-start | bytes 393224 | tf_op jit(solution)/shard_map/ppermute | solution.py:355
  32.0 25.5 %collective-permute-start.6 = (bf16[1024,128]{1,0:T(8,128)(2,1)S(1)}, bf16[1024,128]{1,0:T(8,128)(2,1)S(1)}, u32[]{:S(2)}, u32[]{:S(2)}) collective-permute-start(bf16[1024,128]{1,0:T(8,128)(2,1)S(1)} %get-tuple-element.34), channel_id=1, source_target_pairs={{1,0},{3,2},{5,4},{7,6},{9,8},{11,10},{13,12},{15,14},{17,16},{19,... | collective-permute-start | bytes 786440 | tf_op jit(solution)/shard_map/ppermute | solution.py:425
  33.3 24.2 %collective-permute-start.7 = (bf16[1024,128]{1,0:T(8,128)(2,1)S(1)}, bf16[1024,128]{1,0:T(8,128)(2,1)S(1)}, u32[]{:S(2)}, u32[]{:S(2)}) collective-permute-start(bf16[1024,128]{1,0:T(8,128)(2,1)S(1)} %get-tuple-element.35), channel_id=1, source_target_pairs={{2,0},{3,1},{6,4},{7,5},{10,8},{11,9},{14,12},{15,13},{18,16},{19,... | collective-permute-start | bytes 786440 | tf_op jit(solution)/shard_map/ppermute | solution.py:425
  34.6 22.9 %collective-permute-start.8 = (bf16[1024,128]{1,0:T(8,128)(2,1)S(1)}, bf16[1024,128]{1,0:T(8,128)(2,1)S(1)}, u32[]{:S(2)}, u32[]{:S(2)}) collective-permute-start(bf16[1024,128]{1,0:T(8,128)(2,1)S(1)} %get-tuple-element.36), channel_id=1, source_target_pairs={{2,1},{3,0},{6,5},{7,4},{10,9},{11,8},{14,13},{15,12},{18,17},{19,... | collective-permute-start | bytes 786440 | tf_op jit(solution)/shard_map/ppermute | solution.py:425

commit v3 on v1

--- a/solution.py
+++ b/solution.py
@@ -74,13 +74,12 @@
         output_ref,
         grad_ref,
         query_grad_ref,
-        keys_ref,
-        keys_across_ref,
-        value_ext_ref,
         distance_ref,
         ancestor_ref,
         slope_rows,
         gain_rows,
+        key_acc,
+        value_acc,
         weight_ref,
         probs_ref,
         dscore_ref,
@@ -135,19 +134,15 @@
         distance_ref[rows, :] = jnp.abs(query_depth - key_depth)
         ancestor_ref[rows, :] = jnp.where(allowed, jnp.where(inside, 1.0, 0.0), MASKED)
 
-    for group in range(groups):
-        for s, rows in enumerate(block_rows):
-            if s == 0:
-                key = key_ref[:, group * WIDTH : (group + 1) * WIDTH]
-                value = value_ref[:, group * WIDTH : (group + 1) * WIDTH]
-            else:
-                key = remote[s - 1][group * tokens : (group + 1) * tokens, :]
-                at = (groups + group) * tokens
-                value = remote[s - 1][at : at + tokens, :]
-            keys_ref[group, rows, :] = key
-            keys_across_ref[group, :, rows] = jnp.transpose(key)
-            value_ext_ref[group, rows, 0:WIDTH] = value
-            value_ext_ref[group, rows, WIDTH:] = jnp.full(value.shape, -1.0, jnp.bfloat16)
+    def key_block(kind, group, s):
+        if s == 0:
+            at = pl.multiple_of(group * WIDTH, WIDTH)
+            return (key_ref, value_ref)[kind][:, pl.ds(at, WIDTH)]
+        at = pl.multiple_of((kind * groups + group) * tokens, tokens)
+        return remote[s - 1][pl.ds(at, tokens), :]
+
+    def all_blocks(kind, group):
+        return jnp.concatenate([key_block(kind, group, s) for s in range(blocks)], axis=0)
 
     def stacked(ref, group, first, count):
         heads = [slice((first + i) * WIDTH, (first + i + 1) * WIDTH) for i in range(count)]
@@ -173,15 +168,15 @@
         inverse = 1.0 / sum(a * b for a, b in zip(totals, shrink))
         return [s * inverse for s in shrink]
 
-    def differentiate(group, pair, slot, centred, scales, half):
+    def differentiate(group, pair, centred, scales, half):
         lanes = slice(half * tokens, (half + 1) * tokens)
         to = slice((2 * pair + half) * tokens, (2 * pair + half + 1) * tokens)
         slope_sum, gain_sum = 0.0, 0.0
         for s, rows in enumerate(block_rows):
             probs = weight_ref[pair % 2, rows, lanes] * scales[s]
             dscore = probs * centred[s][:, lanes]
-            probs_ref[slot, rows, to] = probs.astype(jnp.bfloat16)
-            dscore_ref[slot, rows, to] = dscore.astype(jnp.bfloat16)
+            probs_ref[rows, to] = probs.astype(jnp.bfloat16)
+            dscore_ref[rows, to] = dscore.astype(jnp.bfloat16)
             slope_sum = slope_sum + fold_rows(dscore * distance_ref[rows, :])
             gain_sum = gain_sum + fold_rows(dscore * ancestor_ref[rows, :])
         at = pl.ds(group * heads_per_group + 2 * pair + half, 1)
@@ -193,64 +188,58 @@
         for s, rows in enumerate(block_rows):
             part_refs[s][pl.ds(at, tokens), :] = whole[rows].astype(jnp.bfloat16)
 
-    def key_part(group, slot):
-        heads = stacked(query_ref, group, 0, heads_per_group)
-        put_part(group, 0, dot_nn(dscore_ref[slot], heads) * factor)
-
-    def value_part(group, slot):
-        heads = stacked(grad_ref, group, 0, heads_per_group)
-        put_part(group, 1, dot_nn(probs_ref[slot], heads))
-
-    def query_part(group, slot, pair):
+    def key_part(group, first, count):
+        heads = stacked(query_ref, group, first, count)
+        lanes = slice(first * tokens, (first + count) * tokens)
+        return dot_nn(dscore_ref[:, lanes], heads)
+
+    def value_part(group, first, count):
+        heads = stacked(grad_ref, group, first, count)
+        lanes = slice(first * tokens, (first + count) * tokens)
+        return dot_nn(probs_ref[:, lanes], heads)
+
+    def query_part(keys_across, group, pair):
         lanes = slice(2 * pair * tokens, (2 * pair + 2) * tokens)
-        across = dot_nn(keys_across_ref[group], dscore_ref[slot, :, lanes]) * factor
+        across = dot_nn(keys_across, dscore_ref[:, lanes]) * factor
         rows = jnp.transpose(across.astype(jnp.bfloat16))
         for half in range(2):
             at = (2 * pair + half) * WIDTH
             query_grad_ref[group, :, at : at + WIDTH] = rows[half * tokens : (half + 1) * tokens]
 
-    def products(ref, group, other):
-        whole = dot_nt(ref[group], other)
+    def products(left, right):
+        whole = dot_nt(left, right)
         return [whole[rows] for rows in block_rows]
 
-    def advance(group, slot, before, before_slot):
+    @pl.loop(0, groups)
+    def _(group):
+        for index in range(3):
+            load(group, index).wait()
+        keys = all_blocks(0, group)
+        values = all_blocks(1, group)
+        value_ext = jnp.concatenate([values, jnp.full(values.shape, -1.0, jnp.bfloat16)], axis=1)
+        keys_across = jnp.transpose(keys)
+        half_heads = heads_per_group // 2
         for pair in range(pairs):
-            if group is not None:
-                query_pair = stacked(query_ref, group, 2 * pair, 2)
-                grad_pair = stacked(grad_ref, group, 2 * pair, 2)
-                output_pair = stacked(output_ref, group, 2 * pair, 2)
-                grad_ext = jnp.concatenate([grad_pair, grad_pair * output_pair], axis=1)
-                raw = products(keys_ref, group, query_pair)
-                scales = [weigh(group, pair, raw, half) for half in range(2)]
-            if pair == 0:
-                key_part(before, before_slot)
-            if pair == 1:
-                value_part(before, before_slot)
-            if group is not None:
-                centred = products(value_ext_ref, group, grad_ext)
-                for half in range(2):
-                    differentiate(group, pair, slot, centred, scales[half], half)
-            query_part(before, before_slot, pair)
-
-    @pl.loop(0, groups // 2)
-    def _(turn):
-        first, second = 2 * turn, 2 * turn + 1
-        for index in range(3):
-            load(first, index).wait()
-        before = jnp.maximum(first - 1, 0)
-        advance(first, 0, before, 1)
-
-        @pl.when(turn > 0)
-        def _():
-            store(before).start()
-
-        for index in range(3):
-            load(second, index).wait()
-        advance(second, 1, first, 0)
-        store(first).start()
-
-    advance(None, None, groups - 1, 1)
-    store(groups - 1).start()
+            query_pair = stacked(query_ref, group, 2 * pair, 2)
+            grad_pair = stacked(grad_ref, group, 2 * pair, 2)
+            output_pair = stacked(output_ref, group, 2 * pair, 2)
+            grad_ext = jnp.concatenate([grad_pair, grad_pair * output_pair], axis=1)
+            raw = products(keys, query_pair)
+            if pair == pairs // 2:
+                key_acc[...] = key_part(group, 0, half_heads)
+            scales = [weigh(group, pair, raw, half) for half in range(2)]
+            if pair == pairs // 2:
+                value_acc[...] = value_part(group, 0, half_heads)
+            if pair:
+                query_part(keys_across, group, pair - 1)
+            centred = products(value_ext, grad_ext)
+            for half in range(2):
+                differentiate(group, pair, centred, scales[half], half)
+        key_whole = key_acc[...] + key_part(group, half_heads, half_heads)
+        put_part(group, 0, key_whole * factor)
+        put_part(group, 1, value_acc[...] + value_part(group, half_heads, half_heads))
+        query_part(keys_across, group, pairs - 1)
+        store(group).start()
 
     slope_sum = jnp.sum(slope_rows[...], axis=1, keepdims=True)
     gain_sum = jnp.sum(gain_rows[...], axis=1, keepdims=True)
@@ -287,7 +276,7 @@
             out[:, group * WIDTH : (group + 1) * WIDTH] = total.astype(jnp.bfloat16)
 
 
-def bias_kernel(parts_ref, out_ref):
+def bias_kernel(parts_ref, _, out_ref):
     out_ref[...] = jnp.sum(parts_ref[...], axis=0)[0:2, 0 : out_ref.shape[1]]
 
 
@@ -352,16 +341,15 @@
             pltpu.VMEM((groups, tokens, group_columns), bf16),
             pltpu.VMEM((groups, tokens, group_columns), bf16),
             pltpu.VMEM((groups, tokens, group_columns), bf16),
-            pltpu.VMEM((groups, keys_seen, WIDTH), bf16),
-            pltpu.VMEM((groups, WIDTH, keys_seen), bf16),
-            pltpu.VMEM((groups, keys_seen, 2 * WIDTH), bf16),
             pltpu.VMEM((keys_seen, tokens), f32),
             pltpu.VMEM((keys_seen, tokens), f32),
             pltpu.VMEM((heads_all, tokens), f32),
             pltpu.VMEM((heads_all, tokens), f32),
+            pltpu.VMEM((keys_seen, WIDTH), f32),
+            pltpu.VMEM((keys_seen, WIDTH), f32),
             pltpu.VMEM((2, keys_seen, 2 * tokens), f32),
-            pltpu.VMEM((2, keys_seen, group_columns), bf16),
-            pltpu.VMEM((2, keys_seen, group_columns), bf16),
+            pltpu.VMEM((keys_seen, group_columns), bf16),
+            pltpu.VMEM((keys_seen, group_columns), bf16),
             pltpu.VMEM(bias_shape, f32),
             pltpu.SemaphoreType.DMA((3 * groups,)),
             pltpu.SemaphoreType.DMA((groups,)),
@@ -411,11 +399,11 @@
     bias_grads = pl.pallas_call(
         bias_kernel,
         out_shape=jax.ShapeDtypeStruct((2, local_heads), f32),
-        in_specs=[vmem],
+        in_specs=[vmem, hbm],
         out_specs=vmem,
         compiler_params=params,
         name="bias",
-    )(bias_parts)
+    )(bias_parts, key_grads)
     return (query_grads[None], key_grads[None], value_grads[None], bias_grads.T)
 
 

time: 52.6 us -> 53.3 us (1.013)
  blocking collectives: 16.4 us -> 0 us
  starting transfers between devices: 13.5 us -> 21.6 us
  waiting for transfers between devices: 7.58 us -> 15.2 us
  local copies, waits for them, and re-layouts: 0 us -> 0.9 us
    all_to_all x1 -> x0, blocking collectives: 16.4 us -> none  [body(): lax.all_to_all(bias_parts, ('dp', 'ctx'), split_axis=0, concat_axis=0, ti...]
    all_to_all x0 -> x1, starting transfers between devices: none -> 8.17 us  [body(): lax.all_to_all(bias_parts, ('dp', 'ctx'), split_axis=0, concat_axis=0, ti...]
    ppermute x3, waiting for transfers between devices: 0.01 us -> 6.26 us  [body(): parts[s] = lax.ppermute(parts[s], 'ctx', back)]
    all_to_all x0 -> x1, waiting for transfers between devices: none -> 1.33 us  [body(): lax.all_to_all(bias_parts, ('dp', 'ctx'), split_axis=0, concat_axis=0, ti...]
    unnamed x0 -> x2, local copies, waits for them, and re-layouts: none -> 0.9 us
  transfers between devices with their start and end apart: 6 -> 7, of which waited for: 3 -> 5; matrix products, arithmetic and copies ran while one was open for 0% -> 0% of each run, Pallas kernels for 1% -> 1%
where the time goes in v3:
time: 53.3 us; the launch traced here: 53 us
  starting transfers between devices  21.6 us (41%)
  waiting for transfers between devices  15.2 us (29%)
  Pallas kernels  14.6 us (27%)
  local copies, waits for them, and re-layouts  0.9 us (2%)
  between operations  0.71 us (1%)
    pallas_call x1, Pallas kernels, body(): pl.pallas_call(functools.partial(main_kernel, blocks, heads_per_group, gr...  12.1 us
    ppermute x3, starting transfers between devices, body(): lax.ppermute(message, 'ctx', [(i, i ^ s) for i in range(blocks) if i < i...  9.59 us
    all_to_all x1, starting transfers between devices, body(): lax.all_to_all(bias_parts, ('dp', 'ctx'), split_axis=0, concat_axis=0, ti...  8.17 us
    ppermute x3, waiting for transfers between devices, body(): lax.ppermute(message, 'ctx', [(i, i ^ s) for i in range(blocks) if i < i...  7.57 us
    ppermute x3, waiting for transfers between devices, body(): parts[s] = lax.ppermute(parts[s], 'ctx', back)  6.26 us
    ppermute x3, starting transfers between devices, body(): parts[s] = lax.ppermute(parts[s], 'ctx', back)  3.88 us
    all_to_all x1, waiting for transfers between devices, body(): lax.all_to_all(bias_parts, ('dp', 'ctx'), split_axis=0, concat_axis=0, ti...  1.33 us
  transfers between devices with their start and end apart: 7, of which 5 were waited for; matrix products, arithmetic and copies ran while one was open for 0% of the time, Pallas kernels for 1%

profile of v3, /device:TPU:0, one launch (start us, length us, event | category | flops | bytes accessed | tf_op | source)
XLA Modules:
  0.0 53.0 jit_solution(520730190480533114)
XLA Ops:
  0.6 1.0 %pack.1 = bf16[1040,128]{1,0:T(8,128)(2,1)S(1)} custom-call(bf16[128,512]{1,0:T(8,128)(2,1)} %bitcast.11, bf16[128,512]{1,0:T(8,128)(2,1)} %bitcast.13, s32[1,128]{1,0:T(1,128)} %depth_ref.3, s32[1,128]{1,0:T(1,128)} %end_ref.3), custom_call_target="tpu_custom_call" | custom-call | tf_op jit(solution)/shard_map/pack/pallas_call | solution.py:317
  1.7 5.8 %collective-permute-start.2 = (bf16[1040,128]{1,0:T(8,128)(2,1)S(1)}, bf16[1040,128]{1,0:T(8,128)(2,1)S(1)}, u32[]{:S(2)}, u32[]{:S(2)}) collective-permute-start(bf16[1040,128]{1,0:T(8,128)(2,1)S(1)} %pack.1), channel_id=1, source_target_pairs={{0,3},{1,2},{4,7},{5,6},{8,11},{9,10},{12,15},{13,14},{16,19},{17,... | collective-permute-start | bytes 798728 | tf_op jit(solution)/shard_map/ppermute | solution.py:326
  7.5 1.3 %collective-permute-start.1 = (bf16[1040,128]{1,0:T(8,128)(2,1)S(1)}, bf16[1040,128]{1,0:T(8,128)(2,1)S(1)}, u32[]{:S(2)}, u32[]{:S(2)}) collective-permute-start(bf16[1040,128]{1,0:T(8,128)(2,1)S(1)} %pack.1), channel_id=1, source_target_pairs={{0,2},{1,3},{4,6},{5,7},{8,10},{9,11},{12,14},{13,15},{16,18},{17,... | collective-permute-start | bytes 798728 | tf_op jit(solution)/shard_map/ppermute | solution.py:326
  8.8 2.5 %collective-permute-start = (bf16[1040,128]{1,0:T(8,128)(2,1)S(1)}, bf16[1040,128]{1,0:T(8,128)(2,1)S(1)}, u32[]{:S(2)}, u32[]{:S(2)}) collective-permute-start(bf16[1040,128]{1,0:T(8,128)(2,1)S(1)} %pack.1), channel_id=1, source_target_pairs={{0,1},{2,3},{4,5},{6,7},{8,9},{10,11},{12,13},{14,15},{16,17},{18,... | collective-permute-start | bytes 798728 | tf_op jit(solution)/shard_map/ppermute | solution.py:326
  11.3 3.0 %collective-permute-done.2.refs_2_ = bf16[1040,128]{1,0:T(8,128)(2,1)S(1)} collective-permute-done((bf16[1040,128]{1,0:T(8,128)(2,1)S(1)}, bf16[1040,128]{1,0:T(8,128)(2,1)S(1)}, u32[]{:S(2)}, u32[]{:S(2)}) %collective-permute-start.2) | collective-permute-done | bytes 266272 | tf_op jit(solution)/shard_map/ppermute | solution.py:326
  14.3 4.5 %collective-permute-done.1.refs_1_ = bf16[1040,128]{1,0:T(8,128)(2,1)S(1)} collective-permute-done((bf16[1040,128]{1,0:T(8,128)(2,1)S(1)}, bf16[1040,128]{1,0:T(8,128)(2,1)S(1)}, u32[]{:S(2)}, u32[]{:S(2)}) %collective-permute-start.1) | collective-permute-done | bytes 266272 | tf_op jit(solution)/shard_map/ppermute | solution.py:326
  18.8 0.1 collective-permute-done.refs_0_
  18.9 12.1 %attend.1 = (bf16[128,4096]{1,0:T(8,128)(2,1)}, bf16[1024,128]{1,0:T(8,128)(2,1)S(1)}, bf16[1024,128]{1,0:T(8,128)(2,1)S(1)}, bf16[1024,128]{1,0:T(8,128)(2,1)S(...) custom-call(s32[1,8]{1,0:T(1,128)} %lengths_ref.1, f32[32]{0:T(128)} %slope_ref.1, f32[32]{0:T(128)} %gain_ref.1, ...), custom_call_target="tpu_custom_call" | custom-call | flops 2684354560 | bytes 5242880 | tf_op jit(solution)/shard_map/attend/pallas_call | solution.py:332
  31.0 1.3 %collective-permute-start.3 = (bf16[1024,128]{1,0:T(8,128)(2,1)S(1)}, bf16[1024,128]{1,0:T(8,128)(2,1)S(1)}, u32[]{:S(2)}, u32[]{:S(2)}) collective-permute-start(bf16[1024,128]{1,0:T(8,128)(2,1)S(1)} %get-tuple-element.14), channel_id=1, source_target_pairs={{1,0},{3,2},{5,4},{7,6},{9,8},{11,10},{13,12},{15,14},{17,16},{19,... | collective-permute-start | bytes 786440 | tf_op jit(solution)/shard_map/ppermute | solution.py:383
  32.3 1.3 %collective-permute-start.4 = (bf16[1024,128]{1,0:T(8,128)(2,1)S(1)}, bf16[1024,128]{1,0:T(8,128)(2,1)S(1)}, u32[]{:S(2)}, u32[]{:S(2)}) collective-permute-start(bf16[1024,128]{1,0:T(8,128)(2,1)S(1)} %get-tuple-element.15), channel_id=1, source_target_pairs={{2,0},{3,1},{6,4},{7,5},{10,8},{11,9},{14,12},{15,13},{18,16},{19,... | collective-permute-start | bytes 786440 | tf_op jit(solution)/shard_map/ppermute | solution.py:383
  33.6 1.3 %collective-permute-start.5 = (bf16[1024,128]{1,0:T(8,128)(2,1)S(1)}, bf16[1024,128]{1,0:T(8,128)(2,1)S(1)}, u32[]{:S(2)}, u32[]{:S(2)}) collective-permute-start(bf16[1024,128]{1,0:T(8,128)(2,1)S(1)} %get-tuple-element.16), channel_id=1, source_target_pairs={{2,1},{3,0},{6,5},{7,4},{10,9},{11,8},{14,13},{15,12},{18,17},{19,... | collective-permute-start | bytes 786440 | tf_op jit(solution)/shard_map/ppermute | solution.py:383
  34.9 8.2 %all-to-all-start = ((f32[32,8,128]{2,1,0:T(8,128)}), f32[32,8,128]{2,1,0:T(8,128)S(1)}, u32[]{:S(2)}, u32[]{:S(2)}) async-start(f32[32,8,128]{2,1,0:T(8,128)} %bitcast.8), calls=%async_computation | async-start | bytes 262144 | tf_op jit(solution)/shard_map/all_to_all | solution.py:384
  43.1 0.0 collective-permute-done.3.refs_1_
  43.1 0.0 collective-permute-done.4.refs_2_
  43.1 6.3 %collective-permute-done.5.refs_3_ = bf16[1024,128]{1,0:T(8,128)(2,1)S(1)} collective-permute-done((bf16[1024,128]{1,0:T(8,128)(2,1)S(1)}, bf16[1024,128]{1,0:T(8,128)(2,1)S(1)}, u32[]{:S(2)}, u32[]{:S(2)}) %collective-permute-start.5) | collective-permute-done | bytes 262176 | tf_op jit(solution)/shard_map/ppermute | solution.py:383
  49.3 0.8 %combine.1 = (bf16[128,512]{1,0:T(8,128)(2,1)}, bf16[128,512]{1,0:T(8,128)(2,1)}) custom-call(bf16[1024,128]{1,0:T(8,128)(2,1)S(1)} %get-tuple-element.13.refs_0_, bf16[1024,128]{1,0:T(8,128)(2,1)S(1)} %collective-permute-done.3.refs_1_, bf16[1024,128]{1,0:T(8,128)(2,1)S(1)} %collective-permute-done.4.refs_2_, ...), custom_call_target="tpu_custom_call" | custom-call | flops 1048576 | bytes 1310720 | tf_op jit(solution)/shard_map/combine/pallas_call | solution.py:386
  50.1 1.3 %all-to-all-done.parts_ref = f32[32,8,128]{2,1,0:T(8,128)S(1)} async-done(((f32[32,8,128]{2,1,0:T(8,128)}), f32[32,8,128]{2,1,0:T(8,128)S(1)}, u32[]{:S(2)}, u32[]{:S(2)}) %all-to-all-start) | async-done | bytes 131104 | tf_op jit(solution)/shard_map/all_to_all | solution.py:384
  51.5 0.0 copy-start
  51.5 0.9 %copy-done = bf16[128,512]{1,0:T(8,128)(2,1)S(1)} copy-done((bf16[128,512]{1,0:T(8,128)(2,1)S(1)}, bf16[128,512]{1,0:T(8,128)(2,1)}, u32[]{:S(2)}) %copy-start) | copy-done | bytes 131096
  52.4 0.6 %bias.1 = f32[2,8]{1,0:T(2,128)} custom-call(f32[32,8,128]{2,1,0:T(8,128)S(1)} %all-to-all-done.parts_ref, bf16[128,512]{1,0:T(8,128)(2,1)S(1)} %copy-done), custom_call_target="tpu_custom_call" | custom-call | tf_op jit(solution)/shard_map/bias/pallas_call | solution.py:399
Async XLA Ops:
  1.7 12.6 %collective-permute-start.2 = (bf16[1040,128]{1,0:T(8,128)(2,1)S(1)}, bf16[1040,128]{1,0:T(8,128)(2,1)S(1)}, u32[]{:S(2)}, u32[]{:S(2)}) collective-permute-start(bf16[1040,128]{1,0:T(8,128)(2,1)S(1)} %pack.1), channel_id=1, source_target_pairs={{0,3},{1,2},{4,7},{5,6},{8,11},{9,10},{12,15},{13,14},{16,19},{17,... | collective-permute-start | bytes 798728 | tf_op jit(solution)/shard_map/ppermute | solution.py:326
  7.5 11.3 %collective-permute-start.1 = (bf16[1040,128]{1,0:T(8,128)(2,1)S(1)}, bf16[1040,128]{1,0:T(8,128)(2,1)S(1)}, u32[]{:S(2)}, u32[]{:S(2)}) collective-permute-start(bf16[1040,128]{1,0:T(8,128)(2,1)S(1)} %pack.1), channel_id=1, source_target_pairs={{0,2},{1,3},{4,6},{5,7},{8,10},{9,11},{12,14},{13,15},{16,18},{17,... | collective-permute-start | bytes 798728 | tf_op jit(solution)/shard_map/ppermute | solution.py:326
  8.8 10.1 %collective-permute-start = (bf16[1040,128]{1,0:T(8,128)(2,1)S(1)}, bf16[1040,128]{1,0:T(8,128)(2,1)S(1)}, u32[]{:S(2)}, u32[]{:S(2)}) collective-permute-start(bf16[1040,128]{1,0:T(8,128)(2,1)S(1)} %pack.1), channel_id=1, source_target_pairs={{0,1},{2,3},{4,5},{6,7},{8,9},{10,11},{12,13},{14,15},{16,17},{18,... | collective-permute-start | bytes 798728 | tf_op jit(solution)/shard_map/ppermute | solution.py:326
  31.0 12.1 %collective-permute-start.3 = (bf16[1024,128]{1,0:T(8,128)(2,1)S(1)}, bf16[1024,128]{1,0:T(8,128)(2,1)S(1)}, u32[]{:S(2)}, u32[]{:S(2)}) collective-permute-start(bf16[1024,128]{1,0:T(8,128)(2,1)S(1)} %get-tuple-element.14), channel_id=1, source_target_pairs={{1,0},{3,2},{5,4},{7,6},{9,8},{11,10},{13,12},{15,14},{17,16},{19,... | collective-permute-start | bytes 786440 | tf_op jit(solution)/shard_map/ppermute | solution.py:383
  32.3 10.8 %collective-permute-start.4 = (bf16[1024,128]{1,0:T(8,128)(2,1)S(1)}, bf16[1024,128]{1,0:T(8,128)(2,1)S(1)}, u32[]{:S(2)}, u32[]{:S(2)}) collective-permute-start(bf16[1024,128]{1,0:T(8,128)(2,1)S(1)} %get-tuple-element.15), channel_id=1, source_target_pairs={{2,0},{3,1},{6,4},{7,5},{10,8},{11,9},{14,12},{15,13},{18,16},{19,... | collective-permute-start | bytes 786440 | tf_op jit(solution)/shard_map/ppermute | solution.py:383
  33.6 15.8 %collective-permute-start.5 = (bf16[1024,128]{1,0:T(8,128)(2,1)S(1)}, bf16[1024,128]{1,0:T(8,128)(2,1)S(1)}, u32[]{:S(2)}, u32[]{:S(2)}) collective-permute-start(bf16[1024,128]{1,0:T(8,128)(2,1)S(1)} %get-tuple-element.16), channel_id=1, source_target_pairs={{2,1},{3,0},{6,5},{7,4},{10,9},{11,8},{14,13},{15,12},{18,17},{19,... | collective-permute-start | bytes 786440 | tf_op jit(solution)/shard_map/ppermute | solution.py:383
  34.9 16.6 %all-to-all-start = ((f32[32,8,128]{2,1,0:T(8,128)}), f32[32,8,128]{2,1,0:T(8,128)S(1)}, u32[]{:S(2)}, u32[]{:S(2)}) async-start(f32[32,8,128]{2,1,0:T(8,128)} %bitcast.8), calls=%async_computation | async-start | bytes 262144 | tf_op jit(solution)/shard_map/all_to_all | solution.py:384
  51.5 0.9 %copy-start = (bf16[128,512]{1,0:T(8,128)(2,1)S(1)}, bf16[128,512]{1,0:T(8,128)(2,1)}, u32[]{:S(2)}) copy-start(bf16[128,512]{1,0:T(8,128)(2,1)} %get-tuple-element.17._) | copy-start | bytes 393220

commit v4 on v3

v4 whole, which is shorter than its diff:
```python
import functools

import jax
import jax.numpy as jnp
from jax import lax
from jax.experimental import pallas as pl
from jax.experimental.pallas import tpu as pltpu
from jax.sharding import PartitionSpec as P

WIDTH = 128
LOG2E = 1.4426950408889634
MASKED = -1e30
META_ROWS = 16
END_UNIT = 64


def dot_nt(a, b):
    return lax.dot_general(a, b, (((1,), (1,)), ((), ())), preferred_element_type=jnp.float32)


def dot_nn(a, b):
    return lax.dot_general(a, b, (((1,), (0,)), ((), ())), preferred_element_type=jnp.float32)


def fold_rows(block):
    return jnp.sum(block.reshape(block.shape[0] // 8, 8, block.shape[1]), axis=0)


def as_column(row):
    size = row.shape[1]
    return jnp.transpose(jnp.broadcast_to(row, (size, size)))


def pack_kernel(key_ref, value_ref, depth_ref, end_ref, key_message, value_message):
    tokens = key_ref.shape[0]
    groups = key_ref.shape[1] // WIDTH
    for group in range(groups):
        rows = slice(group * tokens, (group + 1) * tokens)
        columns = slice(group * WIDTH, (group + 1) * WIDTH)
        key_message[rows, :] = key_ref[:, columns]
        value_message[rows, :] = value_ref[:, columns]
    depth = depth_ref[...]
    end = end_ref[...]
    end_high = end // END_UNIT
    end_low = end - end_high * END_UNIT
    row = lax.broadcasted_iota(jnp.int32, (META_ROWS, tokens), 0)
    meta = jnp.where(row == 0, depth, jnp.where(row == 1, end_high, end_low))
    meta = meta.astype(jnp.float32).astype(jnp.bfloat16)
    key_message[groups * tokens : groups * tokens + META_ROWS, :] = meta


def fill_tables(groups, lengths_ref, depth_ref, end_ref, remote, distance_ref, ancestor_ref):
    tokens = depth_ref.shape[1]
    here = lax.axis_index("ctx")
    query_pos = here * tokens + lax.broadcasted_iota(jnp.int32, (tokens, tokens), 1)
    start = jnp.zeros((tokens, tokens), jnp.int32)
    bound = jnp.int32(0)
    for index in range(lengths_ref.shape[1]):
        bound = bound + lengths_ref[0, index]
        start = jnp.where(query_pos >= bound, bound, start)
    query_depth = jnp.broadcast_to(depth_ref[...].astype(jnp.float32), (tokens, tokens))
    for s in range(1 + len(remote)):
        rows = slice(s * tokens, (s + 1) * tokens)
        key_pos = (here ^ s) * tokens + lax.broadcasted_iota(jnp.int32, (tokens, tokens), 0)
        if s == 0:
            key_depth = as_column(depth_ref[...].astype(jnp.float32))
            key_end = as_column(end_ref[...].astype(jnp.float32))
        else:
            below = slice(groups * tokens, groups * tokens + META_ROWS)
            meta = remote[s - 1][below, :].astype(jnp.float32)
            key_depth = as_column(meta[0:1])
            key_end = as_column(meta[1:2] * END_UNIT + meta[2:3])
        inside = query_pos.astype(jnp.float32) < key_end
        allowed = (key_pos <= query_pos) & (key_pos >= start)
        distance_ref[rows, :] = jnp.abs(query_depth - key_depth)
        ancestor_ref[rows, :] = jnp.where(allowed, jnp.where(inside, 1.0, 0.0), MASKED)


def all_blocks(own_ref, remote, group):
    tokens = own_ref.shape[0]
    own = own_ref[:, pl.ds(pl.multiple_of(group * WIDTH, WIDTH), WIDTH)]
    at = pl.multiple_of(group * tokens, tokens)
    return jnp.concatenate([own] + [r[pl.ds(at, tokens), :] for r in remote], axis=0)


def stacked(ref, group, first, count):
    heads = [slice((first + i) * WIDTH, (first + i + 1) * WIDTH) for i in range(count)]
    return jnp.concatenate([ref[group, :, h] for h in heads], axis=0)


def group_columns(group, columns):
    return pl.ds(pl.multiple_of(group * columns, columns), columns)


def group_loads(group, sources, targets, sems):
    columns = targets[0].shape[2]
    return [
        pltpu.make_async_copy(
            source.at[:, group_columns(group, columns)],
            target.at[group],
            sems.at[len(sources) * group + index],
        )
        for index, (source, target) in enumerate(zip(sources, targets))
    ]


def put_part(part_refs, group, whole):
    tokens = whole.shape[0] // len(part_refs)
    at = pl.multiple_of(group * tokens, tokens)
    for s, part_ref in enumerate(part_refs):
        part = whole[s * tokens : (s + 1) * tokens].astype(jnp.bfloat16)
        part_ref[pl.ds(at, tokens), :] = part


def weigh_kernel(blocks, heads_per_group, groups, *refs):
    refs = list(refs)
    take = lambda count: [refs.pop(0) for _ in range(count)]
    lengths_ref, slope_ref, gain_ref, depth_ref, end_ref, query_hbm, grad_hbm, key_ref = take(8)
    remote = take(blocks - 1)
    probs_ref, distance_ref, ancestor_ref = take(3)
    part_refs = take(blocks)
    query_ref, grad_ref, weight_ref, value_acc, load_sems = refs
    tokens = query_hbm.shape[0]
    factor = WIDTH**-0.5
    pairs = heads_per_group // 2
    block_rows = [slice(s * tokens, (s + 1) * tokens) for s in range(blocks)]

    def loads(group):
        return group_loads(group, (query_hbm, grad_hbm), (query_ref, grad_ref), load_sems)

    for group in range(groups):
        for load in loads(group):
            load.start()
    fill_tables(groups, lengths_ref, depth_ref, end_ref, remote, distance_ref, ancestor_ref)

    def weigh(group, pair, raw, half):
        head = group * heads_per_group + 2 * pair + half
        gain = gain_ref[head] * LOG2E
        slope = slope_ref[head] * LOG2E
        lanes = slice(half * tokens, (half + 1) * tokens)
        tops, totals = [], []
        for rows in block_rows:
            score = raw[rows, lanes] * (factor * LOG2E) + (
                gain * ancestor_ref[rows, :] - slope * distance_ref[rows, :]
            )
            top = jnp.max(score, axis=0, keepdims=True)
            weight = jnp.exp2(score - top)
            weight_ref[pair % 2, rows, lanes] = weight
            tops.append(top)
            totals.append(jnp.sum(weight, axis=0, keepdims=True))
        top = functools.reduce(jnp.maximum, tops)
        shrink = [jnp.exp2(t - top) for t in tops]
        inverse = 1.0 / sum(a * b for a, b in zip(totals, shrink))
        return [s * inverse for s in shrink]

    def value_part(group, first, count):
        lanes = slice(first * tokens, (first + count) * tokens)
        return dot_nn(probs_ref[group, :, lanes], stacked(grad_ref, group, first, count))

    @pl.loop(0, groups)
    def _(group):
        for load in loads(group):
            load.wait()
        keys = all_blocks(key_ref, remote, group)
        half_heads = heads_per_group // 2
        for pair in range(pairs):
            raw = dot_nt(keys, stacked(query_ref, group, 2 * pair, 2))
            if pair == pairs // 2:
                value_acc[...] = value_part(group, 0, half_heads)
            scales = [weigh(group, pair, raw, half) for half in range(2)]
            for half in range(2):
                lanes = slice(half * tokens, (half + 1) * tokens)
                to = slice((2 * pair + half) * tokens, (2 * pair + half + 1) * tokens)
                for rows, scale in zip(block_rows, scales[half]):
                    probs = weight_ref[pair % 2, rows, lanes] * scale
                    probs_ref[group, rows, to] = probs.astype(jnp.bfloat16)
        put_part(part_refs, group, value_acc[...] + value_part(group, half_heads, half_heads))


def grad_kernel(blocks, heads_per_group, groups, *refs):
    refs = list(refs)
    take = lambda count: [refs.pop(0) for _ in range(count)]
    probs_ref, distance_ref, ancestor_ref = take(3)
    query_hbm, output_hbm, grad_hbm, key_ref, value_ref = take(5)
    remote_key = take(blocks - 1)
    remote_value = take(blocks - 1)
    (query_grad_hbm,) = take(1)
    part_refs = take(blocks)
    (bias_hbm,) = take(1)
    (
        query_ref,
        output_ref,
        grad_ref,
        query_grad_ref,
        dscore_ref,
        key_acc,
        slope_rows,
        gain_rows,
        bias_ref,
        load_sems,
        store_sems,
        bias_sem,
    ) = refs
    tokens = query_hbm.shape[0]
    factor = WIDTH**-0.5
    pairs = heads_per_group // 2
    block_rows = [slice(s * tokens, (s + 1) * tokens) for s in range(blocks)]

    def loads(group):
        sources = (query_hbm, output_hbm, grad_hbm)
        return group_loads(group, sources, (query_ref, output_ref, grad_ref), load_sems)

    def store(group):
        columns = group_columns(group, query_grad_ref.shape[2])
        return pltpu.make_async_copy(
            query_grad_ref.at[group], query_grad_hbm.at[:, columns], store_sems.at[group]
        )

    for group in range(groups):
        for load in loads(group):
            load.start()

    def differentiate(group, pair, centred, half):
        lanes = slice(half * tokens, (half + 1) * tokens)
        to = slice((2 * pair + half) * tokens, (2 * pair + half + 1) * tokens)
        slope_sum, gain_sum = 0.0, 0.0
        for rows in block_rows:
            probs = probs_ref[group, rows, to].astype(jnp.float32)
            dscore = probs * centred[rows, lanes]
            dscore_ref[rows, to] = dscore.astype(jnp.bfloat16)
            slope_sum = slope_sum + fold_rows(dscore * distance_ref[rows, :])
            gain_sum = gain_sum + fold_rows(dscore * ancestor_ref[rows, :])
        at = pl.ds(group * heads_per_group + 2 * pair + half, 1)
        slope_rows[at, :] = -jnp.sum(slope_sum, axis=0, keepdims=True)
        gain_rows[at, :] = jnp.sum(gain_sum, axis=0, keepdims=True)

    def key_part(group, first, count):
        lanes = slice(first * tokens, (first + count) * tokens)
        return dot_nn(dscore_ref[:, lanes], stacked(query_ref, group, first, count))

    def query_part(keys_across, group, pair):
        lanes = slice(2 * pair * tokens, (2 * pair + 2) * tokens)
        across = dot_nn(keys_across, dscore_ref[:, lanes]) * factor
        rows = jnp.transpose(across.astype(jnp.bfloat16))
        for half in range(2):
            at = (2 * pair + half) * WIDTH
            query_grad_ref[group, :, at : at + WIDTH] = rows[half * tokens : (half + 1) * tokens]

    @pl.loop(0, groups)
    def _(group):
        for load in loads(group):
            load.wait()
        values = all_blocks(value_ref, remote_value, group)
        value_ext = jnp.concatenate([values, jnp.full(values.shape, -1.0, jnp.bfloat16)], axis=1)
        keys_across = jnp.transpose(all_blocks(key_ref, remote_key, group))
        half_heads = heads_per_group // 2
        for pair in range(pairs):
            grad_pair = stacked(grad_ref, group, 2 * pair, 2)
            output_pair = stacked(output_ref, group, 2 * pair, 2)
            grad_ext = jnp.concatenate([grad_pair, grad_pair * output_pair], axis=1)
            centred = dot_nt(value_ext, grad_ext)
            if pair == pairs // 2:
                key_acc[...] = key_part(group, 0, half_heads)
            if pair:
                query_part(keys_across, group, pair - 1)
            for half in range(2):
                differentiate(group, pair, centred, half)
        key_whole = key_acc[...] + key_part(group, half_heads, half_heads)
        put_part(part_refs, group, key_whole * factor)
        query_part(keys_across, group, pairs - 1)
        store(group).start()

    slope_sum = jnp.sum(slope_rows[...], axis=1, keepdims=True)
    gain_sum = jnp.sum(gain_rows[...], axis=1, keepdims=True)
    shape = slope_rows.shape
    lane = lax.broadcasted_iota(jnp.int32, shape, 1)
    row = lax.broadcasted_iota(jnp.int32, shape, 0)
    replicas, parts, rows_here, local = bias_ref.shape
    local_heads = shape[0] // parts
    kind = lax.broadcasted_iota(jnp.int32, (rows_here, local), 0)
    for part in range(parts):
        mine = (lane == row - part * local_heads) & (lane < local_heads)
        slope_line = jnp.sum(jnp.where(mine, slope_sum, 0.0), axis=0, keepdims=True)
        gain_line = jnp.sum(jnp.where(mine, gain_sum, 0.0), axis=0, keepdims=True)
        tile = jnp.where(kind == 0, slope_line, jnp.where(kind == 1, gain_line, 0.0))
        bias_ref[:, part] = jnp.broadcast_to(tile[None], (replicas, rows_here, local))
    bias_copy = pltpu.make_async_copy(bias_ref, bias_hbm, bias_sem)
    bias_copy.start()
    for group in range(groups):
        store(group).wait()
    bias_copy.wait()


def combine_kernel(blocks, *refs):
    parts = refs[0:blocks]
    out = refs[blocks]
    tokens = out.shape[0]
    for group in range(out.shape[1] // WIDTH):
        rows = slice(group * tokens, (group + 1) * tokens)
        total = parts[0][rows, :].astype(jnp.float32)
        for s in range(1, blocks):
            total = total + parts[s][rows, :].astype(jnp.float32)
        out[:, group * WIDTH : (group + 1) * WIDTH] = total.astype(jnp.bfloat16)


def bias_kernel(parts_ref, _, __, out_ref):
    out_ref[...] = jnp.sum(parts_ref[...], axis=0)[0:2, 0 : out_ref.shape[1]]


def body(
    queries,
    key_rows,
    values,
    outputs,
    out_grads,
    depths,
    subtree_end,
    file_lengths,
    slopes,
    ancestor_gain,
):
    blocks = lax.axis_size("ctx")
    replicas = lax.axis_size("dp")
    tokens, width_all = queries.shape[1:]
    kv_width = key_rows.shape[2]
    heads_all = width_all // WIDTH
    groups = kv_width // WIDTH
    heads_per_group = heads_all // groups
    columns = heads_per_group * WIDTH
    local_heads = heads_all // blocks
    keys_seen = blocks * tokens
    part_rows = groups * tokens
    bf16, f32 = jnp.bfloat16, jnp.float32
    vmem = pl.BlockSpec(memory_space=pltpu.VMEM)
    smem = pl.BlockSpec(memory_space=pltpu.SMEM)
    hbm = pl.BlockSpec(memory_space=pltpu.HBM)
    params = pltpu.CompilerParams(vmem_limit_bytes=(24 if blocks <= 4 else 48) * 1024 * 1024)
    sem = pltpu.SemaphoreType.DMA

    def hold(array):
        return pltpu.with_memory_space_constraint(array, pltpu.HBM)

    def struct(*shape, dtype=bf16):
        return jax.ShapeDtypeStruct(shape, dtype)

    def cost(matmuls, exponentials):
        return pl.CostEstimate(
            flops=matmuls * 2 * tokens * keys_seen * WIDTH * heads_all,
            bytes_accessed=4 * tokens * width_all,
            transcendentals=exponentials * tokens * keys_seen * heads_all,
        )

    def gather(message):
        return [
            lax.ppermute(message, "ctx", [(i, i ^ s) for i in range(blocks) if i < i ^ s])
            for s in range(1, blocks)
        ]

    def give_back(parts):
        back = [[(i, i ^ s) for i in range(blocks) if i > i ^ s] for s in range(1, blocks)]
        return [parts[0]] + [lax.ppermute(p, "ctx", b) for p, b in zip(parts[1:], back)]

    def combine(parts, name):
        return pl.pallas_call(
            functools.partial(combine_kernel, blocks),
            out_shape=struct(tokens, kv_width),
            in_specs=[vmem] * blocks,
            out_specs=vmem,
            compiler_params=params,
            name=name,
        )(*parts)

    query_held, output_held, grad_held = hold(queries[0]), hold(outputs[0]), hold(out_grads[0])
    key_held, value_held = hold(key_rows[0]), hold(values[0])
    depth_held, end_held = hold(depths), hold(subtree_end)
    key_message, value_message = pl.pallas_call(
        pack_kernel,
        out_shape=[struct(part_rows + META_ROWS, WIDTH), struct(part_rows, WIDTH)],
        in_specs=[vmem] * 4,
        out_specs=[vmem] * 2,
        compiler_params=params,
        name="pack",
    )(key_held, value_held, depth_held, end_held)
    key_blocks = gather(key_message)
    value_blocks = gather(value_message)

    table = struct(keys_seen, tokens, dtype=f32)
    probs, distance, ancestor, *value_parts = pl.pallas_call(
        functools.partial(weigh_kernel, blocks, heads_per_group, groups),
        out_shape=[struct(groups, keys_seen, columns), table, table]
        + [struct(part_rows, WIDTH)] * blocks,
        in_specs=[smem] * 3 + [vmem] * 2 + [hbm] * 2 + [vmem] * blocks,
        out_specs=[vmem] * (3 + blocks),
        scratch_shapes=[
            pltpu.VMEM((groups, tokens, columns), bf16),
            pltpu.VMEM((groups, tokens, columns), bf16),
            pltpu.VMEM((2, keys_seen, 2 * tokens), f32),
            pltpu.VMEM((keys_seen, WIDTH), f32),
            sem((2 * groups,)),
        ],
        compiler_params=params,
        cost_estimate=cost(2, 1),
        name="weigh",
    )(
        hold(file_lengths),
        hold(slopes),
        hold(ancestor_gain),
        depth_held,
        end_held,
        query_held,
        grad_held,
        key_held,
        *key_blocks,
    )
    value_parts = give_back(value_parts)

    bias_shape = (replicas, blocks, 8, WIDTH)
    query_grads, *key_parts, bias_parts = pl.pallas_call(
        functools.partial(grad_kernel, blocks, heads_per_group, groups),
        out_shape=[struct(tokens, width_all)]
        + [struct(part_rows, WIDTH)] * blocks
        + [struct(*bias_shape, dtype=f32)],
        in_specs=[vmem] * 3 + [hbm] * 3 + [vmem] * (2 * blocks),
        out_specs=[hbm] + [vmem] * blocks + [hbm],
        scratch_shapes=[
            pltpu.VMEM((groups, tokens, columns), bf16),
            pltpu.VMEM((groups, tokens, columns), bf16),
            pltpu.VMEM((groups, tokens, columns), bf16),
            pltpu.VMEM((groups, tokens, columns), bf16),
            pltpu.VMEM((keys_seen, columns), bf16),
            pltpu.VMEM((keys_seen, WIDTH), f32),
            pltpu.VMEM((heads_all, tokens), f32),
            pltpu.VMEM((heads_all, tokens), f32),
            pltpu.VMEM(bias_shape, f32),
            sem((3 * groups,)),
            sem((groups,)),
            sem,
        ],
        compiler_params=params,
        cost_estimate=cost(3, 0),
        name="grad",
    )(
        probs,
        distance,
        ancestor,
        query_held,
        output_held,
        grad_held,
        key_held,
        value_held,
        *key_blocks,
        *value_blocks,
    )
    key_parts = give_back(key_parts)
    bias_parts = bias_parts.reshape(replicas * blocks, 8, WIDTH)
    bias_parts = lax.all_to_all(bias_parts, ("dp", "ctx"), split_axis=0, concat_axis=0, tiled=True)
    value_grads = combine(value_parts, "combine_values")
    key_grads = combine(key_parts, "combine_keys")
    bias_grads = pl.pallas_call(
        bias_kernel,
        out_shape=struct(2, local_heads, dtype=f32),
        in_specs=[vmem, hbm, hbm],
        out_specs=vmem,
        compiler_params=params,
        name="bias",
    )(bias_parts, hold(key_grads), hold(value_grads))
    return (query_grads[None], key_grads[None], value_grads[None], bias_grads.T)


def solution(mesh):
    in_specs = (
        P("dp", "ctx", None),
        P("dp", "ctx", None),
        P("dp", "ctx", None),
        P("dp", "ctx", None),
        P("dp", "ctx", None),
        P("dp", "ctx"),
        P("dp", "ctx"),
        P("dp", None),
        P(),
        P(),
    )
    out_specs = (P("dp", "ctx", None), P("dp", "ctx", None), P("dp", "ctx", None), P("ctx", None))
    return jax.shard_map(body, mesh=mesh, in_specs=in_specs, out_specs=out_specs, check_vma=False)
```

time: 53.3 us -> 60.2 us (1.13)
  starting transfers between devices: 21.6 us -> 29.4 us
  waiting for transfers between devices: 15.2 us -> 10.3 us
  Pallas kernels: 14.6 us -> 19.2 us
  local copies, waits for them, and re-layouts: 0.9 us -> 0 us
    ppermute x6 -> x12, starting transfers between devices: 13.5 us -> 23.3 us  [the longest x6 15.5 us: gather(): lax.ppermute(message, 'ctx', [(i, i ^ s) for i in range(blocks) if i < i...]
    pallas_call x4 -> x6, Pallas kernels: 14.6 us -> 19.2 us  [the longest x1 8.08 us: body(): pl.pallas_call(functools.partial(grad_kernel, blocks, heads_per_group, gr...]
    ppermute x6 -> x12, waiting for transfers between devices: 13.8 us -> 10.3 us  [the longest x6 10.3 us: give_back(): lax.ppermute(p, 'ctx', b)]
    all_to_all x1, starting transfers between devices: 8.17 us -> 6.06 us  [body(): lax.all_to_all(bias_parts, ('dp', 'ctx'), split_axis=0, concat_axis=0, ti...]
    all_to_all x1, waiting for transfers between devices: 1.33 us -> 0.01 us  [body(): lax.all_to_all(bias_parts, ('dp', 'ctx'), split_axis=0, concat_axis=0, ti...]
    unnamed x2 -> x0, local copies, waits for them, and re-layouts: 0.9 us -> none
  transfers between devices with their start and end apart: 7 -> 13, of which waited for: 5 -> 5; matrix products, arithmetic and copies ran while one was open for 0% -> 0% of each run, Pallas kernels for 1% -> 29%
where the time goes in v4:
time: 60.2 us; the launch traced here: 59.7 us
  starting transfers between devices  29.4 us (49%)
  Pallas kernels  19.2 us (32%)
  waiting for transfers between devices  10.3 us (17%)
  between operations  0.81 us (1%)
    ppermute x6, starting transfers between devices, gather(): lax.ppermute(message, 'ctx', [(i, i ^ s) for i in range(blocks) if i < i...  15.5 us
    ppermute x6, waiting for transfers between devices, give_back(): lax.ppermute(p, 'ctx', b)  10.3 us
    pallas_call x1, Pallas kernels, body(): pl.pallas_call(functools.partial(grad_kernel, blocks, heads_per_group, gr...  8.08 us
    pallas_call x1, Pallas kernels, body(): pl.pallas_call(functools.partial(weigh_kernel, blocks, heads_per_group, g...  8.07 us
    ppermute x6, starting transfers between devices, give_back(): lax.ppermute(p, 'ctx', b)  7.75 us
    all_to_all x1, starting transfers between devices, body(): lax.all_to_all(bias_parts, ('dp', 'ctx'), split_axis=0, concat_axis=0, ti...  6.06 us
    pallas_call x2, Pallas kernels, combine(): pl.pallas_call(functools.partial(combine_kernel, blocks), out_shape=struc...  1.45 us
  transfers between devices with their start and end apart: 13, of which 5 were waited for; matrix products, arithmetic and copies ran while one was open for 0% of the time, Pallas kernels for 29%

profile of v4, /device:TPU:0, one launch (start us, length us, event | category | flops | bytes accessed | tf_op | source)
XLA Modules:
  0.0 59.7 jit_solution(7318075344881585732)
XLA Ops:
  0.6 1.0 %pack.1 = (bf16[528,128]{1,0:T(8,128)(2,1)S(1)}, bf16[512,128]{1,0:T(8,128)(2,1)S(1)}) custom-call(bf16[128,512]{1,0:T(8,128)(2,1)} %bitcast.15, bf16[128,512]{1,0:T(8,128)(2,1)} %bitcast.18, s32[1,128]{1,0:T(1,128)} %refs_3_.1, s32[1,128]{1,0:T(1,128)} %refs_4_.1), custom_call_target="tpu_custom_call" | custom-call | tf_op jit(solution)/shard_map/pack/pallas_call | solution.py:376
  1.7 4.8 %collective-permute-start = (bf16[528,128]{1,0:T(8,128)(2,1)S(1)}, bf16[528,128]{1,0:T(8,128)(2,1)S(1)}, u32[]{:S(2)}, u32[]{:S(2)}) collective-permute-start(bf16[528,128]{1,0:T(8,128)(2,1)S(1)} %get-tuple-element.19), channel_id=1, source_target_pairs={{0,1},{2,3},{4,5},{6,7},{8,9},{10,11},{12,13},{14,15},{16,17},{18,... | collective-permute-start | bytes 405512 | tf_op jit(solution)/shard_map/ppermute | solution.py:355
  6.5 3.4 %collective-permute-start.1 = (bf16[528,128]{1,0:T(8,128)(2,1)S(1)}, bf16[528,128]{1,0:T(8,128)(2,1)S(1)}, u32[]{:S(2)}, u32[]{:S(2)}) collective-permute-start(bf16[528,128]{1,0:T(8,128)(2,1)S(1)} %get-tuple-element.19), channel_id=1, source_target_pairs={{0,2},{1,3},{4,6},{5,7},{8,10},{9,11},{12,14},{13,15},{16,18},{17,... | collective-permute-start | bytes 405512 | tf_op jit(solution)/shard_map/ppermute | solution.py:355
  10.0 1.3 %collective-permute-start.2 = (bf16[528,128]{1,0:T(8,128)(2,1)S(1)}, bf16[528,128]{1,0:T(8,128)(2,1)S(1)}, u32[]{:S(2)}, u32[]{:S(2)}) collective-permute-start(bf16[528,128]{1,0:T(8,128)(2,1)S(1)} %get-tuple-element.19), channel_id=1, source_target_pairs={{0,3},{1,2},{4,7},{5,6},{8,11},{9,10},{12,15},{13,14},{16,19},{17,... | collective-permute-start | bytes 405512 | tf_op jit(solution)/shard_map/ppermute | solution.py:355
  11.3 3.4 %collective-permute-start.3 = (bf16[512,128]{1,0:T(8,128)(2,1)S(1)}, bf16[512,128]{1,0:T(8,128)(2,1)S(1)}, u32[]{:S(2)}, u32[]{:S(2)}) collective-permute-start(bf16[512,128]{1,0:T(8,128)(2,1)S(1)} %get-tuple-element.23), channel_id=1, source_target_pairs={{0,1},{2,3},{4,5},{6,7},{8,9},{10,11},{12,13},{14,15},{16,17},{18,... | collective-permute-start | bytes 393224 | tf_op jit(solution)/shard_map/ppermute | solution.py:355
  14.6 1.3 %collective-permute-start.4 = (bf16[512,128]{1,0:T(8,128)(2,1)S(1)}, bf16[512,128]{1,0:T(8,128)(2,1)S(1)}, u32[]{:S(2)}, u32[]{:S(2)}) collective-permute-start(bf16[512,128]{1,0:T(8,128)(2,1)S(1)} %get-tuple-element.23), channel_id=1, source_target_pairs={{0,2},{1,3},{4,6},{5,7},{8,10},{9,11},{12,14},{13,15},{16,18},{17,... | collective-permute-start | bytes 393224 | tf_op jit(solution)/shard_map/ppermute | solution.py:355
  16.0 1.3 %collective-permute-start.5 = (bf16[512,128]{1,0:T(8,128)(2,1)S(1)}, bf16[512,128]{1,0:T(8,128)(2,1)S(1)}, u32[]{:S(2)}, u32[]{:S(2)}) collective-permute-start(bf16[512,128]{1,0:T(8,128)(2,1)S(1)} %get-tuple-element.23), channel_id=1, source_target_pairs={{0,3},{1,2},{4,7},{5,6},{8,11},{9,10},{12,15},{13,14},{16,19},{17,... | collective-permute-start | bytes 393224 | tf_op jit(solution)/shard_map/ppermute | solution.py:355
  17.3 8.1 %weigh.1 = (bf16[4,512,1024]{2,1,0:T(8,128)(2,1)S(1)}, f32[512,128]{1,0:T(8,128)S(1)}, f32[512,128]{1,0:T(8,128)S(1)}, bf16[512,128]{1,0:T(8,128)(2,1)S(1)}, bf1...) custom-call(s32[1,8]{1,0:T(1,128)} %refs_0_.1, f32[32]{0:T(128)} %refs_1_.1, ...), custom_call_target="tpu_custom_call" | custom-call | flops 1073741824 | bytes 2097152 | tf_op jit(solution)/shard_map/weigh/pallas_call | solution.py:388
  25.4 1.3 %collective-permute-start.10 = (bf16[512,128]{1,0:T(8,128)(2,1)S(1)}, bf16[512,128]{1,0:T(8,128)(2,1)S(1)}, u32[]{:S(2)}, u32[]{:S(2)}) collective-permute-start(bf16[512,128]{1,0:T(8,128)(2,1)S(1)} %get-tuple-element.31), channel_id=1, source_target_pairs={{2,0},{3,1},{6,4},{7,5},{10,8},{11,9},{14,12},{15,13},{18,16},{19,... | collective-permute-start | bytes 393224 | tf_op jit(solution)/shard_map/ppermute | solution.py:361
  26.7 8.1 %grad.1 = (bf16[128,4096]{1,0:T(8,128)(2,1)}, bf16[512,128]{1,0:T(8,128)(2,1)S(1)}, bf16[512,128]{1,0:T(8,128)(2,1)S(1)}, bf16[512,128]{1,0:T(8,128)(2,1)S(1)}, ...) custom-call(bf16[4,512,1024]{2,1,0:T(8,128)(2,1)S(1)} %get-tuple-element.20.refs_0_, ...), custom_call_target="tpu_custom_call" | custom-call | flops 1610612736 | bytes 2097152 | tf_op jit(solution)/shard_map/grad/pallas_call | solution.py:418
  34.8 6.1 %all-to-all-start = ((f32[32,8,128]{2,1,0:T(8,128)}), f32[32,8,128]{2,1,0:T(8,128)S(1)}, u32[]{:S(2)}, u32[]{:S(2)}) async-start(f32[32,8,128]{2,1,0:T(8,128)} %bitcast.8), calls=%async_computation | async-start | bytes 262144 | tf_op jit(solution)/shard_map/all_to_all | solution.py:456
  40.8 1.3 %collective-permute-start.11 = (bf16[512,128]{1,0:T(8,128)(2,1)S(1)}, bf16[512,128]{1,0:T(8,128)(2,1)S(1)}, u32[]{:S(2)}, u32[]{:S(2)}) collective-permute-start(bf16[512,128]{1,0:T(8,128)(2,1)S(1)} %get-tuple-element.32), channel_id=1, source_target_pairs={{2,1},{3,0},{6,5},{7,4},{10,9},{11,8},{14,13},{15,12},{18,17},{19,... | collective-permute-start | bytes 393224 | tf_op jit(solution)/shard_map/ppermute | solution.py:361
  42.1 1.3 %collective-permute-start.9 = (bf16[512,128]{1,0:T(8,128)(2,1)S(1)}, bf16[512,128]{1,0:T(8,128)(2,1)S(1)}, u32[]{:S(2)}, u32[]{:S(2)}) collective-permute-start(bf16[512,128]{1,0:T(8,128)(2,1)S(1)} %get-tuple-element.30), channel_id=1, source_target_pairs={{1,0},{3,2},{5,4},{7,6},{9,8},{11,10},{13,12},{15,14},{17,16},{19,... | collective-permute-start | bytes 393224 | tf_op jit(solution)/shard_map/ppermute | solution.py:361
  43.4 1.3 %collective-permute-start.6 = (bf16[512,128]{1,0:T(8,128)(2,1)S(1)}, bf16[512,128]{1,0:T(8,128)(2,1)S(1)}, u32[]{:S(2)}, u32[]{:S(2)}) collective-permute-start(bf16[512,128]{1,0:T(8,128)(2,1)S(1)} %get-tuple-element.26), channel_id=1, source_target_pairs={{1,0},{3,2},{5,4},{7,6},{9,8},{11,10},{13,12},{15,14},{17,16},{19,... | collective-permute-start | bytes 393224 | tf_op jit(solution)/shard_map/ppermute | solution.py:361
  44.7 1.3 %collective-permute-start.7 = (bf16[512,128]{1,0:T(8,128)(2,1)S(1)}, bf16[512,128]{1,0:T(8,128)(2,1)S(1)}, u32[]{:S(2)}, u32[]{:S(2)}) collective-permute-start(bf16[512,128]{1,0:T(8,128)(2,1)S(1)} %get-tuple-element.27), channel_id=1, source_target_pairs={{2,0},{3,1},{6,4},{7,5},{10,8},{11,9},{14,12},{15,13},{18,16},{19,... | collective-permute-start | bytes 393224 | tf_op jit(solution)/shard_map/ppermute | solution.py:361
  46.1 1.3 %collective-permute-start.8 = (bf16[512,128]{1,0:T(8,128)(2,1)S(1)}, bf16[512,128]{1,0:T(8,128)(2,1)S(1)}, u32[]{:S(2)}, u32[]{:S(2)}) collective-permute-start(bf16[512,128]{1,0:T(8,128)(2,1)S(1)} %get-tuple-element.28), channel_id=1, source_target_pairs={{2,1},{3,0},{6,5},{7,4},{10,9},{11,8},{14,13},{15,12},{18,17},{19,... | collective-permute-start | bytes 393224 | tf_op jit(solution)/shard_map/ppermute | solution.py:361
  47.4 2.7 %collective-permute-done.11.refs_3_ = bf16[512,128]{1,0:T(8,128)(2,1)S(1)} collective-permute-done((bf16[512,128]{1,0:T(8,128)(2,1)S(1)}, bf16[512,128]{1,0:T(8,128)(2,1)S(1)}, u32[]{:S(2)}, u32[]{:S(2)}) %collective-permute-start.11) | collective-permute-done | bytes 131104 | tf_op jit(solution)/shard_map/ppermute | solution.py:361
  50.0 0.5 collective-permute-done.9.refs_1_
  50.5 0.7 %combine_values.1.__ = bf16[128,512]{1,0:T(8,128)(2,1)} custom-call(bf16[512,128]{1,0:T(8,128)(2,1)S(1)} %get-tuple-element.29.refs_0_, bf16[512,128]{1,0:T(8,128)(2,1)S(1)} %collective-permute-done.9.refs_1_, bf16[512,128]{1,0:T(8,128)(2,1)S(1)} %collective-permute-done.10.refs_2_, bf16[512,128]{1,0:T(8,128)(2,1)S(1)} %collective-permute-done.11.refs_3_), custom_call_target="tpu_custom_call" | custom-call | tf_op jit(solution)/shard_map/combine_values/pallas_call | solution.py:364
  51.2 1.7 %collective-permute-done.6.refs_1_ = bf16[512,128]{1,0:T(8,128)(2,1)S(1)} collective-permute-done((bf16[512,128]{1,0:T(8,128)(2,1)S(1)}, bf16[512,128]{1,0:T(8,128)(2,1)S(1)}, u32[]{:S(2)}, u32[]{:S(2)}) %collective-permute-start.6) | collective-permute-done | bytes 131104 | tf_op jit(solution)/shard_map/ppermute | solution.py:361
  52.9 0.5 collective-permute-done.7.refs_2_
  53.4 5.0 %collective-permute-done.8.refs_3_ = bf16[512,128]{1,0:T(8,128)(2,1)S(1)} collective-permute-done((bf16[512,128]{1,0:T(8,128)(2,1)S(1)}, bf16[512,128]{1,0:T(8,128)(2,1)S(1)}, u32[]{:S(2)}, u32[]{:S(2)}) %collective-permute-start.8) | collective-permute-done | bytes 131104 | tf_op jit(solution)/shard_map/ppermute | solution.py:361
  58.4 0.7 %combine_keys.1._ = bf16[128,512]{1,0:T(8,128)(2,1)} custom-call(bf16[512,128]{1,0:T(8,128)(2,1)S(1)} %get-tuple-element.25.refs_0_, bf16[512,128]{1,0:T(8,128)(2,1)S(1)} %collective-permute-done.6.refs_1_, bf16[512,128]{1,0:T(8,128)(2,1)S(1)} %collective-permute-done.7.refs_2_, bf16[512,128]{1,0:T(8,128)(2,1)S(1)} %collective-permute-done.8.refs_3_), custom_call_target="tpu_custom_call" | custom-call | tf_op jit(solution)/shard_map/combine_keys/pallas_call | solution.py:364
  59.1 0.6 bias.1
  (8 shorter events, 0.0 us)
Async XLA Ops:
  1.7 14.3 %collective-permute-start = (bf16[528,128]{1,0:T(8,128)(2,1)S(1)}, bf16[528,128]{1,0:T(8,128)(2,1)S(1)}, u32[]{:S(2)}, u32[]{:S(2)}) collective-permute-start(bf16[528,128]{1,0:T(8,128)(2,1)S(1)} %get-tuple-element.19), channel_id=1, source_target_pairs={{0,1},{2,3},{4,5},{6,7},{8,9},{10,11},{12,13},{14,15},{16,17},{18,... | collective-permute-start | bytes 405512 | tf_op jit(solution)/shard_map/ppermute | solution.py:355
  6.5 10.7 %collective-permute-start.1 = (bf16[528,128]{1,0:T(8,128)(2,1)S(1)}, bf16[528,128]{1,0:T(8,128)(2,1)S(1)}, u32[]{:S(2)}, u32[]{:S(2)}) collective-permute-start(bf16[528,128]{1,0:T(8,128)(2,1)S(1)} %get-tuple-element.19), channel_id=1, source_target_pairs={{0,2},{1,3},{4,6},{5,7},{8,10},{9,11},{12,14},{13,15},{16,18},{17,... | collective-permute-start | bytes 405512 | tf_op jit(solution)/shard_map/ppermute | solution.py:355
  10.0 7.3 %collective-permute-start.2 = (bf16[528,128]{1,0:T(8,128)(2,1)S(1)}, bf16[528,128]{1,0:T(8,128)(2,1)S(1)}, u32[]{:S(2)}, u32[]{:S(2)}) collective-permute-start(bf16[528,128]{1,0:T(8,128)(2,1)S(1)} %get-tuple-element.19), channel_id=1, source_target_pairs={{0,3},{1,2},{4,7},{5,6},{8,11},{9,10},{12,15},{13,14},{16,19},{17,... | collective-permute-start | bytes 405512 | tf_op jit(solution)/shard_map/ppermute | solution.py:355
  11.3 15.4 %collective-permute-start.3 = (bf16[512,128]{1,0:T(8,128)(2,1)S(1)}, bf16[512,128]{1,0:T(8,128)(2,1)S(1)}, u32[]{:S(2)}, u32[]{:S(2)}) collective-permute-start(bf16[512,128]{1,0:T(8,128)(2,1)S(1)} %get-tuple-element.23), channel_id=1, source_target_pairs={{0,1},{2,3},{4,5},{6,7},{8,9},{10,11},{12,13},{14,15},{16,17},{18,... | collective-permute-start | bytes 393224 | tf_op jit(solution)/shard_map/ppermute | solution.py:355
  14.6 12.0 %collective-permute-start.4 = (bf16[512,128]{1,0:T(8,128)(2,1)S(1)}, bf16[512,128]{1,0:T(8,128)(2,1)S(1)}, u32[]{:S(2)}, u32[]{:S(2)}) collective-permute-start(bf16[512,128]{1,0:T(8,128)(2,1)S(1)} %get-tuple-element.23), channel_id=1, source_target_pairs={{0,2},{1,3},{4,6},{5,7},{8,10},{9,11},{12,14},{13,15},{16,18},{17,... | collective-permute-start | bytes 393224 | tf_op jit(solution)/shard_map/ppermute | solution.py:355
  16.0 10.7 %collective-permute-start.5 = (bf16[512,128]{1,0:T(8,128)(2,1)S(1)}, bf16[512,128]{1,0:T(8,128)(2,1)S(1)}, u32[]{:S(2)}, u32[]{:S(2)}) collective-permute-start(bf16[512,128]{1,0:T(8,128)(2,1)S(1)} %get-tuple-element.23), channel_id=1, source_target_pairs={{0,3},{1,2},{4,7},{5,6},{8,11},{9,10},{12,15},{13,14},{16,19},{17,... | collective-permute-start | bytes 393224 | tf_op jit(solution)/shard_map/ppermute | solution.py:355
  25.4 20.7 %collective-permute-start.10 = (bf16[512,128]{1,0:T(8,128)(2,1)S(1)}, bf16[512,128]{1,0:T(8,128)(2,1)S(1)}, u32[]{:S(2)}, u32[]{:S(2)}) collective-permute-start(bf16[512,128]{1,0:T(8,128)(2,1)S(1)} %get-tuple-element.31), channel_id=1, source_target_pairs={{2,0},{3,1},{6,4},{7,5},{10,8},{11,9},{14,12},{15,13},{18,16},{19,... | collective-permute-start | bytes 393224 | tf_op jit(solution)/shard_map/ppermute | solution.py:361
  34.8 24.3 %all-to-all-start = ((f32[32,8,128]{2,1,0:T(8,128)}), f32[32,8,128]{2,1,0:T(8,128)S(1)}, u32[]{:S(2)}, u32[]{:S(2)}) async-start(f32[32,8,128]{2,1,0:T(8,128)} %bitcast.8), calls=%async_computation | async-start | bytes 262144 | tf_op jit(solution)/shard_map/all_to_all | solution.py:456
  40.8 9.2 %collective-permute-start.11 = (bf16[512,128]{1,0:T(8,128)(2,1)S(1)}, bf16[512,128]{1,0:T(8,128)(2,1)S(1)}, u32[]{:S(2)}, u32[]{:S(2)}) collective-permute-start(bf16[512,128]{1,0:T(8,128)(2,1)S(1)} %get-tuple-element.32), channel_id=1, source_target_pairs={{2,1},{3,0},{6,5},{7,4},{10,9},{11,8},{14,13},{15,12},{18,17},{19,... | collective-permute-start | bytes 393224 | tf_op jit(solution)/shard_map/ppermute | solution.py:361
  42.1 8.4 %collective-permute-start.9 = (bf16[512,128]{1,0:T(8,128)(2,1)S(1)}, bf16[512,128]{1,0:T(8,128)(2,1)S(1)}, u32[]{:S(2)}, u32[]{:S(2)}) collective-permute-start(bf16[512,128]{1,0:T(8,128)(2,1)S(1)} %get-tuple-element.30), channel_id=1, source_target_pairs={{1,0},{3,2},{5,4},{7,6},{9,8},{11,10},{13,12},{15,14},{17,16},{19,... | collective-permute-start | bytes 393224 | tf_op jit(solution)/shard_map/ppermute | solution.py:361
  43.4 9.5 %collective-permute-start.6 = (bf16[512,128]{1,0:T(8,128)(2,1)S(1)}, bf16[512,128]{1,0:T(8,128)(2,1)S(1)}, u32[]{:S(2)}, u32[]{:S(2)}) collective-permute-start(bf16[512,128]{1,0:T(8,128)(2,1)S(1)} %get-tuple-element.26), channel_id=1, source_target_pairs={{1,0},{3,2},{5,4},{7,6},{9,8},{11,10},{13,12},{15,14},{17,16},{19,... | collective-permute-start | bytes 393224 | tf_op jit(solution)/shard_map/ppermute | solution.py:361
  44.7 8.7 %collective-permute-start.7 = (bf16[512,128]{1,0:T(8,128)(2,1)S(1)}, bf16[512,128]{1,0:T(8,128)(2,1)S(1)}, u32[]{:S(2)}, u32[]{:S(2)}) collective-permute-start(bf16[512,128]{1,0:T(8,128)(2,1)S(1)} %get-tuple-element.27), channel_id=1, source_target_pairs={{2,0},{3,1},{6,4},{7,5},{10,8},{11,9},{14,12},{15,13},{18,16},{19,... | collective-permute-start | bytes 393224 | tf_op jit(solution)/shard_map/ppermute | solution.py:361
  46.1 12.3 %collective-permute-start.8 = (bf16[512,128]{1,0:T(8,128)(2,1)S(1)}, bf16[512,128]{1,0:T(8,128)(2,1)S(1)}, u32[]{:S(2)}, u32[]{:S(2)}) collective-permute-start(bf16[512,128]{1,0:T(8,128)(2,1)S(1)} %get-tuple-element.28), channel_id=1, source_target_pairs={{2,1},{3,0},{6,5},{7,4},{10,9},{11,8},{14,13},{15,12},{18,17},{19,... | collective-permute-start | bytes 393224 | tf_op jit(solution)/shard_map/ppermute | solution.py:361

commit v5 on v4

v5 whole, which is shorter than its diff:
```python
import functools

import jax
import jax.numpy as jnp
from jax import lax
from jax.experimental import pallas as pl
from jax.experimental.pallas import tpu as pltpu
from jax.sharding import PartitionSpec as P

WIDTH = 128
LOG2E = 1.4426950408889634
MASKED = -1e30
META_ROWS = 16
END_UNIT = 64


def dot_nt(a, b):
    return lax.dot_general(a, b, (((1,), (1,)), ((), ())), preferred_element_type=jnp.float32)


def dot_nn(a, b):
    return lax.dot_general(a, b, (((1,), (0,)), ((), ())), preferred_element_type=jnp.float32)


def fold_rows(block):
    return jnp.sum(block.reshape(block.shape[0] // 8, 8, block.shape[1]), axis=0)


def as_column(row):
    size = row.shape[1]
    return jnp.transpose(jnp.broadcast_to(row, (size, size)))


def pack_kernel(key_ref, value_ref, depth_ref, end_ref, message_ref):
    tokens = key_ref.shape[0]
    groups = key_ref.shape[1] // WIDTH
    for kind, ref in enumerate((key_ref, value_ref)):
        for group in range(groups):
            at = (kind * groups + group) * tokens
            message_ref[at : at + tokens, :] = ref[:, group * WIDTH : (group + 1) * WIDTH]
    depth = depth_ref[...]
    end = end_ref[...]
    end_high = end // END_UNIT
    end_low = end - end_high * END_UNIT
    row = lax.broadcasted_iota(jnp.int32, (META_ROWS, tokens), 0)
    meta = jnp.where(row == 0, depth, jnp.where(row == 1, end_high, end_low))
    meta = meta.astype(jnp.float32).astype(jnp.bfloat16)
    message_ref[2 * groups * tokens : 2 * groups * tokens + META_ROWS, :] = meta


def fill_tables(groups, lengths_ref, depth_ref, end_ref, remote, distance_ref, ancestor_ref):
    tokens = depth_ref.shape[1]
    here = lax.axis_index("ctx")
    query_pos = here * tokens + lax.broadcasted_iota(jnp.int32, (tokens, tokens), 1)
    start = jnp.zeros((tokens, tokens), jnp.int32)
    bound = jnp.int32(0)
    for index in range(lengths_ref.shape[1]):
        bound = bound + lengths_ref[0, index]
        start = jnp.where(query_pos >= bound, bound, start)
    query_depth = jnp.broadcast_to(depth_ref[...].astype(jnp.float32), (tokens, tokens))
    for s in range(1 + len(remote)):
        rows = slice(s * tokens, (s + 1) * tokens)
        key_pos = (here ^ s) * tokens + lax.broadcasted_iota(jnp.int32, (tokens, tokens), 0)
        if s == 0:
            key_depth = as_column(depth_ref[...].astype(jnp.float32))
            key_end = as_column(end_ref[...].astype(jnp.float32))
        else:
            below = slice(2 * groups * tokens, 2 * groups * tokens + META_ROWS)
            meta = remote[s - 1][below, :].astype(jnp.float32)
            key_depth = as_column(meta[0:1])
            key_end = as_column(meta[1:2] * END_UNIT + meta[2:3])
        inside = query_pos.astype(jnp.float32) < key_end
        allowed = (key_pos <= query_pos) & (key_pos >= start)
        distance_ref[rows, :] = jnp.abs(query_depth - key_depth)
        ancestor_ref[rows, :] = jnp.where(allowed, jnp.where(inside, 1.0, 0.0), MASKED)


def all_blocks(own_ref, remote, kind, groups, group):
    tokens = own_ref.shape[0]
    own = own_ref[:, pl.ds(pl.multiple_of(group * WIDTH, WIDTH), WIDTH)]
    at = pl.multiple_of((kind * groups + group) * tokens, tokens)
    return jnp.concatenate([own] + [r[pl.ds(at, tokens), :] for r in remote], axis=0)


def stacked(ref, group, first, count):
    heads = [slice((first + i) * WIDTH, (first + i + 1) * WIDTH) for i in range(count)]
    return jnp.concatenate([ref[group, :, h] for h in heads], axis=0)


def group_columns(group, columns):
    return pl.ds(pl.multiple_of(group * columns, columns), columns)


def group_loads(group, sources, targets, sems):
    columns = targets[0].shape[2]
    return [
        pltpu.make_async_copy(
            source.at[:, group_columns(group, columns)],
            target.at[group],
            sems.at[len(sources) * group + index],
        )
        for index, (source, target) in enumerate(zip(sources, targets))
    ]


def score_kernel(blocks, heads_per_group, groups, *refs):
    refs = list(refs)
    take = lambda count: [refs.pop(0) for _ in range(count)]
    lengths_ref, slope_ref, gain_ref, depth_ref, end_ref = take(5)
    query_hbm, output_hbm, grad_hbm, key_ref, value_ref = take(5)
    remote = take(blocks - 1)
    dscore_ref, own_probs_ref, distance_ref, ancestor_ref = take(4)
    part_refs = take(blocks - 1)
    query_ref, output_ref, grad_ref, weight_ref, probs_ref, key_acc, value_acc, load_sems = refs
    tokens = query_hbm.shape[0]
    factor = WIDTH**-0.5
    pairs = heads_per_group // 2
    block_rows = [slice(s * tokens, (s + 1) * tokens) for s in range(blocks)]

    def loads(group):
        sources = (query_hbm, output_hbm, grad_hbm)
        return group_loads(group, sources, (query_ref, output_ref, grad_ref), load_sems)

    for group in range(groups):
        for load in loads(group):
            load.start()
    fill_tables(groups, lengths_ref, depth_ref, end_ref, remote, distance_ref, ancestor_ref)

    def weigh(group, pair, raw, half):
        head = group * heads_per_group + 2 * pair + half
        gain = gain_ref[head] * LOG2E
        slope = slope_ref[head] * LOG2E
        lanes = slice(half * tokens, (half + 1) * tokens)
        tops, totals = [], []
        for rows in block_rows:
            score = raw[rows, lanes] * (factor * LOG2E) + (
                gain * ancestor_ref[rows, :] - slope * distance_ref[rows, :]
            )
            top = jnp.max(score, axis=0, keepdims=True)
            weight = jnp.exp2(score - top)
            weight_ref[pair % 2, rows, lanes] = weight
            tops.append(top)
            totals.append(jnp.sum(weight, axis=0, keepdims=True))
        top = functools.reduce(jnp.maximum, tops)
        shrink = [jnp.exp2(t - top) for t in tops]
        inverse = 1.0 / sum(a * b for a, b in zip(totals, shrink))
        return [s * inverse for s in shrink]

    def differentiate(group, pair, centred, scales, half):
        lanes = slice(half * tokens, (half + 1) * tokens)
        to = slice((2 * pair + half) * tokens, (2 * pair + half + 1) * tokens)
        for s, (rows, scale) in enumerate(zip(block_rows, scales)):
            probs = weight_ref[pair % 2, rows, lanes] * scale
            dscore_ref[group, rows, to] = (probs * centred[rows, lanes]).astype(jnp.bfloat16)
            probs_b = probs.astype(jnp.bfloat16)
            if s == 0:
                own_probs_ref[group, :, to] = probs_b
            else:
                probs_ref[(s - 1) * tokens : s * tokens, to] = probs_b

    def key_part(group, first, count):
        lanes = slice(first * tokens, (first + count) * tokens)
        return dot_nn(dscore_ref[group, tokens:, lanes], stacked(query_ref, group, first, count))

    def value_part(group, first, count):
        lanes = slice(first * tokens, (first + count) * tokens)
        return dot_nn(probs_ref[:, lanes], stacked(grad_ref, group, first, count))

    def put_part(group, kind, whole):
        at = pl.multiple_of((kind * groups + group) * tokens, tokens)
        for s, part_ref in enumerate(part_refs):
            part = whole[s * tokens : (s + 1) * tokens].astype(jnp.bfloat16)
            part_ref[pl.ds(at, tokens), :] = part

    @pl.loop(0, groups)
    def _(group):
        for load in loads(group):
            load.wait()
        keys = all_blocks(key_ref, remote, 0, groups, group)
        values = all_blocks(value_ref, remote, 1, groups, group)
        value_ext = jnp.concatenate([values, jnp.full(values.shape, -1.0, jnp.bfloat16)], axis=1)
        half_heads = heads_per_group // 2
        for pair in range(pairs):
            query_pair = stacked(query_ref, group, 2 * pair, 2)
            grad_pair = stacked(grad_ref, group, 2 * pair, 2)
            output_pair = stacked(output_ref, group, 2 * pair, 2)
            grad_ext = jnp.concatenate([grad_pair, grad_pair * output_pair], axis=1)
            raw = dot_nt(keys, query_pair)
            if pair == pairs // 2:
                key_acc[...] = key_part(group, 0, half_heads)
            scales = [weigh(group, pair, raw, half) for half in range(2)]
            if pair == pairs // 2:
                value_acc[...] = value_part(group, 0, half_heads)
            centred = dot_nt(value_ext, grad_ext)
            for half in range(2):
                differentiate(group, pair, centred, scales[half], half)
        key_whole = key_acc[...] + key_part(group, half_heads, half_heads)
        put_part(group, 0, key_whole * factor)
        put_part(group, 1, value_acc[...] + value_part(group, half_heads, half_heads))


def local_kernel(blocks, heads_per_group, groups, *refs):
    refs = list(refs)
    take = lambda count: [refs.pop(0) for _ in range(count)]
    dscore_ref, own_probs_ref, distance_ref, ancestor_ref = take(4)
    query_hbm, grad_hbm, key_ref = take(3)
    remote = take(blocks - 1)
    query_grad_hbm, own_part_ref, bias_hbm = take(3)
    (
        query_ref,
        grad_ref,
        query_grad_ref,
        slope_rows,
        gain_rows,
        bias_ref,
        load_sems,
        store_sems,
        bias_sem,
    ) = refs
    tokens = query_hbm.shape[0]
    factor = WIDTH**-0.5
    pairs = heads_per_group // 2
    block_rows = [slice(s * tokens, (s + 1) * tokens) for s in range(blocks)]

    def loads(group):
        return group_loads(group, (query_hbm, grad_hbm), (query_ref, grad_ref), load_sems)

    def store(group):
        columns = group_columns(group, query_grad_ref.shape[2])
        return pltpu.make_async_copy(
            query_grad_ref.at[group], query_grad_hbm.at[:, columns], store_sems.at[group]
        )

    for group in range(groups):
        for load in loads(group):
            load.start()

    def sum_up(group, head):
        lanes = slice(head * tokens, (head + 1) * tokens)
        slope_sum, gain_sum = 0.0, 0.0
        for rows in block_rows:
            dscore = dscore_ref[group, rows, lanes].astype(jnp.float32)
            slope_sum = slope_sum + fold_rows(dscore * distance_ref[rows, :])
            gain_sum = gain_sum + fold_rows(dscore * ancestor_ref[rows, :])
        at = pl.ds(group * heads_per_group + head, 1)
        slope_rows[at, :] = -jnp.sum(slope_sum, axis=0, keepdims=True)
        gain_rows[at, :] = jnp.sum(gain_sum, axis=0, keepdims=True)

    @pl.loop(0, groups)
    def _(group):
        for load in loads(group):
            load.wait()
        keys_across = jnp.transpose(all_blocks(key_ref, remote, 0, groups, group))
        at = pl.multiple_of(group * tokens, tokens)
        own = dot_nn(dscore_ref[group, 0:tokens, :], stacked(query_ref, group, 0, heads_per_group))
        own_part_ref[pl.ds(at, tokens), :] = (own * factor).astype(jnp.bfloat16)
        for pair in range(pairs):
            lanes = slice(2 * pair * tokens, (2 * pair + 2) * tokens)
            across = dot_nn(keys_across, dscore_ref[group, :, lanes]) * factor
            for half in range(2):
                sum_up(group, 2 * pair + half)
            rows = jnp.transpose(across.astype(jnp.bfloat16))
            for half in range(2):
                to = slice((2 * pair + half) * WIDTH, (2 * pair + half + 1) * WIDTH)
                query_grad_ref[group, :, to] = rows[half * tokens : (half + 1) * tokens]
        at = pl.multiple_of((groups + group) * tokens, tokens)
        own = dot_nn(own_probs_ref[group], stacked(grad_ref, group, 0, heads_per_group))
        own_part_ref[pl.ds(at, tokens), :] = own.astype(jnp.bfloat16)
        store(group).start()

    slope_sum = jnp.sum(slope_rows[...], axis=1, keepdims=True)
    gain_sum = jnp.sum(gain_rows[...], axis=1, keepdims=True)
    shape = slope_rows.shape
    lane = lax.broadcasted_iota(jnp.int32, shape, 1)
    row = lax.broadcasted_iota(jnp.int32, shape, 0)
    replicas, parts, rows_here, local = bias_ref.shape
    local_heads = shape[0] // parts
    kind = lax.broadcasted_iota(jnp.int32, (rows_here, local), 0)
    for part in range(parts):
        mine = (lane == row - part * local_heads) & (lane < local_heads)
        slope_line = jnp.sum(jnp.where(mine, slope_sum, 0.0), axis=0, keepdims=True)
        gain_line = jnp.sum(jnp.where(mine, gain_sum, 0.0), axis=0, keepdims=True)
        tile = jnp.where(kind == 0, slope_line, jnp.where(kind == 1, gain_line, 0.0))
        bias_ref[:, part] = jnp.broadcast_to(tile[None], (replicas, rows_here, local))
    bias_copy = pltpu.make_async_copy(bias_ref, bias_hbm, bias_sem)
    bias_copy.start()
    for group in range(groups):
        store(group).wait()
    bias_copy.wait()


def combine_kernel(blocks, *refs):
    parts = refs[0:blocks]
    key_out, value_out = refs[blocks:]
    tokens = key_out.shape[0]
    groups = key_out.shape[1] // WIDTH
    for kind, out in enumerate((key_out, value_out)):
        for group in range(groups):
            at = (kind * groups + group) * tokens
            total = parts[0][at : at + tokens, :].astype(jnp.float32)
            for s in range(1, blocks):
                total = total + parts[s][at : at + tokens, :].astype(jnp.float32)
            out[:, group * WIDTH : (group + 1) * WIDTH] = total.astype(jnp.bfloat16)


def bias_kernel(parts_ref, _, out_ref):
    out_ref[...] = jnp.sum(parts_ref[...], axis=0)[0:2, 0 : out_ref.shape[1]]


def body(
    queries,
    key_rows,
    values,
    outputs,
    out_grads,
    depths,
    subtree_end,
    file_lengths,
    slopes,
    ancestor_gain,
):
    blocks = lax.axis_size("ctx")
    replicas = lax.axis_size("dp")
    tokens, width_all = queries.shape[1:]
    kv_width = key_rows.shape[2]
    heads_all = width_all // WIDTH
    groups = kv_width // WIDTH
    heads_per_group = heads_all // groups
    columns = heads_per_group * WIDTH
    local_heads = heads_all // blocks
    keys_seen = blocks * tokens
    message_rows = 2 * groups * tokens
    bf16, f32 = jnp.bfloat16, jnp.float32
    vmem = pl.BlockSpec(memory_space=pltpu.VMEM)
    smem = pl.BlockSpec(memory_space=pltpu.SMEM)
    hbm = pl.BlockSpec(memory_space=pltpu.HBM)
    params = pltpu.CompilerParams(vmem_limit_bytes=(24 if blocks <= 4 else 48) * 1024 * 1024)
    sem = pltpu.SemaphoreType.DMA

    def hold(array):
        return pltpu.with_memory_space_constraint(array, pltpu.HBM)

    def struct(*shape, dtype=bf16):
        return jax.ShapeDtypeStruct(shape, dtype)

    def cost(matmuls, exponentials):
        return pl.CostEstimate(
            flops=matmuls * 2 * tokens * keys_seen * WIDTH * heads_all,
            bytes_accessed=4 * tokens * width_all,
            transcendentals=exponentials * tokens * keys_seen * heads_all,
        )

    query_held, output_held, grad_held = hold(queries[0]), hold(outputs[0]), hold(out_grads[0])
    key_held, value_held = hold(key_rows[0]), hold(values[0])
    depth_held, end_held = hold(depths), hold(subtree_end)
    message = pl.pallas_call(
        pack_kernel,
        out_shape=struct(message_rows + META_ROWS, WIDTH),
        in_specs=[vmem] * 4,
        out_specs=vmem,
        compiler_params=params,
        name="pack",
    )(key_held, value_held, depth_held, end_held)
    arrived = [
        lax.ppermute(message, "ctx", [(i, i ^ s) for i in range(blocks) if i < i ^ s])
        for s in range(1, blocks)
    ]

    table = struct(keys_seen, tokens, dtype=f32)
    wide = pltpu.VMEM((groups, tokens, columns), bf16)
    dscore, own_probs, distance, ancestor, *parts = pl.pallas_call(
        functools.partial(score_kernel, blocks, heads_per_group, groups),
        out_shape=[
            struct(groups, keys_seen, columns),
            struct(groups, tokens, columns),
            table,
            table,
        ]
        + [struct(message_rows, WIDTH)] * (blocks - 1),
        in_specs=[smem] * 3 + [vmem] * 2 + [hbm] * 3 + [vmem] * (1 + blocks),
        out_specs=[vmem] * (3 + blocks),
        scratch_shapes=[
            wide,
            wide,
            wide,
            pltpu.VMEM((2, keys_seen, 2 * tokens), f32),
            pltpu.VMEM((keys_seen - tokens, columns), bf16),
            pltpu.VMEM((keys_seen - tokens, WIDTH), f32),
            pltpu.VMEM((keys_seen - tokens, WIDTH), f32),
            sem((3 * groups,)),
        ],
        compiler_params=params,
        cost_estimate=cost(4, 1),
        name="scores",
    )(
        hold(file_lengths),
        hold(slopes),
        hold(ancestor_gain),
        depth_held,
        end_held,
        query_held,
        output_held,
        grad_held,
        key_held,
        value_held,
        *arrived,
    )
    returned = []
    for s in reversed(range(1, blocks)):
        back = [(i, i ^ s) for i in range(blocks) if i > i ^ s]
        returned.append(lax.ppermute(parts[s - 1], "ctx", back))

    bias_shape = (replicas, blocks, 8, WIDTH)
    query_grads, own_part, bias_parts = pl.pallas_call(
        functools.partial(local_kernel, blocks, heads_per_group, groups),
        out_shape=[
            struct(tokens, width_all),
            struct(message_rows, WIDTH),
            struct(*bias_shape, dtype=f32),
        ],
        in_specs=[vmem] * 4 + [hbm] * 2 + [vmem] * blocks,
        out_specs=[hbm, vmem, hbm],
        scratch_shapes=[
            wide,
            wide,
            wide,
            pltpu.VMEM((heads_all, tokens), f32),
            pltpu.VMEM((heads_all, tokens), f32),
            pltpu.VMEM(bias_shape, f32),
            sem((2 * groups,)),
            sem((groups,)),
            sem,
        ],
        compiler_params=params,
        cost_estimate=cost(2, 0),
        name="local",
    )(dscore, own_probs, distance, ancestor, query_held, grad_held, key_held, *arrived)
    bias_parts = bias_parts.reshape(replicas * blocks, 8, WIDTH)
    bias_parts = lax.all_to_all(bias_parts, ("dp", "ctx"), split_axis=0, concat_axis=0, tiled=True)
    key_grads, value_grads = pl.pallas_call(
        functools.partial(combine_kernel, blocks),
        out_shape=[struct(tokens, kv_width)] * 2,
        in_specs=[vmem] * blocks,
        out_specs=[vmem] * 2,
        compiler_params=params,
        name="combine",
    )(own_part, *returned)
    bias_grads = pl.pallas_call(
        bias_kernel,
        out_shape=struct(2, local_heads, dtype=f32),
        in_specs=[vmem, hbm],
        out_specs=vmem,
        compiler_params=params,
        name="bias",
    )(bias_parts, hold(key_grads))
    return (query_grads[None], key_grads[None], value_grads[None], bias_grads.T)


def solution(mesh):
    in_specs = (
        P("dp", "ctx", None),
        P("dp", "ctx", None),
        P("dp", "ctx", None),
        P("dp", "ctx", None),
        P("dp", "ctx", None),
        P("dp", "ctx"),
        P("dp", "ctx"),
        P("dp", None),
        P(),
        P(),
    )
    out_specs = (P("dp", "ctx", None), P("dp", "ctx", None), P("dp", "ctx", None), P("ctx", None))
    return jax.shard_map(body, mesh=mesh, in_specs=in_specs, out_specs=out_specs, check_vma=False)
```

time: 60.2 us -> 57.8 us (0.960)
  starting transfers between devices: 29.4 us -> 23.6 us
  waiting for transfers between devices: 10.3 us -> 15.2 us
  Pallas kernels: 19.2 us -> 18.1 us
    ppermute x12 -> x6, starting transfers between devices: 23.3 us -> 13.5 us  [the longest x3 9.59 us: body(): lax.ppermute(message, 'ctx', [(i, i ^ s) for i in range(blocks) if i < i...]
    all_to_all x1, waiting for transfers between devices: 0.01 us -> 7.58 us  [body(): lax.all_to_all(bias_parts, ('dp', 'ctx'), split_axis=0, concat_axis=0, ti...]
    all_to_all x1, starting transfers between devices: 6.06 us -> 10.1 us  [body(): lax.all_to_all(bias_parts, ('dp', 'ctx'), split_axis=0, concat_axis=0, ti...]
    ppermute x12 -> x6, waiting for transfers between devices: 10.3 us -> 7.58 us  [the longest x3 7.57 us: body(): lax.ppermute(message, 'ctx', [(i, i ^ s) for i in range(blocks) if i < i...]
    pallas_call x5 -> x4, Pallas kernels: 18.6 us -> 17.5 us  [the longest x1 9.58 us: body(): pl.pallas_call(functools.partial(score_kernel, blocks, heads_per_group, g...]
  transfers between devices with their start and end apart: 13 -> 7, of which waited for: 5 -> 4; matrix products, arithmetic and copies ran while one was open for 0% -> 0% of each run, Pallas kernels for 29% -> 12%
where the time goes in v5:
time: 57.8 us; the launch traced here: 57.5 us
  starting transfers between devices  23.6 us (41%)
  Pallas kernels  18.1 us (31%)
  waiting for transfers between devices  15.2 us (26%)
  between operations  0.73 us (1%)
    all_to_all x1, starting transfers between devices, body(): lax.all_to_all(bias_parts, ('dp', 'ctx'), split_axis=0, concat_axis=0, ti...  10.1 us
    ppermute x3, starting transfers between devices, body(): lax.ppermute(message, 'ctx', [(i, i ^ s) for i in range(blocks) if i < i...  9.59 us
    pallas_call x1, Pallas kernels, body(): pl.pallas_call(functools.partial(score_kernel, blocks, heads_per_group, g...  9.58 us
    all_to_all x1, waiting for transfers between devices, body(): lax.all_to_all(bias_parts, ('dp', 'ctx'), split_axis=0, concat_axis=0, ti...  7.58 us
    ppermute x3, waiting for transfers between devices, body(): lax.ppermute(message, 'ctx', [(i, i ^ s) for i in range(blocks) if i < i...  7.57 us
    pallas_call x1, Pallas kernels, body(): pl.pallas_call(functools.partial(local_kernel, blocks, heads_per_group, g...  6.05 us
    ppermute x3, starting transfers between devices, body(): returned.append(lax.ppermute(parts[s - 1], 'ctx', back))  3.88 us
  transfers between devices with their start and end apart: 7, of which 4 were waited for; matrix products, arithmetic and copies ran while one was open for 0% of the time, Pallas kernels for 12%

profile of v5, /device:TPU:0, one launch (start us, length us, event | category | flops | bytes accessed | tf_op | source)
XLA Modules:
  0.0 57.5 jit_solution(7776221290141387896)
XLA Ops:
  0.6 1.0 %pack.1 = bf16[1040,128]{1,0:T(8,128)(2,1)S(1)} custom-call(bf16[128,512]{1,0:T(8,128)(2,1)} %bitcast.14, bf16[128,512]{1,0:T(8,128)(2,1)} %bitcast.18, s32[1,128]{1,0:T(1,128)} %refs_3_.1, s32[1,128]{1,0:T(1,128)} %refs_4_.1), custom_call_target="tpu_custom_call" | custom-call | tf_op jit(solution)/shard_map/pack/pallas_call | solution.py:356
  1.7 5.8 %collective-permute-start.2 = (bf16[1040,128]{1,0:T(8,128)(2,1)S(1)}, bf16[1040,128]{1,0:T(8,128)(2,1)S(1)}, u32[]{:S(2)}, u32[]{:S(2)}) collective-permute-start(bf16[1040,128]{1,0:T(8,128)(2,1)S(1)} %pack.1), channel_id=1, source_target_pairs={{0,3},{1,2},{4,7},{5,6},{8,11},{9,10},{12,15},{13,14},{16,19},{17,... | collective-permute-start | bytes 798728 | tf_op jit(solution)/shard_map/ppermute | solution.py:365
  7.5 1.3 %collective-permute-start.1 = (bf16[1040,128]{1,0:T(8,128)(2,1)S(1)}, bf16[1040,128]{1,0:T(8,128)(2,1)S(1)}, u32[]{:S(2)}, u32[]{:S(2)}) collective-permute-start(bf16[1040,128]{1,0:T(8,128)(2,1)S(1)} %pack.1), channel_id=1, source_target_pairs={{0,2},{1,3},{4,6},{5,7},{8,10},{9,11},{12,14},{13,15},{16,18},{17,... | collective-permute-start | bytes 798728 | tf_op jit(solution)/shard_map/ppermute | solution.py:365
  8.8 2.5 %collective-permute-start = (bf16[1040,128]{1,0:T(8,128)(2,1)S(1)}, bf16[1040,128]{1,0:T(8,128)(2,1)S(1)}, u32[]{:S(2)}, u32[]{:S(2)}) collective-permute-start(bf16[1040,128]{1,0:T(8,128)(2,1)S(1)} %pack.1), channel_id=1, source_target_pairs={{0,1},{2,3},{4,5},{6,7},{8,9},{10,11},{12,13},{14,15},{16,17},{18,... | collective-permute-start | bytes 798728 | tf_op jit(solution)/shard_map/ppermute | solution.py:365
  11.3 3.0 %collective-permute-done.2.refs_12_.refs_9_ = bf16[1040,128]{1,0:T(8,128)(2,1)S(1)} collective-permute-done((bf16[1040,128]{1,0:T(8,128)(2,1)S(1)}, bf16[1040,128]{1,0:T(8,128)(2,1)S(1)}, u32[]{:S(2)}, u32[]{:S(2)}) %collective-permute-start.2) | collective-permute-done | bytes 266272 | tf_op jit(solution)/shard_map/ppermute | solution.py:365
  14.3 4.5 %collective-permute-done.1.refs_11_.refs_8_ = bf16[1040,128]{1,0:T(8,128)(2,1)S(1)} collective-permute-done((bf16[1040,128]{1,0:T(8,128)(2,1)S(1)}, bf16[1040,128]{1,0:T(8,128)(2,1)S(1)}, u32[]{:S(2)}, u32[]{:S(2)}) %collective-permute-start.1) | collective-permute-done | bytes 266272 | tf_op jit(solution)/shard_map/ppermute | solution.py:365
  18.8 0.1 collective-permute-done.refs_10_.refs_7_
  18.9 9.6 %scores.1 = (bf16[4,512,1024]{2,1,0:T(8,128)(2,1)S(1)}, bf16[4,128,1024]{2,1,0:T(8,128)(2,1)S(1)}, f32[512,128]{1,0:T(8,128)S(1)}, f32[512,128]{1,0:T(8,128)S(1)...) custom-call(s32[1,8]{1,0:T(1,128)} %refs_0_.1, f32[32]{0:T(128)} %refs_1_.1, ...), custom_call_target="tpu_custom_call" | custom-call | flops 2147483648 | bytes 2097152 | tf_op jit(solution)/shard_map/scores/pallas_call | solution.py:371
  28.4 1.3 %collective-permute-start.3 = (bf16[1024,128]{1,0:T(8,128)(2,1)S(1)}, bf16[1024,128]{1,0:T(8,128)(2,1)S(1)}, u32[]{:S(2)}, u32[]{:S(2)}) collective-permute-start(bf16[1024,128]{1,0:T(8,128)(2,1)S(1)} %get-tuple-element.22), channel_id=1, source_target_pairs={{2,1},{3,0},{6,5},{7,4},{10,9},{11,8},{14,13},{15,12},{18,17},{19,... | collective-permute-start | bytes 786440 | tf_op jit(solution)/shard_map/ppermute | solution.py:411
  29.7 1.3 %collective-permute-start.4 = (bf16[1024,128]{1,0:T(8,128)(2,1)S(1)}, bf16[1024,128]{1,0:T(8,128)(2,1)S(1)}, u32[]{:S(2)}, u32[]{:S(2)}) collective-permute-start(bf16[1024,128]{1,0:T(8,128)(2,1)S(1)} %get-tuple-element.23), channel_id=1, source_target_pairs={{2,0},{3,1},{6,4},{7,5},{10,8},{11,9},{14,12},{15,13},{18,16},{19,... | collective-permute-start | bytes 786440 | tf_op jit(solution)/shard_map/ppermute | solution.py:411
  31.0 1.3 %collective-permute-start.5 = (bf16[1024,128]{1,0:T(8,128)(2,1)S(1)}, bf16[1024,128]{1,0:T(8,128)(2,1)S(1)}, u32[]{:S(2)}, u32[]{:S(2)}) collective-permute-start(bf16[1024,128]{1,0:T(8,128)(2,1)S(1)} %get-tuple-element.24), channel_id=1, source_target_pairs={{1,0},{3,2},{5,4},{7,6},{9,8},{11,10},{13,12},{15,14},{17,16},{19,... | collective-permute-start | bytes 786440 | tf_op jit(solution)/shard_map/ppermute | solution.py:411
  32.3 6.0 %local.1 = (bf16[128,4096]{1,0:T(8,128)(2,1)}, bf16[1024,128]{1,0:T(8,128)(2,1)S(1)}, f32[8,4,8,128]{3,2,1,0:T(8,128)}) custom-call(bf16[4,512,1024]{2,1,0:T(8,128)(2,1)S(1)} %get-tuple-element.16.refs_0_, bf16[4,128,1024]{2,1,0:T(8,128)(2,1)S(1)} %get-tuple-element.17.refs_1_, f32[512,128]{1,0:T(8,128)S(1)} %get-tuple-element.18.refs_2_, ...), custom_call_target="tpu_custom_call" | custom-call | flops 1073741824 | bytes 2097152 | tf_op jit(solution)/shard_map/local/pallas_call | solution.py:414
  38.4 10.1 %all-to-all-start = ((f32[32,8,128]{2,1,0:T(8,128)}), f32[32,8,128]{2,1,0:T(8,128)S(1)}, u32[]{:S(2)}, u32[]{:S(2)}) async-start(f32[32,8,128]{2,1,0:T(8,128)} %bitcast.8), calls=%async_computation | async-start | bytes 262144 | tf_op jit(solution)/shard_map/all_to_all | solution.py:439
  48.5 0.0 collective-permute-done.3.refs_1_
  48.5 0.0 collective-permute-done.4.refs_2_
  48.5 0.0 collective-permute-done.5.refs_3_
  48.5 0.8 %combine.1 = (bf16[128,512]{1,0:T(8,128)(2,1)}, bf16[128,512]{1,0:T(8,128)(2,1)}) custom-call(bf16[1024,128]{1,0:T(8,128)(2,1)S(1)} %get-tuple-element.21.refs_0_, bf16[1024,128]{1,0:T(8,128)(2,1)S(1)} %collective-permute-done.3.refs_1_, bf16[1024,128]{1,0:T(8,128)(2,1)S(1)} %collective-permute-done.4.refs_2_, ...), custom_call_target="tpu_custom_call" | custom-call | tf_op jit(solution)/shard_map/combine/pallas_call | solution.py:440
  49.3 7.6 %all-to-all-done.parts_ref = f32[32,8,128]{2,1,0:T(8,128)S(1)} async-done(((f32[32,8,128]{2,1,0:T(8,128)}), f32[32,8,128]{2,1,0:T(8,128)S(1)}, u32[]{:S(2)}, u32[]{:S(2)}) %all-to-all-start) | async-done | bytes 131104 | tf_op jit(solution)/shard_map/all_to_all | solution.py:439
  56.9 0.6 %bias.1 = f32[2,8]{1,0:T(2,128)} custom-call(f32[32,8,128]{2,1,0:T(8,128)S(1)} %all-to-all-done.parts_ref, bf16[128,512]{1,0:T(8,128)(2,1)} %get-tuple-element.25._), custom_call_target="tpu_custom_call" | custom-call | tf_op jit(solution)/shard_map/bias/pallas_call | solution.py:448
Async XLA Ops:
  1.7 12.6 %collective-permute-start.2 = (bf16[1040,128]{1,0:T(8,128)(2,1)S(1)}, bf16[1040,128]{1,0:T(8,128)(2,1)S(1)}, u32[]{:S(2)}, u32[]{:S(2)}) collective-permute-start(bf16[1040,128]{1,0:T(8,128)(2,1)S(1)} %pack.1), channel_id=1, source_target_pairs={{0,3},{1,2},{4,7},{5,6},{8,11},{9,10},{12,15},{13,14},{16,19},{17,... | collective-permute-start | bytes 798728 | tf_op jit(solution)/shard_map/ppermute | solution.py:365
  7.5 11.3 %collective-permute-start.1 = (bf16[1040,128]{1,0:T(8,128)(2,1)S(1)}, bf16[1040,128]{1,0:T(8,128)(2,1)S(1)}, u32[]{:S(2)}, u32[]{:S(2)}) collective-permute-start(bf16[1040,128]{1,0:T(8,128)(2,1)S(1)} %pack.1), channel_id=1, source_target_pairs={{0,2},{1,3},{4,6},{5,7},{8,10},{9,11},{12,14},{13,15},{16,18},{17,... | collective-permute-start | bytes 798728 | tf_op jit(solution)/shard_map/ppermute | solution.py:365
  8.8 10.1 %collective-permute-start = (bf16[1040,128]{1,0:T(8,128)(2,1)S(1)}, bf16[1040,128]{1,0:T(8,128)(2,1)S(1)}, u32[]{:S(2)}, u32[]{:S(2)}) collective-permute-start(bf16[1040,128]{1,0:T(8,128)(2,1)S(1)} %pack.1), channel_id=1, source_target_pairs={{0,1},{2,3},{4,5},{6,7},{8,9},{10,11},{12,13},{14,15},{16,17},{18,... | collective-permute-start | bytes 798728 | tf_op jit(solution)/shard_map/ppermute | solution.py:365
  28.4 20.1 %collective-permute-start.3 = (bf16[1024,128]{1,0:T(8,128)(2,1)S(1)}, bf16[1024,128]{1,0:T(8,128)(2,1)S(1)}, u32[]{:S(2)}, u32[]{:S(2)}) collective-permute-start(bf16[1024,128]{1,0:T(8,128)(2,1)S(1)} %get-tuple-element.22), channel_id=1, source_target_pairs={{2,1},{3,0},{6,5},{7,4},{10,9},{11,8},{14,13},{15,12},{18,17},{19,... | collective-permute-start | bytes 786440 | tf_op jit(solution)/shard_map/ppermute | solution.py:411
  29.7 18.8 %collective-permute-start.4 = (bf16[1024,128]{1,0:T(8,128)(2,1)S(1)}, bf16[1024,128]{1,0:T(8,128)(2,1)S(1)}, u32[]{:S(2)}, u32[]{:S(2)}) collective-permute-start(bf16[1024,128]{1,0:T(8,128)(2,1)S(1)} %get-tuple-element.23), channel_id=1, source_target_pairs={{2,0},{3,1},{6,4},{7,5},{10,8},{11,9},{14,12},{15,13},{18,16},{19,... | collective-permute-start | bytes 786440 | tf_op jit(solution)/shard_map/ppermute | solution.py:411
  31.0 17.5 %collective-permute-start.5 = (bf16[1024,128]{1,0:T(8,128)(2,1)S(1)}, bf16[1024,128]{1,0:T(8,128)(2,1)S(1)}, u32[]{:S(2)}, u32[]{:S(2)}) collective-permute-start(bf16[1024,128]{1,0:T(8,128)(2,1)S(1)} %get-tuple-element.24), channel_id=1, source_target_pairs={{1,0},{3,2},{5,4},{7,6},{9,8},{11,10},{13,12},{15,14},{17,16},{19,... | collective-permute-start | bytes 786440 | tf_op jit(solution)/shard_map/ppermute | solution.py:411
  38.4 18.5 %all-to-all-start = ((f32[32,8,128]{2,1,0:T(8,128)}), f32[32,8,128]{2,1,0:T(8,128)S(1)}, u32[]{:S(2)}, u32[]{:S(2)}) async-start(f32[32,8,128]{2,1,0:T(8,128)} %bitcast.8), calls=%async_computation | async-start | bytes 262144 | tf_op jit(solution)/shard_map/all_to_all | solution.py:439

commit v6 on v2

v6 whole, which is shorter than its diff:
```python
import functools

import jax
import jax.numpy as jnp
from jax import lax
from jax.experimental import pallas as pl
from jax.experimental.pallas import tpu as pltpu
from jax.sharding import PartitionSpec as P

WIDTH = 128
LOG2E = 1.4426950408889634
MASKED = -1e30
META_ROWS = 16
END_UNIT = 64
CHUNKS = 2


def dot_nt(a, b):
    return lax.dot_general(a, b, (((1,), (1,)), ((), ())), preferred_element_type=jnp.float32)


def dot_nn(a, b):
    return lax.dot_general(a, b, (((1,), (0,)), ((), ())), preferred_element_type=jnp.float32)


def fold_rows(block):
    return jnp.sum(block.reshape(block.shape[0] // 8, 8, block.shape[1]), axis=0)


def as_column(row):
    size = row.shape[1]
    return jnp.transpose(jnp.broadcast_to(row, (size, size)))


def pack_kernel(key_ref, value_ref, depth_ref, end_ref, *message_refs):
    tokens = key_ref.shape[0]
    groups = key_ref.shape[1] // WIDTH // len(message_refs)
    for chunk, message_ref in enumerate(message_refs):
        for kind, ref in enumerate((key_ref, value_ref)):
            for group in range(groups):
                at = (kind * groups + group) * tokens
                source = slice((chunk * groups + group) * WIDTH, (chunk * groups + group + 1) * WIDTH)
                message_ref[at : at + tokens, :] = ref[:, source]
    depth = depth_ref[...]
    end = end_ref[...]
    end_high = end // END_UNIT
    end_low = end - end_high * END_UNIT
    row = lax.broadcasted_iota(jnp.int32, (META_ROWS, tokens), 0)
    meta = jnp.where(row == 0, depth, jnp.where(row == 1, end_high, end_low))
    meta = meta.astype(jnp.float32).astype(jnp.bfloat16)
    message_refs[0][2 * groups * tokens : 2 * groups * tokens + META_ROWS, :] = meta


def fill_tables(groups, lengths_ref, depth_ref, end_ref, remote, distance_ref, ancestor_ref):
    tokens = depth_ref.shape[1]
    here = lax.axis_index("ctx")
    query_pos = here * tokens + lax.broadcasted_iota(jnp.int32, (tokens, tokens), 1)
    start = jnp.zeros((tokens, tokens), jnp.int32)
    bound = jnp.int32(0)
    for index in range(lengths_ref.shape[1]):
        bound = bound + lengths_ref[0, index]
        start = jnp.where(query_pos >= bound, bound, start)
    query_depth = jnp.broadcast_to(depth_ref[...].astype(jnp.float32), (tokens, tokens))
    for s in range(1 + len(remote)):
        rows = slice(s * tokens, (s + 1) * tokens)
        key_pos = (here ^ s) * tokens + lax.broadcasted_iota(jnp.int32, (tokens, tokens), 0)
        if s == 0:
            key_depth = as_column(depth_ref[...].astype(jnp.float32))
            key_end = as_column(end_ref[...].astype(jnp.float32))
        else:
            below = slice(2 * groups * tokens, 2 * groups * tokens + META_ROWS)
            meta = remote[s - 1][below, :].astype(jnp.float32)
            key_depth = as_column(meta[0:1])
            key_end = as_column(meta[1:2] * END_UNIT + meta[2:3])
        inside = query_pos.astype(jnp.float32) < key_end
        allowed = (key_pos <= query_pos) & (key_pos >= start)
        distance_ref[rows, :] = jnp.abs(query_depth - key_depth)
        ancestor_ref[rows, :] = jnp.where(allowed, jnp.where(inside, 1.0, 0.0), MASKED)


def all_blocks(own_ref, remote, kind, first_group, groups, group):
    tokens = own_ref.shape[0]
    own = own_ref[:, pl.ds(pl.multiple_of((first_group + group) * WIDTH, WIDTH), WIDTH)]
    at = pl.multiple_of((kind * groups + group) * tokens, tokens)
    return jnp.concatenate([own] + [r[pl.ds(at, tokens), :] for r in remote], axis=0)


def stacked(ref, group, first, count):
    heads = [slice((first + i) * WIDTH, (first + i + 1) * WIDTH) for i in range(count)]
    return jnp.concatenate([ref[group, :, h] for h in heads], axis=0)


def query_part(keys_across, dscore, query_grad_ref, group, pair):
    tokens = query_grad_ref.shape[1]
    rows = jnp.transpose((dot_nn(keys_across, dscore) * WIDTH**-0.5).astype(jnp.bfloat16))
    for half in range(2):
        to = slice((2 * pair + half) * WIDTH, (2 * pair + half + 1) * WIDTH)
        query_grad_ref[group, :, to] = rows[half * tokens : (half + 1) * tokens]


def group_copy(whole_hbm, first_group, group, ref, sem, outward=False):
    columns = ref.shape[2]
    at = pl.multiple_of((first_group + group) * columns, columns)
    far, near = whole_hbm.at[:, pl.ds(at, columns)], ref.at[group]
    return pltpu.make_async_copy(*((near, far) if outward else (far, near)), sem.at[group])


def main_kernel(blocks, heads_per_group, groups, chunk, last_chunk, *refs):
    refs = list(refs)
    take = lambda count: [refs.pop(0) for _ in range(count)]
    slope_ref, gain_ref, query_hbm, output_hbm, grad_hbm, key_ref, value_ref = take(7)
    remote = take(blocks - 1)
    if chunk == 0:
        lengths_ref, depth_ref, end_ref = take(3)
    else:
        distance_ref, ancestor_ref, sums_before = take(3)
        parts_before = take(blocks)
    part_refs = take(blocks)
    if chunk == 0:
        distance_ref, ancestor_ref = take(2)
    if last_chunk:
        dscore_ref, bias_ref = take(2)
    else:
        query_grad_hbm, sums_ref = take(2)
    query_ref, output_ref, grad_ref, weight_ref, probs_ref, key_acc, value_acc = take(7)
    load_sems = take(3)
    if last_chunk:
        (sums_ref,) = refs
    else:
        dscore_ref, query_grad_ref, store_sem = refs
    tokens = query_hbm.shape[0]
    factor = WIDTH**-0.5
    pairs = heads_per_group // 2
    first_group = chunk * groups
    block_rows = [slice(s * tokens, (s + 1) * tokens) for s in range(blocks)]

    def loads(group):
        sources = (query_hbm, output_hbm, grad_hbm)
        targets = (query_ref, output_ref, grad_ref)
        return [
            group_copy(source, first_group, group, target, sem)
            for source, target, sem in zip(sources, targets, load_sems)
        ]

    def store(group):
        return group_copy(query_grad_hbm, first_group, group, query_grad_ref, store_sem, True)

    for group in range(groups):
        for load in loads(group):
            load.start()

    if chunk == 0:
        fill_tables(groups, lengths_ref, depth_ref, end_ref, remote, distance_ref, ancestor_ref)
    else:
        for s in range(blocks):
            for kind in range(2):
                size = first_group * tokens
                at = kind * (first_group + groups) * tokens
                part_refs[s][at : at + size, :] = parts_before[s][kind * size : (kind + 1) * size, :]

    def weigh(group, pair, raw, half):
        head = (first_group + group) * heads_per_group + 2 * pair + half
        gain = gain_ref[head] * LOG2E
        slope = slope_ref[head] * LOG2E
        lanes = slice(half * tokens, (half + 1) * tokens)
        tops, totals = [], []
        for rows in block_rows:
            score = raw[rows, lanes] * (factor * LOG2E) + (
                gain * ancestor_ref[rows, :] - slope * distance_ref[rows, :]
            )
            top = jnp.max(score, axis=0, keepdims=True)
            weight = jnp.exp2(score - top)
            weight_ref[pair % 2, rows, lanes] = weight
            tops.append(top)
            totals.append(jnp.sum(weight, axis=0, keepdims=True))
        top = functools.reduce(jnp.maximum, tops)
        shrink = [jnp.exp2(t - top) for t in tops]
        inverse = 1.0 / sum(a * b for a, b in zip(totals, shrink))
        return [s * inverse for s in shrink]

    def differentiate(group, pair, slot, centred, scales, half):
        lanes = slice(half * tokens, (half + 1) * tokens)
        to = slice((2 * pair + half) * tokens, (2 * pair + half + 1) * tokens)
        slope_sum, gain_sum = 0.0, 0.0
        for rows, scale in zip(block_rows, scales):
            probs = weight_ref[pair % 2, rows, lanes] * scale
            dscore = probs * centred[rows, lanes]
            probs_ref[rows, to] = probs.astype(jnp.bfloat16)
            dscore_ref[slot, rows, to] = dscore.astype(jnp.bfloat16)
            slope_sum = slope_sum + fold_rows(dscore * distance_ref[rows, :])
            gain_sum = gain_sum + fold_rows(dscore * ancestor_ref[rows, :])
        at = pl.ds((first_group + group) * heads_per_group + 2 * pair + half, 1)
        sums_ref[0, at, :] = -jnp.sum(slope_sum, axis=0, keepdims=True)
        sums_ref[1, at, :] = jnp.sum(gain_sum, axis=0, keepdims=True)

    def key_part(group, slot, first, count):
        lanes = slice(first * tokens, (first + count) * tokens)
        return dot_nn(dscore_ref[slot, :, lanes], stacked(query_ref, group, first, count))

    def value_part(group, first, count):
        lanes = slice(first * tokens, (first + count) * tokens)
        return dot_nn(probs_ref[:, lanes], stacked(grad_ref, group, first, count))

    def put_part(group, kind, whole):
        at = (kind * (first_group + groups) + first_group + group) * tokens
        for s, rows in enumerate(block_rows):
            to = pl.ds(pl.multiple_of(at, tokens), tokens)
            part_refs[s][to, :] = whole[rows].astype(jnp.bfloat16)

    @pl.loop(0, groups)
    def _(group):
        for load in loads(group):
            load.wait()
        slot = group if last_chunk else 0
        keys = all_blocks(key_ref, remote, 0, first_group, groups, group)
        values = all_blocks(value_ref, remote, 1, first_group, groups, group)
        value_ext = jnp.concatenate([values, jnp.full(values.shape, -1.0, jnp.bfloat16)], axis=1)
        keys_across = None if last_chunk else jnp.transpose(keys)

        def query_pair_part(pair):
            if not last_chunk:
                lanes = slice(2 * pair * tokens, (2 * pair + 2) * tokens)
                query_part(keys_across, dscore_ref[slot, :, lanes], query_grad_ref, group, pair)

        half_heads = heads_per_group // 2
        for pair in range(pairs):
            query_pair = stacked(query_ref, group, 2 * pair, 2)
            grad_pair = stacked(grad_ref, group, 2 * pair, 2)
            output_pair = stacked(output_ref, group, 2 * pair, 2)
            grad_ext = jnp.concatenate([grad_pair, grad_pair * output_pair], axis=1)
            raw = dot_nt(keys, query_pair)
            if pair == pairs // 2:
                key_acc[...] = key_part(group, slot, 0, half_heads)
            scales = [weigh(group, pair, raw, half) for half in range(2)]
            if pair == pairs // 2:
                value_acc[...] = value_part(group, 0, half_heads)
            if pair:
                query_pair_part(pair - 1)
            centred = dot_nt(value_ext, grad_ext)
            for half in range(2):
                differentiate(group, pair, slot, centred, scales[half], half)
        key_whole = key_acc[...] + key_part(group, slot, half_heads, half_heads)
        put_part(group, 0, key_whole * factor)
        put_part(group, 1, value_acc[...] + value_part(group, half_heads, half_heads))
        query_pair_part(pairs - 1)
        if not last_chunk:
            store(group).start()

    if last_chunk:
        heads = heads_per_group * first_group
        rows = [
            jnp.concatenate([sums_before[kind, 0:heads, :], sums_ref[kind, heads:, :]], axis=0)
            for kind in range(2)
        ]
        sums = [jnp.sum(r, axis=1, keepdims=True) for r in rows]
        shape = rows[0].shape
        diagonal = lax.broadcasted_iota(jnp.int32, shape, 0) == lax.broadcasted_iota(
            jnp.int32, shape, 1
        )
        lines = [
            jnp.sum(jnp.where(diagonal, column, 0.0), axis=0, keepdims=True) for column in sums
        ]
        row = lax.broadcasted_iota(jnp.int32, bias_ref.shape[1:], 0)
        tile = jnp.where(row == 0, lines[0], jnp.where(row == 1, lines[1], 0.0))
        bias_ref[...] = jnp.broadcast_to(tile[None], bias_ref.shape)
    else:
        for group in range(groups):
            store(group).wait()


def query_kernel(blocks, groups, first_group, *refs):
    dscore_ref, key_ref = refs[0:2]
    remote = refs[2 : 1 + blocks]
    _, query_grad_hbm, query_grad_ref, store_sem = refs[1 + blocks :]
    tokens = key_ref.shape[0]

    def store(group):
        return group_copy(query_grad_hbm, first_group, group, query_grad_ref, store_sem, True)

    @pl.loop(0, groups)
    def _(group):
        keys_across = jnp.transpose(all_blocks(key_ref, remote, 0, first_group, groups, group))
        for pair in range(query_grad_ref.shape[2] // WIDTH // 2):
            lanes = slice(2 * pair * tokens, (2 * pair + 2) * tokens)
            query_part(keys_across, dscore_ref[group, :, lanes], query_grad_ref, group, pair)
        store(group).start()

    for group in range(groups):
        store(group).wait()


def combine_kernel(blocks, *refs):
    parts = refs[0:blocks]
    key_out, value_out = refs[blocks:]
    tokens = key_out.shape[0]
    groups = key_out.shape[1] // WIDTH
    for kind, out in enumerate((key_out, value_out)):
        for group in range(groups):
            at = (kind * groups + group) * tokens
            total = parts[0][at : at + tokens, :].astype(jnp.float32)
            for s in range(1, blocks):
                total = total + parts[s][at : at + tokens, :].astype(jnp.float32)
            out[:, group * WIDTH : (group + 1) * WIDTH] = total.astype(jnp.bfloat16)


def spread_kernel(sums_ref, _, spread_ref):
    total = jnp.sum(sums_ref[...], axis=0)
    share = spread_ref.shape[2]
    for block in range(spread_ref.shape[0]):
        spread_ref[block] = total[:, block * share : (block + 1) * share]


def bias_kernel(parts_ref, _, out_ref):
    out_ref[...] = jnp.sum(parts_ref[...], axis=0)[0:2]


def body(
    queries,
    key_rows,
    values,
    outputs,
    out_grads,
    depths,
    subtree_end,
    file_lengths,
    slopes,
    ancestor_gain,
):
    blocks = lax.axis_size("ctx")
    replicas = lax.axis_size("dp")
    tokens, width_all = queries.shape[1:]
    kv_width = key_rows.shape[2]
    heads_all = width_all // WIDTH
    kv_heads = kv_width // WIDTH
    heads_per_group = heads_all // kv_heads
    group_columns = heads_per_group * WIDTH
    local_heads = heads_all // blocks
    keys_seen = blocks * tokens
    groups = kv_heads // CHUNKS
    bf16, f32 = jnp.bfloat16, jnp.float32
    vmem = pl.BlockSpec(memory_space=pltpu.VMEM)
    smem = pl.BlockSpec(memory_space=pltpu.SMEM)
    hbm = pl.BlockSpec(memory_space=pltpu.HBM)
    params = pltpu.CompilerParams(vmem_limit_bytes=(36 if blocks <= 4 else 48) * 1024 * 1024)

    def hold(array):
        return pltpu.with_memory_space_constraint(array, pltpu.HBM)

    def struct(shape, dtype):
        return jax.ShapeDtypeStruct(shape, dtype)

    key_held, value_held = hold(key_rows[0]), hold(values[0])
    depth_held, end_held = hold(depths), hold(subtree_end)
    chunk_rows = 2 * groups * tokens
    messages = pl.pallas_call(
        pack_kernel,
        out_shape=[
            struct((chunk_rows + (0 if chunk else META_ROWS), WIDTH), bf16)
            for chunk in range(CHUNKS)
        ],
        in_specs=[vmem] * 4,
        out_specs=[vmem] * CHUNKS,
        compiler_params=params,
        name="pack",
    )(key_held, value_held, depth_held, end_held)
    arrived = [
        [
            lax.ppermute(message, "ctx", [(i, i ^ s) for i in range(blocks) if i < i ^ s])
            for s in range(1, blocks)
        ]
        for message in messages
    ]

    matmul_flops = 2 * tokens * keys_seen * WIDTH * heads_all
    table = struct((keys_seen, tokens), f32)
    sums = struct((2, heads_all, tokens), f32)
    wide = pltpu.VMEM((groups, tokens, group_columns), bf16)
    group_sems = pltpu.SemaphoreType.DMA((groups,))
    for chunk in range(CHUNKS):
        last_chunk = chunk == CHUNKS - 1
        operands = [
            hold(slopes),
            hold(ancestor_gain),
            hold(queries[0]),
            hold(outputs[0]),
            hold(out_grads[0]),
            key_held,
            value_held,
            *arrived[chunk],
        ]
        specs = [smem] * 2 + [hbm] * 3 + [vmem] * (1 + blocks)
        out_shape = [struct(((chunk + 1) * chunk_rows, WIDTH), bf16)] * blocks
        if chunk == 0:
            operands = operands + [hold(file_lengths), depth_held, end_held]
            specs = specs + [smem, vmem, vmem]
            out_shape = out_shape + [table, table]
        else:
            operands = operands + [*tables, sums_before, *parts]
            specs = specs + [vmem] * (3 + blocks)
        out_specs = [vmem] * len(out_shape)
        scratch = [
            wide,
            wide,
            wide,
            pltpu.VMEM((2, keys_seen, 2 * tokens), f32),
            pltpu.VMEM((keys_seen, group_columns), bf16),
            pltpu.VMEM((keys_seen, WIDTH), f32),
            pltpu.VMEM((keys_seen, WIDTH), f32),
            group_sems,
            group_sems,
            group_sems,
        ]
        if last_chunk:
            out_shape = out_shape + [
                struct((groups, keys_seen, group_columns), bf16),
                struct((replicas, 8, WIDTH), f32),
            ]
            out_specs = out_specs + [vmem, vmem]
            scratch = scratch + [pltpu.VMEM(sums.shape, f32)]
        else:
            out_shape = out_shape + [struct((tokens, width_all), bf16), sums]
            out_specs = out_specs + [hbm, vmem]
            dscore_slot = pltpu.VMEM((1, keys_seen, group_columns), bf16)
            scratch = scratch + [dscore_slot, wide, group_sems]
        results = pl.pallas_call(
            functools.partial(main_kernel, blocks, heads_per_group, groups, chunk, last_chunk),
            out_shape=out_shape,
            in_specs=specs,
            out_specs=out_specs,
            scratch_shapes=scratch,
            compiler_params=params,
            cost_estimate=pl.CostEstimate(
                flops=5 * matmul_flops // CHUNKS,
                bytes_accessed=10 * tokens * width_all // CHUNKS,
                transcendentals=tokens * keys_seen * heads_all // CHUNKS,
            ),
            name=f"attend_{chunk}",
        )(*operands)
        parts = list(results[0:blocks])
        if chunk == 0:
            tables = results[blocks : 2 + blocks]
        if last_chunk:
            dscore, sums_here = results[-2:]
        else:
            query_grads, sums_before = results[-2:]

    returned = [parts[0]]
    for s in reversed(range(1, blocks)):
        back = [(i, i ^ s) for i in range(blocks) if i > i ^ s]
        returned.append(lax.ppermute(parts[s], "ctx", back))
    sums_of_all = lax.all_to_all(sums_here, "dp", split_axis=0, concat_axis=0, tiled=True)
    query_grads = pl.pallas_call(
        functools.partial(query_kernel, blocks, groups, (CHUNKS - 1) * groups),
        out_shape=struct((tokens, width_all), bf16),
        in_specs=[vmem] * (1 + blocks) + [hbm],
        out_specs=hbm,
        scratch_shapes=[wide, group_sems],
        input_output_aliases={1 + blocks: 0},
        compiler_params=params,
        cost_estimate=pl.CostEstimate(
            flops=matmul_flops // CHUNKS,
            bytes_accessed=2 * tokens * width_all // CHUNKS,
            transcendentals=0,
        ),
        name="query",
    )(dscore, key_held, *arrived[CHUNKS - 1], query_grads)
    spread = pl.pallas_call(
        spread_kernel,
        out_shape=struct((blocks, 8, local_heads), f32),
        in_specs=[vmem, hbm],
        out_specs=vmem,
        compiler_params=params,
        name="spread",
    )(sums_of_all, hold(query_grads))
    bias_parts = lax.all_to_all(spread, "ctx", split_axis=0, concat_axis=0, tiled=True)
    key_grads, value_grads = pl.pallas_call(
        functools.partial(combine_kernel, blocks),
        out_shape=[struct((tokens, kv_width), bf16)] * 2,
        in_specs=[vmem] * blocks,
        out_specs=[vmem] * 2,
        compiler_params=params,
        name="combine",
    )(*returned)
    bias_grads = pl.pallas_call(
        bias_kernel,
        out_shape=struct((2, local_heads), f32),
        in_specs=[vmem, hbm],
        out_specs=vmem,
        compiler_params=params,
        name="bias",
    )(bias_parts, hold(key_grads))
    return (query_grads[None], key_grads[None], value_grads[None], bias_grads.T)


def solution(mesh):
    in_specs = (
        P("dp", "ctx", None),
        P("dp", "ctx", None),
        P("dp", "ctx", None),
        P("dp", "ctx", None),
        P("dp", "ctx", None),
        P("dp", "ctx"),
        P("dp", "ctx"),
        P("dp", None),
        P(),
        P(),
    )
    out_specs = (P("dp", "ctx", None), P("dp", "ctx", None), P("dp", "ctx", None), P("ctx", None))
    return jax.shard_map(body, mesh=mesh, in_specs=in_specs, out_specs=out_specs, check_vma=False)
```

time: 58.7 us -> 60.8 us (1.036)
  blocking collectives: 21 us -> 0 us
  starting transfers between devices: 19.4 us -> 30.3 us
  waiting for transfers between devices: 0.02 us -> 7.31 us
  Pallas kernels: 17.1 us -> 21.2 us
  local copies, waits for them, and re-layouts: 0 us -> 0.61 us
    all_to_all x2 -> x0, blocking collectives: 21 us -> none  [the longest x1 10.5 us: body(): lax.all_to_all(spread, 'ctx', split_axis=0, concat_axis=0, tiled=True)]
    all_to_all x0 -> x2, starting transfers between devices: none -> 10.9 us  [the longest x1 6.01 us: body(): lax.all_to_all(spread, 'ctx', split_axis=0, concat_axis=0, tiled=True)]
    all_to_all x0 -> x2, waiting for transfers between devices: none -> 7.28 us  [the longest x1 3.9 us: body(): lax.all_to_all(spread, 'ctx', split_axis=0, concat_axis=0, tiled=True)]
    pallas_call x0 -> x1, Pallas kernels: none -> 2.45 us  [body(): pl.pallas_call(functools.partial(query_kernel, blocks, groups, (CHUNKS -...]
    pallas_call x1, Pallas kernels: 0.08 us -> 1.44 us  [body(): pl.pallas_call(spread_kernel, out_shape=struct((blocks, 8, local_heads),...]
    unnamed x0 -> x2, local copies, waits for them, and re-layouts: none -> 0.61 us
  transfers between devices with their start and end apart: 9 -> 11, of which waited for: 0 -> 2; matrix products, arithmetic and copies ran while one was open for 0% -> 0% of each run, Pallas kernels for 14% -> 20%
where the time goes in v6:
time: 60.8 us; the launch traced here: 60.2 us
  starting transfers between devices  30.3 us (50%)
  Pallas kernels  21.2 us (35%)
  waiting for transfers between devices  7.31 us (12%)
  between operations  0.8 us (1%)
  local copies, waits for them, and re-layouts  0.61 us (1%)
    ppermute x6, starting transfers between devices, body(): lax.ppermute(message, 'ctx', [(i, i ^ s) for i in range(blocks) if i < i...  15.5 us
    pallas_call x2, Pallas kernels, body(): pl.pallas_call(functools.partial(main_kernel, blocks, heads_per_group, gr...  14.9 us
    all_to_all x1, starting transfers between devices, body(): lax.all_to_all(spread, 'ctx', split_axis=0, concat_axis=0, tiled=True)  6.01 us
    all_to_all x1, starting transfers between devices, body(): lax.all_to_all(sums_here, 'dp', split_axis=0, concat_axis=0, tiled=True)  4.86 us
    all_to_all x1, waiting for transfers between devices, body(): lax.all_to_all(spread, 'ctx', split_axis=0, concat_axis=0, tiled=True)  3.9 us
    ppermute x3, starting transfers between devices, body(): returned.append(lax.ppermute(parts[s], 'ctx', back))  3.86 us
    all_to_all x1, waiting for transfers between devices, body(): lax.all_to_all(sums_here, 'dp', split_axis=0, concat_axis=0, tiled=True)  3.39 us
    pallas_call x1, Pallas kernels, body(): pl.pallas_call(functools.partial(query_kernel, blocks, groups, (CHUNKS -...  2.45 us
  transfers between devices with their start and end apart: 11, of which 2 were waited for; matrix products, arithmetic and copies ran while one was open for 0% of the time, Pallas kernels for 20%

profile of v6, /device:TPU:0, one launch (start us, length us, event | category | flops | bytes accessed | tf_op | source)
XLA Modules:
  0.0 60.2 jit_solution(16419113254890888721)
XLA Ops:
  0.6 1.0 %pack.1 = (bf16[528,128]{1,0:T(8,128)(2,1)S(1)}, bf16[512,128]{1,0:T(8,128)(2,1)S(1)}) custom-call(bf16[128,512]{1,0:T(8,128)(2,1)} %bitcast.10, bf16[128,512]{1,0:T(8,128)(2,1)} %bitcast.15, s32[1,128]{1,0:T(1,128)} %refs_11_.1, s32[1,128]{1,0:T(1,128)} %refs_12_.1), custom_call_target="tpu_custom_call" | custom-call | tf_op jit(solution)/shard_map/pack/pallas_call | solution.py:355
  1.7 5.8 %collective-permute-start.5 = (bf16[528,128]{1,0:T(8,128)(2,1)S(1)}, bf16[528,128]{1,0:T(8,128)(2,1)S(1)}, u32[]{:S(2)}, u32[]{:S(2)}) collective-permute-start(bf16[528,128]{1,0:T(8,128)(2,1)S(1)} %get-tuple-element.23), channel_id=1, source_target_pairs={{0,3},{1,2},{4,7},{5,6},{8,11},{9,10},{12,15},{13,14},{16,19},{17,... | collective-permute-start | bytes 405512 | tf_op jit(solution)/shard_map/ppermute | solution.py:368
  7.5 1.3 %collective-permute-start.4 = (bf16[528,128]{1,0:T(8,128)(2,1)S(1)}, bf16[528,128]{1,0:T(8,128)(2,1)S(1)}, u32[]{:S(2)}, u32[]{:S(2)}) collective-permute-start(bf16[528,128]{1,0:T(8,128)(2,1)S(1)} %get-tuple-element.23), channel_id=1, source_target_pairs={{0,2},{1,3},{4,6},{5,7},{8,10},{9,11},{12,14},{13,15},{16,18},{17,... | collective-permute-start | bytes 405512 | tf_op jit(solution)/shard_map/ppermute | solution.py:368
  8.8 2.5 %collective-permute-start.3 = (bf16[528,128]{1,0:T(8,128)(2,1)S(1)}, bf16[528,128]{1,0:T(8,128)(2,1)S(1)}, u32[]{:S(2)}, u32[]{:S(2)}) collective-permute-start(bf16[528,128]{1,0:T(8,128)(2,1)S(1)} %get-tuple-element.23), channel_id=1, source_target_pairs={{0,1},{2,3},{4,5},{6,7},{8,9},{10,11},{12,13},{14,15},{16,17},{18,... | collective-permute-start | bytes 405512 | tf_op jit(solution)/shard_map/ppermute | solution.py:368
  11.3 1.3 %collective-permute-start.2 = (bf16[512,128]{1,0:T(8,128)(2,1)S(1)}, bf16[512,128]{1,0:T(8,128)(2,1)S(1)}, u32[]{:S(2)}, u32[]{:S(2)}) collective-permute-start(bf16[512,128]{1,0:T(8,128)(2,1)S(1)} %get-tuple-element.22), channel_id=1, source_target_pairs={{0,3},{1,2},{4,7},{5,6},{8,11},{9,10},{12,15},{13,14},{16,19},{17,... | collective-permute-start | bytes 393224 | tf_op jit(solution)/shard_map/ppermute | solution.py:368
  12.6 1.3 %collective-permute-start.1 = (bf16[512,128]{1,0:T(8,128)(2,1)S(1)}, bf16[512,128]{1,0:T(8,128)(2,1)S(1)}, u32[]{:S(2)}, u32[]{:S(2)}) collective-permute-start(bf16[512,128]{1,0:T(8,128)(2,1)S(1)} %get-tuple-element.22), channel_id=1, source_target_pairs={{0,2},{1,3},{4,6},{5,7},{8,10},{9,11},{12,14},{13,15},{16,18},{17,... | collective-permute-start | bytes 393224 | tf_op jit(solution)/shard_map/ppermute | solution.py:368
  13.9 0.0 collective-permute-done.5.refs_9_
  13.9 3.4 %collective-permute-start = (bf16[512,128]{1,0:T(8,128)(2,1)S(1)}, bf16[512,128]{1,0:T(8,128)(2,1)S(1)}, u32[]{:S(2)}, u32[]{:S(2)}) collective-permute-start(bf16[512,128]{1,0:T(8,128)(2,1)S(1)} %get-tuple-element.22), channel_id=1, source_target_pairs={{0,1},{2,3},{4,5},{6,7},{8,9},{10,11},{12,13},{14,15},{16,17},{18,... | collective-permute-start | bytes 393224 | tf_op jit(solution)/shard_map/ppermute | solution.py:368
  17.3 0.0 collective-permute-done.4.refs_8_
  17.3 7.6 %attend_0.1 = (bf16[512,128]{1,0:T(8,128)(2,1)S(1)}, bf16[512,128]{1,0:T(8,128)(2,1)S(1)}, bf16[512,128]{1,0:T(8,128)(2,1)S(1)}, bf16[512,128]{1,0:T(8,128)(2,1)...) custom-call(f32[32]{0:T(128)} %refs_0_.3, ...), custom_call_target="tpu_custom_call" | custom-call | flops 1342177280 | bytes 2621440 | tf_op jit(solution)/shard_map/attend_0/pallas_call | solution.py:425
  24.9 7.3 %attend_1.1 = (bf16[1024,128]{1,0:T(8,128)(2,1)S(1)}, bf16[1024,128]{1,0:T(8,128)(2,1)}, bf16[1024,128]{1,0:T(8,128)(2,1)}, bf16[1024,128]{1,0:T(8,128)(2,1)}, b...) custom-call(f32[32]{0:T(128)} %refs_0_.3, f32[32]{0:T(128)} %refs_1_.3, bf16[128,4096]{1,0:T(8,128)(2,1)} %bitcast.20, ...), custom_call_target="tpu_custom_call" | custom-call | flops 1342177280 | bytes 2621440 | tf_op jit(solution)/shard_map/attend_1/pallas_call | solution.py:425
  32.2 0.0 copy-start
  32.2 0.6 %copy-done = f32[8,8,128]{2,1,0:T(8,128)} copy-done((f32[8,8,128]{2,1,0:T(8,128)}, f32[8,8,128]{2,1,0:T(8,128)S(1)}, u32[]{:S(2)}) %copy-start) | copy-done | bytes 32792
  32.8 1.3 %collective-permute-start.6 = (bf16[1024,128]{1,0:T(8,128)(2,1)}, bf16[1024,128]{1,0:T(8,128)(2,1)S(1)}, u32[]{:S(2)}, u32[]{:S(2)}) collective-permute-start(bf16[1024,128]{1,0:T(8,128)(2,1)} %get-tuple-element.34), channel_id=1, source_target_pairs={{2,1},{3,0},{6,5},{7,4},{10,9},{11,8},{14,13},{15,12},{18,17},{19,... | collective-permute-start | bytes 786440 | tf_op jit(solution)/shard_map/ppermute | solution.py:450
  34.1 1.3 %collective-permute-start.7 = (bf16[1024,128]{1,0:T(8,128)(2,1)}, bf16[1024,128]{1,0:T(8,128)(2,1)S(1)}, u32[]{:S(2)}, u32[]{:S(2)}) collective-permute-start(bf16[1024,128]{1,0:T(8,128)(2,1)} %get-tuple-element.35), channel_id=1, source_target_pairs={{2,0},{3,1},{6,4},{7,5},{10,8},{11,9},{14,12},{15,13},{18,16},{19,... | collective-permute-start | bytes 786440 | tf_op jit(solution)/shard_map/ppermute | solution.py:450
  35.4 1.3 %collective-permute-start.8 = (bf16[1024,128]{1,0:T(8,128)(2,1)}, bf16[1024,128]{1,0:T(8,128)(2,1)S(1)}, u32[]{:S(2)}, u32[]{:S(2)}) collective-permute-start(bf16[1024,128]{1,0:T(8,128)(2,1)} %get-tuple-element.36), channel_id=1, source_target_pairs={{1,0},{3,2},{5,4},{7,6},{9,8},{11,10},{13,12},{15,14},{17,16},{19,... | collective-permute-start | bytes 786440 | tf_op jit(solution)/shard_map/ppermute | solution.py:450
  36.7 4.9 %all-to-all-start = ((f32[8,8,128]{2,1,0:T(8,128)}), f32[8,8,128]{2,1,0:T(8,128)}, u32[]{:S(2)}, u32[]{:S(2)}) async-start(f32[8,8,128]{2,1,0:T(8,128)} %copy-done), calls=%async_computation | async-start | bytes 65536 | tf_op jit(solution)/shard_map/all_to_all | solution.py:451
  41.6 2.5 %query.1._ = bf16[128,4096]{1,0:T(8,128)(2,1)} custom-call(bf16[2,512,1024]{2,1,0:T(8,128)(2,1)S(1)} %get-tuple-element.31.refs_0_, bf16[128,512]{1,0:T(8,128)(2,1)} %bitcast.13, bf16[512,128]{1,0:T(8,128)(2,1)S(1)} %collective-permute-done.refs_7_.refs_2_, ...), custom_call_target="tpu_custom_call", output_to_operand_aliasing={{}: (5, {})} | custom-call | flops 268435456 | bytes 524288 | tf_op jit(solution)/shard_map/query/pallas_call | solution.py:452
  44.0 3.4 %all-to-all-done.sums_ref = f32[8,8,128]{2,1,0:T(8,128)} async-done(((f32[8,8,128]{2,1,0:T(8,128)}), f32[8,8,128]{2,1,0:T(8,128)}, u32[]{:S(2)}, u32[]{:S(2)}) %all-to-all-start) | async-done | bytes 32800 | tf_op jit(solution)/shard_map/all_to_all | solution.py:451
  47.4 1.4 %spread.1 = f32[4,8,8]{2,1,0:T(8,128)} custom-call(f32[8,8,128]{2,1,0:T(8,128)} %all-to-all-done.sums_ref, bf16[128,4096]{1,0:T(8,128)(2,1)} %query.1._), custom_call_target="tpu_custom_call" | custom-call | tf_op jit(solution)/shard_map/spread/pallas_call | solution.py:467
  48.9 6.0 %all-to-all-start.1 = ((f32[4,8,8]{2,1,0:T(8,128)}), f32[4,8,8]{2,1,0:T(8,128)S(1)}, u32[]{:S(2)}, u32[]{:S(2)}) async-start(f32[4,8,8]{2,1,0:T(8,128)} %spread.1), calls=%async_computation.1 | async-start | bytes 32768 | tf_op jit(solution)/shard_map/all_to_all | solution.py:475
  54.9 0.8 %combine.1 = (bf16[128,512]{1,0:T(8,128)(2,1)}, bf16[128,512]{1,0:T(8,128)(2,1)}) custom-call(bf16[1024,128]{1,0:T(8,128)(2,1)S(1)} %get-tuple-element.33.refs_0_, bf16[1024,128]{1,0:T(8,128)(2,1)S(1)} %collective-permute-done.6.refs_1_, bf16[1024,128]{1,0:T(8,128)(2,1)S(1)} %collective-permute-done.7.refs_2_, ...), custom_call_target="tpu_custom_call" | custom-call | tf_op jit(solution)/shard_map/combine/pallas_call | solution.py:476
  55.7 3.9 %all-to-all-done.1.parts_ref = f32[4,8,8]{2,1,0:T(8,128)S(1)} async-done(((f32[4,8,8]{2,1,0:T(8,128)}), f32[4,8,8]{2,1,0:T(8,128)S(1)}, u32[]{:S(2)}, u32[]{:S(2)}) %all-to-all-start.1) | async-done | bytes 1056 | tf_op jit(solution)/shard_map/all_to_all | solution.py:475
  59.6 0.6 bias.1
  (7 shorter events, 0.0 us)
Async XLA Ops:
  1.7 12.2 %collective-permute-start.5 = (bf16[528,128]{1,0:T(8,128)(2,1)S(1)}, bf16[528,128]{1,0:T(8,128)(2,1)S(1)}, u32[]{:S(2)}, u32[]{:S(2)}) collective-permute-start(bf16[528,128]{1,0:T(8,128)(2,1)S(1)} %get-tuple-element.23), channel_id=1, source_target_pairs={{0,3},{1,2},{4,7},{5,6},{8,11},{9,10},{12,15},{13,14},{16,19},{17,... | collective-permute-start | bytes 405512 | tf_op jit(solution)/shard_map/ppermute | solution.py:368
  7.5 9.8 %collective-permute-start.4 = (bf16[528,128]{1,0:T(8,128)(2,1)S(1)}, bf16[528,128]{1,0:T(8,128)(2,1)S(1)}, u32[]{:S(2)}, u32[]{:S(2)}) collective-permute-start(bf16[528,128]{1,0:T(8,128)(2,1)S(1)} %get-tuple-element.23), channel_id=1, source_target_pairs={{0,2},{1,3},{4,6},{5,7},{8,10},{9,11},{12,14},{13,15},{16,18},{17,... | collective-permute-start | bytes 405512 | tf_op jit(solution)/shard_map/ppermute | solution.py:368
  8.8 8.5 %collective-permute-start.3 = (bf16[528,128]{1,0:T(8,128)(2,1)S(1)}, bf16[528,128]{1,0:T(8,128)(2,1)S(1)}, u32[]{:S(2)}, u32[]{:S(2)}) collective-permute-start(bf16[528,128]{1,0:T(8,128)(2,1)S(1)} %get-tuple-element.23), channel_id=1, source_target_pairs={{0,1},{2,3},{4,5},{6,7},{8,9},{10,11},{12,13},{14,15},{16,17},{18,... | collective-permute-start | bytes 405512 | tf_op jit(solution)/shard_map/ppermute | solution.py:368
  11.3 13.6 %collective-permute-start.2 = (bf16[512,128]{1,0:T(8,128)(2,1)S(1)}, bf16[512,128]{1,0:T(8,128)(2,1)S(1)}, u32[]{:S(2)}, u32[]{:S(2)}) collective-permute-start(bf16[512,128]{1,0:T(8,128)(2,1)S(1)} %get-tuple-element.22), channel_id=1, source_target_pairs={{0,3},{1,2},{4,7},{5,6},{8,11},{9,10},{12,15},{13,14},{16,19},{17,... | collective-permute-start | bytes 393224 | tf_op jit(solution)/shard_map/ppermute | solution.py:368
  12.6 12.3 %collective-permute-start.1 = (bf16[512,128]{1,0:T(8,128)(2,1)S(1)}, bf16[512,128]{1,0:T(8,128)(2,1)S(1)}, u32[]{:S(2)}, u32[]{:S(2)}) collective-permute-start(bf16[512,128]{1,0:T(8,128)(2,1)S(1)} %get-tuple-element.22), channel_id=1, source_target_pairs={{0,2},{1,3},{4,6},{5,7},{8,10},{9,11},{12,14},{13,15},{16,18},{17,... | collective-permute-start | bytes 393224 | tf_op jit(solution)/shard_map/ppermute | solution.py:368
  13.9 11.0 %collective-permute-start = (bf16[512,128]{1,0:T(8,128)(2,1)S(1)}, bf16[512,128]{1,0:T(8,128)(2,1)S(1)}, u32[]{:S(2)}, u32[]{:S(2)}) collective-permute-start(bf16[512,128]{1,0:T(8,128)(2,1)S(1)} %get-tuple-element.22), channel_id=1, source_target_pairs={{0,1},{2,3},{4,5},{6,7},{8,9},{10,11},{12,13},{14,15},{16,17},{18,... | collective-permute-start | bytes 393224 | tf_op jit(solution)/shard_map/ppermute | solution.py:368
  32.2 0.6 %copy-start = (f32[8,8,128]{2,1,0:T(8,128)}, f32[8,8,128]{2,1,0:T(8,128)S(1)}, u32[]{:S(2)}) copy-start(f32[8,8,128]{2,1,0:T(8,128)S(1)} %get-tuple-element.39) | copy-start | bytes 98308
  32.8 22.1 %collective-permute-start.6 = (bf16[1024,128]{1,0:T(8,128)(2,1)}, bf16[1024,128]{1,0:T(8,128)(2,1)S(1)}, u32[]{:S(2)}, u32[]{:S(2)}) collective-permute-start(bf16[1024,128]{1,0:T(8,128)(2,1)} %get-tuple-element.34), channel_id=1, source_target_pairs={{2,1},{3,0},{6,5},{7,4},{10,9},{11,8},{14,13},{15,12},{18,17},{19,... | collective-permute-start | bytes 786440 | tf_op jit(solution)/shard_map/ppermute | solution.py:450
  34.1 20.8 %collective-permute-start.7 = (bf16[1024,128]{1,0:T(8,128)(2,1)}, bf16[1024,128]{1,0:T(8,128)(2,1)S(1)}, u32[]{:S(2)}, u32[]{:S(2)}) collective-permute-start(bf16[1024,128]{1,0:T(8,128)(2,1)} %get-tuple-element.35), channel_id=1, source_target_pairs={{2,0},{3,1},{6,4},{7,5},{10,8},{11,9},{14,12},{15,13},{18,16},{19,... | collective-permute-start | bytes 786440 | tf_op jit(solution)/shard_map/ppermute | solution.py:450
  35.4 19.5 %collective-permute-start.8 = (bf16[1024,128]{1,0:T(8,128)(2,1)}, bf16[1024,128]{1,0:T(8,128)(2,1)S(1)}, u32[]{:S(2)}, u32[]{:S(2)}) collective-permute-start(bf16[1024,128]{1,0:T(8,128)(2,1)} %get-tuple-element.36), channel_id=1, source_target_pairs={{1,0},{3,2},{5,4},{7,6},{9,8},{11,10},{13,12},{15,14},{17,16},{19,... | collective-permute-start | bytes 786440 | tf_op jit(solution)/shard_map/ppermute | solution.py:450
  36.7 10.7 %all-to-all-start = ((f32[8,8,128]{2,1,0:T(8,128)}), f32[8,8,128]{2,1,0:T(8,128)}, u32[]{:S(2)}, u32[]{:S(2)}) async-start(f32[8,8,128]{2,1,0:T(8,128)} %copy-done), calls=%async_computation | async-start | bytes 65536 | tf_op jit(solution)/shard_map/all_to_all | solution.py:451
  48.9 10.7 %all-to-all-start.1 = ((f32[4,8,8]{2,1,0:T(8,128)}), f32[4,8,8]{2,1,0:T(8,128)S(1)}, u32[]{:S(2)}, u32[]{:S(2)}) async-start(f32[4,8,8]{2,1,0:T(8,128)} %spread.1), calls=%async_computation.1 | async-start | bytes 32768 | tf_op jit(solution)/shard_map/all_to_all | solution.py:475

commit v7 on v5

--- a/solution.py
+++ b/solution.py
@@ -109,9 +109,11 @@
     lengths_ref, slope_ref, gain_ref, depth_ref, end_ref = take(5)
     query_hbm, output_hbm, grad_hbm, key_ref, value_ref = take(5)
     remote = take(blocks - 1)
-    dscore_ref, own_probs_ref, distance_ref, ancestor_ref = take(4)
+    dscore_ref, own_probs_ref = take(2)
     part_refs = take(blocks - 1)
-    query_ref, output_ref, grad_ref, weight_ref, probs_ref, key_acc, value_acc, load_sems = refs
+    (bias_ref,) = take(1)
+    query_ref, output_ref, grad_ref, weight_ref, probs_ref, key_acc, value_acc = take(7)
+    distance_ref, ancestor_ref, slope_rows, gain_rows, load_sems = refs
     tokens = query_hbm.shape[0]
     factor = WIDTH**-0.5
     pairs = heads_per_group // 2
@@ -149,14 +151,21 @@
     def differentiate(group, pair, centred, scales, half):
         lanes = slice(half * tokens, (half + 1) * tokens)
         to = slice((2 * pair + half) * tokens, (2 * pair + half + 1) * tokens)
+        slope_sum, gain_sum = 0.0, 0.0
         for s, (rows, scale) in enumerate(zip(block_rows, scales)):
             probs = weight_ref[pair % 2, rows, lanes] * scale
-            dscore_ref[group, rows, to] = (probs * centred[rows, lanes]).astype(jnp.bfloat16)
+            dscore = probs * centred[rows, lanes]
+            dscore_ref[group, rows, to] = dscore.astype(jnp.bfloat16)
+            slope_sum = slope_sum + fold_rows(dscore * distance_ref[rows, :])
+            gain_sum = gain_sum + fold_rows(dscore * ancestor_ref[rows, :])
             probs_b = probs.astype(jnp.bfloat16)
             if s == 0:
                 own_probs_ref[group, :, to] = probs_b
             else:
                 probs_ref[(s - 1) * tokens : s * tokens, to] = probs_b
+        at = pl.ds(group * heads_per_group + 2 * pair + half, 1)
+        slope_rows[at, :] = -jnp.sum(slope_sum, axis=0, keepdims=True)
+        gain_rows[at, :] = jnp.sum(gain_sum, axis=0, keepdims=True)
 
     def key_part(group, first, count):
         lanes = slice(first * tokens, (first + count) * tokens)
@@ -198,76 +207,6 @@
         put_part(group, 0, key_whole * factor)
         put_part(group, 1, value_acc[...] + value_part(group, half_heads, half_heads))
 
-
-def local_kernel(blocks, heads_per_group, groups, *refs):
-    refs = list(refs)
-    take = lambda count: [refs.pop(0) for _ in range(count)]
-    dscore_ref, own_probs_ref, distance_ref, ancestor_ref = take(4)
-    query_hbm, grad_hbm, key_ref = take(3)
-    remote = take(blocks - 1)
-    query_grad_hbm, own_part_ref, bias_hbm = take(3)
-    (
-        query_ref,
-        grad_ref,
-        query_grad_ref,
-        slope_rows,
-        gain_rows,
-        bias_ref,
-        load_sems,
-        store_sems,
-        bias_sem,
-    ) = refs
-    tokens = query_hbm.shape[0]
-    factor = WIDTH**-0.5
-    pairs = heads_per_group // 2
-    block_rows = [slice(s * tokens, (s + 1) * tokens) for s in range(blocks)]
-
-    def loads(group):
-        return group_loads(group, (query_hbm, grad_hbm), (query_ref, grad_ref), load_sems)
-
-    def store(group):
-        columns = group_columns(group, query_grad_ref.shape[2])
-        return pltpu.make_async_copy(
-            query_grad_ref.at[group], query_grad_hbm.at[:, columns], store_sems.at[group]
-        )
-
-    for group in range(groups):
-        for load in loads(group):
-            load.start()
-
-    def sum_up(group, head):
-        lanes = slice(head * tokens, (head + 1) * tokens)
-        slope_sum, gain_sum = 0.0, 0.0
-        for rows in block_rows:
-            dscore = dscore_ref[group, rows, lanes].astype(jnp.float32)
-            slope_sum = slope_sum + fold_rows(dscore * distance_ref[rows, :])
-            gain_sum = gain_sum + fold_rows(dscore * ancestor_ref[rows, :])
-        at = pl.ds(group * heads_per_group + head, 1)
-        slope_rows[at, :] = -jnp.sum(slope_sum, axis=0, keepdims=True)
-        gain_rows[at, :] = jnp.sum(gain_sum, axis=0, keepdims=True)
-
-    @pl.loop(0, groups)
-    def _(group):
-        for load in loads(group):
-            load.wait()
-        keys_across = jnp.transpose(all_blocks(key_ref, remote, 0, groups, group))
-        at = pl.multiple_of(group * tokens, tokens)
-        own = dot_nn(dscore_ref[group, 0:tokens, :], stacked(query_ref, group, 0, heads_per_group))
-        own_part_ref[pl.ds(at, tokens), :] = (own * factor).astype(jnp.bfloat16)
-        for pair in range(pairs):
-            lanes = slice(2 * pair * tokens, (2 * pair + 2) * tokens)
-            across = dot_nn(keys_across, dscore_ref[group, :, lanes]) * factor
-            for half in range(2):
-                sum_up(group, 2 * pair + half)
-            rows = jnp.transpose(across.astype(jnp.bfloat16))
-            for half in range(2):
-                to = slice((2 * pair + half) * WIDTH, (2 * pair + half + 1) * WIDTH)
-                query_grad_ref[group, :, to] = rows[half * tokens : (half + 1) * tokens]
-        at = pl.multiple_of((groups + group) * tokens, tokens)
-        own = dot_nn(own_probs_ref[group], stacked(grad_ref, group, 0, heads_per_group))
-        own_part_ref[pl.ds(at, tokens), :] = own.astype(jnp.bfloat16)
-        store(group).start()
-
     slope_sum = jnp.sum(slope_rows[...], axis=1, keepdims=True)
     gain_sum = jnp.sum(gain_rows[...], axis=1, keepdims=True)
     shape = slope_rows.shape
@@ -282,11 +221,56 @@
         gain_line = jnp.sum(jnp.where(mine, gain_sum, 0.0), axis=0, keepdims=True)
         tile = jnp.where(kind == 0, slope_line, jnp.where(kind == 1, gain_line, 0.0))
         bias_ref[:, part] = jnp.broadcast_to(tile[None], (replicas, rows_here, local))
-    bias_copy = pltpu.make_async_copy(bias_ref, bias_hbm, bias_sem)
-    bias_copy.start()
+
+
+def local_kernel(blocks, heads_per_group, groups, *refs):
+    refs = list(refs)
+    take = lambda count: [refs.pop(0) for _ in range(count)]
+    dscore_ref, own_probs_ref = take(2)
+    query_hbm, grad_hbm, key_ref = take(3)
+    remote = take(blocks - 1)
+    query_grad_hbm, own_part_ref = take(2)
+    query_ref, grad_ref, query_grad_ref, load_sems, store_sems = refs
+    tokens = query_hbm.shape[0]
+    factor = WIDTH**-0.5
+    pairs = heads_per_group // 2
+    block_rows = [slice(s * tokens, (s + 1) * tokens) for s in range(blocks)]
+
+    def loads(group):
+        return group_loads(group, (query_hbm, grad_hbm), (query_ref, grad_ref), load_sems)
+
+    def store(group):
+        columns = group_columns(group, query_grad_ref.shape[2])
+        return pltpu.make_async_copy(
+            query_grad_ref.at[group], query_grad_hbm.at[:, columns], store_sems.at[group]
+        )
+
+    for group in range(groups):
+        for load in loads(group):
+            load.start()
+
+    @pl.loop(0, groups)
+    def _(group):
+        for load in loads(group):
+            load.wait()
+        keys_across = jnp.transpose(all_blocks(key_ref, remote, 0, groups, group))
+        at = pl.multiple_of(group * tokens, tokens)
+        own = dot_nn(dscore_ref[group, 0:tokens, :], stacked(query_ref, group, 0, heads_per_group))
+        own_part_ref[pl.ds(at, tokens), :] = (own * factor).astype(jnp.bfloat16)
+        for pair in range(pairs):
+            lanes = slice(2 * pair * tokens, (2 * pair + 2) * tokens)
+            across = dot_nn(keys_across, dscore_ref[group, :, lanes]) * factor
+            rows = jnp.transpose(across.astype(jnp.bfloat16))
+            for half in range(2):
+                to = slice((2 * pair + half) * WIDTH, (2 * pair + half + 1) * WIDTH)
+                query_grad_ref[group, :, to] = rows[half * tokens : (half + 1) * tokens]
+        at = pl.multiple_of((groups + group) * tokens, tokens)
+        own = dot_nn(own_probs_ref[group], stacked(grad_ref, group, 0, heads_per_group))
+        own_part_ref[pl.ds(at, tokens), :] = own.astype(jnp.bfloat16)
+        store(group).start()
+
     for group in range(groups):
         store(group).wait()
-    bias_copy.wait()
 
 
 def combine_kernel(blocks, *refs):
@@ -366,19 +350,18 @@
         for s in range(1, blocks)
     ]
 
-    table = struct(keys_seen, tokens, dtype=f32)
     wide = pltpu.VMEM((groups, tokens, columns), bf16)
-    dscore, own_probs, distance, ancestor, *parts = pl.pallas_call(
+    bias_shape = (replicas, blocks, 8, WIDTH)
+    dscore, own_probs, *parts, bias_parts = pl.pallas_call(
         functools.partial(score_kernel, blocks, heads_per_group, groups),
         out_shape=[
             struct(groups, keys_seen, columns),
             struct(groups, tokens, columns),
-            table,
-            table,
         ]
-        + [struct(message_rows, WIDTH)] * (blocks - 1),
+        + [struct(message_rows, WIDTH)] * (blocks - 1)
+        + [struct(*bias_shape, dtype=f32)],
         in_specs=[smem] * 3 + [vmem] * 2 + [hbm] * 3 + [vmem] * (1 + blocks),
-        out_specs=[vmem] * (3 + blocks),
+        out_specs=[vmem] * (2 + blocks),
         scratch_shapes=[
             wide,
             wide,
@@ -387,6 +370,10 @@
             pltpu.VMEM((keys_seen - tokens, columns), bf16),
             pltpu.VMEM((keys_seen - tokens, WIDTH), f32),
             pltpu.VMEM((keys_seen - tokens, WIDTH), f32),
+            pltpu.VMEM((keys_seen, tokens), f32),
+            pltpu.VMEM((keys_seen, tokens), f32),
+            pltpu.VMEM((heads_all, tokens), f32),
+            pltpu.VMEM((heads_all, tokens), f32),
             sem((3 * groups,)),
         ],
         compiler_params=params,
@@ -410,33 +397,18 @@
         back = [(i, i ^ s) for i in range(blocks) if i > i ^ s]
         returned.append(lax.ppermute(parts[s - 1], "ctx", back))
 
-    bias_shape = (replicas, blocks, 8, WIDTH)
-    query_grads, own_part, bias_parts = pl.pallas_call(
+    bias_parts = bias_parts.reshape(replicas * blocks, 8, WIDTH)
+    bias_parts = lax.all_to_all(bias_parts, ("dp", "ctx"), split_axis=0, concat_axis=0, tiled=True)
+    query_grads, own_part = pl.pallas_call(
         functools.partial(local_kernel, blocks, heads_per_group, groups),
-        out_shape=[
-            struct(tokens, width_all),
-            struct(message_rows, WIDTH),
-            struct(*bias_shape, dtype=f32),
-        ],
-        in_specs=[vmem] * 4 + [hbm] * 2 + [vmem] * blocks,
-        out_specs=[hbm, vmem, hbm],
-        scratch_shapes=[
-            wide,
-            wide,
-            wide,
-            pltpu.VMEM((heads_all, tokens), f32),
-            pltpu.VMEM((heads_all, tokens), f32),
-            pltpu.VMEM(bias_shape, f32),
-            sem((2 * groups,)),
-            sem((groups,)),
-            sem,
-        ],
+        out_shape=[struct(tokens, width_all), struct(message_rows, WIDTH)],
+        in_specs=[vmem] * 2 + [hbm] * 2 + [vmem] * blocks,
+        out_specs=[hbm, vmem],
+        scratch_shapes=[wide, wide, wide, sem((2 * groups,)), sem((groups,))],
         compiler_params=params,
         cost_estimate=cost(2, 0),
         name="local",
-    )(dscore, own_probs, distance, ancestor, query_held, grad_held, key_held, *arrived)
-    bias_parts = bias_parts.reshape(replicas * blocks, 8, WIDTH)
-    bias_parts = lax.all_to_all(bias_parts, ("dp", "ctx"), split_axis=0, concat_axis=0, tiled=True)
+    )(dscore, own_probs, query_held, grad_held, key_held, *arrived)
     key_grads, value_grads = pl.pallas_call(
         functools.partial(combine_kernel, blocks),
         out_shape=[struct(tokens, kv_width)] * 2,

time: 57.8 us -> 55.4 us (0.958)
  waiting for transfers between devices: 15.2 us -> 8.44 us
  local copies, waits for them, and re-layouts: 0 us -> 4.12 us
    all_to_all x1, waiting for transfers between devices: 7.58 us -> 0.86 us  [body(): lax.all_to_all(bias_parts, ('dp', 'ctx'), split_axis=0, concat_axis=0, ti...]
    unnamed x0 -> x4, local copies, waits for them, and re-layouts: none -> 4.12 us
    pallas_call x1, Pallas kernels: 9.58 us -> 11.2 us  [body(): pl.pallas_call(functools.partial(score_kernel, blocks, heads_per_group, g...]
    pallas_call x1, Pallas kernels: 6.05 us -> 4.52 us  [body(): pl.pallas_call(functools.partial(local_kernel, blocks, heads_per_group, g...]
  transfers between devices with their start and end apart: 7 -> 7, of which waited for: 4 -> 4; matrix products, arithmetic and copies ran while one was open for 0% -> 0% of each run, Pallas kernels for 12% -> 10%
where the time goes in v7:
time: 55.4 us; the launch traced here: 55 us
  starting transfers between devices  23.5 us (42%)
  Pallas kernels  18.2 us (33%)
  waiting for transfers between devices  8.44 us (15%)
  local copies, waits for them, and re-layouts  4.12 us (7%)
  between operations  0.74 us (1%)
    pallas_call x1, Pallas kernels, body(): pl.pallas_call(functools.partial(score_kernel, blocks, heads_per_group, g...  11.2 us
    all_to_all x1, starting transfers between devices, body(): lax.all_to_all(bias_parts, ('dp', 'ctx'), split_axis=0, concat_axis=0, ti...  10.1 us
    ppermute x3, starting transfers between devices, body(): lax.ppermute(message, 'ctx', [(i, i ^ s) for i in range(blocks) if i < i...  9.59 us
    ppermute x3, waiting for transfers between devices, body(): lax.ppermute(message, 'ctx', [(i, i ^ s) for i in range(blocks) if i < i...  7.57 us
    pallas_call x1, Pallas kernels, body(): pl.pallas_call(functools.partial(local_kernel, blocks, heads_per_group, g...  4.52 us
    unnamed x4, local copies, waits for them, and re-layouts  4.12 us
    ppermute x3, starting transfers between devices, body(): returned.append(lax.ppermute(parts[s - 1], 'ctx', back))  3.86 us
  transfers between devices with their start and end apart: 7, of which 4 were waited for; matrix products, arithmetic and copies ran while one was open for 0% of the time, Pallas kernels for 10%

profile of v7, /device:TPU:0, one launch (start us, length us, event | category | flops | bytes accessed | tf_op | source)
XLA Modules:
  0.0 55.0 jit_solution(13885791867715318809)
XLA Ops:
  0.6 1.0 %pack.1 = bf16[1040,128]{1,0:T(8,128)(2,1)S(1)} custom-call(bf16[128,512]{1,0:T(8,128)(2,1)} %bitcast.14, bf16[128,512]{1,0:T(8,128)(2,1)} %bitcast.18, s32[1,128]{1,0:T(1,128)} %refs_3_.1, s32[1,128]{1,0:T(1,128)} %refs_4_.1), custom_call_target="tpu_custom_call" | custom-call | tf_op jit(solution)/shard_map/pack/pallas_call | solution.py:340
  1.7 5.8 %collective-permute-start.2 = (bf16[1040,128]{1,0:T(8,128)(2,1)S(1)}, bf16[1040,128]{1,0:T(8,128)(2,1)S(1)}, u32[]{:S(2)}, u32[]{:S(2)}) collective-permute-start(bf16[1040,128]{1,0:T(8,128)(2,1)S(1)} %pack.1), channel_id=1, source_target_pairs={{0,3},{1,2},{4,7},{5,6},{8,11},{9,10},{12,15},{13,14},{16,19},{17,... | collective-permute-start | bytes 798728 | tf_op jit(solution)/shard_map/ppermute | solution.py:349
  7.5 1.3 %collective-permute-start.1 = (bf16[1040,128]{1,0:T(8,128)(2,1)S(1)}, bf16[1040,128]{1,0:T(8,128)(2,1)S(1)}, u32[]{:S(2)}, u32[]{:S(2)}) collective-permute-start(bf16[1040,128]{1,0:T(8,128)(2,1)S(1)} %pack.1), channel_id=1, source_target_pairs={{0,2},{1,3},{4,6},{5,7},{8,10},{9,11},{12,14},{13,15},{16,18},{17,... | collective-permute-start | bytes 798728 | tf_op jit(solution)/shard_map/ppermute | solution.py:349
  8.8 2.5 %collective-permute-start = (bf16[1040,128]{1,0:T(8,128)(2,1)S(1)}, bf16[1040,128]{1,0:T(8,128)(2,1)S(1)}, u32[]{:S(2)}, u32[]{:S(2)}) collective-permute-start(bf16[1040,128]{1,0:T(8,128)(2,1)S(1)} %pack.1), channel_id=1, source_target_pairs={{0,1},{2,3},{4,5},{6,7},{8,9},{10,11},{12,13},{14,15},{16,17},{18,... | collective-permute-start | bytes 798728 | tf_op jit(solution)/shard_map/ppermute | solution.py:349
  11.3 3.0 %collective-permute-done.2.refs_12_.refs_7_ = bf16[1040,128]{1,0:T(8,128)(2,1)S(1)} collective-permute-done((bf16[1040,128]{1,0:T(8,128)(2,1)S(1)}, bf16[1040,128]{1,0:T(8,128)(2,1)S(1)}, u32[]{:S(2)}, u32[]{:S(2)}) %collective-permute-start.2) | collective-permute-done | bytes 266272 | tf_op jit(solution)/shard_map/ppermute | solution.py:349
  14.3 4.5 %collective-permute-done.1.refs_11_.refs_6_ = bf16[1040,128]{1,0:T(8,128)(2,1)S(1)} collective-permute-done((bf16[1040,128]{1,0:T(8,128)(2,1)S(1)}, bf16[1040,128]{1,0:T(8,128)(2,1)S(1)}, u32[]{:S(2)}, u32[]{:S(2)}) %collective-permute-start.1) | collective-permute-done | bytes 266272 | tf_op jit(solution)/shard_map/ppermute | solution.py:349
  18.8 0.1 collective-permute-done.refs_10_.refs_5_
  18.9 11.2 %scores.1 = (bf16[4,512,1024]{2,1,0:T(8,128)(2,1)S(1)}, bf16[4,128,1024]{2,1,0:T(8,128)(2,1)S(1)}, bf16[1024,128]{1,0:T(8,128)(2,1)S(1)}, bf16[1024,128]{1,0:T(8...) custom-call(s32[1,8]{1,0:T(1,128)} %refs_0_.1, f32[32]{0:T(128)} %refs_1_.1, f32[32]{0:T(128)} %refs_2_.1, ...), custom_call_target="tpu_custom_call" | custom-call | flops 2147483648 | bytes 2097152 | tf_op jit(solution)/shard_map/scores/pallas_call | solution.py:355
  30.1 0.0 copy-start
  30.1 1.9 %copy-done = bf16[4,512,1024]{2,1,0:T(8,128)(2,1)} copy-done((bf16[4,512,1024]{2,1,0:T(8,128)(2,1)}, bf16[4,512,1024]{2,1,0:T(8,128)(2,1)S(1)}, u32[]{:S(2)}) %copy-start) | copy-done | bytes 4194328
  32.0 1.3 %collective-permute-start.3 = (bf16[1024,128]{1,0:T(8,128)(2,1)S(1)}, bf16[1024,128]{1,0:T(8,128)(2,1)S(1)}, u32[]{:S(2)}, u32[]{:S(2)}) collective-permute-start(bf16[1024,128]{1,0:T(8,128)(2,1)S(1)} %get-tuple-element.18), channel_id=1, source_target_pairs={{2,1},{3,0},{6,5},{7,4},{10,9},{11,8},{14,13},{15,12},{18,17},{19,... | collective-permute-start | bytes 786440 | tf_op jit(solution)/shard_map/ppermute | solution.py:398
  33.3 1.3 %collective-permute-start.4 = (bf16[1024,128]{1,0:T(8,128)(2,1)S(1)}, bf16[1024,128]{1,0:T(8,128)(2,1)S(1)}, u32[]{:S(2)}, u32[]{:S(2)}) collective-permute-start(bf16[1024,128]{1,0:T(8,128)(2,1)S(1)} %get-tuple-element.19), channel_id=1, source_target_pairs={{2,0},{3,1},{6,4},{7,5},{10,8},{11,9},{14,12},{15,13},{18,16},{19,... | collective-permute-start | bytes 786440 | tf_op jit(solution)/shard_map/ppermute | solution.py:398
  34.6 1.3 %collective-permute-start.5 = (bf16[1024,128]{1,0:T(8,128)(2,1)S(1)}, bf16[1024,128]{1,0:T(8,128)(2,1)S(1)}, u32[]{:S(2)}, u32[]{:S(2)}) collective-permute-start(bf16[1024,128]{1,0:T(8,128)(2,1)S(1)} %get-tuple-element.20), channel_id=1, source_target_pairs={{1,0},{3,2},{5,4},{7,6},{9,8},{11,10},{13,12},{15,14},{17,16},{19,... | collective-permute-start | bytes 786440 | tf_op jit(solution)/shard_map/ppermute | solution.py:398
  35.9 10.1 %all-to-all-start = ((f32[32,8,128]{2,1,0:T(8,128)}), f32[32,8,128]{2,1,0:T(8,128)S(1)}, u32[]{:S(2)}, u32[]{:S(2)}) async-start(f32[32,8,128]{2,1,0:T(8,128)} %bitcast.8), calls=%async_computation | async-start | bytes 262144 | tf_op jit(solution)/shard_map/all_to_all | solution.py:401
  46.0 0.0 copy-start.1
  46.0 2.2 %copy-done.1 = bf16[4,512,1024]{2,1,0:T(8,128)(2,1)S(1)} copy-done((bf16[4,512,1024]{2,1,0:T(8,128)(2,1)S(1)}, bf16[4,512,1024]{2,1,0:T(8,128)(2,1)}, u32[]{:S(2)}) %copy-start.1) | copy-done | bytes 4194328
  48.2 4.5 %local.1 = (bf16[128,4096]{1,0:T(8,128)(2,1)}, bf16[1024,128]{1,0:T(8,128)(2,1)S(1)}) custom-call(bf16[4,512,1024]{2,1,0:T(8,128)(2,1)S(1)} %copy-done.1, bf16[4,128,1024]{2,1,0:T(8,128)(2,1)S(1)} %get-tuple-element.15.refs_1_, bf16[128,4096]{1,0:T(8,128)(2,1)} %bitcast.11, bf16[128,4096]{1,0:T(8,128)(2,1)} %bitcast.13, bf16[128,512]{1,0:T(8,128)(2,1)} %bitcast.16, ...), custom_call_target="tpu_custom_call" | custom-call | flops 1073741824 | bytes 2097152 | tf_op jit(solution)/shard_map/local/pallas_call | solution.py:402
  52.7 0.0 collective-permute-done.3.refs_1_
  52.7 0.0 collective-permute-done.4.refs_2_
  52.7 0.0 collective-permute-done.5.refs_3_
  52.8 0.8 %combine.1 = (bf16[128,512]{1,0:T(8,128)(2,1)}, bf16[128,512]{1,0:T(8,128)(2,1)}) custom-call(bf16[1024,128]{1,0:T(8,128)(2,1)S(1)} %get-tuple-element.17.refs_0_, bf16[1024,128]{1,0:T(8,128)(2,1)S(1)} %collective-permute-done.3.refs_1_, bf16[1024,128]{1,0:T(8,128)(2,1)S(1)} %collective-permute-done.4.refs_2_, ...), custom_call_target="tpu_custom_call" | custom-call | tf_op jit(solution)/shard_map/combine/pallas_call | solution.py:412
  53.6 0.9 %all-to-all-done.parts_ref = f32[32,8,128]{2,1,0:T(8,128)S(1)} async-done(((f32[32,8,128]{2,1,0:T(8,128)}), f32[32,8,128]{2,1,0:T(8,128)S(1)}, u32[]{:S(2)}, u32[]{:S(2)}) %all-to-all-start) | async-done | bytes 131104 | tf_op jit(solution)/shard_map/all_to_all | solution.py:401
  54.4 0.6 %bias.1 = f32[2,8]{1,0:T(2,128)} custom-call(f32[32,8,128]{2,1,0:T(8,128)S(1)} %all-to-all-done.parts_ref, bf16[128,512]{1,0:T(8,128)(2,1)} %get-tuple-element.21._), custom_call_target="tpu_custom_call" | custom-call | tf_op jit(solution)/shard_map/bias/pallas_call | solution.py:420
Async XLA Ops:
  1.7 12.6 %collective-permute-start.2 = (bf16[1040,128]{1,0:T(8,128)(2,1)S(1)}, bf16[1040,128]{1,0:T(8,128)(2,1)S(1)}, u32[]{:S(2)}, u32[]{:S(2)}) collective-permute-start(bf16[1040,128]{1,0:T(8,128)(2,1)S(1)} %pack.1), channel_id=1, source_target_pairs={{0,3},{1,2},{4,7},{5,6},{8,11},{9,10},{12,15},{13,14},{16,19},{17,... | collective-permute-start | bytes 798728 | tf_op jit(solution)/shard_map/ppermute | solution.py:349
  7.5 11.3 %collective-permute-start.1 = (bf16[1040,128]{1,0:T(8,128)(2,1)S(1)}, bf16[1040,128]{1,0:T(8,128)(2,1)S(1)}, u32[]{:S(2)}, u32[]{:S(2)}) collective-permute-start(bf16[1040,128]{1,0:T(8,128)(2,1)S(1)} %pack.1), channel_id=1, source_target_pairs={{0,2},{1,3},{4,6},{5,7},{8,10},{9,11},{12,14},{13,15},{16,18},{17,... | collective-permute-start | bytes 798728 | tf_op jit(solution)/shard_map/ppermute | solution.py:349
  8.8 10.1 %collective-permute-start = (bf16[1040,128]{1,0:T(8,128)(2,1)S(1)}, bf16[1040,128]{1,0:T(8,128)(2,1)S(1)}, u32[]{:S(2)}, u32[]{:S(2)}) collective-permute-start(bf16[1040,128]{1,0:T(8,128)(2,1)S(1)} %pack.1), channel_id=1, source_target_pairs={{0,1},{2,3},{4,5},{6,7},{8,9},{10,11},{12,13},{14,15},{16,17},{18,... | collective-permute-start | bytes 798728 | tf_op jit(solution)/shard_map/ppermute | solution.py:349
  30.1 2.0 %copy-start = (bf16[4,512,1024]{2,1,0:T(8,128)(2,1)}, bf16[4,512,1024]{2,1,0:T(8,128)(2,1)S(1)}, u32[]{:S(2)}) copy-start(bf16[4,512,1024]{2,1,0:T(8,128)(2,1)S(1)} %get-tuple-element.14.refs_0_) | copy-start | bytes 12582916
  32.0 20.7 %collective-permute-start.3 = (bf16[1024,128]{1,0:T(8,128)(2,1)S(1)}, bf16[1024,128]{1,0:T(8,128)(2,1)S(1)}, u32[]{:S(2)}, u32[]{:S(2)}) collective-permute-start(bf16[1024,128]{1,0:T(8,128)(2,1)S(1)} %get-tuple-element.18), channel_id=1, source_target_pairs={{2,1},{3,0},{6,5},{7,4},{10,9},{11,8},{14,13},{15,12},{18,17},{19,... | collective-permute-start | bytes 786440 | tf_op jit(solution)/shard_map/ppermute | solution.py:398
  33.3 19.4 %collective-permute-start.4 = (bf16[1024,128]{1,0:T(8,128)(2,1)S(1)}, bf16[1024,128]{1,0:T(8,128)(2,1)S(1)}, u32[]{:S(2)}, u32[]{:S(2)}) collective-permute-start(bf16[1024,128]{1,0:T(8,128)(2,1)S(1)} %get-tuple-element.19), channel_id=1, source_target_pairs={{2,0},{3,1},{6,4},{7,5},{10,8},{11,9},{14,12},{15,13},{18,16},{19,... | collective-permute-start | bytes 786440 | tf_op jit(solution)/shard_map/ppermute | solution.py:398
  34.6 18.1 %collective-permute-start.5 = (bf16[1024,128]{1,0:T(8,128)(2,1)S(1)}, bf16[1024,128]{1,0:T(8,128)(2,1)S(1)}, u32[]{:S(2)}, u32[]{:S(2)}) collective-permute-start(bf16[1024,128]{1,0:T(8,128)(2,1)S(1)} %get-tuple-element.20), channel_id=1, source_target_pairs={{1,0},{3,2},{5,4},{7,6},{9,8},{11,10},{13,12},{15,14},{17,16},{19,... | collective-permute-start | bytes 786440 | tf_op jit(solution)/shard_map/ppermute | solution.py:398
  35.9 18.5 %all-to-all-start = ((f32[32,8,128]{2,1,0:T(8,128)}), f32[32,8,128]{2,1,0:T(8,128)S(1)}, u32[]{:S(2)}, u32[]{:S(2)}) async-start(f32[32,8,128]{2,1,0:T(8,128)} %bitcast.8), calls=%async_computation | async-start | bytes 262144 | tf_op jit(solution)/shard_map/all_to_all | solution.py:401
  46.0 2.2 %copy-start.1 = (bf16[4,512,1024]{2,1,0:T(8,128)(2,1)S(1)}, bf16[4,512,1024]{2,1,0:T(8,128)(2,1)}, u32[]{:S(2)}) copy-start(bf16[4,512,1024]{2,1,0:T(8,128)(2,1)} %copy-done) | copy-start | bytes 12582916

commit v8 on v3

--- a/solution.py
+++ b/solution.py
@@ -48,6 +48,12 @@
     message_ref[2 * groups * tokens : 2 * groups * tokens + META_ROWS, :] = meta
 
 
+def prepare_kernel(query_in, output_in, grad_in, query_out, grad_out, product_out):
+    query_out[...] = query_in[...]
+    grad_out[...] = grad_in[...]
+    product_out[...] = grad_in[...] * output_in[...]
+
+
 def main_kernel(
     blocks,
     heads_per_group,
@@ -57,22 +63,19 @@
     gain_ref,
     depth_ref,
     end_ref,
-    query_hbm,
-    output_hbm,
-    grad_hbm,
+    query_ref,
+    grad_ref,
+    product_ref,
     key_ref,
     value_ref,
     *refs,
 ):
-    tokens = query_hbm.shape[0]
+    tokens = query_ref.shape[0]
     remote = refs[0 : blocks - 1]
     query_grad_hbm = refs[blocks - 1]
     part_refs = refs[blocks : 2 * blocks]
     bias_hbm = refs[2 * blocks]
     (
-        query_ref,
-        output_ref,
-        grad_ref,
         query_grad_ref,
         distance_ref,
         ancestor_ref,
@@ -84,7 +87,6 @@
         probs_ref,
         dscore_ref,
         bias_ref,
-        load_sems,
         store_sems,
         bias_sem,
     ) = refs[2 * blocks + 1 :]
@@ -92,23 +94,11 @@
     group_columns = heads_per_group * WIDTH
     pairs = heads_per_group // 2
 
-    def load(group, index):
-        wide = pl.ds(pl.multiple_of(group * group_columns, group_columns), group_columns)
-        source = (query_hbm, output_hbm, grad_hbm)[index]
-        to = (query_ref, output_ref, grad_ref)[index]
-        return pltpu.make_async_copy(
-            source.at[:, wide], to.at[group], load_sems.at[3 * group + index]
-        )
-
     def store(group):
         wide = pl.ds(pl.multiple_of(group * group_columns, group_columns), group_columns)
         return pltpu.make_async_copy(
             query_grad_ref.at[group], query_grad_hbm.at[:, wide], store_sems.at[group]
         )
-
-    for group in range(groups):
-        for index in range(3):
-            load(group, index).start()
 
     here = lax.axis_index("ctx")
     query_pos = here * tokens + lax.broadcasted_iota(jnp.int32, (tokens, tokens), 1)
@@ -145,8 +135,9 @@
         return jnp.concatenate([key_block(kind, group, s) for s in range(blocks)], axis=0)
 
     def stacked(ref, group, first, count):
-        heads = [slice((first + i) * WIDTH, (first + i + 1) * WIDTH) for i in range(count)]
-        return jnp.concatenate([ref[group, :, h] for h in heads], axis=0)
+        at = pl.multiple_of(group * group_columns, group_columns) + first * WIDTH
+        heads = [pl.ds(pl.multiple_of(at + i * WIDTH, WIDTH), WIDTH) for i in range(count)]
+        return jnp.concatenate([ref[:, head] for head in heads], axis=0)
 
     def weigh(group, pair, raw, half):
         head = group * heads_per_group + 2 * pair + half
@@ -212,8 +203,6 @@
 
     @pl.loop(0, groups)
     def _(group):
-        for index in range(3):
-            load(group, index).wait()
         keys = all_blocks(0, group)
         values = all_blocks(1, group)
         value_ext = jnp.concatenate([values, jnp.full(values.shape, -1.0, jnp.bfloat16)], axis=1)
@@ -222,8 +211,8 @@
         for pair in range(pairs):
             query_pair = stacked(query_ref, group, 2 * pair, 2)
             grad_pair = stacked(grad_ref, group, 2 * pair, 2)
-            output_pair = stacked(output_ref, group, 2 * pair, 2)
-            grad_ext = jnp.concatenate([grad_pair, grad_pair * output_pair], axis=1)
+            product_pair = stacked(product_ref, group, 2 * pair, 2)
+            grad_ext = jnp.concatenate([grad_pair, product_pair], axis=1)
             raw = products(keys, query_pair)
             if pair == pairs // 2:
                 key_acc[...] = key_part(group, 0, half_heads)
@@ -306,7 +295,7 @@
     vmem = pl.BlockSpec(memory_space=pltpu.VMEM)
     smem = pl.BlockSpec(memory_space=pltpu.SMEM)
     hbm = pl.BlockSpec(memory_space=pltpu.HBM)
-    params = pltpu.CompilerParams(vmem_limit_bytes=(40 if blocks <= 4 else 56) * 1024 * 1024)
+    params = pltpu.CompilerParams(vmem_limit_bytes=(24 if blocks <= 4 else 44) * 1024 * 1024)
 
     def hold(array):
         return pltpu.with_memory_space_constraint(array, pltpu.HBM)
@@ -327,6 +316,18 @@
         for s in range(1, blocks)
     ]
 
+    prepared = pl.pallas_call(
+        prepare_kernel,
+        out_shape=[jax.ShapeDtypeStruct((tokens, width_all), bf16)] * 3,
+        in_specs=[vmem] * 3,
+        out_specs=[vmem] * 3,
+        compiler_params=params,
+        cost_estimate=pl.CostEstimate(
+            flops=tokens * width_all, bytes_accessed=12 * tokens * width_all, transcendentals=0
+        ),
+        name="prepare",
+    )(hold(queries[0]), hold(outputs[0]), hold(out_grads[0]))
+
     bias_shape = (replicas, blocks, 8, WIDTH)
     matmul_flops = 2 * tokens * keys_seen * WIDTH * heads_all
     results = pl.pallas_call(
@@ -334,12 +335,9 @@
         out_shape=[jax.ShapeDtypeStruct((tokens, width_all), bf16)]
         + [jax.ShapeDtypeStruct((message_rows, WIDTH), bf16)] * blocks
         + [jax.ShapeDtypeStruct(bias_shape, f32)],
-        in_specs=[smem] * 3 + [vmem] * 2 + [hbm] * 3 + [vmem] * (1 + blocks),
+        in_specs=[smem] * 3 + [vmem] * (6 + blocks),
         out_specs=[hbm] + [vmem] * blocks + [hbm],
         scratch_shapes=[
-            pltpu.VMEM((groups, tokens, group_columns), bf16),
-            pltpu.VMEM((groups, tokens, group_columns), bf16),
-            pltpu.VMEM((groups, tokens, group_columns), bf16),
             pltpu.VMEM((groups, tokens, group_columns), bf16),
             pltpu.VMEM((keys_seen, tokens), f32),
             pltpu.VMEM((keys_seen, tokens), f32),
@@ -351,7 +349,6 @@
             pltpu.VMEM((keys_seen, group_columns), bf16),
             pltpu.VMEM((keys_seen, group_columns), bf16),
             pltpu.VMEM(bias_shape, f32),
-            pltpu.SemaphoreType.DMA((3 * groups,)),
             pltpu.SemaphoreType.DMA((groups,)),
             pltpu.SemaphoreType.DMA,
         ],
@@ -368,9 +365,7 @@
         hold(ancestor_gain),
         depth_held,
         end_held,
-        hold(queries[0]),
-        hold(outputs[0]),
-        hold(out_grads[0]),
+        *prepared,
         key_held,
         value_held,
         *arrived,
@@ -378,7 +373,7 @@
     query_grads = results[0]
     parts = list(results[1 : 1 + blocks])
     bias_parts = results[1 + blocks].reshape(replicas * blocks, 8, WIDTH)
-    for s in range(1, blocks):
+    for s in reversed(range(1, blocks)):
         back = [(i, i ^ s) for i in range(blocks) if i > i ^ s]
         parts[s] = lax.ppermute(parts[s], "ctx", back)
     bias_parts = lax.all_to_all(bias_parts, ("dp", "ctx"), split_axis=0, concat_axis=0, tiled=True)
@@ -395,7 +390,7 @@
             transcendentals=0,
         ),
         name="combine",
-    )(*parts)
+    )(parts[0], *reversed(parts[1:]))
     bias_grads = pl.pallas_call(
         bias_kernel,
         out_shape=jax.ShapeDtypeStruct((2, local_heads), f32),
@@ -403,7 +398,7 @@
         out_specs=vmem,
         compiler_params=params,
         name="bias",
-    )(bias_parts, key_grads)
+    )(bias_parts, hold(key_grads))
     return (query_grads[None], key_grads[None], value_grads[None], bias_grads.T)
 
 

time: 53.3 us -> 53.6 us (level)
  waiting for transfers between devices: 15.2 us -> 13.1 us
  starting transfers between devices: 21.6 us -> 23.6 us
  Pallas kernels: 14.6 us -> 16 us
  local copies, waits for them, and re-layouts: 0.9 us -> 0 us
    all_to_all x1, waiting for transfers between devices: 1.33 us -> 4.88 us  [body(): lax.all_to_all(bias_parts, ('dp', 'ctx'), split_axis=0, concat_axis=0, ti...]
    ppermute x3, waiting for transfers between devices: 6.26 us -> 2.72 us  [body(): parts[s] = lax.ppermute(parts[s], 'ctx', back)]
    ppermute x3, waiting for transfers between devices: 7.57 us -> 5.47 us  [body(): lax.ppermute(message, 'ctx', [(i, i ^ s) for i in range(blocks) if i < i...]
    pallas_call x0 -> x1, Pallas kernels: none -> 2.1 us  [body(): pl.pallas_call(prepare_kernel, out_shape=[jax.ShapeDtypeStruct((tokens, w...]
    all_to_all x1, starting transfers between devices: 8.17 us -> 10.1 us  [body(): lax.all_to_all(bias_parts, ('dp', 'ctx'), split_axis=0, concat_axis=0, ti...]
    unnamed x2 -> x0, local copies, waits for them, and re-layouts: 0.9 us -> none
    pallas_call x1, Pallas kernels: 12.1 us -> 11.5 us  [body(): pl.pallas_call(functools.partial(main_kernel, blocks, heads_per_group, gr...]
  transfers between devices with their start and end apart: 7 -> 7, of which waited for: 5 -> 5; matrix products, arithmetic and copies ran while one was open for 0% -> 0% of each run, Pallas kernels for 1% -> 5%
where the time goes in v8:
time: 53.6 us; the launch traced here: 53.3 us
  starting transfers between devices  23.6 us (44%)
  Pallas kernels  16 us (30%)
  waiting for transfers between devices  13.1 us (24%)
  between operations  0.71 us (1%)
    pallas_call x1, Pallas kernels, body(): pl.pallas_call(functools.partial(main_kernel, blocks, heads_per_group, gr...  11.5 us
    all_to_all x1, starting transfers between devices, body(): lax.all_to_all(bias_parts, ('dp', 'ctx'), split_axis=0, concat_axis=0, ti...  10.1 us
    ppermute x3, starting transfers between devices, body(): lax.ppermute(message, 'ctx', [(i, i ^ s) for i in range(blocks) if i < i...  9.59 us
    ppermute x3, waiting for transfers between devices, body(): lax.ppermute(message, 'ctx', [(i, i ^ s) for i in range(blocks) if i < i...  5.47 us
    all_to_all x1, waiting for transfers between devices, body(): lax.all_to_all(bias_parts, ('dp', 'ctx'), split_axis=0, concat_axis=0, ti...  4.88 us
    ppermute x3, starting transfers between devices, body(): parts[s] = lax.ppermute(parts[s], 'ctx', back)  3.88 us
    ppermute x3, waiting for transfers between devices, body(): parts[s] = lax.ppermute(parts[s], 'ctx', back)  2.72 us
    pallas_call x1, Pallas kernels, body(): pl.pallas_call(prepare_kernel, out_shape=[jax.ShapeDtypeStruct((tokens, w...  2.1 us
  transfers between devices with their start and end apart: 7, of which 5 were waited for; matrix products, arithmetic and copies ran while one was open for 0% of the time, Pallas kernels for 5%

profile of v8, /device:TPU:0, one launch (start us, length us, event | category | flops | bytes accessed | tf_op | source)
XLA Modules:
  0.0 53.3 jit_solution(14147620091276666095)
XLA Ops:
  0.6 1.0 %pack.1 = bf16[1040,128]{1,0:T(8,128)(2,1)S(1)} custom-call(bf16[128,512]{1,0:T(8,128)(2,1)} %bitcast.14, bf16[128,512]{1,0:T(8,128)(2,1)} %bitcast.16, s32[1,128]{1,0:T(1,128)} %depth_ref.3, s32[1,128]{1,0:T(1,128)} %end_ref.3), custom_call_target="tpu_custom_call" | custom-call | tf_op jit(solution)/shard_map/pack/pallas_call | solution.py:306
  1.7 5.8 %collective-permute-start.2 = (bf16[1040,128]{1,0:T(8,128)(2,1)S(1)}, bf16[1040,128]{1,0:T(8,128)(2,1)S(1)}, u32[]{:S(2)}, u32[]{:S(2)}) collective-permute-start(bf16[1040,128]{1,0:T(8,128)(2,1)S(1)} %pack.1), channel_id=1, source_target_pairs={{0,3},{1,2},{4,7},{5,6},{8,11},{9,10},{12,15},{13,14},{16,19},{17,... | collective-permute-start | bytes 798728 | tf_op jit(solution)/shard_map/ppermute | solution.py:315
  7.5 1.3 %collective-permute-start.1 = (bf16[1040,128]{1,0:T(8,128)(2,1)S(1)}, bf16[1040,128]{1,0:T(8,128)(2,1)S(1)}, u32[]{:S(2)}, u32[]{:S(2)}) collective-permute-start(bf16[1040,128]{1,0:T(8,128)(2,1)S(1)} %pack.1), channel_id=1, source_target_pairs={{0,2},{1,3},{4,6},{5,7},{8,10},{9,11},{12,14},{13,15},{16,18},{17,... | collective-permute-start | bytes 798728 | tf_op jit(solution)/shard_map/ppermute | solution.py:315
  8.8 2.5 %collective-permute-start = (bf16[1040,128]{1,0:T(8,128)(2,1)S(1)}, bf16[1040,128]{1,0:T(8,128)(2,1)S(1)}, u32[]{:S(2)}, u32[]{:S(2)}) collective-permute-start(bf16[1040,128]{1,0:T(8,128)(2,1)S(1)} %pack.1), channel_id=1, source_target_pairs={{0,1},{2,3},{4,5},{6,7},{8,9},{10,11},{12,13},{14,15},{16,17},{18,... | collective-permute-start | bytes 798728 | tf_op jit(solution)/shard_map/ppermute | solution.py:315
  11.3 2.1 %prepare.1 = (bf16[128,4096]{1,0:T(8,128)(2,1)S(1)}, bf16[128,4096]{1,0:T(8,128)(2,1)S(1)}, bf16[128,4096]{1,0:T(8,128)(2,1)S(1)}) custom-call(bf16[128,4096]{1,0:T(8,128)(2,1)} %bitcast.10, bf16[128,4096]{1,0:T(8,128)(2,1)} %bitcast.11, bf16[128,4096]{1,0:T(8,128)(2,1)} %bitcast.12), custom_call_target="tpu_custom_call" | custom-call | flops 524288 | bytes 6291456 | tf_op jit(solution)/shard_map/prepare/pallas_call | solution.py:319
  13.4 0.9 %collective-permute-done.2.refs_2_ = bf16[1040,128]{1,0:T(8,128)(2,1)S(1)} collective-permute-done((bf16[1040,128]{1,0:T(8,128)(2,1)S(1)}, bf16[1040,128]{1,0:T(8,128)(2,1)S(1)}, u32[]{:S(2)}, u32[]{:S(2)}) %collective-permute-start.2) | collective-permute-done | bytes 266272 | tf_op jit(solution)/shard_map/ppermute | solution.py:315
  14.3 4.5 %collective-permute-done.1.refs_1_ = bf16[1040,128]{1,0:T(8,128)(2,1)S(1)} collective-permute-done((bf16[1040,128]{1,0:T(8,128)(2,1)S(1)}, bf16[1040,128]{1,0:T(8,128)(2,1)S(1)}, u32[]{:S(2)}, u32[]{:S(2)}) %collective-permute-start.1) | collective-permute-done | bytes 266272 | tf_op jit(solution)/shard_map/ppermute | solution.py:315
  18.8 0.1 collective-permute-done.refs_0_
  18.9 11.5 %attend.1 = (bf16[128,4096]{1,0:T(8,128)(2,1)}, bf16[1024,128]{1,0:T(8,128)(2,1)S(1)}, bf16[1024,128]{1,0:T(8,128)(2,1)S(1)}, bf16[1024,128]{1,0:T(8,128)(2,1)S(...) custom-call(s32[1,8]{1,0:T(1,128)} %lengths_ref.1, f32[32]{0:T(128)} %slope_ref.1, f32[32]{0:T(128)} %gain_ref.1, ...), custom_call_target="tpu_custom_call" | custom-call | flops 2684354560 | bytes 5242880 | tf_op jit(solution)/shard_map/attend/pallas_call | solution.py:333
  30.3 1.3 %collective-permute-start.3 = (bf16[1024,128]{1,0:T(8,128)(2,1)S(1)}, bf16[1024,128]{1,0:T(8,128)(2,1)S(1)}, u32[]{:S(2)}, u32[]{:S(2)}) collective-permute-start(bf16[1024,128]{1,0:T(8,128)(2,1)S(1)} %get-tuple-element.20), channel_id=1, source_target_pairs={{2,1},{3,0},{6,5},{7,4},{10,9},{11,8},{14,13},{15,12},{18,17},{19,... | collective-permute-start | bytes 786440 | tf_op jit(solution)/shard_map/ppermute | solution.py:378
  31.6 1.3 %collective-permute-start.4 = (bf16[1024,128]{1,0:T(8,128)(2,1)S(1)}, bf16[1024,128]{1,0:T(8,128)(2,1)S(1)}, u32[]{:S(2)}, u32[]{:S(2)}) collective-permute-start(bf16[1024,128]{1,0:T(8,128)(2,1)S(1)} %get-tuple-element.21), channel_id=1, source_target_pairs={{2,0},{3,1},{6,4},{7,5},{10,8},{11,9},{14,12},{15,13},{18,16},{19,... | collective-permute-start | bytes 786440 | tf_op jit(solution)/shard_map/ppermute | solution.py:378
  32.9 1.3 %collective-permute-start.5 = (bf16[1024,128]{1,0:T(8,128)(2,1)S(1)}, bf16[1024,128]{1,0:T(8,128)(2,1)S(1)}, u32[]{:S(2)}, u32[]{:S(2)}) collective-permute-start(bf16[1024,128]{1,0:T(8,128)(2,1)S(1)} %get-tuple-element.22), channel_id=1, source_target_pairs={{1,0},{3,2},{5,4},{7,6},{9,8},{11,10},{13,12},{15,14},{17,16},{19,... | collective-permute-start | bytes 786440 | tf_op jit(solution)/shard_map/ppermute | solution.py:378
  34.2 10.1 %all-to-all-start = ((f32[32,8,128]{2,1,0:T(8,128)}), f32[32,8,128]{2,1,0:T(8,128)S(1)}, u32[]{:S(2)}, u32[]{:S(2)}) async-start(f32[32,8,128]{2,1,0:T(8,128)} %bitcast.8), calls=%async_computation | async-start | bytes 262144 | tf_op jit(solution)/shard_map/all_to_all | solution.py:379
  44.3 0.0 collective-permute-done.3.refs_1_
  44.3 2.7 %collective-permute-done.4.refs_2_ = bf16[1024,128]{1,0:T(8,128)(2,1)S(1)} collective-permute-done((bf16[1024,128]{1,0:T(8,128)(2,1)S(1)}, bf16[1024,128]{1,0:T(8,128)(2,1)S(1)}, u32[]{:S(2)}, u32[]{:S(2)}) %collective-permute-start.4) | collective-permute-done | bytes 262176 | tf_op jit(solution)/shard_map/ppermute | solution.py:378
  47.0 0.0 collective-permute-done.5.refs_3_
  47.0 0.8 %combine.1 = (bf16[128,512]{1,0:T(8,128)(2,1)}, bf16[128,512]{1,0:T(8,128)(2,1)}) custom-call(bf16[1024,128]{1,0:T(8,128)(2,1)S(1)} %get-tuple-element.19.refs_0_, bf16[1024,128]{1,0:T(8,128)(2,1)S(1)} %collective-permute-done.3.refs_1_, bf16[1024,128]{1,0:T(8,128)(2,1)S(1)} %collective-permute-done.4.refs_2_, ...), custom_call_target="tpu_custom_call" | custom-call | flops 1048576 | bytes 1310720 | tf_op jit(solution)/shard_map/combine/pallas_call | solution.py:381
  47.8 4.9 %all-to-all-done.parts_ref = f32[32,8,128]{2,1,0:T(8,128)S(1)} async-done(((f32[32,8,128]{2,1,0:T(8,128)}), f32[32,8,128]{2,1,0:T(8,128)S(1)}, u32[]{:S(2)}, u32[]{:S(2)}) %all-to-all-start) | async-done | bytes 131104 | tf_op jit(solution)/shard_map/all_to_all | solution.py:379
  52.7 0.6 %bias.1 = f32[2,8]{1,0:T(2,128)} custom-call(f32[32,8,128]{2,1,0:T(8,128)S(1)} %all-to-all-done.parts_ref, bf16[128,512]{1,0:T(8,128)(2,1)} %get-tuple-element.23._), custom_call_target="tpu_custom_call" | custom-call | tf_op jit(solution)/shard_map/bias/pallas_call | solution.py:394
Async XLA Ops:
  1.7 12.6 %collective-permute-start.2 = (bf16[1040,128]{1,0:T(8,128)(2,1)S(1)}, bf16[1040,128]{1,0:T(8,128)(2,1)S(1)}, u32[]{:S(2)}, u32[]{:S(2)}) collective-permute-start(bf16[1040,128]{1,0:T(8,128)(2,1)S(1)} %pack.1), channel_id=1, source_target_pairs={{0,3},{1,2},{4,7},{5,6},{8,11},{9,10},{12,15},{13,14},{16,19},{17,... | collective-permute-start | bytes 798728 | tf_op jit(solution)/shard_map/ppermute | solution.py:315
  7.5 11.3 %collective-permute-start.1 = (bf16[1040,128]{1,0:T(8,128)(2,1)S(1)}, bf16[1040,128]{1,0:T(8,128)(2,1)S(1)}, u32[]{:S(2)}, u32[]{:S(2)}) collective-permute-start(bf16[1040,128]{1,0:T(8,128)(2,1)S(1)} %pack.1), channel_id=1, source_target_pairs={{0,2},{1,3},{4,6},{5,7},{8,10},{9,11},{12,14},{13,15},{16,18},{17,... | collective-permute-start | bytes 798728 | tf_op jit(solution)/shard_map/ppermute | solution.py:315
  8.8 10.1 %collective-permute-start = (bf16[1040,128]{1,0:T(8,128)(2,1)S(1)}, bf16[1040,128]{1,0:T(8,128)(2,1)S(1)}, u32[]{:S(2)}, u32[]{:S(2)}) collective-permute-start(bf16[1040,128]{1,0:T(8,128)(2,1)S(1)} %pack.1), channel_id=1, source_target_pairs={{0,1},{2,3},{4,5},{6,7},{8,9},{10,11},{12,13},{14,15},{16,17},{18,... | collective-permute-start | bytes 798728 | tf_op jit(solution)/shard_map/ppermute | solution.py:315
  30.3 14.0 %collective-permute-start.3 = (bf16[1024,128]{1,0:T(8,128)(2,1)S(1)}, bf16[1024,128]{1,0:T(8,128)(2,1)S(1)}, u32[]{:S(2)}, u32[]{:S(2)}) collective-permute-start(bf16[1024,128]{1,0:T(8,128)(2,1)S(1)} %get-tuple-element.20), channel_id=1, source_target_pairs={{2,1},{3,0},{6,5},{7,4},{10,9},{11,8},{14,13},{15,12},{18,17},{19,... | collective-permute-start | bytes 786440 | tf_op jit(solution)/shard_map/ppermute | solution.py:378
  31.6 15.4 %collective-permute-start.4 = (bf16[1024,128]{1,0:T(8,128)(2,1)S(1)}, bf16[1024,128]{1,0:T(8,128)(2,1)S(1)}, u32[]{:S(2)}, u32[]{:S(2)}) collective-permute-start(bf16[1024,128]{1,0:T(8,128)(2,1)S(1)} %get-tuple-element.21), channel_id=1, source_target_pairs={{2,0},{3,1},{6,4},{7,5},{10,8},{11,9},{14,12},{15,13},{18,16},{19,... | collective-permute-start | bytes 786440 | tf_op jit(solution)/shard_map/ppermute | solution.py:378
  32.9 14.1 %collective-permute-start.5 = (bf16[1024,128]{1,0:T(8,128)(2,1)S(1)}, bf16[1024,128]{1,0:T(8,128)(2,1)S(1)}, u32[]{:S(2)}, u32[]{:S(2)}) collective-permute-start(bf16[1024,128]{1,0:T(8,128)(2,1)S(1)} %get-tuple-element.22), channel_id=1, source_target_pairs={{1,0},{3,2},{5,4},{7,6},{9,8},{11,10},{13,12},{15,14},{17,16},{19,... | collective-permute-start | bytes 786440 | tf_op jit(solution)/shard_map/ppermute | solution.py:378
  34.2 18.5 %all-to-all-start = ((f32[32,8,128]{2,1,0:T(8,128)}), f32[32,8,128]{2,1,0:T(8,128)S(1)}, u32[]{:S(2)}, u32[]{:S(2)}) async-start(f32[32,8,128]{2,1,0:T(8,128)} %bitcast.8), calls=%async_computation | async-start | bytes 262144 | tf_op jit(solution)/shard_map/all_to_all | solution.py:379

commit v9 on v8

--- a/solution.py
+++ b/solution.py
@@ -251,6 +251,12 @@
     bias_copy.wait()
 
 
+def add_kernel(mine_ref, theirs_ref, next_ref, sum_ref, next_out):
+    total = mine_ref[...].astype(jnp.float32) + theirs_ref[...].astype(jnp.float32)
+    sum_ref[...] = total.astype(jnp.bfloat16)
+    next_out[...] = next_ref[...]
+
+
 def combine_kernel(blocks, *refs):
     parts = refs[0:blocks]
     key_out, value_out = refs[blocks:]
@@ -311,10 +317,16 @@
         compiler_params=params,
         name="pack",
     )(key_held, value_held, depth_held, end_held)
-    arrived = [
-        lax.ppermute(message, "ctx", [(i, i ^ s) for i in range(blocks) if i < i ^ s])
-        for s in range(1, blocks)
-    ]
+    if blocks == 4:
+        along_y = lax.ppermute(message, "ctx", [(0, 2), (1, 3)])
+        along_x = lax.ppermute(message, "ctx", [(0, 1), (2, 3)])
+        across = lax.ppermute(along_y, "ctx", [(2, 3), (3, 2)])
+        arrived = [along_x, along_y, across]
+    else:
+        arrived = [
+            lax.ppermute(message, "ctx", [(i, i ^ s) for i in range(blocks) if i < i ^ s])
+            for s in range(1, blocks)
+        ]
 
     prepared = pl.pallas_call(
         prepare_kernel,
@@ -373,15 +385,29 @@
     query_grads = results[0]
     parts = list(results[1 : 1 + blocks])
     bias_parts = results[1 + blocks].reshape(replicas * blocks, 8, WIDTH)
-    for s in reversed(range(1, blocks)):
-        back = [(i, i ^ s) for i in range(blocks) if i > i ^ s]
-        parts[s] = lax.ppermute(parts[s], "ctx", back)
+    if blocks == 4:
+        across = lax.ppermute(parts[3], "ctx", [(3, 2), (2, 3)])
+        along_y, along_x = pl.pallas_call(
+            add_kernel,
+            out_shape=[jax.ShapeDtypeStruct(parts[0].shape, bf16)] * 2,
+            in_specs=[vmem] * 3,
+            out_specs=[vmem] * 2,
+            compiler_params=params,
+            name="add",
+        )(parts[2], across, parts[1])
+        along_y = lax.ppermute(along_y, "ctx", [(2, 0), (3, 1)])
+        along_x = lax.ppermute(along_x, "ctx", [(1, 0), (3, 2)])
+        parts = [parts[0], along_y, along_x]
+    else:
+        for s in range(1, blocks):
+            back = [(i, i ^ s) for i in range(blocks) if i > i ^ s]
+            parts[s] = lax.ppermute(parts[s], "ctx", back)
     bias_parts = lax.all_to_all(bias_parts, ("dp", "ctx"), split_axis=0, concat_axis=0, tiled=True)
 
     key_grads, value_grads = pl.pallas_call(
-        functools.partial(combine_kernel, blocks),
+        functools.partial(combine_kernel, len(parts)),
         out_shape=[jax.ShapeDtypeStruct((tokens, kv_width), bf16)] * 2,
-        in_specs=[vmem] * blocks,
+        in_specs=[vmem] * len(parts),
         out_specs=[vmem] * 2,
         compiler_params=params,
         cost_estimate=pl.CostEstimate(
@@ -390,7 +416,7 @@
             transcendentals=0,
         ),
         name="combine",
-    )(parts[0], *reversed(parts[1:]))
+    )(*parts)
     bias_grads = pl.pallas_call(
         bias_kernel,
         out_shape=jax.ShapeDtypeStruct((2, local_heads), f32),

time: 53.6 us -> 61 us (1.14)
  starting transfers between devices: 23.6 us -> 33.8 us
  waiting for transfers between devices: 13.1 us -> 10.2 us
    all_to_all x1, starting transfers between devices: 10.1 us -> 21.6 us  [body(): lax.all_to_all(bias_parts, ('dp', 'ctx'), split_axis=0, concat_axis=0, ti...]
    ppermute x6, waiting for transfers between devices: 8.19 us -> 2.57 us  [the longest x1 2.2 us: body(): along_y = lax.ppermute(message, 'ctx', [(0, 2), (1, 3)])]
    all_to_all x1, waiting for transfers between devices: 4.88 us -> 7.62 us  [body(): lax.all_to_all(bias_parts, ('dp', 'ctx'), split_axis=0, concat_axis=0, ti...]
    ppermute x6, starting transfers between devices: 13.5 us -> 12.2 us  [the longest x1 4.89 us: body(): along_y = lax.ppermute(message, 'ctx', [(0, 2), (1, 3)])]
  transfers between devices with their start and end apart: 7 -> 7, of which waited for: 5 -> 3; matrix products, arithmetic and copies ran while one was open for 0% -> 0% of each run, Pallas kernels for 5% -> 5%
where the time goes in v9:
time: 61 us; the launch traced here: 60.7 us
  starting transfers between devices  33.8 us (55%)
  Pallas kernels  16 us (26%)
  waiting for transfers between devices  10.2 us (17%)
  between operations  0.73 us (1%)
    all_to_all x1, starting transfers between devices, body(): lax.all_to_all(bias_parts, ('dp', 'ctx'), split_axis=0, concat_axis=0, ti...  21.6 us
    pallas_call x1, Pallas kernels, body(): pl.pallas_call(functools.partial(main_kernel, blocks, heads_per_group, gr...  11.4 us
    all_to_all x1, waiting for transfers between devices, body(): lax.all_to_all(bias_parts, ('dp', 'ctx'), split_axis=0, concat_axis=0, ti...  7.62 us
    ppermute x1, starting transfers between devices, body(): along_y = lax.ppermute(message, 'ctx', [(0, 2), (1, 3)])  4.89 us
    ppermute x1, starting transfers between devices, body(): along_x = lax.ppermute(message, 'ctx', [(0, 1), (2, 3)])  3.41 us
    ppermute x1, waiting for transfers between devices, body(): along_y = lax.ppermute(message, 'ctx', [(0, 2), (1, 3)])  2.2 us
    pallas_call x1, Pallas kernels, body(): pl.pallas_call(prepare_kernel, out_shape=[jax.ShapeDtypeStruct((tokens, w...  2.1 us
    ppermute x1, starting transfers between devices, body(): along_y = lax.ppermute(along_y, 'ctx', [(2, 0), (3, 1)])  1.29 us
  transfers between devices with their start and end apart: 7, of which 3 were waited for; matrix products, arithmetic and copies ran while one was open for 0% of the time, Pallas kernels for 5%

profile of v9, /device:TPU:0, one launch (start us, length us, event | category | flops | bytes accessed | tf_op | source)
XLA Modules:
  0.0 60.7 jit_solution(5707544304012271660)
XLA Ops:
  0.6 1.0 %pack.1 = bf16[1040,128]{1,0:T(8,128)(2,1)S(1)} custom-call(bf16[128,512]{1,0:T(8,128)(2,1)} %bitcast.14, bf16[128,512]{1,0:T(8,128)(2,1)} %bitcast.16, s32[1,128]{1,0:T(1,128)} %depth_ref.3, s32[1,128]{1,0:T(1,128)} %end_ref.3), custom_call_target="tpu_custom_call" | custom-call | tf_op jit(solution)/shard_map/pack/pallas_call | solution.py:312
  1.7 4.9 %collective-permute-start.1 = (bf16[1040,128]{1,0:T(8,128)(2,1)S(1)}, bf16[1040,128]{1,0:T(8,128)(2,1)S(1)}, u32[]{:S(2)}, u32[]{:S(2)}) collective-permute-start(bf16[1040,128]{1,0:T(8,128)(2,1)S(1)} %pack.1), channel_id=1, source_target_pairs={{0,2},{1,3},{4,6},{5,7},{8,10},{9,11},{12,14},{13,15},{16,18},{17,... | collective-permute-start | bytes 798728 | tf_op jit(solution)/shard_map/ppermute | solution.py:321
  6.6 3.4 %collective-permute-start = (bf16[1040,128]{1,0:T(8,128)(2,1)S(1)}, bf16[1040,128]{1,0:T(8,128)(2,1)S(1)}, u32[]{:S(2)}, u32[]{:S(2)}) collective-permute-start(bf16[1040,128]{1,0:T(8,128)(2,1)S(1)} %pack.1), channel_id=1, source_target_pairs={{0,1},{2,3},{4,5},{6,7},{8,9},{10,11},{12,13},{14,15},{16,17},{18,... | collective-permute-start | bytes 798728 | tf_op jit(solution)/shard_map/ppermute | solution.py:322
  10.0 2.2 %collective-permute-done.1.refs_1_ = bf16[1040,128]{1,0:T(8,128)(2,1)S(1)} collective-permute-done((bf16[1040,128]{1,0:T(8,128)(2,1)S(1)}, bf16[1040,128]{1,0:T(8,128)(2,1)S(1)}, u32[]{:S(2)}, u32[]{:S(2)}) %collective-permute-start.1) | collective-permute-done | bytes 266272 | tf_op jit(solution)/shard_map/ppermute | solution.py:321
  12.2 0.7 %collective-permute-start.2 = (bf16[1040,128]{1,0:T(8,128)(2,1)S(1)}, bf16[1040,128]{1,0:T(8,128)(2,1)S(1)}, u32[]{:S(2)}, u32[]{:S(2)}) collective-permute-start(bf16[1040,128]{1,0:T(8,128)(2,1)S(1)} %collective-permute-done.1.refs_1_), channel_id=1, source_target_pairs={{2,3},{3,2},{6,7},{7,6},{10,11},{11,10},{14,15},{15,14},{18,19},{1... | collective-permute-start | bytes 798728 | tf_op jit(solution)/shard_map/ppermute | solution.py:323
  12.8 2.1 %prepare.1 = (bf16[128,4096]{1,0:T(8,128)(2,1)S(1)}, bf16[128,4096]{1,0:T(8,128)(2,1)S(1)}, bf16[128,4096]{1,0:T(8,128)(2,1)S(1)}) custom-call(bf16[128,4096]{1,0:T(8,128)(2,1)} %bitcast.10, bf16[128,4096]{1,0:T(8,128)(2,1)} %bitcast.11, bf16[128,4096]{1,0:T(8,128)(2,1)} %bitcast.12), custom_call_target="tpu_custom_call" | custom-call | flops 524288 | bytes 6291456 | tf_op jit(solution)/shard_map/prepare/pallas_call | solution.py:331
  15.0 0.4 collective-permute-done.refs_0_
  15.3 0.0 collective-permute-done.2.refs_2_
  15.3 11.4 %attend.1 = (bf16[128,4096]{1,0:T(8,128)(2,1)}, bf16[1024,128]{1,0:T(8,128)(2,1)S(1)}, bf16[1024,128]{1,0:T(8,128)(2,1)S(1)}, bf16[1024,128]{1,0:T(8,128)(2,1)S(...) custom-call(s32[1,8]{1,0:T(1,128)} %lengths_ref.1, f32[32]{0:T(128)} %slope_ref.1, f32[32]{0:T(128)} %gain_ref.1, ...), custom_call_target="tpu_custom_call" | custom-call | flops 2684354560 | bytes 5242880 | tf_op jit(solution)/shard_map/attend/pallas_call | solution.py:345
  26.8 0.7 %collective-permute-start.3 = (bf16[1024,128]{1,0:T(8,128)(2,1)S(1)}, bf16[1024,128]{1,0:T(8,128)(2,1)S(1)}, u32[]{:S(2)}, u32[]{:S(2)}) collective-permute-start(bf16[1024,128]{1,0:T(8,128)(2,1)S(1)} %get-tuple-element.23), channel_id=1, source_target_pairs={{3,2},{2,3},{7,6},{6,7},{11,10},{10,11},{15,14},{14,15},{19,18},{1... | collective-permute-start | bytes 786440 | tf_op jit(solution)/shard_map/ppermute | solution.py:389
  27.4 0.0 collective-permute-done.3.theirs_ref
  27.5 0.1 add.1
  27.5 1.3 %collective-permute-start.4 = (bf16[1024,128]{1,0:T(8,128)(2,1)S(1)}, bf16[1024,128]{1,0:T(8,128)(2,1)S(1)}, u32[]{:S(2)}, u32[]{:S(2)}) collective-permute-start(bf16[1024,128]{1,0:T(8,128)(2,1)S(1)} %get-tuple-element.25), channel_id=1, source_target_pairs={{2,0},{3,1},{6,4},{7,5},{10,8},{11,9},{14,12},{15,13},{18,16},{19,... | collective-permute-start | bytes 786440 | tf_op jit(solution)/shard_map/ppermute | solution.py:398
  28.8 1.3 %collective-permute-start.5 = (bf16[1024,128]{1,0:T(8,128)(2,1)S(1)}, bf16[1024,128]{1,0:T(8,128)(2,1)S(1)}, u32[]{:S(2)}, u32[]{:S(2)}) collective-permute-start(bf16[1024,128]{1,0:T(8,128)(2,1)S(1)} %get-tuple-element.26), channel_id=1, source_target_pairs={{1,0},{3,2},{5,4},{7,6},{9,8},{11,10},{13,12},{15,14},{17,16},{19,... | collective-permute-start | bytes 786440 | tf_op jit(solution)/shard_map/ppermute | solution.py:399
  30.1 21.6 %all-to-all-start = ((f32[32,8,128]{2,1,0:T(8,128)}), f32[32,8,128]{2,1,0:T(8,128)S(1)}, u32[]{:S(2)}, u32[]{:S(2)}) async-start(f32[32,8,128]{2,1,0:T(8,128)} %bitcast.8), calls=%async_computation | async-start | bytes 262144 | tf_op jit(solution)/shard_map/all_to_all | solution.py:405
  51.7 0.0 collective-permute-done.4.refs_1_
  51.7 0.0 collective-permute-done.5.refs_2_
  51.7 0.8 %combine.1 = (bf16[128,512]{1,0:T(8,128)(2,1)}, bf16[128,512]{1,0:T(8,128)(2,1)}) custom-call(bf16[1024,128]{1,0:T(8,128)(2,1)S(1)} %get-tuple-element.21.refs_0_, bf16[1024,128]{1,0:T(8,128)(2,1)S(1)} %collective-permute-done.4.refs_1_, bf16[1024,128]{1,0:T(8,128)(2,1)S(1)} %collective-permute-done.5.refs_2_), custom_call_target="tpu_custom_call" | custom-call | flops 1048576 | bytes 1310720 | tf_op jit(solution)/shard_map/combine/pallas_call | solution.py:407
  52.5 7.6 %all-to-all-done.parts_ref = f32[32,8,128]{2,1,0:T(8,128)S(1)} async-done(((f32[32,8,128]{2,1,0:T(8,128)}), f32[32,8,128]{2,1,0:T(8,128)S(1)}, u32[]{:S(2)}, u32[]{:S(2)}) %all-to-all-start) | async-done | bytes 131104 | tf_op jit(solution)/shard_map/all_to_all | solution.py:405
  60.1 0.6 bias.1
Async XLA Ops:
  1.7 10.5 %collective-permute-start.1 = (bf16[1040,128]{1,0:T(8,128)(2,1)S(1)}, bf16[1040,128]{1,0:T(8,128)(2,1)S(1)}, u32[]{:S(2)}, u32[]{:S(2)}) collective-permute-start(bf16[1040,128]{1,0:T(8,128)(2,1)S(1)} %pack.1), channel_id=1, source_target_pairs={{0,2},{1,3},{4,6},{5,7},{8,10},{9,11},{12,14},{13,15},{16,18},{17,... | collective-permute-start | bytes 798728 | tf_op jit(solution)/shard_map/ppermute | solution.py:321
  6.6 8.8 %collective-permute-start = (bf16[1040,128]{1,0:T(8,128)(2,1)S(1)}, bf16[1040,128]{1,0:T(8,128)(2,1)S(1)}, u32[]{:S(2)}, u32[]{:S(2)}) collective-permute-start(bf16[1040,128]{1,0:T(8,128)(2,1)S(1)} %pack.1), channel_id=1, source_target_pairs={{0,1},{2,3},{4,5},{6,7},{8,9},{10,11},{12,13},{14,15},{16,17},{18,... | collective-permute-start | bytes 798728 | tf_op jit(solution)/shard_map/ppermute | solution.py:322
  12.2 3.1 %collective-permute-start.2 = (bf16[1040,128]{1,0:T(8,128)(2,1)S(1)}, bf16[1040,128]{1,0:T(8,128)(2,1)S(1)}, u32[]{:S(2)}, u32[]{:S(2)}) collective-permute-start(bf16[1040,128]{1,0:T(8,128)(2,1)S(1)} %collective-permute-done.1.refs_1_), channel_id=1, source_target_pairs={{2,3},{3,2},{6,7},{7,6},{10,11},{11,10},{14,15},{15,14},{18,19},{1... | collective-permute-start | bytes 798728 | tf_op jit(solution)/shard_map/ppermute | solution.py:323
  26.8 0.7 %collective-permute-start.3 = (bf16[1024,128]{1,0:T(8,128)(2,1)S(1)}, bf16[1024,128]{1,0:T(8,128)(2,1)S(1)}, u32[]{:S(2)}, u32[]{:S(2)}) collective-permute-start(bf16[1024,128]{1,0:T(8,128)(2,1)S(1)} %get-tuple-element.23), channel_id=1, source_target_pairs={{3,2},{2,3},{7,6},{6,7},{11,10},{10,11},{15,14},{14,15},{19,18},{1... | collective-permute-start | bytes 786440 | tf_op jit(solution)/shard_map/ppermute | solution.py:389
  27.5 24.2 %collective-permute-start.4 = (bf16[1024,128]{1,0:T(8,128)(2,1)S(1)}, bf16[1024,128]{1,0:T(8,128)(2,1)S(1)}, u32[]{:S(2)}, u32[]{:S(2)}) collective-permute-start(bf16[1024,128]{1,0:T(8,128)(2,1)S(1)} %get-tuple-element.25), channel_id=1, source_target_pairs={{2,0},{3,1},{6,4},{7,5},{10,8},{11,9},{14,12},{15,13},{18,16},{19,... | collective-permute-start | bytes 786440 | tf_op jit(solution)/shard_map/ppermute | solution.py:398
  28.8 22.9 %collective-permute-start.5 = (bf16[1024,128]{1,0:T(8,128)(2,1)S(1)}, bf16[1024,128]{1,0:T(8,128)(2,1)S(1)}, u32[]{:S(2)}, u32[]{:S(2)}) collective-permute-start(bf16[1024,128]{1,0:T(8,128)(2,1)S(1)} %get-tuple-element.26), channel_id=1, source_target_pairs={{1,0},{3,2},{5,4},{7,6},{9,8},{11,10},{13,12},{15,14},{17,16},{19,... | collective-permute-start | bytes 786440 | tf_op jit(solution)/shard_map/ppermute | solution.py:399
  30.1 30.0 %all-to-all-start = ((f32[32,8,128]{2,1,0:T(8,128)}), f32[32,8,128]{2,1,0:T(8,128)S(1)}, u32[]{:S(2)}, u32[]{:S(2)}) async-start(f32[32,8,128]{2,1,0:T(8,128)} %bitcast.8), calls=%async_computation | async-start | bytes 262144 | tf_op jit(solution)/shard_map/all_to_all | solution.py:405

commit v10 on v8

--- a/solution.py
+++ b/solution.py
@@ -74,7 +74,7 @@
     remote = refs[0 : blocks - 1]
     query_grad_hbm = refs[blocks - 1]
     part_refs = refs[blocks : 2 * blocks]
-    bias_hbm = refs[2 * blocks]
+    bias_ref = refs[2 * blocks]
     (
         query_grad_ref,
         distance_ref,
@@ -86,9 +86,7 @@
         weight_ref,
         probs_ref,
         dscore_ref,
-        bias_ref,
         store_sems,
-        bias_sem,
     ) = refs[2 * blocks + 1 :]
     factor = WIDTH**-0.5
     group_columns = heads_per_group * WIDTH
@@ -230,30 +228,23 @@
         query_part(keys_across, group, pairs - 1)
         store(group).start()
 
-    slope_sum = jnp.sum(slope_rows[...], axis=1, keepdims=True)
-    gain_sum = jnp.sum(gain_rows[...], axis=1, keepdims=True)
     shape = slope_rows.shape
-    lane = lax.broadcasted_iota(jnp.int32, shape, 1)
-    row = lax.broadcasted_iota(jnp.int32, shape, 0)
-    replicas, parts, rows_here, local = bias_ref.shape
-    local_heads = shape[0] // parts
-    kind = lax.broadcasted_iota(jnp.int32, (rows_here, local), 0)
-    for part in range(parts):
-        mine = (lane == row - part * local_heads) & (lane < local_heads)
-        slope_line = jnp.sum(jnp.where(mine, slope_sum, 0.0), axis=0, keepdims=True)
-        gain_line = jnp.sum(jnp.where(mine, gain_sum, 0.0), axis=0, keepdims=True)
-        tile = jnp.where(kind == 0, slope_line, jnp.where(kind == 1, gain_line, 0.0))
-        bias_ref[:, part] = jnp.broadcast_to(tile[None], (replicas, rows_here, local))
-    bias_copy = pltpu.make_async_copy(bias_ref, bias_hbm, bias_sem)
-    bias_copy.start()
+    diagonal = lax.broadcasted_iota(jnp.int32, shape, 0) == lax.broadcasted_iota(
+        jnp.int32, shape, 1
+    )
+    lines = []
+    for rows in (slope_rows, gain_rows):
+        column = jnp.sum(rows[...], axis=1, keepdims=True)
+        lines.append(jnp.sum(jnp.where(diagonal, column, 0.0), axis=0, keepdims=True))
+    row = lax.broadcasted_iota(jnp.int32, bias_ref.shape, 0)
+    bias_ref[...] = jnp.where(row == 0, lines[0], jnp.where(row == 1, lines[1], 0.0))
     for group in range(groups):
         store(group).wait()
-    bias_copy.wait()
 
 
 def combine_kernel(blocks, *refs):
     parts = refs[0:blocks]
-    key_out, value_out = refs[blocks:]
+    bias_ref, key_out, value_out, bias_out = refs[blocks:]
     tokens = key_out.shape[0]
     groups = key_out.shape[1] // WIDTH
     for kind, out in enumerate((key_out, value_out)):
@@ -263,10 +254,13 @@
             for s in range(1, blocks):
                 total = total + parts[s][at : at + tokens, :].astype(jnp.float32)
             out[:, group * WIDTH : (group + 1) * WIDTH] = total.astype(jnp.bfloat16)
-
-
-def bias_kernel(parts_ref, _, out_ref):
-    out_ref[...] = jnp.sum(parts_ref[...], axis=0)[0:2, 0 : out_ref.shape[1]]
+    here = lax.axis_index("ctx")
+    share = bias_out.shape[1]
+    mine = bias_ref[0:2, 0:share]
+    for block in range(1, blocks):
+        other = bias_ref[0:2, block * share : (block + 1) * share]
+        mine = jnp.where(here == block, other, mine)
+    bias_out[...] = mine
 
 
 def body(
@@ -328,7 +322,7 @@
         name="prepare",
     )(hold(queries[0]), hold(outputs[0]), hold(out_grads[0]))
 
-    bias_shape = (replicas, blocks, 8, WIDTH)
+    bias_shape = (8, WIDTH)
     matmul_flops = 2 * tokens * keys_seen * WIDTH * heads_all
     results = pl.pallas_call(
         functools.partial(main_kernel, blocks, heads_per_group, groups),
@@ -336,7 +330,7 @@
         + [jax.ShapeDtypeStruct((message_rows, WIDTH), bf16)] * blocks
         + [jax.ShapeDtypeStruct(bias_shape, f32)],
         in_specs=[smem] * 3 + [vmem] * (6 + blocks),
-        out_specs=[hbm] + [vmem] * blocks + [hbm],
+        out_specs=[hbm] + [vmem] * (blocks + 1),
         scratch_shapes=[
             pltpu.VMEM((groups, tokens, group_columns), bf16),
             pltpu.VMEM((keys_seen, tokens), f32),
@@ -348,9 +342,7 @@
             pltpu.VMEM((2, keys_seen, 2 * tokens), f32),
             pltpu.VMEM((keys_seen, group_columns), bf16),
             pltpu.VMEM((keys_seen, group_columns), bf16),
-            pltpu.VMEM(bias_shape, f32),
             pltpu.SemaphoreType.DMA((groups,)),
-            pltpu.SemaphoreType.DMA,
         ],
         compiler_params=params,
         cost_estimate=pl.CostEstimate(
@@ -372,17 +364,22 @@
     )
     query_grads = results[0]
     parts = list(results[1 : 1 + blocks])
-    bias_parts = results[1 + blocks].reshape(replicas * blocks, 8, WIDTH)
-    for s in reversed(range(1, blocks)):
+    bias = results[1 + blocks]
+    for s in range(1, blocks):
         back = [(i, i ^ s) for i in range(blocks) if i > i ^ s]
         parts[s] = lax.ppermute(parts[s], "ctx", back)
-    bias_parts = lax.all_to_all(bias_parts, ("dp", "ctx"), split_axis=0, concat_axis=0, tiled=True)
-
-    key_grads, value_grads = pl.pallas_call(
+    for axis, size in (("ctx", blocks), ("dp", replicas)):
+        bit = 1
+        while bit < size:
+            bias = bias + lax.ppermute(bias, axis, [(i, i ^ bit) for i in range(size)])
+            bit = 2 * bit
+
+    key_grads, value_grads, bias_grads = pl.pallas_call(
         functools.partial(combine_kernel, blocks),
-        out_shape=[jax.ShapeDtypeStruct((tokens, kv_width), bf16)] * 2,
-        in_specs=[vmem] * blocks,
-        out_specs=[vmem] * 2,
+        out_shape=[jax.ShapeDtypeStruct((tokens, kv_width), bf16)] * 2
+        + [jax.ShapeDtypeStruct((2, local_heads), f32)],
+        in_specs=[vmem] * (blocks + 1),
+        out_specs=[vmem] * 3,
         compiler_params=params,
         cost_estimate=pl.CostEstimate(
             flops=2 * message_rows * WIDTH * blocks,
@@ -390,15 +387,7 @@
             transcendentals=0,
         ),
         name="combine",
-    )(parts[0], *reversed(parts[1:]))
-    bias_grads = pl.pallas_call(
-        bias_kernel,
-        out_shape=jax.ShapeDtypeStruct((2, local_heads), f32),
-        in_specs=[vmem, hbm],
-        out_specs=vmem,
-        compiler_params=params,
-        name="bias",
-    )(bias_parts, hold(key_grads))
+    )(*parts, bias)
     return (query_grads[None], key_grads[None], value_grads[None], bias_grads.T)
 
 

time: 53.6 us -> 60.7 us (1.13)
  starting transfers between devices: 23.6 us -> 28.5 us
  waiting for transfers between devices: 13.1 us -> 15.7 us
    ppermute x0 -> x5, starting transfers between devices: none -> 15 us  [body(): bias = bias + lax.ppermute(bias, axis, [(i, i ^ bit) for i in range(size)])]
    ppermute x0 -> x5, waiting for transfers between devices: none -> 10.2 us  [body(): bias = bias + lax.ppermute(bias, axis, [(i, i ^ bit) for i in range(size)])]
    all_to_all x1 -> x0, starting transfers between devices: 10.1 us -> none  [body(): lax.all_to_all(bias_parts, ('dp', 'ctx'), split_axis=0, concat_axis=0, ti...]
    all_to_all x1 -> x0, waiting for transfers between devices: 4.88 us -> none  [body(): lax.all_to_all(bias_parts, ('dp', 'ctx'), split_axis=0, concat_axis=0, ti...]
    ppermute x3, waiting for transfers between devices: 2.72 us -> 0.01 us  [body(): parts[s] = lax.ppermute(parts[s], 'ctx', back)]
  transfers between devices with their start and end apart: 7 -> 11, of which waited for: 5 -> 8; matrix products, arithmetic and copies ran while one was open for 0% -> 0% of each run, Pallas kernels for 5% -> 3%
where the time goes in v10:
time: 60.7 us; the launch traced here: 60.4 us
  starting transfers between devices  28.5 us (47%)
  waiting for transfers between devices  15.7 us (26%)
  Pallas kernels  15.5 us (26%)
  between operations  0.71 us (1%)
    ppermute x5, starting transfers between devices, body(): bias = bias + lax.ppermute(bias, axis, [(i, i ^ bit) for i in range(size)])  15 us
    pallas_call x1, Pallas kernels, body(): pl.pallas_call(functools.partial(main_kernel, blocks, heads_per_group, gr...  11.4 us
    ppermute x5, waiting for transfers between devices, body(): bias = bias + lax.ppermute(bias, axis, [(i, i ^ bit) for i in range(size)])  10.2 us
    ppermute x3, starting transfers between devices, body(): lax.ppermute(message, 'ctx', [(i, i ^ s) for i in range(blocks) if i < i...  9.59 us
    ppermute x3, waiting for transfers between devices, body(): lax.ppermute(message, 'ctx', [(i, i ^ s) for i in range(blocks) if i < i...  5.47 us
    ppermute x3, starting transfers between devices, body(): parts[s] = lax.ppermute(parts[s], 'ctx', back)  3.88 us
    pallas_call x1, Pallas kernels, body(): pl.pallas_call(prepare_kernel, out_shape=[jax.ShapeDtypeStruct((tokens, w...  2.1 us
  transfers between devices with their start and end apart: 11, of which 8 were waited for; matrix products, arithmetic and copies ran while one was open for 0% of the time, Pallas kernels for 3%

profile of v10, /device:TPU:0, one launch (start us, length us, event | category | flops | bytes accessed | tf_op | source)
XLA Modules:
  0.0 60.4 jit_solution(9154870498619575946)
XLA Ops:
  0.6 1.0 %pack.1 = bf16[1040,128]{1,0:T(8,128)(2,1)S(1)} custom-call(bf16[128,512]{1,0:T(8,128)(2,1)} %bitcast.12, bf16[128,512]{1,0:T(8,128)(2,1)} %bitcast.14, s32[1,128]{1,0:T(1,128)} %depth_ref.3, s32[1,128]{1,0:T(1,128)} %end_ref.3), custom_call_target="tpu_custom_call" | custom-call | tf_op jit(solution)/shard_map/pack/pallas_call | solution.py:300
  1.7 5.8 %collective-permute-start.2 = (bf16[1040,128]{1,0:T(8,128)(2,1)S(1)}, bf16[1040,128]{1,0:T(8,128)(2,1)S(1)}, u32[]{:S(2)}, u32[]{:S(2)}) collective-permute-start(bf16[1040,128]{1,0:T(8,128)(2,1)S(1)} %pack.1), channel_id=1, source_target_pairs={{0,3},{1,2},{4,7},{5,6},{8,11},{9,10},{12,15},{13,14},{16,19},{17,... | collective-permute-start | bytes 798728 | tf_op jit(solution)/shard_map/ppermute | solution.py:309
  7.5 1.3 %collective-permute-start.1 = (bf16[1040,128]{1,0:T(8,128)(2,1)S(1)}, bf16[1040,128]{1,0:T(8,128)(2,1)S(1)}, u32[]{:S(2)}, u32[]{:S(2)}) collective-permute-start(bf16[1040,128]{1,0:T(8,128)(2,1)S(1)} %pack.1), channel_id=1, source_target_pairs={{0,2},{1,3},{4,6},{5,7},{8,10},{9,11},{12,14},{13,15},{16,18},{17,... | collective-permute-start | bytes 798728 | tf_op jit(solution)/shard_map/ppermute | solution.py:309
  8.8 2.5 %collective-permute-start = (bf16[1040,128]{1,0:T(8,128)(2,1)S(1)}, bf16[1040,128]{1,0:T(8,128)(2,1)S(1)}, u32[]{:S(2)}, u32[]{:S(2)}) collective-permute-start(bf16[1040,128]{1,0:T(8,128)(2,1)S(1)} %pack.1), channel_id=1, source_target_pairs={{0,1},{2,3},{4,5},{6,7},{8,9},{10,11},{12,13},{14,15},{16,17},{18,... | collective-permute-start | bytes 798728 | tf_op jit(solution)/shard_map/ppermute | solution.py:309
  11.3 2.1 %prepare.1 = (bf16[128,4096]{1,0:T(8,128)(2,1)S(1)}, bf16[128,4096]{1,0:T(8,128)(2,1)S(1)}, bf16[128,4096]{1,0:T(8,128)(2,1)S(1)}) custom-call(bf16[128,4096]{1,0:T(8,128)(2,1)} %bitcast.9, bf16[128,4096]{1,0:T(8,128)(2,1)} %bitcast.10, bf16[128,4096]{1,0:T(8,128)(2,1)} %bitcast.11), custom_call_target="tpu_custom_call" | custom-call | flops 524288 | bytes 6291456 | tf_op jit(solution)/shard_map/prepare/pallas_call | solution.py:313
  13.4 0.9 %collective-permute-done.2.refs_2_ = bf16[1040,128]{1,0:T(8,128)(2,1)S(1)} collective-permute-done((bf16[1040,128]{1,0:T(8,128)(2,1)S(1)}, bf16[1040,128]{1,0:T(8,128)(2,1)S(1)}, u32[]{:S(2)}, u32[]{:S(2)}) %collective-permute-start.2) | collective-permute-done | bytes 266272 | tf_op jit(solution)/shard_map/ppermute | solution.py:309
  14.3 4.5 %collective-permute-done.1.refs_1_ = bf16[1040,128]{1,0:T(8,128)(2,1)S(1)} collective-permute-done((bf16[1040,128]{1,0:T(8,128)(2,1)S(1)}, bf16[1040,128]{1,0:T(8,128)(2,1)S(1)}, u32[]{:S(2)}, u32[]{:S(2)}) %collective-permute-start.1) | collective-permute-done | bytes 266272 | tf_op jit(solution)/shard_map/ppermute | solution.py:309
  18.8 0.1 collective-permute-done.refs_0_
  18.9 11.4 %attend.1 = (bf16[128,4096]{1,0:T(8,128)(2,1)}, bf16[1024,128]{1,0:T(8,128)(2,1)S(1)}, bf16[1024,128]{1,0:T(8,128)(2,1)S(1)}, bf16[1024,128]{1,0:T(8,128)(2,1)S(...) custom-call(s32[1,8]{1,0:T(1,128)} %lengths_ref.1, f32[32]{0:T(128)} %slope_ref.1, f32[32]{0:T(128)} %gain_ref.1, ...), custom_call_target="tpu_custom_call" | custom-call | flops 2684354560 | bytes 5242880 | tf_op jit(solution)/shard_map/attend/pallas_call | solution.py:327
  30.3 1.3 %collective-permute-start.3 = (bf16[1024,128]{1,0:T(8,128)(2,1)S(1)}, bf16[1024,128]{1,0:T(8,128)(2,1)S(1)}, u32[]{:S(2)}, u32[]{:S(2)}) collective-permute-start(bf16[1024,128]{1,0:T(8,128)(2,1)S(1)} %get-tuple-element.21), channel_id=1, source_target_pairs={{1,0},{3,2},{5,4},{7,6},{9,8},{11,10},{13,12},{15,14},{17,16},{19,... | collective-permute-start | bytes 786440 | tf_op jit(solution)/shard_map/ppermute | solution.py:370
  31.6 1.3 %collective-permute-start.4 = (bf16[1024,128]{1,0:T(8,128)(2,1)S(1)}, bf16[1024,128]{1,0:T(8,128)(2,1)S(1)}, u32[]{:S(2)}, u32[]{:S(2)}) collective-permute-start(bf16[1024,128]{1,0:T(8,128)(2,1)S(1)} %get-tuple-element.22), channel_id=1, source_target_pairs={{2,0},{3,1},{6,4},{7,5},{10,8},{11,9},{14,12},{15,13},{18,16},{19,... | collective-permute-start | bytes 786440 | tf_op jit(solution)/shard_map/ppermute | solution.py:370
  32.9 1.3 %collective-permute-start.5 = (bf16[1024,128]{1,0:T(8,128)(2,1)S(1)}, bf16[1024,128]{1,0:T(8,128)(2,1)S(1)}, u32[]{:S(2)}, u32[]{:S(2)}) collective-permute-start(bf16[1024,128]{1,0:T(8,128)(2,1)S(1)} %get-tuple-element.23), channel_id=1, source_target_pairs={{2,1},{3,0},{6,5},{7,4},{10,9},{11,8},{14,13},{15,12},{18,17},{19,... | collective-permute-start | bytes 786440 | tf_op jit(solution)/shard_map/ppermute | solution.py:370
  34.2 2.7 %collective-permute-start.6 = (f32[8,128]{1,0:T(8,128)S(1)}, f32[8,128]{1,0:T(8,128)S(1)}, u32[]{:S(2)}, u32[]{:S(2)}) collective-permute-start(f32[8,128]{1,0:T(8,128)S(1)} %get-tuple-element.24), channel_id=1, source_target_pairs={{0,1},{1,0},{2,3},{3,2},{4,5},{5,4},{6,7},{7,6},{8,9},{9,8},{10,11... | collective-permute-start | bytes 12296 | tf_op jit(solution)/shard_map/ppermute | solution.py:374
  36.9 3.5 %collective-permute-done.6 = f32[8,128]{1,0:T(8,128)S(1)} collective-permute-done((f32[8,128]{1,0:T(8,128)S(1)}, f32[8,128]{1,0:T(8,128)S(1)}, u32[]{:S(2)}, u32[]{:S(2)}) %collective-permute-start.6) | collective-permute-done | bytes 4128 | tf_op jit(solution)/shard_map/ppermute | solution.py:374
  40.4 8.1 %collective-permute-start.7 = (f32[8,128]{1,0:T(8,128)S(1)}, f32[8,128]{1,0:T(8,128)S(1)}, u32[]{:S(2)}, u32[]{:S(2)}) collective-permute-start(f32[8,128]{1,0:T(8,128)S(1)} %add.15), channel_id=1, source_target_pairs={{0,2},{1,3},{2,0},{3,1},{4,6},{5,7},{6,4},{7,5},{8,10},{9,11},{10,... | collective-permute-start | bytes 12296 | tf_op jit(solution)/shard_map/ppermute | solution.py:374
  48.5 1.6 %collective-permute-done.7 = f32[8,128]{1,0:T(8,128)S(1)} collective-permute-done((f32[8,128]{1,0:T(8,128)S(1)}, f32[8,128]{1,0:T(8,128)S(1)}, u32[]{:S(2)}, u32[]{:S(2)}) %collective-permute-start.7) | collective-permute-done | bytes 4128 | tf_op jit(solution)/shard_map/ppermute | solution.py:374
  50.1 0.0 collective-permute-start.8
  50.1 1.2 %collective-permute-done.8 = f32[8,128]{1,0:T(8,128)S(1)} collective-permute-done((f32[8,128]{1,0:T(8,128)S(1)}, f32[8,128]{1,0:T(8,128)S(1)}, u32[]{:S(2)}, u32[]{:S(2)}) %collective-permute-start.8) | collective-permute-done | bytes 4128 | tf_op jit(solution)/shard_map/ppermute | solution.py:374
  51.3 1.6 %collective-permute-start.9 = (f32[8,128]{1,0:T(8,128)S(1)}, f32[8,128]{1,0:T(8,128)S(1)}, u32[]{:S(2)}, u32[]{:S(2)}) collective-permute-start(f32[8,128]{1,0:T(8,128)S(1)} %add.17), channel_id=1, source_target_pairs={{0,8},{4,12},{8,0},{12,4},{16,24},{20,28},{24,16},{28,20},{1,9},{5... | collective-permute-start | bytes 12296 | tf_op jit(solution)/shard_map/ppermute | solution.py:374
  52.8 2.0 %collective-permute-done.9 = f32[8,128]{1,0:T(8,128)S(1)} collective-permute-done((f32[8,128]{1,0:T(8,128)S(1)}, f32[8,128]{1,0:T(8,128)S(1)}, u32[]{:S(2)}, u32[]{:S(2)}) %collective-permute-start.9) | collective-permute-done | bytes 4128 | tf_op jit(solution)/shard_map/ppermute | solution.py:374
  54.9 2.6 %collective-permute-start.10 = (f32[8,128]{1,0:T(8,128)S(1)}, f32[8,128]{1,0:T(8,128)S(1)}, u32[]{:S(2)}, u32[]{:S(2)}) collective-permute-start(f32[8,128]{1,0:T(8,128)S(1)} %add.18), channel_id=1, source_target_pairs={{0,16},{4,20},{8,24},{12,28},{16,0},{20,4},{24,8},{28,12},{1,17},{... | collective-permute-start | bytes 12296 | tf_op jit(solution)/shard_map/ppermute | solution.py:374
  57.5 1.9 %collective-permute-done.10 = f32[8,128]{1,0:T(8,128)S(1)} collective-permute-done((f32[8,128]{1,0:T(8,128)S(1)}, f32[8,128]{1,0:T(8,128)S(1)}, u32[]{:S(2)}, u32[]{:S(2)}) %collective-permute-start.10) | collective-permute-done | bytes 4128 | tf_op jit(solution)/shard_map/ppermute | solution.py:374
  59.4 0.0 collective-permute-done.4.refs_2_
  59.4 1.0 %combine.1 = (bf16[128,512]{1,0:T(8,128)(2,1)}, bf16[128,512]{1,0:T(8,128)(2,1)}, f32[2,8]{1,0:T(2,128)}) custom-call(bf16[1024,128]{1,0:T(8,128)(2,1)S(1)} %get-tuple-element.20.refs_0_, bf16[1024,128]{1,0:T(8,128)(2,1)S(1)} %collective-permute-done.3.refs_1_, bf16[1024,128]{1,0:T(8,128)(2,1)S(1)} %collective-permute-done.4.refs_2_, ...), custom_call_target="tpu_custom_call" | custom-call | flops 1048576 | bytes 1310720 | tf_op jit(solution)/shard_map/combine/pallas_call | solution.py:377
  (7 shorter events, 0.0 us)
Async XLA Ops:
  1.7 12.6 %collective-permute-start.2 = (bf16[1040,128]{1,0:T(8,128)(2,1)S(1)}, bf16[1040,128]{1,0:T(8,128)(2,1)S(1)}, u32[]{:S(2)}, u32[]{:S(2)}) collective-permute-start(bf16[1040,128]{1,0:T(8,128)(2,1)S(1)} %pack.1), channel_id=1, source_target_pairs={{0,3},{1,2},{4,7},{5,6},{8,11},{9,10},{12,15},{13,14},{16,19},{17,... | collective-permute-start | bytes 798728 | tf_op jit(solution)/shard_map/ppermute | solution.py:309
  7.5 11.3 %collective-permute-start.1 = (bf16[1040,128]{1,0:T(8,128)(2,1)S(1)}, bf16[1040,128]{1,0:T(8,128)(2,1)S(1)}, u32[]{:S(2)}, u32[]{:S(2)}) collective-permute-start(bf16[1040,128]{1,0:T(8,128)(2,1)S(1)} %pack.1), channel_id=1, source_target_pairs={{0,2},{1,3},{4,6},{5,7},{8,10},{9,11},{12,14},{13,15},{16,18},{17,... | collective-permute-start | bytes 798728 | tf_op jit(solution)/shard_map/ppermute | solution.py:309
  8.8 10.1 %collective-permute-start = (bf16[1040,128]{1,0:T(8,128)(2,1)S(1)}, bf16[1040,128]{1,0:T(8,128)(2,1)S(1)}, u32[]{:S(2)}, u32[]{:S(2)}) collective-permute-start(bf16[1040,128]{1,0:T(8,128)(2,1)S(1)} %pack.1), channel_id=1, source_target_pairs={{0,1},{2,3},{4,5},{6,7},{8,9},{10,11},{12,13},{14,15},{16,17},{18,... | collective-permute-start | bytes 798728 | tf_op jit(solution)/shard_map/ppermute | solution.py:309
  30.3 29.1 %collective-permute-start.3 = (bf16[1024,128]{1,0:T(8,128)(2,1)S(1)}, bf16[1024,128]{1,0:T(8,128)(2,1)S(1)}, u32[]{:S(2)}, u32[]{:S(2)}) collective-permute-start(bf16[1024,128]{1,0:T(8,128)(2,1)S(1)} %get-tuple-element.21), channel_id=1, source_target_pairs={{1,0},{3,2},{5,4},{7,6},{9,8},{11,10},{13,12},{15,14},{17,16},{19,... | collective-permute-start | bytes 786440 | tf_op jit(solution)/shard_map/ppermute | solution.py:370
  31.6 27.8 %collective-permute-start.4 = (bf16[1024,128]{1,0:T(8,128)(2,1)S(1)}, bf16[1024,128]{1,0:T(8,128)(2,1)S(1)}, u32[]{:S(2)}, u32[]{:S(2)}) collective-permute-start(bf16[1024,128]{1,0:T(8,128)(2,1)S(1)} %get-tuple-element.22), channel_id=1, source_target_pairs={{2,0},{3,1},{6,4},{7,5},{10,8},{11,9},{14,12},{15,13},{18,16},{19,... | collective-permute-start | bytes 786440 | tf_op jit(solution)/shard_map/ppermute | solution.py:370
  32.9 26.5 %collective-permute-start.5 = (bf16[1024,128]{1,0:T(8,128)(2,1)S(1)}, bf16[1024,128]{1,0:T(8,128)(2,1)S(1)}, u32[]{:S(2)}, u32[]{:S(2)}) collective-permute-start(bf16[1024,128]{1,0:T(8,128)(2,1)S(1)} %get-tuple-element.23), channel_id=1, source_target_pairs={{2,1},{3,0},{6,5},{7,4},{10,9},{11,8},{14,13},{15,12},{18,17},{19,... | collective-permute-start | bytes 786440 | tf_op jit(solution)/shard_map/ppermute | solution.py:370
  34.2 6.2 %collective-permute-start.6 = (f32[8,128]{1,0:T(8,128)S(1)}, f32[8,128]{1,0:T(8,128)S(1)}, u32[]{:S(2)}, u32[]{:S(2)}) collective-permute-start(f32[8,128]{1,0:T(8,128)S(1)} %get-tuple-element.24), channel_id=1, source_target_pairs={{0,1},{1,0},{2,3},{3,2},{4,5},{5,4},{6,7},{7,6},{8,9},{9,8},{10,11... | collective-permute-start | bytes 12296 | tf_op jit(solution)/shard_map/ppermute | solution.py:374
  40.4 9.7 %collective-permute-start.7 = (f32[8,128]{1,0:T(8,128)S(1)}, f32[8,128]{1,0:T(8,128)S(1)}, u32[]{:S(2)}, u32[]{:S(2)}) collective-permute-start(f32[8,128]{1,0:T(8,128)S(1)} %add.15), channel_id=1, source_target_pairs={{0,2},{1,3},{2,0},{3,1},{4,6},{5,7},{6,4},{7,5},{8,10},{9,11},{10,... | collective-permute-start | bytes 12296 | tf_op jit(solution)/shard_map/ppermute | solution.py:374
  50.1 1.2 %collective-permute-start.8 = (f32[8,128]{1,0:T(8,128)S(1)}, f32[8,128]{1,0:T(8,128)S(1)}, u32[]{:S(2)}, u32[]{:S(2)}) collective-permute-start(f32[8,128]{1,0:T(8,128)S(1)} %add.16), channel_id=1, source_target_pairs={{0,4},{4,0},{8,12},{12,8},{16,20},{20,16},{24,28},{28,24},{1,5},{5... | collective-permute-start | bytes 12296 | tf_op jit(solution)/shard_map/ppermute | solution.py:374
  51.3 3.6 %collective-permute-start.9 = (f32[8,128]{1,0:T(8,128)S(1)}, f32[8,128]{1,0:T(8,128)S(1)}, u32[]{:S(2)}, u32[]{:S(2)}) collective-permute-start(f32[8,128]{1,0:T(8,128)S(1)} %add.17), channel_id=1, source_target_pairs={{0,8},{4,12},{8,0},{12,4},{16,24},{20,28},{24,16},{28,20},{1,9},{5... | collective-permute-start | bytes 12296 | tf_op jit(solution)/shard_map/ppermute | solution.py:374
  54.9 4.5 %collective-permute-start.10 = (f32[8,128]{1,0:T(8,128)S(1)}, f32[8,128]{1,0:T(8,128)S(1)}, u32[]{:S(2)}, u32[]{:S(2)}) collective-permute-start(f32[8,128]{1,0:T(8,128)S(1)} %add.18), channel_id=1, source_target_pairs={{0,16},{4,20},{8,24},{12,28},{16,0},{20,4},{24,8},{28,12},{1,17},{... | collective-permute-start | bytes 12296 | tf_op jit(solution)/shard_map/ppermute | solution.py:374

commit v11 on v8

--- a/solution.py
+++ b/solution.py
@@ -58,6 +58,7 @@
     blocks,
     heads_per_group,
     groups,
+    shifts,
     lengths_ref,
     slope_ref,
     gain_ref,
@@ -71,7 +72,7 @@
     *refs,
 ):
     tokens = query_ref.shape[0]
-    remote = refs[0 : blocks - 1]
+    remote = [refs[shifts.index(s)] for s in range(1, blocks)]
     query_grad_hbm = refs[blocks - 1]
     part_refs = refs[blocks : 2 * blocks]
     bias_hbm = refs[2 * blocks]
@@ -311,9 +312,10 @@
         compiler_params=params,
         name="pack",
     )(key_held, value_held, depth_held, end_held)
+    shifts = [s for s in range(1, blocks) if s != 2] + [2]
     arrived = [
         lax.ppermute(message, "ctx", [(i, i ^ s) for i in range(blocks) if i < i ^ s])
-        for s in range(1, blocks)
+        for s in shifts
     ]
 
     prepared = pl.pallas_call(
@@ -331,7 +333,7 @@
     bias_shape = (replicas, blocks, 8, WIDTH)
     matmul_flops = 2 * tokens * keys_seen * WIDTH * heads_all
     results = pl.pallas_call(
-        functools.partial(main_kernel, blocks, heads_per_group, groups),
+        functools.partial(main_kernel, blocks, heads_per_group, groups, shifts),
         out_shape=[jax.ShapeDtypeStruct((tokens, width_all), bf16)]
         + [jax.ShapeDtypeStruct((message_rows, WIDTH), bf16)] * blocks
         + [jax.ShapeDtypeStruct(bias_shape, f32)],
@@ -373,7 +375,7 @@
     query_grads = results[0]
     parts = list(results[1 : 1 + blocks])
     bias_parts = results[1 + blocks].reshape(replicas * blocks, 8, WIDTH)
-    for s in reversed(range(1, blocks)):
+    for s in [2] + [s for s in range(1, blocks) if s != 2]:
         back = [(i, i ^ s) for i in range(blocks) if i > i ^ s]
         parts[s] = lax.ppermute(parts[s], "ctx", back)
     bias_parts = lax.all_to_all(bias_parts, ("dp", "ctx"), split_axis=0, concat_axis=0, tiled=True)
@@ -390,7 +392,7 @@
             transcendentals=0,
         ),
         name="combine",
-    )(parts[0], *reversed(parts[1:]))
+    )(parts[0], parts[2], parts[1], *parts[3:])
     bias_grads = pl.pallas_call(
         bias_kernel,
         out_shape=jax.ShapeDtypeStruct((2, local_heads), f32),

time: 53.6 us -> 53 us (0.989)
  starting transfers between devices: 23.6 us -> 21.7 us
  waiting for transfers between devices: 13.1 us -> 14.3 us
    all_to_all x1, waiting for transfers between devices: 4.88 us -> 0.75 us  [body(): lax.all_to_all(bias_parts, ('dp', 'ctx'), split_axis=0, concat_axis=0, ti...]
    ppermute x3, waiting for transfers between devices: 2.72 us -> 6.84 us  [body(): parts[s] = lax.ppermute(parts[s], 'ctx', back)]
    all_to_all x1, starting transfers between devices: 10.1 us -> 8.17 us  [body(): lax.all_to_all(bias_parts, ('dp', 'ctx'), split_axis=0, concat_axis=0, ti...]
    ppermute x3, waiting for transfers between devices: 5.47 us -> 6.76 us  [body(): lax.ppermute(message, 'ctx', [(i, i ^ s) for i in range(blocks) if i < i...]
  transfers between devices with their start and end apart: 7 -> 7, of which waited for: 5 -> 4; matrix products, arithmetic and copies ran while one was open for 0% -> 0% of each run, Pallas kernels for 5% -> 5%
where the time goes in v11:
time: 53 us; the launch traced here: 52.7 us
  starting transfers between devices  21.7 us (41%)
  Pallas kernels  16 us (30%)
  waiting for transfers between devices  14.3 us (27%)
  between operations  0.72 us (1%)
    pallas_call x1, Pallas kernels, body(): pl.pallas_call(functools.partial(main_kernel, blocks, heads_per_group, gr...  11.5 us
    ppermute x3, starting transfers between devices, body(): lax.ppermute(message, 'ctx', [(i, i ^ s) for i in range(blocks) if i < i...  9.6 us
    all_to_all x1, starting transfers between devices, body(): lax.all_to_all(bias_parts, ('dp', 'ctx'), split_axis=0, concat_axis=0, ti...  8.17 us
    ppermute x3, waiting for transfers between devices, body(): parts[s] = lax.ppermute(parts[s], 'ctx', back)  6.84 us
    ppermute x3, waiting for transfers between devices, body(): lax.ppermute(message, 'ctx', [(i, i ^ s) for i in range(blocks) if i < i...  6.76 us
    ppermute x3, starting transfers between devices, body(): parts[s] = lax.ppermute(parts[s], 'ctx', back)  3.88 us
    pallas_call x1, Pallas kernels, body(): pl.pallas_call(prepare_kernel, out_shape=[jax.ShapeDtypeStruct((tokens, w...  2.1 us
  transfers between devices with their start and end apart: 7, of which 4 were waited for; matrix products, arithmetic and copies ran while one was open for 0% of the time, Pallas kernels for 5%

profile of v11, /device:TPU:0, one launch (start us, length us, event | category | flops | bytes accessed | tf_op | source)
XLA Modules:
  0.0 52.7 jit_solution(5777559356811519262)
XLA Ops:
  0.6 1.0 %pack.1 = bf16[1040,128]{1,0:T(8,128)(2,1)S(1)} custom-call(bf16[128,512]{1,0:T(8,128)(2,1)} %bitcast.14, bf16[128,512]{1,0:T(8,128)(2,1)} %bitcast.16, s32[1,128]{1,0:T(1,128)} %depth_ref.3, s32[1,128]{1,0:T(1,128)} %end_ref.3), custom_call_target="tpu_custom_call" | custom-call | tf_op jit(solution)/shard_map/pack/pallas_call | solution.py:307
  1.7 4.9 %collective-permute-start.2 = (bf16[1040,128]{1,0:T(8,128)(2,1)S(1)}, bf16[1040,128]{1,0:T(8,128)(2,1)S(1)}, u32[]{:S(2)}, u32[]{:S(2)}) collective-permute-start(bf16[1040,128]{1,0:T(8,128)(2,1)S(1)} %pack.1), channel_id=1, source_target_pairs={{0,2},{1,3},{4,6},{5,7},{8,10},{9,11},{12,14},{13,15},{16,18},{17,... | collective-permute-start | bytes 798728 | tf_op jit(solution)/shard_map/ppermute | solution.py:317
  6.6 2.2 %collective-permute-start.1 = (bf16[1040,128]{1,0:T(8,128)(2,1)S(1)}, bf16[1040,128]{1,0:T(8,128)(2,1)S(1)}, u32[]{:S(2)}, u32[]{:S(2)}) collective-permute-start(bf16[1040,128]{1,0:T(8,128)(2,1)S(1)} %pack.1), channel_id=1, source_target_pairs={{0,3},{1,2},{4,7},{5,6},{8,11},{9,10},{12,15},{13,14},{16,19},{17,... | collective-permute-start | bytes 798728 | tf_op jit(solution)/shard_map/ppermute | solution.py:317
  8.8 2.5 %collective-permute-start = (bf16[1040,128]{1,0:T(8,128)(2,1)S(1)}, bf16[1040,128]{1,0:T(8,128)(2,1)S(1)}, u32[]{:S(2)}, u32[]{:S(2)}) collective-permute-start(bf16[1040,128]{1,0:T(8,128)(2,1)S(1)} %pack.1), channel_id=1, source_target_pairs={{0,1},{2,3},{4,5},{6,7},{8,9},{10,11},{12,13},{14,15},{16,17},{18,... | collective-permute-start | bytes 798728 | tf_op jit(solution)/shard_map/ppermute | solution.py:317
  11.3 2.1 %prepare.1 = (bf16[128,4096]{1,0:T(8,128)(2,1)S(1)}, bf16[128,4096]{1,0:T(8,128)(2,1)S(1)}, bf16[128,4096]{1,0:T(8,128)(2,1)S(1)}) custom-call(bf16[128,4096]{1,0:T(8,128)(2,1)} %bitcast.10, bf16[128,4096]{1,0:T(8,128)(2,1)} %bitcast.11, bf16[128,4096]{1,0:T(8,128)(2,1)} %bitcast.12), custom_call_target="tpu_custom_call" | custom-call | flops 524288 | bytes 6291456 | tf_op jit(solution)/shard_map/prepare/pallas_call | solution.py:321
  13.4 4.5 %collective-permute-done.2.refs_2_ = bf16[1040,128]{1,0:T(8,128)(2,1)S(1)} collective-permute-done((bf16[1040,128]{1,0:T(8,128)(2,1)S(1)}, bf16[1040,128]{1,0:T(8,128)(2,1)S(1)}, u32[]{:S(2)}, u32[]{:S(2)}) %collective-permute-start.2) | collective-permute-done | bytes 266272 | tf_op jit(solution)/shard_map/ppermute | solution.py:317
  17.9 0.0 collective-permute-done.1.refs_1_
  17.9 2.3 %collective-permute-done.refs_0_ = bf16[1040,128]{1,0:T(8,128)(2,1)S(1)} collective-permute-done((bf16[1040,128]{1,0:T(8,128)(2,1)S(1)}, bf16[1040,128]{1,0:T(8,128)(2,1)S(1)}, u32[]{:S(2)}, u32[]{:S(2)}) %collective-permute-start) | collective-permute-done | bytes 266272 | tf_op jit(solution)/shard_map/ppermute | solution.py:317
  20.2 11.5 %attend.1 = (bf16[128,4096]{1,0:T(8,128)(2,1)}, bf16[1024,128]{1,0:T(8,128)(2,1)S(1)}, bf16[1024,128]{1,0:T(8,128)(2,1)S(1)}, bf16[1024,128]{1,0:T(8,128)(2,1)S(...) custom-call(s32[1,8]{1,0:T(1,128)} %lengths_ref.1, f32[32]{0:T(128)} %slope_ref.1, f32[32]{0:T(128)} %gain_ref.1, ...), custom_call_target="tpu_custom_call" | custom-call | flops 2684354560 | bytes 5242880 | tf_op jit(solution)/shard_map/attend/pallas_call | solution.py:335
  31.6 1.3 %collective-permute-start.3 = (bf16[1024,128]{1,0:T(8,128)(2,1)S(1)}, bf16[1024,128]{1,0:T(8,128)(2,1)S(1)}, u32[]{:S(2)}, u32[]{:S(2)}) collective-permute-start(bf16[1024,128]{1,0:T(8,128)(2,1)S(1)} %get-tuple-element.20), channel_id=1, source_target_pairs={{2,0},{3,1},{6,4},{7,5},{10,8},{11,9},{14,12},{15,13},{18,16},{19,... | collective-permute-start | bytes 786440 | tf_op jit(solution)/shard_map/ppermute | solution.py:380
  32.9 1.3 %collective-permute-start.4 = (bf16[1024,128]{1,0:T(8,128)(2,1)S(1)}, bf16[1024,128]{1,0:T(8,128)(2,1)S(1)}, u32[]{:S(2)}, u32[]{:S(2)}) collective-permute-start(bf16[1024,128]{1,0:T(8,128)(2,1)S(1)} %get-tuple-element.21), channel_id=1, source_target_pairs={{1,0},{3,2},{5,4},{7,6},{9,8},{11,10},{13,12},{15,14},{17,16},{19,... | collective-permute-start | bytes 786440 | tf_op jit(solution)/shard_map/ppermute | solution.py:380
  34.2 1.3 %collective-permute-start.5 = (bf16[1024,128]{1,0:T(8,128)(2,1)S(1)}, bf16[1024,128]{1,0:T(8,128)(2,1)S(1)}, u32[]{:S(2)}, u32[]{:S(2)}) collective-permute-start(bf16[1024,128]{1,0:T(8,128)(2,1)S(1)} %get-tuple-element.22), channel_id=1, source_target_pairs={{2,1},{3,0},{6,5},{7,4},{10,9},{11,8},{14,13},{15,12},{18,17},{19,... | collective-permute-start | bytes 786440 | tf_op jit(solution)/shard_map/ppermute | solution.py:380
  35.5 8.2 %all-to-all-start = ((f32[32,8,128]{2,1,0:T(8,128)}), f32[32,8,128]{2,1,0:T(8,128)S(1)}, u32[]{:S(2)}, u32[]{:S(2)}) async-start(f32[32,8,128]{2,1,0:T(8,128)} %bitcast.8), calls=%async_computation | async-start | bytes 262144 | tf_op jit(solution)/shard_map/all_to_all | solution.py:381
  43.7 0.0 collective-permute-done.3.refs_1_
  43.7 0.0 collective-permute-done.4.refs_2_
  43.7 6.8 %collective-permute-done.5.refs_3_ = bf16[1024,128]{1,0:T(8,128)(2,1)S(1)} collective-permute-done((bf16[1024,128]{1,0:T(8,128)(2,1)S(1)}, bf16[1024,128]{1,0:T(8,128)(2,1)S(1)}, u32[]{:S(2)}, u32[]{:S(2)}) %collective-permute-start.5) | collective-permute-done | bytes 262176 | tf_op jit(solution)/shard_map/ppermute | solution.py:380
  50.6 0.8 %combine.1 = (bf16[128,512]{1,0:T(8,128)(2,1)}, bf16[128,512]{1,0:T(8,128)(2,1)}) custom-call(bf16[1024,128]{1,0:T(8,128)(2,1)S(1)} %get-tuple-element.19.refs_0_, bf16[1024,128]{1,0:T(8,128)(2,1)S(1)} %collective-permute-done.3.refs_1_, bf16[1024,128]{1,0:T(8,128)(2,1)S(1)} %collective-permute-done.4.refs_2_, ...), custom_call_target="tpu_custom_call" | custom-call | flops 1048576 | bytes 1310720 | tf_op jit(solution)/shard_map/combine/pallas_call | solution.py:383
  51.4 0.8 %all-to-all-done.parts_ref = f32[32,8,128]{2,1,0:T(8,128)S(1)} async-done(((f32[32,8,128]{2,1,0:T(8,128)}), f32[32,8,128]{2,1,0:T(8,128)S(1)}, u32[]{:S(2)}, u32[]{:S(2)}) %all-to-all-start) | async-done | bytes 131104 | tf_op jit(solution)/shard_map/all_to_all | solution.py:381
  52.1 0.6 %bias.1 = f32[2,8]{1,0:T(2,128)} custom-call(f32[32,8,128]{2,1,0:T(8,128)S(1)} %all-to-all-done.parts_ref, bf16[128,512]{1,0:T(8,128)(2,1)} %get-tuple-element.23._), custom_call_target="tpu_custom_call" | custom-call | tf_op jit(solution)/shard_map/bias/pallas_call | solution.py:396
Async XLA Ops:
  1.7 16.2 %collective-permute-start.2 = (bf16[1040,128]{1,0:T(8,128)(2,1)S(1)}, bf16[1040,128]{1,0:T(8,128)(2,1)S(1)}, u32[]{:S(2)}, u32[]{:S(2)}) collective-permute-start(bf16[1040,128]{1,0:T(8,128)(2,1)S(1)} %pack.1), channel_id=1, source_target_pairs={{0,2},{1,3},{4,6},{5,7},{8,10},{9,11},{12,14},{13,15},{16,18},{17,... | collective-permute-start | bytes 798728 | tf_op jit(solution)/shard_map/ppermute | solution.py:317
  6.6 11.3 %collective-permute-start.1 = (bf16[1040,128]{1,0:T(8,128)(2,1)S(1)}, bf16[1040,128]{1,0:T(8,128)(2,1)S(1)}, u32[]{:S(2)}, u32[]{:S(2)}) collective-permute-start(bf16[1040,128]{1,0:T(8,128)(2,1)S(1)} %pack.1), channel_id=1, source_target_pairs={{0,3},{1,2},{4,7},{5,6},{8,11},{9,10},{12,15},{13,14},{16,19},{17,... | collective-permute-start | bytes 798728 | tf_op jit(solution)/shard_map/ppermute | solution.py:317
  8.8 11.4 %collective-permute-start = (bf16[1040,128]{1,0:T(8,128)(2,1)S(1)}, bf16[1040,128]{1,0:T(8,128)(2,1)S(1)}, u32[]{:S(2)}, u32[]{:S(2)}) collective-permute-start(bf16[1040,128]{1,0:T(8,128)(2,1)S(1)} %pack.1), channel_id=1, source_target_pairs={{0,1},{2,3},{4,5},{6,7},{8,9},{10,11},{12,13},{14,15},{16,17},{18,... | collective-permute-start | bytes 798728 | tf_op jit(solution)/shard_map/ppermute | solution.py:317
  31.6 12.1 %collective-permute-start.3 = (bf16[1024,128]{1,0:T(8,128)(2,1)S(1)}, bf16[1024,128]{1,0:T(8,128)(2,1)S(1)}, u32[]{:S(2)}, u32[]{:S(2)}) collective-permute-start(bf16[1024,128]{1,0:T(8,128)(2,1)S(1)} %get-tuple-element.20), channel_id=1, source_target_pairs={{2,0},{3,1},{6,4},{7,5},{10,8},{11,9},{14,12},{15,13},{18,16},{19,... | collective-permute-start | bytes 786440 | tf_op jit(solution)/shard_map/ppermute | solution.py:380
  32.9 10.8 %collective-permute-start.4 = (bf16[1024,128]{1,0:T(8,128)(2,1)S(1)}, bf16[1024,128]{1,0:T(8,128)(2,1)S(1)}, u32[]{:S(2)}, u32[]{:S(2)}) collective-permute-start(bf16[1024,128]{1,0:T(8,128)(2,1)S(1)} %get-tuple-element.21), channel_id=1, source_target_pairs={{1,0},{3,2},{5,4},{7,6},{9,8},{11,10},{13,12},{15,14},{17,16},{19,... | collective-permute-start | bytes 786440 | tf_op jit(solution)/shard_map/ppermute | solution.py:380
  34.2 16.3 %collective-permute-start.5 = (bf16[1024,128]{1,0:T(8,128)(2,1)S(1)}, bf16[1024,128]{1,0:T(8,128)(2,1)S(1)}, u32[]{:S(2)}, u32[]{:S(2)}) collective-permute-start(bf16[1024,128]{1,0:T(8,128)(2,1)S(1)} %get-tuple-element.22), channel_id=1, source_target_pairs={{2,1},{3,0},{6,5},{7,4},{10,9},{11,8},{14,13},{15,12},{18,17},{19,... | collective-permute-start | bytes 786440 | tf_op jit(solution)/shard_map/ppermute | solution.py:380
  35.5 16.6 %all-to-all-start = ((f32[32,8,128]{2,1,0:T(8,128)}), f32[32,8,128]{2,1,0:T(8,128)S(1)}, u32[]{:S(2)}, u32[]{:S(2)}) async-start(f32[32,8,128]{2,1,0:T(8,128)} %bitcast.8), calls=%async_computation | async-start | bytes 262144 | tf_op jit(solution)/shard_map/all_to_all | solution.py:381

commit v12 on v11

--- a/solution.py
+++ b/solution.py
@@ -225,11 +225,11 @@
             centred = products(value_ext, grad_ext)
             for half in range(2):
                 differentiate(group, pair, centred, scales[half], half)
+        query_part(keys_across, group, pairs - 1)
+        store(group).start()
         key_whole = key_acc[...] + key_part(group, half_heads, half_heads)
         put_part(group, 0, key_whole * factor)
         put_part(group, 1, value_acc[...] + value_part(group, half_heads, half_heads))
-        query_part(keys_across, group, pairs - 1)
-        store(group).start()
 
     slope_sum = jnp.sum(slope_rows[...], axis=1, keepdims=True)
     gain_sum = jnp.sum(gain_rows[...], axis=1, keepdims=True)
@@ -312,7 +312,7 @@
         compiler_params=params,
         name="pack",
     )(key_held, value_held, depth_held, end_held)
-    shifts = [s for s in range(1, blocks) if s != 2] + [2]
+    shifts = list(range(1, blocks))
     arrived = [
         lax.ppermute(message, "ctx", [(i, i ^ s) for i in range(blocks) if i < i ^ s])
         for s in shifts

time: 53 us -> 52.6 us (level)
  waiting for transfers between devices: 14.3 us -> 13.5 us
    ppermute x3, waiting for transfers between devices: 6.76 us -> 5.47 us  [body(): lax.ppermute(message, 'ctx', [(i, i ^ s) for i in range(blocks) if i < i...]
    ppermute x3, waiting for transfers between devices: 6.84 us -> 8.04 us  [body(): parts[s] = lax.ppermute(parts[s], 'ctx', back)]
    all_to_all x1, waiting for transfers between devices: 0.75 us -> 0.01 us  [body(): lax.all_to_all(bias_parts, ('dp', 'ctx'), split_axis=0, concat_axis=0, ti...]
  transfers between devices with their start and end apart: 7 -> 7, of which waited for: 4 -> 4; matrix products, arithmetic and copies ran while one was open for 0% -> 0% of each run, Pallas kernels for 5% -> 6%
where the time goes in v12:
time: 52.6 us; the launch traced here: 52.3 us
  starting transfers between devices  21.6 us (41%)
  Pallas kernels  16.5 us (31%)
  waiting for transfers between devices  13.5 us (26%)
  between operations  0.72 us (1%)
    pallas_call x1, Pallas kernels, body(): pl.pallas_call(functools.partial(main_kernel, blocks, heads_per_group, gr...  11.9 us
    ppermute x3, starting transfers between devices, body(): lax.ppermute(message, 'ctx', [(i, i ^ s) for i in range(blocks) if i < i...  9.59 us
    all_to_all x1, starting transfers between devices, body(): lax.all_to_all(bias_parts, ('dp', 'ctx'), split_axis=0, concat_axis=0, ti...  8.15 us
    ppermute x3, waiting for transfers between devices, body(): parts[s] = lax.ppermute(parts[s], 'ctx', back)  8.04 us
    ppermute x3, waiting for transfers between devices, body(): lax.ppermute(message, 'ctx', [(i, i ^ s) for i in range(blocks) if i < i...  5.47 us
    ppermute x3, starting transfers between devices, body(): parts[s] = lax.ppermute(parts[s], 'ctx', back)  3.88 us
    pallas_call x1, Pallas kernels, body(): pl.pallas_call(prepare_kernel, out_shape=[jax.ShapeDtypeStruct((tokens, w...  2.1 us
  transfers between devices with their start and end apart: 7, of which 4 were waited for; matrix products, arithmetic and copies ran while one was open for 0% of the time, Pallas kernels for 6%

profile of v12, /device:TPU:0, one launch (start us, length us, event | category | flops | bytes accessed | tf_op | source)
XLA Modules:
  0.0 52.3 jit_solution(14588706941089758658)
XLA Ops:
  0.6 1.0 %pack.1 = bf16[1040,128]{1,0:T(8,128)(2,1)S(1)} custom-call(bf16[128,512]{1,0:T(8,128)(2,1)} %bitcast.14, bf16[128,512]{1,0:T(8,128)(2,1)} %bitcast.16, s32[1,128]{1,0:T(1,128)} %depth_ref.3, s32[1,128]{1,0:T(1,128)} %end_ref.3), custom_call_target="tpu_custom_call" | custom-call | tf_op jit(solution)/shard_map/pack/pallas_call | solution.py:307
  1.7 5.8 %collective-permute-start.2 = (bf16[1040,128]{1,0:T(8,128)(2,1)S(1)}, bf16[1040,128]{1,0:T(8,128)(2,1)S(1)}, u32[]{:S(2)}, u32[]{:S(2)}) collective-permute-start(bf16[1040,128]{1,0:T(8,128)(2,1)S(1)} %pack.1), channel_id=1, source_target_pairs={{0,3},{1,2},{4,7},{5,6},{8,11},{9,10},{12,15},{13,14},{16,19},{17,... | collective-permute-start | bytes 798728 | tf_op jit(solution)/shard_map/ppermute | solution.py:317
  7.5 1.3 %collective-permute-start.1 = (bf16[1040,128]{1,0:T(8,128)(2,1)S(1)}, bf16[1040,128]{1,0:T(8,128)(2,1)S(1)}, u32[]{:S(2)}, u32[]{:S(2)}) collective-permute-start(bf16[1040,128]{1,0:T(8,128)(2,1)S(1)} %pack.1), channel_id=1, source_target_pairs={{0,2},{1,3},{4,6},{5,7},{8,10},{9,11},{12,14},{13,15},{16,18},{17,... | collective-permute-start | bytes 798728 | tf_op jit(solution)/shard_map/ppermute | solution.py:317
  8.8 2.5 %collective-permute-start = (bf16[1040,128]{1,0:T(8,128)(2,1)S(1)}, bf16[1040,128]{1,0:T(8,128)(2,1)S(1)}, u32[]{:S(2)}, u32[]{:S(2)}) collective-permute-start(bf16[1040,128]{1,0:T(8,128)(2,1)S(1)} %pack.1), channel_id=1, source_target_pairs={{0,1},{2,3},{4,5},{6,7},{8,9},{10,11},{12,13},{14,15},{16,17},{18,... | collective-permute-start | bytes 798728 | tf_op jit(solution)/shard_map/ppermute | solution.py:317
  11.3 2.1 %prepare.1 = (bf16[128,4096]{1,0:T(8,128)(2,1)S(1)}, bf16[128,4096]{1,0:T(8,128)(2,1)S(1)}, bf16[128,4096]{1,0:T(8,128)(2,1)S(1)}) custom-call(bf16[128,4096]{1,0:T(8,128)(2,1)} %bitcast.10, bf16[128,4096]{1,0:T(8,128)(2,1)} %bitcast.11, bf16[128,4096]{1,0:T(8,128)(2,1)} %bitcast.12), custom_call_target="tpu_custom_call" | custom-call | flops 524288 | bytes 6291456 | tf_op jit(solution)/shard_map/prepare/pallas_call | solution.py:321
  13.4 0.9 %collective-permute-done.2.refs_2_ = bf16[1040,128]{1,0:T(8,128)(2,1)S(1)} collective-permute-done((bf16[1040,128]{1,0:T(8,128)(2,1)S(1)}, bf16[1040,128]{1,0:T(8,128)(2,1)S(1)}, u32[]{:S(2)}, u32[]{:S(2)}) %collective-permute-start.2) | collective-permute-done | bytes 266272 | tf_op jit(solution)/shard_map/ppermute | solution.py:317
  14.3 4.5 %collective-permute-done.1.refs_1_ = bf16[1040,128]{1,0:T(8,128)(2,1)S(1)} collective-permute-done((bf16[1040,128]{1,0:T(8,128)(2,1)S(1)}, bf16[1040,128]{1,0:T(8,128)(2,1)S(1)}, u32[]{:S(2)}, u32[]{:S(2)}) %collective-permute-start.1) | collective-permute-done | bytes 266272 | tf_op jit(solution)/shard_map/ppermute | solution.py:317
  18.8 0.1 collective-permute-done.refs_0_
  18.9 11.9 %attend.1 = (bf16[128,4096]{1,0:T(8,128)(2,1)}, bf16[1024,128]{1,0:T(8,128)(2,1)S(1)}, bf16[1024,128]{1,0:T(8,128)(2,1)S(1)}, bf16[1024,128]{1,0:T(8,128)(2,1)S(...) custom-call(s32[1,8]{1,0:T(1,128)} %lengths_ref.1, f32[32]{0:T(128)} %slope_ref.1, f32[32]{0:T(128)} %gain_ref.1, ...), custom_call_target="tpu_custom_call" | custom-call | flops 2684354560 | bytes 5242880 | tf_op jit(solution)/shard_map/attend/pallas_call | solution.py:335
  30.8 1.3 %collective-permute-start.3 = (bf16[1024,128]{1,0:T(8,128)(2,1)S(1)}, bf16[1024,128]{1,0:T(8,128)(2,1)S(1)}, u32[]{:S(2)}, u32[]{:S(2)}) collective-permute-start(bf16[1024,128]{1,0:T(8,128)(2,1)S(1)} %get-tuple-element.20), channel_id=1, source_target_pairs={{2,0},{3,1},{6,4},{7,5},{10,8},{11,9},{14,12},{15,13},{18,16},{19,... | collective-permute-start | bytes 786440 | tf_op jit(solution)/shard_map/ppermute | solution.py:380
  32.1 1.3 %collective-permute-start.4 = (bf16[1024,128]{1,0:T(8,128)(2,1)S(1)}, bf16[1024,128]{1,0:T(8,128)(2,1)S(1)}, u32[]{:S(2)}, u32[]{:S(2)}) collective-permute-start(bf16[1024,128]{1,0:T(8,128)(2,1)S(1)} %get-tuple-element.21), channel_id=1, source_target_pairs={{1,0},{3,2},{5,4},{7,6},{9,8},{11,10},{13,12},{15,14},{17,16},{19,... | collective-permute-start | bytes 786440 | tf_op jit(solution)/shard_map/ppermute | solution.py:380
  33.4 1.3 %collective-permute-start.5 = (bf16[1024,128]{1,0:T(8,128)(2,1)S(1)}, bf16[1024,128]{1,0:T(8,128)(2,1)S(1)}, u32[]{:S(2)}, u32[]{:S(2)}) collective-permute-start(bf16[1024,128]{1,0:T(8,128)(2,1)S(1)} %get-tuple-element.22), channel_id=1, source_target_pairs={{2,1},{3,0},{6,5},{7,4},{10,9},{11,8},{14,13},{15,12},{18,17},{19,... | collective-permute-start | bytes 786440 | tf_op jit(solution)/shard_map/ppermute | solution.py:380
  34.7 8.2 %all-to-all-start = ((f32[32,8,128]{2,1,0:T(8,128)}), f32[32,8,128]{2,1,0:T(8,128)S(1)}, u32[]{:S(2)}, u32[]{:S(2)}) async-start(f32[32,8,128]{2,1,0:T(8,128)} %bitcast.8), calls=%async_computation | async-start | bytes 262144 | tf_op jit(solution)/shard_map/all_to_all | solution.py:381
  42.8 0.0 collective-permute-done.3.refs_1_
  42.9 0.0 collective-permute-done.4.refs_2_
  42.9 8.0 %collective-permute-done.5.refs_3_ = bf16[1024,128]{1,0:T(8,128)(2,1)S(1)} collective-permute-done((bf16[1024,128]{1,0:T(8,128)(2,1)S(1)}, bf16[1024,128]{1,0:T(8,128)(2,1)S(1)}, u32[]{:S(2)}, u32[]{:S(2)}) %collective-permute-start.5) | collective-permute-done | bytes 262176 | tf_op jit(solution)/shard_map/ppermute | solution.py:380
  50.9 0.8 %combine.1 = (bf16[128,512]{1,0:T(8,128)(2,1)}, bf16[128,512]{1,0:T(8,128)(2,1)}) custom-call(bf16[1024,128]{1,0:T(8,128)(2,1)S(1)} %get-tuple-element.19.refs_0_, bf16[1024,128]{1,0:T(8,128)(2,1)S(1)} %collective-permute-done.3.refs_1_, bf16[1024,128]{1,0:T(8,128)(2,1)S(1)} %collective-permute-done.4.refs_2_, ...), custom_call_target="tpu_custom_call" | custom-call | flops 1048576 | bytes 1310720 | tf_op jit(solution)/shard_map/combine/pallas_call | solution.py:383
  51.7 0.0 all-to-all-done.parts_ref
  51.7 0.6 %bias.1 = f32[2,8]{1,0:T(2,128)} custom-call(f32[32,8,128]{2,1,0:T(8,128)S(1)} %all-to-all-done.parts_ref, bf16[128,512]{1,0:T(8,128)(2,1)} %get-tuple-element.23._), custom_call_target="tpu_custom_call" | custom-call | tf_op jit(solution)/shard_map/bias/pallas_call | solution.py:396
Async XLA Ops:
  1.7 12.6 %collective-permute-start.2 = (bf16[1040,128]{1,0:T(8,128)(2,1)S(1)}, bf16[1040,128]{1,0:T(8,128)(2,1)S(1)}, u32[]{:S(2)}, u32[]{:S(2)}) collective-permute-start(bf16[1040,128]{1,0:T(8,128)(2,1)S(1)} %pack.1), channel_id=1, source_target_pairs={{0,3},{1,2},{4,7},{5,6},{8,11},{9,10},{12,15},{13,14},{16,19},{17,... | collective-permute-start | bytes 798728 | tf_op jit(solution)/shard_map/ppermute | solution.py:317
  7.5 11.3 %collective-permute-start.1 = (bf16[1040,128]{1,0:T(8,128)(2,1)S(1)}, bf16[1040,128]{1,0:T(8,128)(2,1)S(1)}, u32[]{:S(2)}, u32[]{:S(2)}) collective-permute-start(bf16[1040,128]{1,0:T(8,128)(2,1)S(1)} %pack.1), channel_id=1, source_target_pairs={{0,2},{1,3},{4,6},{5,7},{8,10},{9,11},{12,14},{13,15},{16,18},{17,... | collective-permute-start | bytes 798728 | tf_op jit(solution)/shard_map/ppermute | solution.py:317
  8.8 10.1 %collective-permute-start = (bf16[1040,128]{1,0:T(8,128)(2,1)S(1)}, bf16[1040,128]{1,0:T(8,128)(2,1)S(1)}, u32[]{:S(2)}, u32[]{:S(2)}) collective-permute-start(bf16[1040,128]{1,0:T(8,128)(2,1)S(1)} %pack.1), channel_id=1, source_target_pairs={{0,1},{2,3},{4,5},{6,7},{8,9},{10,11},{12,13},{14,15},{16,17},{18,... | collective-permute-start | bytes 798728 | tf_op jit(solution)/shard_map/ppermute | solution.py:317
  30.8 12.1 %collective-permute-start.3 = (bf16[1024,128]{1,0:T(8,128)(2,1)S(1)}, bf16[1024,128]{1,0:T(8,128)(2,1)S(1)}, u32[]{:S(2)}, u32[]{:S(2)}) collective-permute-start(bf16[1024,128]{1,0:T(8,128)(2,1)S(1)} %get-tuple-element.20), channel_id=1, source_target_pairs={{2,0},{3,1},{6,4},{7,5},{10,8},{11,9},{14,12},{15,13},{18,16},{19,... | collective-permute-start | bytes 786440 | tf_op jit(solution)/shard_map/ppermute | solution.py:380
  32.1 10.8 %collective-permute-start.4 = (bf16[1024,128]{1,0:T(8,128)(2,1)S(1)}, bf16[1024,128]{1,0:T(8,128)(2,1)S(1)}, u32[]{:S(2)}, u32[]{:S(2)}) collective-permute-start(bf16[1024,128]{1,0:T(8,128)(2,1)S(1)} %get-tuple-element.21), channel_id=1, source_target_pairs={{1,0},{3,2},{5,4},{7,6},{9,8},{11,10},{13,12},{15,14},{17,16},{19,... | collective-permute-start | bytes 786440 | tf_op jit(solution)/shard_map/ppermute | solution.py:380
  33.4 17.5 %collective-permute-start.5 = (bf16[1024,128]{1,0:T(8,128)(2,1)S(1)}, bf16[1024,128]{1,0:T(8,128)(2,1)S(1)}, u32[]{:S(2)}, u32[]{:S(2)}) collective-permute-start(bf16[1024,128]{1,0:T(8,128)(2,1)S(1)} %get-tuple-element.22), channel_id=1, source_target_pairs={{2,1},{3,0},{6,5},{7,4},{10,9},{11,8},{14,13},{15,12},{18,17},{19,... | collective-permute-start | bytes 786440 | tf_op jit(solution)/shard_map/ppermute | solution.py:380
  34.7 17.0 %all-to-all-start = ((f32[32,8,128]{2,1,0:T(8,128)}), f32[32,8,128]{2,1,0:T(8,128)S(1)}, u32[]{:S(2)}, u32[]{:S(2)}) async-start(f32[32,8,128]{2,1,0:T(8,128)} %bitcast.8), calls=%async_computation | async-start | bytes 262144 | tf_op jit(solution)/shard_map/all_to_all | solution.py:381

commit v13 on v11

--- a/solution.py
+++ b/solution.py
@@ -31,27 +31,128 @@
     return jnp.transpose(jnp.broadcast_to(row, (size, size)))
 
 
-def pack_kernel(key_ref, value_ref, depth_ref, end_ref, message_ref):
-    tokens = key_ref.shape[0]
-    groups = key_ref.shape[1] // WIDTH
-    for kind, ref in enumerate((key_ref, value_ref)):
-        for group in range(groups):
-            at = (kind * groups + group) * tokens
-            message_ref[at : at + tokens, :] = ref[:, group * WIDTH : (group + 1) * WIDTH]
-    depth = depth_ref[...]
-    end = end_ref[...]
-    end_high = end // END_UNIT
-    end_low = end - end_high * END_UNIT
-    row = lax.broadcasted_iota(jnp.int32, (META_ROWS, tokens), 0)
-    meta = jnp.where(row == 0, depth, jnp.where(row == 1, end_high, end_low))
-    meta = meta.astype(jnp.float32).astype(jnp.bfloat16)
-    message_ref[2 * groups * tokens : 2 * groups * tokens + META_ROWS, :] = meta
-
-
-def prepare_kernel(query_in, output_in, grad_in, query_out, grad_out, product_out):
+def pack_kernel(blocks, key_hbm, value_hbm, depth_hbm, end_hbm, message_ref, depth_ref, end_ref, sems):
+    tokens, columns = key_hbm.shape
+    groups = columns // WIDTH
+
+    @pl.when(lax.axis_index("ctx") != blocks - 1)
+    def _():
+        copies = [
+            pltpu.make_async_copy(depth_hbm, depth_ref, sems.at[0]),
+            pltpu.make_async_copy(end_hbm, end_ref, sems.at[1]),
+        ]
+        for kind, hbm in enumerate((key_hbm, value_hbm)):
+            for group in range(groups):
+                index = kind * groups + group
+                copies.append(
+                    pltpu.make_async_copy(
+                        hbm.at[:, group * WIDTH : (group + 1) * WIDTH],
+                        message_ref.at[index * tokens : (index + 1) * tokens, :],
+                        sems.at[2 + index],
+                    )
+                )
+        for copy in copies:
+            copy.start()
+        copies[0].wait()
+        copies[1].wait()
+        end = end_ref[...]
+        end_high = end // END_UNIT
+        end_low = end - end_high * END_UNIT
+        row = lax.broadcasted_iota(jnp.int32, (META_ROWS, tokens), 0)
+        meta = jnp.where(row == 0, depth_ref[...], jnp.where(row == 1, end_high, end_low))
+        meta = meta.astype(jnp.float32).astype(jnp.bfloat16)
+        message_ref[2 * groups * tokens : 2 * groups * tokens + META_ROWS, :] = meta
+        for copy in copies[2:]:
+            copy.wait()
+
+
+def table(lengths_ref, depth_ref, s, key_depth, key_end):
+    shape = key_depth.shape
+    here = lax.axis_index("ctx")
+    query_pos = here * shape[1] + lax.broadcasted_iota(jnp.int32, shape, 1)
+    key_pos = (here ^ s) * shape[0] + lax.broadcasted_iota(jnp.int32, shape, 0)
+    start = jnp.zeros(shape, jnp.int32)
+    bound = jnp.int32(0)
+    for index in range(lengths_ref.shape[1]):
+        bound = bound + lengths_ref[0, index]
+        start = jnp.where(query_pos >= bound, bound, start)
+    inside = query_pos.astype(jnp.float32) < key_end
+    allowed = (key_pos <= query_pos) & (key_pos >= start)
+    distance = jnp.abs(depth_ref[...].astype(jnp.float32) - key_depth)
+    return distance, jnp.where(allowed, jnp.where(inside, 1.0, 0.0), MASKED)
+
+
+def prepare_kernel(
+    heads_per_group,
+    groups,
+    lengths_ref,
+    slope_ref,
+    gain_ref,
+    depth_ref,
+    end_ref,
+    query_in,
+    output_in,
+    grad_in,
+    key_ref,
+    value_ref,
+    query_out,
+    grad_out,
+    product_out,
+    distance_ref,
+    ancestor_ref,
+    weight_ref,
+    dscore_ref,
+    rows_ref,
+):
+    tokens = query_in.shape[0]
+    factor = WIDTH**-0.5
     query_out[...] = query_in[...]
     grad_out[...] = grad_in[...]
     product_out[...] = grad_in[...] * output_in[...]
+    distance, ancestor = table(
+        lengths_ref,
+        depth_ref,
+        0,
+        as_column(depth_ref[...].astype(jnp.float32)),
+        as_column(end_ref[...].astype(jnp.float32)),
+    )
+    distance_ref[...] = distance
+    ancestor_ref[...] = ancestor
+
+    @pl.loop(0, groups)
+    def _(group):
+        own = pl.ds(pl.multiple_of(group * WIDTH, WIDTH), WIDTH)
+        key, value = key_ref[:, own], value_ref[:, own]
+        value_ext = jnp.concatenate([value, jnp.full(value.shape, -1.0, jnp.bfloat16)], axis=1)
+        for pair in range(heads_per_group // 2):
+            first = group * heads_per_group + 2 * pair
+            both = pl.ds(pl.multiple_of(first * WIDTH, 2 * WIDTH), 2 * WIDTH)
+
+            def stack(array):
+                return jnp.concatenate([array[:, 0:WIDTH], array[:, WIDTH:]], axis=0)
+
+            grad = grad_in[:, both]
+            grad_ext = jnp.concatenate([stack(grad), stack(grad * output_in[:, both])], axis=1)
+            raw = dot_nt(key, stack(query_in[:, both]))
+            centred = dot_nt(value_ext, grad_ext)
+            for half in range(2):
+                head = first + half
+                gain = gain_ref[head] * LOG2E
+                slope = slope_ref[head] * LOG2E
+                lanes = slice(half * tokens, (half + 1) * tokens)
+                distance, ancestor = distance_ref[...], ancestor_ref[...]
+                score = raw[:, lanes] * (factor * LOG2E) + (gain * ancestor - slope * distance)
+                top = jnp.max(score, axis=0, keepdims=True)
+                weight = jnp.exp2(score - top)
+                dscore = weight * centred[:, lanes]
+                to = pl.ds(pl.multiple_of(head * tokens, tokens), tokens)
+                weight_ref[:, to] = weight
+                dscore_ref[:, to] = dscore
+                at = pl.ds(head, 1)
+                rows_ref[0, at, :] = top
+                rows_ref[1, at, :] = jnp.sum(weight, axis=0, keepdims=True)
+                rows_ref[2, at, :] = jnp.sum(dscore * distance, axis=0, keepdims=True)
+                rows_ref[3, at, :] = jnp.sum(dscore * ancestor, axis=0, keepdims=True)
 
 
 def main_kernel(
@@ -63,12 +164,13 @@
     slope_ref,
     gain_ref,
     depth_ref,
-    end_ref,
     query_ref,
     grad_ref,
     product_ref,
+    own_weight_ref,
+    own_dscore_ref,
+    own_rows_ref,
     key_ref,
-    value_ref,
     *refs,
 ):
     tokens = query_ref.shape[0]
@@ -101,39 +203,24 @@
             query_grad_ref.at[group], query_grad_hbm.at[:, wide], store_sems.at[group]
         )
 
-    here = lax.axis_index("ctx")
-    query_pos = here * tokens + lax.broadcasted_iota(jnp.int32, (tokens, tokens), 1)
-    start = jnp.zeros((tokens, tokens), jnp.int32)
-    bound = jnp.int32(0)
-    for index in range(lengths_ref.shape[1]):
-        bound = bound + lengths_ref[0, index]
-        start = jnp.where(query_pos >= bound, bound, start)
-    query_depth = jnp.broadcast_to(depth_ref[...].astype(jnp.float32), (tokens, tokens))
     block_rows = [slice(s * tokens, (s + 1) * tokens) for s in range(blocks)]
-    for s, rows in enumerate(block_rows):
-        key_pos = (here ^ s) * tokens + lax.broadcasted_iota(jnp.int32, (tokens, tokens), 0)
-        if s == 0:
-            key_depth = as_column(depth_ref[...].astype(jnp.float32))
-            key_end = as_column(end_ref[...].astype(jnp.float32))
-        else:
-            below = slice(2 * groups * tokens, 2 * groups * tokens + META_ROWS)
-            meta = remote[s - 1][below, :].astype(jnp.float32)
-            key_depth = as_column(meta[0:1])
-            key_end = as_column(meta[1:2] * END_UNIT + meta[2:3])
-        inside = query_pos.astype(jnp.float32) < key_end
-        allowed = (key_pos <= query_pos) & (key_pos >= start)
-        distance_ref[rows, :] = jnp.abs(query_depth - key_depth)
-        ancestor_ref[rows, :] = jnp.where(allowed, jnp.where(inside, 1.0, 0.0), MASKED)
-
-    def key_block(kind, group, s):
-        if s == 0:
-            at = pl.multiple_of(group * WIDTH, WIDTH)
-            return (key_ref, value_ref)[kind][:, pl.ds(at, WIDTH)]
+    remote_rows = block_rows[:-1]
+    below = slice(2 * groups * tokens, 2 * groups * tokens + META_ROWS)
+    for s in range(1, blocks):
+        meta = remote[s - 1][below, :].astype(jnp.float32)
+        distance, ancestor = table(
+            lengths_ref,
+            depth_ref,
+            s,
+            as_column(meta[0:1]),
+            as_column(meta[1:2] * END_UNIT + meta[2:3]),
+        )
+        distance_ref[remote_rows[s - 1], :] = distance
+        ancestor_ref[remote_rows[s - 1], :] = ancestor
+
+    def remote_blocks(kind, group):
         at = pl.multiple_of((kind * groups + group) * tokens, tokens)
-        return remote[s - 1][pl.ds(at, tokens), :]
-
-    def all_blocks(kind, group):
-        return jnp.concatenate([key_block(kind, group, s) for s in range(blocks)], axis=0)
+        return jnp.concatenate([r[pl.ds(at, tokens), :] for r in remote], axis=0)
 
     def stacked(ref, group, first, count):
         at = pl.multiple_of(group * group_columns, group_columns) + first * WIDTH
@@ -145,9 +232,9 @@
         gain = gain_ref[head] * LOG2E
         slope = slope_ref[head] * LOG2E
         lanes = slice(half * tokens, (half + 1) * tokens)
-        tops, totals = [], []
-        for s, rows in enumerate(block_rows):
-            score = raw[s][:, lanes] * (factor * LOG2E) + (
+        tops, totals = [own_rows_ref[0, pl.ds(head, 1), :]], [own_rows_ref[1, pl.ds(head, 1), :]]
+        for rows in remote_rows:
+            score = raw[rows, lanes] * (factor * LOG2E) + (
                 gain * ancestor_ref[rows, :] - slope * distance_ref[rows, :]
             )
             top = jnp.max(score, axis=0, keepdims=True)
@@ -163,17 +250,26 @@
     def differentiate(group, pair, centred, scales, half):
         lanes = slice(half * tokens, (half + 1) * tokens)
         to = slice((2 * pair + half) * tokens, (2 * pair + half + 1) * tokens)
+        head = group * heads_per_group + 2 * pair + half
+        own = pl.ds(pl.multiple_of(head * tokens, tokens), tokens)
+        own_rows = block_rows[0]
+        probs_ref[own_rows, to] = (own_weight_ref[:, own] * scales[0]).astype(jnp.bfloat16)
+        dscore_ref[own_rows, to] = (own_dscore_ref[:, own] * scales[0]).astype(jnp.bfloat16)
         slope_sum, gain_sum = 0.0, 0.0
-        for s, rows in enumerate(block_rows):
+        for s, rows in enumerate(remote_rows, 1):
             probs = weight_ref[pair % 2, rows, lanes] * scales[s]
-            dscore = probs * centred[s][:, lanes]
-            probs_ref[rows, to] = probs.astype(jnp.bfloat16)
-            dscore_ref[rows, to] = dscore.astype(jnp.bfloat16)
+            dscore = probs * centred[rows, lanes]
+            probs_ref[block_rows[s], to] = probs.astype(jnp.bfloat16)
+            dscore_ref[block_rows[s], to] = dscore.astype(jnp.bfloat16)
             slope_sum = slope_sum + fold_rows(dscore * distance_ref[rows, :])
             gain_sum = gain_sum + fold_rows(dscore * ancestor_ref[rows, :])
-        at = pl.ds(group * heads_per_group + 2 * pair + half, 1)
-        slope_rows[at, :] = -jnp.sum(slope_sum, axis=0, keepdims=True)
-        gain_rows[at, :] = jnp.sum(gain_sum, axis=0, keepdims=True)
+        at = pl.ds(head, 1)
+        slope_rows[at, :] = -(
+            jnp.sum(slope_sum, axis=0, keepdims=True) + own_rows_ref[2, at, :] * scales[0]
+        )
+        gain_rows[at, :] = (
+            jnp.sum(gain_sum, axis=0, keepdims=True) + own_rows_ref[3, at, :] * scales[0]
+        )
 
     def put_part(group, kind, whole):
         at = pl.multiple_of((kind * groups + group) * tokens, tokens)
@@ -198,23 +294,20 @@
             at = (2 * pair + half) * WIDTH
             query_grad_ref[group, :, at : at + WIDTH] = rows[half * tokens : (half + 1) * tokens]
 
-    def products(left, right):
-        whole = dot_nt(left, right)
-        return [whole[rows] for rows in block_rows]
-
     @pl.loop(0, groups)
     def _(group):
-        keys = all_blocks(0, group)
-        values = all_blocks(1, group)
+        keys = remote_blocks(0, group)
+        values = remote_blocks(1, group)
         value_ext = jnp.concatenate([values, jnp.full(values.shape, -1.0, jnp.bfloat16)], axis=1)
-        keys_across = jnp.transpose(keys)
+        own_key = key_ref[:, pl.ds(pl.multiple_of(group * WIDTH, WIDTH), WIDTH)]
+        keys_across = jnp.transpose(jnp.concatenate([own_key, keys], axis=0))
         half_heads = heads_per_group // 2
         for pair in range(pairs):
             query_pair = stacked(query_ref, group, 2 * pair, 2)
             grad_pair = stacked(grad_ref, group, 2 * pair, 2)
             product_pair = stacked(product_ref, group, 2 * pair, 2)
             grad_ext = jnp.concatenate([grad_pair, product_pair], axis=1)
-            raw = products(keys, query_pair)
+            raw = dot_nt(keys, query_pair)
             if pair == pairs // 2:
                 key_acc[...] = key_part(group, 0, half_heads)
             scales = [weigh(group, pair, raw, half) for half in range(2)]
@@ -222,7 +315,7 @@
                 value_acc[...] = value_part(group, 0, half_heads)
             if pair:
                 query_part(keys_across, group, pair - 1)
-            centred = products(value_ext, grad_ext)
+            centred = dot_nt(value_ext, grad_ext)
             for half in range(2):
                 differentiate(group, pair, centred, scales[half], half)
         key_whole = key_acc[...] + key_part(group, half_heads, half_heads)
@@ -305,30 +398,53 @@
     depth_held, end_held = hold(depths), hold(subtree_end)
     message_rows = 2 * groups * tokens
     message = pl.pallas_call(
-        pack_kernel,
+        functools.partial(pack_kernel, blocks),
         out_shape=jax.ShapeDtypeStruct((message_rows + META_ROWS, WIDTH), bf16),
-        in_specs=[vmem] * 4,
+        in_specs=[hbm] * 4,
         out_specs=vmem,
+        scratch_shapes=[
+            pltpu.VMEM((1, tokens), jnp.int32),
+            pltpu.VMEM((1, tokens), jnp.int32),
+            pltpu.SemaphoreType.DMA((2 + 2 * groups,)),
+        ],
         compiler_params=params,
         name="pack",
     )(key_held, value_held, depth_held, end_held)
-    shifts = [s for s in range(1, blocks) if s != 2] + [2]
+    shifts = list(range(1, blocks))
     arrived = [
         lax.ppermute(message, "ctx", [(i, i ^ s) for i in range(blocks) if i < i ^ s])
         for s in shifts
     ]
 
-    prepared = pl.pallas_call(
-        prepare_kernel,
-        out_shape=[jax.ShapeDtypeStruct((tokens, width_all), bf16)] * 3,
-        in_specs=[vmem] * 3,
-        out_specs=[vmem] * 3,
+    lengths_held, slope_held, gain_held = hold(file_lengths), hold(slopes), hold(ancestor_gain)
+    own_table = jax.ShapeDtypeStruct((tokens, tokens), f32)
+    own_scores = jax.ShapeDtypeStruct((tokens, heads_all * tokens), f32)
+    query_here, grad_here, product_here, _, _, own_weight, own_dscore, own_rows = pl.pallas_call(
+        functools.partial(prepare_kernel, heads_per_group, groups),
+        out_shape=[jax.ShapeDtypeStruct((tokens, width_all), bf16)] * 3
+        + [own_table, own_table, own_scores, own_scores]
+        + [jax.ShapeDtypeStruct((4, heads_all, tokens), f32)],
+        in_specs=[smem] * 3 + [vmem] * 7,
+        out_specs=[vmem] * 8,
         compiler_params=params,
         cost_estimate=pl.CostEstimate(
-            flops=tokens * width_all, bytes_accessed=12 * tokens * width_all, transcendentals=0
+            flops=4 * tokens * tokens * width_all,
+            bytes_accessed=12 * tokens * width_all,
+            transcendentals=tokens * tokens * heads_all,
         ),
         name="prepare",
-    )(hold(queries[0]), hold(outputs[0]), hold(out_grads[0]))
+    )(
+        lengths_held,
+        slope_held,
+        gain_held,
+        depth_held,
+        end_held,
+        hold(queries[0]),
+        hold(outputs[0]),
+        hold(out_grads[0]),
+        key_held,
+        value_held,
+    )
 
     bias_shape = (replicas, blocks, 8, WIDTH)
     matmul_flops = 2 * tokens * keys_seen * WIDTH * heads_all
@@ -337,17 +453,17 @@
         out_shape=[jax.ShapeDtypeStruct((tokens, width_all), bf16)]
         + [jax.ShapeDtypeStruct((message_rows, WIDTH), bf16)] * blocks
         + [jax.ShapeDtypeStruct(bias_shape, f32)],
-        in_specs=[smem] * 3 + [vmem] * (6 + blocks),
+        in_specs=[smem] * 3 + [vmem] * (7 + blocks),
         out_specs=[hbm] + [vmem] * blocks + [hbm],
         scratch_shapes=[
             pltpu.VMEM((groups, tokens, group_columns), bf16),
-            pltpu.VMEM((keys_seen, tokens), f32),
-            pltpu.VMEM((keys_seen, tokens), f32),
+            pltpu.VMEM((keys_seen - tokens, tokens), f32),
+            pltpu.VMEM((keys_seen - tokens, tokens), f32),
             pltpu.VMEM((heads_all, tokens), f32),
             pltpu.VMEM((heads_all, tokens), f32),
             pltpu.VMEM((keys_seen, WIDTH), f32),
             pltpu.VMEM((keys_seen, WIDTH), f32),
-            pltpu.VMEM((2, keys_seen, 2 * tokens), f32),
+            pltpu.VMEM((2, keys_seen - tokens, 2 * tokens), f32),
             pltpu.VMEM((keys_seen, group_columns), bf16),
             pltpu.VMEM((keys_seen, group_columns), bf16),
             pltpu.VMEM(bias_shape, f32),
@@ -362,14 +478,17 @@
         ),
         name="attend",
     )(
-        hold(file_lengths),
-        hold(slopes),
-        hold(ancestor_gain),
+        lengths_held,
+        slope_held,
+        gain_held,
         depth_held,
-        end_held,
-        *prepared,
+        query_here,
+        grad_here,
+        product_here,
+        own_weight,
+        own_dscore,
+        own_rows,
         key_held,
-        value_held,
         *arrived,
     )
     query_grads = results[0]

time: 53 us -> 51.5 us (0.972)
  waiting for transfers between devices: 14.3 us -> 10.7 us
  Pallas kernels: 16 us -> 18.2 us
    ppermute x3, waiting for transfers between devices: 6.76 us -> 2.53 us  [body(): lax.ppermute(message, 'ctx', [(i, i ^ s) for i in range(blocks) if i < i...]
    pallas_call x2, Pallas kernels: 3.13 us -> 5.99 us  [the longest x1 4.98 us: body(): pl.pallas_call(functools.partial(prepare_kernel, heads_per_group, groups)...]
    ppermute x3, waiting for transfers between devices: 6.84 us -> 8.11 us  [body(): parts[s] = lax.ppermute(parts[s], 'ctx', back)]
    all_to_all x1, waiting for transfers between devices: 0.75 us -> 0.01 us  [body(): lax.all_to_all(bias_parts, ('dp', 'ctx'), split_axis=0, concat_axis=0, ti...]
    pallas_call x1, Pallas kernels: 11.5 us -> 10.8 us  [body(): pl.pallas_call(functools.partial(main_kernel, blocks, heads_per_group, gr...]
  transfers between devices with their start and end apart: 7 -> 7, of which waited for: 4 -> 2; matrix products, arithmetic and copies ran while one was open for 0% -> 0% of each run, Pallas kernels for 5% -> 11%
where the time goes in v13:
time: 51.5 us; the launch traced here: 51.1 us
  starting transfers between devices  21.6 us (42%)
  Pallas kernels  18.2 us (35%)
  waiting for transfers between devices  10.7 us (21%)
  between operations  0.72 us (1%)
    pallas_call x1, Pallas kernels, body(): pl.pallas_call(functools.partial(main_kernel, blocks, heads_per_group, gr...  10.8 us
    ppermute x3, starting transfers between devices, body(): lax.ppermute(message, 'ctx', [(i, i ^ s) for i in range(blocks) if i < i...  9.58 us
    all_to_all x1, starting transfers between devices, body(): lax.all_to_all(bias_parts, ('dp', 'ctx'), split_axis=0, concat_axis=0, ti...  8.16 us
    ppermute x3, waiting for transfers between devices, body(): parts[s] = lax.ppermute(parts[s], 'ctx', back)  8.11 us
    pallas_call x1, Pallas kernels, body(): pl.pallas_call(functools.partial(prepare_kernel, heads_per_group, groups)...  4.98 us
    ppermute x3, starting transfers between devices, body(): parts[s] = lax.ppermute(parts[s], 'ctx', back)  3.88 us
    ppermute x3, waiting for transfers between devices, body(): lax.ppermute(message, 'ctx', [(i, i ^ s) for i in range(blocks) if i < i...  2.53 us
  transfers between devices with their start and end apart: 7, of which 2 were waited for; matrix products, arithmetic and copies ran while one was open for 0% of the time, Pallas kernels for 11%

profile of v13, /device:TPU:0, one launch (start us, length us, event | category | flops | bytes accessed | tf_op | source)
XLA Modules:
  0.0 51.1 jit_solution(17488091904060108700)
XLA Ops:
  0.6 1.0 %pack.1 = bf16[1040,128]{1,0:T(8,128)(2,1)S(1)} custom-call(bf16[128,512]{1,0:T(8,128)(2,1)} %bitcast.15, bf16[128,512]{1,0:T(8,128)(2,1)} %bitcast.13, s32[1,128]{1,0:T(1,128)} %depth_ref.3, s32[1,128]{1,0:T(1,128)} %end_hbm.1), custom_call_target="tpu_custom_call" | custom-call | tf_op jit(solution)/shard_map/pack/pallas_call | solution.py:400
  1.6 4.9 %collective-permute-start.2 = (bf16[1040,128]{1,0:T(8,128)(2,1)S(1)}, bf16[1040,128]{1,0:T(8,128)(2,1)S(1)}, u32[]{:S(2)}, u32[]{:S(2)}) collective-permute-start(bf16[1040,128]{1,0:T(8,128)(2,1)S(1)} %pack.1), channel_id=1, source_target_pairs={{0,3},{1,2},{4,7},{5,6},{8,11},{9,10},{12,15},{13,14},{16,19},{17,... | collective-permute-start | bytes 798728 | tf_op jit(solution)/shard_map/ppermute | solution.py:415
  6.6 1.3 %collective-permute-start.1 = (bf16[1040,128]{1,0:T(8,128)(2,1)S(1)}, bf16[1040,128]{1,0:T(8,128)(2,1)S(1)}, u32[]{:S(2)}, u32[]{:S(2)}) collective-permute-start(bf16[1040,128]{1,0:T(8,128)(2,1)S(1)} %pack.1), channel_id=1, source_target_pairs={{0,2},{1,3},{4,6},{5,7},{8,10},{9,11},{12,14},{13,15},{16,18},{17,... | collective-permute-start | bytes 798728 | tf_op jit(solution)/shard_map/ppermute | solution.py:415
  7.9 3.4 %collective-permute-start = (bf16[1040,128]{1,0:T(8,128)(2,1)S(1)}, bf16[1040,128]{1,0:T(8,128)(2,1)S(1)}, u32[]{:S(2)}, u32[]{:S(2)}) collective-permute-start(bf16[1040,128]{1,0:T(8,128)(2,1)S(1)} %pack.1), channel_id=1, source_target_pairs={{0,1},{2,3},{4,5},{6,7},{8,9},{10,11},{12,13},{14,15},{16,17},{18,... | collective-permute-start | bytes 798728 | tf_op jit(solution)/shard_map/ppermute | solution.py:415
  11.2 5.0 %prepare.1 = (bf16[128,4096]{1,0:T(8,128)(2,1)S(1)}, bf16[128,4096]{1,0:T(8,128)(2,1)S(1)}, bf16[128,4096]{1,0:T(8,128)(2,1)S(1)}, f32[128,128]{1,0:T(8,128)}, f...) custom-call(s32[1,8]{1,0:T(1,128)} %lengths_ref.3, ...), custom_call_target="tpu_custom_call" | custom-call | flops 268435456 | bytes 6291456 | tf_op jit(solution)/shard_map/prepare/pallas_call | solution.py:422
  16.2 0.0 collective-permute-done.2.refs_2_
  16.2 2.5 %collective-permute-done.1.refs_1_ = bf16[1040,128]{1,0:T(8,128)(2,1)S(1)} collective-permute-done((bf16[1040,128]{1,0:T(8,128)(2,1)S(1)}, bf16[1040,128]{1,0:T(8,128)(2,1)S(1)}, u32[]{:S(2)}, u32[]{:S(2)}) %collective-permute-start.1) | collective-permute-done | bytes 266272 | tf_op jit(solution)/shard_map/ppermute | solution.py:415
  18.8 0.0 collective-permute-done.refs_0_
  18.8 10.8 %attend.1 = (bf16[128,4096]{1,0:T(8,128)(2,1)}, bf16[1024,128]{1,0:T(8,128)(2,1)S(1)}, bf16[1024,128]{1,0:T(8,128)(2,1)S(1)}, bf16[1024,128]{1,0:T(8,128)(2,1)S(...) custom-call(s32[1,8]{1,0:T(1,128)} %lengths_ref.3, f32[32]{0:T(128)} %slope_ref.3, f32[32]{0:T(128)} %gain_ref.3, ...), custom_call_target="tpu_custom_call" | custom-call | flops 2684354560 | bytes 5242880 | tf_op jit(solution)/shard_map/attend/pallas_call | solution.py:451
  29.5 1.3 %collective-permute-start.3 = (bf16[1024,128]{1,0:T(8,128)(2,1)S(1)}, bf16[1024,128]{1,0:T(8,128)(2,1)S(1)}, u32[]{:S(2)}, u32[]{:S(2)}) collective-permute-start(bf16[1024,128]{1,0:T(8,128)(2,1)S(1)} %get-tuple-element.26), channel_id=1, source_target_pairs={{2,0},{3,1},{6,4},{7,5},{10,8},{11,9},{14,12},{15,13},{18,16},{19,... | collective-permute-start | bytes 786440 | tf_op jit(solution)/shard_map/ppermute | solution.py:499
  30.8 1.3 %collective-permute-start.4 = (bf16[1024,128]{1,0:T(8,128)(2,1)S(1)}, bf16[1024,128]{1,0:T(8,128)(2,1)S(1)}, u32[]{:S(2)}, u32[]{:S(2)}) collective-permute-start(bf16[1024,128]{1,0:T(8,128)(2,1)S(1)} %get-tuple-element.27), channel_id=1, source_target_pairs={{1,0},{3,2},{5,4},{7,6},{9,8},{11,10},{13,12},{15,14},{17,16},{19,... | collective-permute-start | bytes 786440 | tf_op jit(solution)/shard_map/ppermute | solution.py:499
  32.1 1.3 %collective-permute-start.5 = (bf16[1024,128]{1,0:T(8,128)(2,1)S(1)}, bf16[1024,128]{1,0:T(8,128)(2,1)S(1)}, u32[]{:S(2)}, u32[]{:S(2)}) collective-permute-start(bf16[1024,128]{1,0:T(8,128)(2,1)S(1)} %get-tuple-element.28), channel_id=1, source_target_pairs={{2,1},{3,0},{6,5},{7,4},{10,9},{11,8},{14,13},{15,12},{18,17},{19,... | collective-permute-start | bytes 786440 | tf_op jit(solution)/shard_map/ppermute | solution.py:499
  33.4 8.2 %all-to-all-start = ((f32[32,8,128]{2,1,0:T(8,128)}), f32[32,8,128]{2,1,0:T(8,128)S(1)}, u32[]{:S(2)}, u32[]{:S(2)}) async-start(f32[32,8,128]{2,1,0:T(8,128)} %bitcast.8), calls=%async_computation | async-start | bytes 262144 | tf_op jit(solution)/shard_map/all_to_all | solution.py:500
  41.6 0.0 collective-permute-done.3.refs_1_
  41.6 0.0 collective-permute-done.4.refs_2_
  41.6 8.1 %collective-permute-done.5.refs_3_ = bf16[1024,128]{1,0:T(8,128)(2,1)S(1)} collective-permute-done((bf16[1024,128]{1,0:T(8,128)(2,1)S(1)}, bf16[1024,128]{1,0:T(8,128)(2,1)S(1)}, u32[]{:S(2)}, u32[]{:S(2)}) %collective-permute-start.5) | collective-permute-done | bytes 262176 | tf_op jit(solution)/shard_map/ppermute | solution.py:499
  49.7 0.8 %combine.1 = (bf16[128,512]{1,0:T(8,128)(2,1)}, bf16[128,512]{1,0:T(8,128)(2,1)}) custom-call(bf16[1024,128]{1,0:T(8,128)(2,1)S(1)} %get-tuple-element.25.refs_0_, bf16[1024,128]{1,0:T(8,128)(2,1)S(1)} %collective-permute-done.3.refs_1_, bf16[1024,128]{1,0:T(8,128)(2,1)S(1)} %collective-permute-done.4.refs_2_, ...), custom_call_target="tpu_custom_call" | custom-call | flops 1048576 | bytes 1310720 | tf_op jit(solution)/shard_map/combine/pallas_call | solution.py:502
  50.5 0.0 all-to-all-done.parts_ref
  50.5 0.6 %bias.1 = f32[2,8]{1,0:T(2,128)} custom-call(f32[32,8,128]{2,1,0:T(8,128)S(1)} %all-to-all-done.parts_ref, bf16[128,512]{1,0:T(8,128)(2,1)} %get-tuple-element.29._), custom_call_target="tpu_custom_call" | custom-call | tf_op jit(solution)/shard_map/bias/pallas_call | solution.py:515
Async XLA Ops:
  1.6 14.6 %collective-permute-start.2 = (bf16[1040,128]{1,0:T(8,128)(2,1)S(1)}, bf16[1040,128]{1,0:T(8,128)(2,1)S(1)}, u32[]{:S(2)}, u32[]{:S(2)}) collective-permute-start(bf16[1040,128]{1,0:T(8,128)(2,1)S(1)} %pack.1), channel_id=1, source_target_pairs={{0,3},{1,2},{4,7},{5,6},{8,11},{9,10},{12,15},{13,14},{16,19},{17,... | collective-permute-start | bytes 798728 | tf_op jit(solution)/shard_map/ppermute | solution.py:415
  6.6 12.2 %collective-permute-start.1 = (bf16[1040,128]{1,0:T(8,128)(2,1)S(1)}, bf16[1040,128]{1,0:T(8,128)(2,1)S(1)}, u32[]{:S(2)}, u32[]{:S(2)}) collective-permute-start(bf16[1040,128]{1,0:T(8,128)(2,1)S(1)} %pack.1), channel_id=1, source_target_pairs={{0,2},{1,3},{4,6},{5,7},{8,10},{9,11},{12,14},{13,15},{16,18},{17,... | collective-permute-start | bytes 798728 | tf_op jit(solution)/shard_map/ppermute | solution.py:415
  7.9 10.9 %collective-permute-start = (bf16[1040,128]{1,0:T(8,128)(2,1)S(1)}, bf16[1040,128]{1,0:T(8,128)(2,1)S(1)}, u32[]{:S(2)}, u32[]{:S(2)}) collective-permute-start(bf16[1040,128]{1,0:T(8,128)(2,1)S(1)} %pack.1), channel_id=1, source_target_pairs={{0,1},{2,3},{4,5},{6,7},{8,9},{10,11},{12,13},{14,15},{16,17},{18,... | collective-permute-start | bytes 798728 | tf_op jit(solution)/shard_map/ppermute | solution.py:415
  29.5 12.1 %collective-permute-start.3 = (bf16[1024,128]{1,0:T(8,128)(2,1)S(1)}, bf16[1024,128]{1,0:T(8,128)(2,1)S(1)}, u32[]{:S(2)}, u32[]{:S(2)}) collective-permute-start(bf16[1024,128]{1,0:T(8,128)(2,1)S(1)} %get-tuple-element.26), channel_id=1, source_target_pairs={{2,0},{3,1},{6,4},{7,5},{10,8},{11,9},{14,12},{15,13},{18,16},{19,... | collective-permute-start | bytes 786440 | tf_op jit(solution)/shard_map/ppermute | solution.py:499
  30.8 10.8 %collective-permute-start.4 = (bf16[1024,128]{1,0:T(8,128)(2,1)S(1)}, bf16[1024,128]{1,0:T(8,128)(2,1)S(1)}, u32[]{:S(2)}, u32[]{:S(2)}) collective-permute-start(bf16[1024,128]{1,0:T(8,128)(2,1)S(1)} %get-tuple-element.27), channel_id=1, source_target_pairs={{1,0},{3,2},{5,4},{7,6},{9,8},{11,10},{13,12},{15,14},{17,16},{19,... | collective-permute-start | bytes 786440 | tf_op jit(solution)/shard_map/ppermute | solution.py:499
  32.1 17.6 %collective-permute-start.5 = (bf16[1024,128]{1,0:T(8,128)(2,1)S(1)}, bf16[1024,128]{1,0:T(8,128)(2,1)S(1)}, u32[]{:S(2)}, u32[]{:S(2)}) collective-permute-start(bf16[1024,128]{1,0:T(8,128)(2,1)S(1)} %get-tuple-element.28), channel_id=1, source_target_pairs={{2,1},{3,0},{6,5},{7,4},{10,9},{11,8},{14,13},{15,12},{18,17},{19,... | collective-permute-start | bytes 786440 | tf_op jit(solution)/shard_map/ppermute | solution.py:499
  33.4 17.1 %all-to-all-start = ((f32[32,8,128]{2,1,0:T(8,128)}), f32[32,8,128]{2,1,0:T(8,128)S(1)}, u32[]{:S(2)}, u32[]{:S(2)}) async-start(f32[32,8,128]{2,1,0:T(8,128)} %bitcast.8), calls=%async_computation | async-start | bytes 262144 | tf_op jit(solution)/shard_map/all_to_all | solution.py:500

commit v14 on v13

--- a/solution.py
+++ b/solution.py
@@ -345,22 +345,23 @@
     bias_copy.wait()
 
 
-def combine_kernel(blocks, *refs):
-    parts = refs[0:blocks]
-    key_out, value_out = refs[blocks:]
+def gather_parts_kernel(*refs):
+    total = refs[0][...].astype(jnp.float32)
+    for part in refs[1:-1]:
+        total = total + part[...].astype(jnp.float32)
+    refs[-1][...] = total
+
+
+def combine_kernel(sum_ref, part_ref, bias_parts, key_out, value_out, bias_out):
     tokens = key_out.shape[0]
     groups = key_out.shape[1] // WIDTH
     for kind, out in enumerate((key_out, value_out)):
         for group in range(groups):
             at = (kind * groups + group) * tokens
-            total = parts[0][at : at + tokens, :].astype(jnp.float32)
-            for s in range(1, blocks):
-                total = total + parts[s][at : at + tokens, :].astype(jnp.float32)
+            rows = slice(at, at + tokens)
+            total = sum_ref[rows, :] + part_ref[rows, :].astype(jnp.float32)
             out[:, group * WIDTH : (group + 1) * WIDTH] = total.astype(jnp.bfloat16)
-
-
-def bias_kernel(parts_ref, _, out_ref):
-    out_ref[...] = jnp.sum(parts_ref[...], axis=0)[0:2, 0 : out_ref.shape[1]]
+    bias_out[...] = jnp.sum(bias_parts[...], axis=0)[0:2, 0 : bias_out.shape[1]]
 
 
 def body(
@@ -410,7 +411,7 @@
         compiler_params=params,
         name="pack",
     )(key_held, value_held, depth_held, end_held)
-    shifts = list(range(1, blocks))
+    shifts = [s for s in range(blocks - 1, 0, -1) if s != 2] + [2]
     arrived = [
         lax.ppermute(message, "ctx", [(i, i ^ s) for i in range(blocks) if i < i ^ s])
         for s in shifts
@@ -499,27 +500,29 @@
         parts[s] = lax.ppermute(parts[s], "ctx", back)
     bias_parts = lax.all_to_all(bias_parts, ("dp", "ctx"), split_axis=0, concat_axis=0, tiled=True)
 
-    key_grads, value_grads = pl.pallas_call(
-        functools.partial(combine_kernel, blocks),
-        out_shape=[jax.ShapeDtypeStruct((tokens, kv_width), bf16)] * 2,
-        in_specs=[vmem] * blocks,
-        out_specs=[vmem] * 2,
+    early = [parts[0], parts[2], parts[1], *parts[3:-1]] if blocks > 3 else parts[:-1]
+    parts_sum = pl.pallas_call(
+        gather_parts_kernel,
+        out_shape=jax.ShapeDtypeStruct((message_rows, WIDTH), f32),
+        in_specs=[vmem] * len(early),
+        out_specs=vmem,
         compiler_params=params,
         cost_estimate=pl.CostEstimate(
             flops=2 * message_rows * WIDTH * blocks,
             bytes_accessed=2 * message_rows * WIDTH * (blocks + 1),
             transcendentals=0,
         ),
+        name="sum_parts",
+    )(*early)
+    key_grads, value_grads, bias_grads = pl.pallas_call(
+        combine_kernel,
+        out_shape=[jax.ShapeDtypeStruct((tokens, kv_width), bf16)] * 2
+        + [jax.ShapeDtypeStruct((2, local_heads), f32)],
+        in_specs=[vmem] * 3,
+        out_specs=[vmem] * 3,
+        compiler_params=params,
         name="combine",
-    )(parts[0], parts[2], parts[1], *parts[3:])
-    bias_grads = pl.pallas_call(
-        bias_kernel,
-        out_shape=jax.ShapeDtypeStruct((2, local_heads), f32),
-        in_specs=[vmem, hbm],
-        out_specs=vmem,
-        compiler_params=params,
-        name="bias",
-    )(bias_parts, hold(key_grads))
+    )(parts_sum, parts[-1], bias_parts)
     return (query_grads[None], key_grads[None], value_grads[None], bias_grads.T)
 
 

time: 51.5 us -> 52.5 us (1.019)
  waiting for transfers between devices: 10.7 us -> 13 us
  starting transfers between devices: 21.6 us -> 20.7 us
  Pallas kernels: 18.2 us -> 17.6 us
    all_to_all x1, waiting for transfers between devices: 0.01 us -> 8.29 us  [body(): lax.all_to_all(bias_parts, ('dp', 'ctx'), split_axis=0, concat_axis=0, ti...]
    ppermute x3, waiting for transfers between devices: 8.11 us -> 0.01 us  [body(): parts[s] = lax.ppermute(parts[s], 'ctx', back)]
    ppermute x3, waiting for transfers between devices: 2.53 us -> 4.75 us  [body(): lax.ppermute(message, 'ctx', [(i, i ^ s) for i in range(blocks) if i < i...]
    ppermute x3, starting transfers between devices: 9.58 us -> 8.71 us  [body(): lax.ppermute(message, 'ctx', [(i, i ^ s) for i in range(blocks) if i < i...]
    pallas_call x2, Pallas kernels: 1.39 us -> 0.83 us  [the longest x1 0.74 us: body(): pl.pallas_call(combine_kernel, out_shape=[jax.ShapeDtypeStruct((tokens, k...]
  transfers between devices with their start and end apart: 7 -> 7, of which waited for: 2 -> 3; matrix products, arithmetic and copies ran while one was open for 0% -> 0% of each run, Pallas kernels for 11% -> 10%
where the time goes in v14:
time: 52.5 us; the launch traced here: 52.1 us
  starting transfers between devices  20.7 us (39%)
  Pallas kernels  17.6 us (34%)
  waiting for transfers between devices  13 us (25%)
  between operations  0.73 us (1%)
    pallas_call x1, Pallas kernels, body(): pl.pallas_call(functools.partial(main_kernel, blocks, heads_per_group, gr...  10.8 us
    ppermute x3, starting transfers between devices, body(): lax.ppermute(message, 'ctx', [(i, i ^ s) for i in range(blocks) if i < i...  8.71 us
    all_to_all x1, waiting for transfers between devices, body(): lax.all_to_all(bias_parts, ('dp', 'ctx'), split_axis=0, concat_axis=0, ti...  8.29 us
    all_to_all x1, starting transfers between devices, body(): lax.all_to_all(bias_parts, ('dp', 'ctx'), split_axis=0, concat_axis=0, ti...  8.16 us
    pallas_call x1, Pallas kernels, body(): pl.pallas_call(functools.partial(prepare_kernel, heads_per_group, groups)...  4.98 us
    ppermute x3, waiting for transfers between devices, body(): lax.ppermute(message, 'ctx', [(i, i ^ s) for i in range(blocks) if i < i...  4.75 us
    ppermute x3, starting transfers between devices, body(): parts[s] = lax.ppermute(parts[s], 'ctx', back)  3.88 us
  transfers between devices with their start and end apart: 7, of which 3 were waited for; matrix products, arithmetic and copies ran while one was open for 0% of the time, Pallas kernels for 10%

profile of v14, /device:TPU:0, one launch (start us, length us, event | category | flops | bytes accessed | tf_op | source)
XLA Modules:
  0.0 52.1 jit_solution(8930338650242647299)
XLA Ops:
  0.6 1.0 %pack.1 = bf16[1040,128]{1,0:T(8,128)(2,1)S(1)} custom-call(bf16[128,512]{1,0:T(8,128)(2,1)} %bitcast.15, bf16[128,512]{1,0:T(8,128)(2,1)} %bitcast.13, s32[1,128]{1,0:T(1,128)} %depth_ref.3, s32[1,128]{1,0:T(1,128)} %end_hbm.1), custom_call_target="tpu_custom_call" | custom-call | tf_op jit(solution)/shard_map/pack/pallas_call | solution.py:401
  1.6 4.9 %collective-permute-start.2 = (bf16[1040,128]{1,0:T(8,128)(2,1)S(1)}, bf16[1040,128]{1,0:T(8,128)(2,1)S(1)}, u32[]{:S(2)}, u32[]{:S(2)}) collective-permute-start(bf16[1040,128]{1,0:T(8,128)(2,1)S(1)} %pack.1), channel_id=1, source_target_pairs={{0,2},{1,3},{4,6},{5,7},{8,10},{9,11},{12,14},{13,15},{16,18},{17,... | collective-permute-start | bytes 798728 | tf_op jit(solution)/shard_map/ppermute | solution.py:416
  6.5 2.5 %collective-permute-start.1 = (bf16[1040,128]{1,0:T(8,128)(2,1)S(1)}, bf16[1040,128]{1,0:T(8,128)(2,1)S(1)}, u32[]{:S(2)}, u32[]{:S(2)}) collective-permute-start(bf16[1040,128]{1,0:T(8,128)(2,1)S(1)} %pack.1), channel_id=1, source_target_pairs={{0,1},{2,3},{4,5},{6,7},{8,9},{10,11},{12,13},{14,15},{16,17},{18,... | collective-permute-start | bytes 798728 | tf_op jit(solution)/shard_map/ppermute | solution.py:416
  9.1 1.3 %collective-permute-start = (bf16[1040,128]{1,0:T(8,128)(2,1)S(1)}, bf16[1040,128]{1,0:T(8,128)(2,1)S(1)}, u32[]{:S(2)}, u32[]{:S(2)}) collective-permute-start(bf16[1040,128]{1,0:T(8,128)(2,1)S(1)} %pack.1), channel_id=1, source_target_pairs={{0,3},{1,2},{4,7},{5,6},{8,11},{9,10},{12,15},{13,14},{16,19},{17,... | collective-permute-start | bytes 798728 | tf_op jit(solution)/shard_map/ppermute | solution.py:416
  10.4 5.0 %prepare.1 = (bf16[128,4096]{1,0:T(8,128)(2,1)S(1)}, bf16[128,4096]{1,0:T(8,128)(2,1)S(1)}, bf16[128,4096]{1,0:T(8,128)(2,1)S(1)}, f32[128,128]{1,0:T(8,128)}, f...) custom-call(s32[1,8]{1,0:T(1,128)} %lengths_ref.3, ...), custom_call_target="tpu_custom_call" | custom-call | flops 268435456 | bytes 6291456 | tf_op jit(solution)/shard_map/prepare/pallas_call | solution.py:423
  15.4 2.5 %collective-permute-done.2.refs_2_ = bf16[1040,128]{1,0:T(8,128)(2,1)S(1)} collective-permute-done((bf16[1040,128]{1,0:T(8,128)(2,1)S(1)}, bf16[1040,128]{1,0:T(8,128)(2,1)S(1)}, u32[]{:S(2)}, u32[]{:S(2)}) %collective-permute-start.2) | collective-permute-done | bytes 266272 | tf_op jit(solution)/shard_map/ppermute | solution.py:416
  17.9 0.0 collective-permute-done.1.refs_1_
  17.9 2.2 %collective-permute-done.refs_0_ = bf16[1040,128]{1,0:T(8,128)(2,1)S(1)} collective-permute-done((bf16[1040,128]{1,0:T(8,128)(2,1)S(1)}, bf16[1040,128]{1,0:T(8,128)(2,1)S(1)}, u32[]{:S(2)}, u32[]{:S(2)}) %collective-permute-start) | collective-permute-done | bytes 266272 | tf_op jit(solution)/shard_map/ppermute | solution.py:416
  20.1 10.8 %attend.1 = (bf16[128,4096]{1,0:T(8,128)(2,1)}, bf16[1024,128]{1,0:T(8,128)(2,1)S(1)}, bf16[1024,128]{1,0:T(8,128)(2,1)S(1)}, bf16[1024,128]{1,0:T(8,128)(2,1)S(...) custom-call(s32[1,8]{1,0:T(1,128)} %lengths_ref.3, f32[32]{0:T(128)} %slope_ref.3, f32[32]{0:T(128)} %gain_ref.3, ...), custom_call_target="tpu_custom_call" | custom-call | flops 2684354560 | bytes 5242880 | tf_op jit(solution)/shard_map/attend/pallas_call | solution.py:452
  30.9 1.3 %collective-permute-start.3 = (bf16[1024,128]{1,0:T(8,128)(2,1)S(1)}, bf16[1024,128]{1,0:T(8,128)(2,1)S(1)}, u32[]{:S(2)}, u32[]{:S(2)}) collective-permute-start(bf16[1024,128]{1,0:T(8,128)(2,1)S(1)} %get-tuple-element.27), channel_id=1, source_target_pairs={{2,0},{3,1},{6,4},{7,5},{10,8},{11,9},{14,12},{15,13},{18,16},{19,... | collective-permute-start | bytes 786440 | tf_op jit(solution)/shard_map/ppermute | solution.py:500
  32.2 1.3 %collective-permute-start.4 = (bf16[1024,128]{1,0:T(8,128)(2,1)S(1)}, bf16[1024,128]{1,0:T(8,128)(2,1)S(1)}, u32[]{:S(2)}, u32[]{:S(2)}) collective-permute-start(bf16[1024,128]{1,0:T(8,128)(2,1)S(1)} %get-tuple-element.28), channel_id=1, source_target_pairs={{1,0},{3,2},{5,4},{7,6},{9,8},{11,10},{13,12},{15,14},{17,16},{19,... | collective-permute-start | bytes 786440 | tf_op jit(solution)/shard_map/ppermute | solution.py:500
  33.5 1.3 %collective-permute-start.5 = (bf16[1024,128]{1,0:T(8,128)(2,1)S(1)}, bf16[1024,128]{1,0:T(8,128)(2,1)S(1)}, u32[]{:S(2)}, u32[]{:S(2)}) collective-permute-start(bf16[1024,128]{1,0:T(8,128)(2,1)S(1)} %get-tuple-element.29), channel_id=1, source_target_pairs={{2,1},{3,0},{6,5},{7,4},{10,9},{11,8},{14,13},{15,12},{18,17},{19,... | collective-permute-start | bytes 786440 | tf_op jit(solution)/shard_map/ppermute | solution.py:500
  34.8 8.2 %all-to-all-start = ((f32[32,8,128]{2,1,0:T(8,128)}), f32[32,8,128]{2,1,0:T(8,128)S(1)}, u32[]{:S(2)}, u32[]{:S(2)}) async-start(f32[32,8,128]{2,1,0:T(8,128)} %bitcast.6), calls=%async_computation | async-start | bytes 262144 | tf_op jit(solution)/shard_map/all_to_all | solution.py:501
  42.9 0.0 collective-permute-done.3.refs_1_
  43.0 0.0 collective-permute-done.4.refs_2_
  43.0 0.1 sum_parts.1.sum_ref
  43.1 8.3 %all-to-all-done.bias_parts = f32[32,8,128]{2,1,0:T(8,128)S(1)} async-done(((f32[32,8,128]{2,1,0:T(8,128)}), f32[32,8,128]{2,1,0:T(8,128)S(1)}, u32[]{:S(2)}, u32[]{:S(2)}) %all-to-all-start) | async-done | bytes 131104 | tf_op jit(solution)/shard_map/all_to_all | solution.py:501
  51.4 0.0 collective-permute-done.5.part_ref
  51.4 0.7 %combine.1 = (bf16[128,512]{1,0:T(8,128)(2,1)}, bf16[128,512]{1,0:T(8,128)(2,1)}, f32[2,8]{1,0:T(2,128)}) custom-call(f32[1024,128]{1,0:T(8,128)S(1)} %sum_parts.1.sum_ref, bf16[1024,128]{1,0:T(8,128)(2,1)S(1)} %collective-permute-done.5.part_ref, f32[32,8,128]{2,1,0:T(8,128)S(1)} %all-to-all-done.bias_parts), custom_call_target="tpu_custom_call" | custom-call | tf_op jit(solution)/shard_map/combine/pallas_call | solution.py:517
Async XLA Ops:
  1.6 16.2 %collective-permute-start.2 = (bf16[1040,128]{1,0:T(8,128)(2,1)S(1)}, bf16[1040,128]{1,0:T(8,128)(2,1)S(1)}, u32[]{:S(2)}, u32[]{:S(2)}) collective-permute-start(bf16[1040,128]{1,0:T(8,128)(2,1)S(1)} %pack.1), channel_id=1, source_target_pairs={{0,2},{1,3},{4,6},{5,7},{8,10},{9,11},{12,14},{13,15},{16,18},{17,... | collective-permute-start | bytes 798728 | tf_op jit(solution)/shard_map/ppermute | solution.py:416
  6.5 11.3 %collective-permute-start.1 = (bf16[1040,128]{1,0:T(8,128)(2,1)S(1)}, bf16[1040,128]{1,0:T(8,128)(2,1)S(1)}, u32[]{:S(2)}, u32[]{:S(2)}) collective-permute-start(bf16[1040,128]{1,0:T(8,128)(2,1)S(1)} %pack.1), channel_id=1, source_target_pairs={{0,1},{2,3},{4,5},{6,7},{8,9},{10,11},{12,13},{14,15},{16,17},{18,... | collective-permute-start | bytes 798728 | tf_op jit(solution)/shard_map/ppermute | solution.py:416
  9.1 11.0 %collective-permute-start = (bf16[1040,128]{1,0:T(8,128)(2,1)S(1)}, bf16[1040,128]{1,0:T(8,128)(2,1)S(1)}, u32[]{:S(2)}, u32[]{:S(2)}) collective-permute-start(bf16[1040,128]{1,0:T(8,128)(2,1)S(1)} %pack.1), channel_id=1, source_target_pairs={{0,3},{1,2},{4,7},{5,6},{8,11},{9,10},{12,15},{13,14},{16,19},{17,... | collective-permute-start | bytes 798728 | tf_op jit(solution)/shard_map/ppermute | solution.py:416
  30.9 12.1 %collective-permute-start.3 = (bf16[1024,128]{1,0:T(8,128)(2,1)S(1)}, bf16[1024,128]{1,0:T(8,128)(2,1)S(1)}, u32[]{:S(2)}, u32[]{:S(2)}) collective-permute-start(bf16[1024,128]{1,0:T(8,128)(2,1)S(1)} %get-tuple-element.27), channel_id=1, source_target_pairs={{2,0},{3,1},{6,4},{7,5},{10,8},{11,9},{14,12},{15,13},{18,16},{19,... | collective-permute-start | bytes 786440 | tf_op jit(solution)/shard_map/ppermute | solution.py:500
  32.2 10.8 %collective-permute-start.4 = (bf16[1024,128]{1,0:T(8,128)(2,1)S(1)}, bf16[1024,128]{1,0:T(8,128)(2,1)S(1)}, u32[]{:S(2)}, u32[]{:S(2)}) collective-permute-start(bf16[1024,128]{1,0:T(8,128)(2,1)S(1)} %get-tuple-element.28), channel_id=1, source_target_pairs={{1,0},{3,2},{5,4},{7,6},{9,8},{11,10},{13,12},{15,14},{17,16},{19,... | collective-permute-start | bytes 786440 | tf_op jit(solution)/shard_map/ppermute | solution.py:500
  33.5 17.9 %collective-permute-start.5 = (bf16[1024,128]{1,0:T(8,128)(2,1)S(1)}, bf16[1024,128]{1,0:T(8,128)(2,1)S(1)}, u32[]{:S(2)}, u32[]{:S(2)}) collective-permute-start(bf16[1024,128]{1,0:T(8,128)(2,1)S(1)} %get-tuple-element.29), channel_id=1, source_target_pairs={{2,1},{3,0},{6,5},{7,4},{10,9},{11,8},{14,13},{15,12},{18,17},{19,... | collective-permute-start | bytes 786440 | tf_op jit(solution)/shard_map/ppermute | solution.py:500
  34.8 16.6 %all-to-all-start = ((f32[32,8,128]{2,1,0:T(8,128)}), f32[32,8,128]{2,1,0:T(8,128)S(1)}, u32[]{:S(2)}, u32[]{:S(2)}) async-start(f32[32,8,128]{2,1,0:T(8,128)} %bitcast.6), calls=%async_computation | async-start | bytes 262144 | tf_op jit(solution)/shard_map/all_to_all | solution.py:501

commit v15 on v14

--- a/solution.py
+++ b/solution.py
@@ -411,7 +411,7 @@
         compiler_params=params,
         name="pack",
     )(key_held, value_held, depth_held, end_held)
-    shifts = [s for s in range(blocks - 1, 0, -1) if s != 2] + [2]
+    shifts = list(range(1, blocks))
     arrived = [
         lax.ppermute(message, "ctx", [(i, i ^ s) for i in range(blocks) if i < i ^ s])
         for s in shifts

time: 52.5 us -> 51.2 us (0.975)
  waiting for transfers between devices: 13 us -> 10.8 us
  starting transfers between devices: 20.7 us -> 21.6 us
    ppermute x3, waiting for transfers between devices: 4.75 us -> 2.53 us  [body(): lax.ppermute(message, 'ctx', [(i, i ^ s) for i in range(blocks) if i < i...]
    ppermute x3, starting transfers between devices: 8.71 us -> 9.58 us  [body(): lax.ppermute(message, 'ctx', [(i, i ^ s) for i in range(blocks) if i < i...]
  transfers between devices with their start and end apart: 7 -> 7, of which waited for: 3 -> 2; matrix products, arithmetic and copies ran while one was open for 0% -> 0% of each run, Pallas kernels for 10% -> 10%
where the time goes in v15:
time: 51.2 us; the launch traced here: 50.8 us
  starting transfers between devices  21.6 us (42%)
  Pallas kernels  17.6 us (34%)
  waiting for transfers between devices  10.8 us (21%)
  between operations  0.73 us (1%)
    pallas_call x1, Pallas kernels, body(): pl.pallas_call(functools.partial(main_kernel, blocks, heads_per_group, gr...  10.8 us
    ppermute x3, starting transfers between devices, body(): lax.ppermute(message, 'ctx', [(i, i ^ s) for i in range(blocks) if i < i...  9.58 us
    all_to_all x1, waiting for transfers between devices, body(): lax.all_to_all(bias_parts, ('dp', 'ctx'), split_axis=0, concat_axis=0, ti...  8.29 us
    all_to_all x1, starting transfers between devices, body(): lax.all_to_all(bias_parts, ('dp', 'ctx'), split_axis=0, concat_axis=0, ti...  8.16 us
    pallas_call x1, Pallas kernels, body(): pl.pallas_call(functools.partial(prepare_kernel, heads_per_group, groups)...  4.98 us
    ppermute x3, starting transfers between devices, body(): parts[s] = lax.ppermute(parts[s], 'ctx', back)  3.88 us
    ppermute x3, waiting for transfers between devices, body(): lax.ppermute(message, 'ctx', [(i, i ^ s) for i in range(blocks) if i < i...  2.53 us
  transfers between devices with their start and end apart: 7, of which 2 were waited for; matrix products, arithmetic and copies ran while one was open for 0% of the time, Pallas kernels for 10%

profile of v15, /device:TPU:0, one launch (start us, length us, event | category | flops | bytes accessed | tf_op | source)
XLA Modules:
  0.0 50.8 jit_solution(10442155165513529870)
XLA Ops:
  0.6 1.0 %pack.1 = bf16[1040,128]{1,0:T(8,128)(2,1)S(1)} custom-call(bf16[128,512]{1,0:T(8,128)(2,1)} %bitcast.15, bf16[128,512]{1,0:T(8,128)(2,1)} %bitcast.13, s32[1,128]{1,0:T(1,128)} %depth_ref.3, s32[1,128]{1,0:T(1,128)} %end_hbm.1), custom_call_target="tpu_custom_call" | custom-call | tf_op jit(solution)/shard_map/pack/pallas_call | solution.py:401
  1.6 4.9 %collective-permute-start.2 = (bf16[1040,128]{1,0:T(8,128)(2,1)S(1)}, bf16[1040,128]{1,0:T(8,128)(2,1)S(1)}, u32[]{:S(2)}, u32[]{:S(2)}) collective-permute-start(bf16[1040,128]{1,0:T(8,128)(2,1)S(1)} %pack.1), channel_id=1, source_target_pairs={{0,3},{1,2},{4,7},{5,6},{8,11},{9,10},{12,15},{13,14},{16,19},{17,... | collective-permute-start | bytes 798728 | tf_op jit(solution)/shard_map/ppermute | solution.py:416
  6.6 1.3 %collective-permute-start.1 = (bf16[1040,128]{1,0:T(8,128)(2,1)S(1)}, bf16[1040,128]{1,0:T(8,128)(2,1)S(1)}, u32[]{:S(2)}, u32[]{:S(2)}) collective-permute-start(bf16[1040,128]{1,0:T(8,128)(2,1)S(1)} %pack.1), channel_id=1, source_target_pairs={{0,2},{1,3},{4,6},{5,7},{8,10},{9,11},{12,14},{13,15},{16,18},{17,... | collective-permute-start | bytes 798728 | tf_op jit(solution)/shard_map/ppermute | solution.py:416
  7.9 3.4 %collective-permute-start = (bf16[1040,128]{1,0:T(8,128)(2,1)S(1)}, bf16[1040,128]{1,0:T(8,128)(2,1)S(1)}, u32[]{:S(2)}, u32[]{:S(2)}) collective-permute-start(bf16[1040,128]{1,0:T(8,128)(2,1)S(1)} %pack.1), channel_id=1, source_target_pairs={{0,1},{2,3},{4,5},{6,7},{8,9},{10,11},{12,13},{14,15},{16,17},{18,... | collective-permute-start | bytes 798728 | tf_op jit(solution)/shard_map/ppermute | solution.py:416
  11.2 5.0 %prepare.1 = (bf16[128,4096]{1,0:T(8,128)(2,1)S(1)}, bf16[128,4096]{1,0:T(8,128)(2,1)S(1)}, bf16[128,4096]{1,0:T(8,128)(2,1)S(1)}, f32[128,128]{1,0:T(8,128)}, f...) custom-call(s32[1,8]{1,0:T(1,128)} %lengths_ref.3, ...), custom_call_target="tpu_custom_call" | custom-call | flops 268435456 | bytes 6291456 | tf_op jit(solution)/shard_map/prepare/pallas_call | solution.py:423
  16.2 0.0 collective-permute-done.2.refs_2_
  16.2 2.5 %collective-permute-done.1.refs_1_ = bf16[1040,128]{1,0:T(8,128)(2,1)S(1)} collective-permute-done((bf16[1040,128]{1,0:T(8,128)(2,1)S(1)}, bf16[1040,128]{1,0:T(8,128)(2,1)S(1)}, u32[]{:S(2)}, u32[]{:S(2)}) %collective-permute-start.1) | collective-permute-done | bytes 266272 | tf_op jit(solution)/shard_map/ppermute | solution.py:416
  18.8 0.0 collective-permute-done.refs_0_
  18.8 10.8 %attend.1 = (bf16[128,4096]{1,0:T(8,128)(2,1)}, bf16[1024,128]{1,0:T(8,128)(2,1)S(1)}, bf16[1024,128]{1,0:T(8,128)(2,1)S(1)}, bf16[1024,128]{1,0:T(8,128)(2,1)S(...) custom-call(s32[1,8]{1,0:T(1,128)} %lengths_ref.3, f32[32]{0:T(128)} %slope_ref.3, f32[32]{0:T(128)} %gain_ref.3, ...), custom_call_target="tpu_custom_call" | custom-call | flops 2684354560 | bytes 5242880 | tf_op jit(solution)/shard_map/attend/pallas_call | solution.py:452
  29.6 1.3 %collective-permute-start.3 = (bf16[1024,128]{1,0:T(8,128)(2,1)S(1)}, bf16[1024,128]{1,0:T(8,128)(2,1)S(1)}, u32[]{:S(2)}, u32[]{:S(2)}) collective-permute-start(bf16[1024,128]{1,0:T(8,128)(2,1)S(1)} %get-tuple-element.27), channel_id=1, source_target_pairs={{2,0},{3,1},{6,4},{7,5},{10,8},{11,9},{14,12},{15,13},{18,16},{19,... | collective-permute-start | bytes 786440 | tf_op jit(solution)/shard_map/ppermute | solution.py:500
  30.9 1.3 %collective-permute-start.4 = (bf16[1024,128]{1,0:T(8,128)(2,1)S(1)}, bf16[1024,128]{1,0:T(8,128)(2,1)S(1)}, u32[]{:S(2)}, u32[]{:S(2)}) collective-permute-start(bf16[1024,128]{1,0:T(8,128)(2,1)S(1)} %get-tuple-element.28), channel_id=1, source_target_pairs={{1,0},{3,2},{5,4},{7,6},{9,8},{11,10},{13,12},{15,14},{17,16},{19,... | collective-permute-start | bytes 786440 | tf_op jit(solution)/shard_map/ppermute | solution.py:500
  32.2 1.3 %collective-permute-start.5 = (bf16[1024,128]{1,0:T(8,128)(2,1)S(1)}, bf16[1024,128]{1,0:T(8,128)(2,1)S(1)}, u32[]{:S(2)}, u32[]{:S(2)}) collective-permute-start(bf16[1024,128]{1,0:T(8,128)(2,1)S(1)} %get-tuple-element.29), channel_id=1, source_target_pairs={{2,1},{3,0},{6,5},{7,4},{10,9},{11,8},{14,13},{15,12},{18,17},{19,... | collective-permute-start | bytes 786440 | tf_op jit(solution)/shard_map/ppermute | solution.py:500
  33.5 8.2 %all-to-all-start = ((f32[32,8,128]{2,1,0:T(8,128)}), f32[32,8,128]{2,1,0:T(8,128)S(1)}, u32[]{:S(2)}, u32[]{:S(2)}) async-start(f32[32,8,128]{2,1,0:T(8,128)} %bitcast.6), calls=%async_computation | async-start | bytes 262144 | tf_op jit(solution)/shard_map/all_to_all | solution.py:501
  41.6 0.0 collective-permute-done.3.refs_1_
  41.6 0.0 collective-permute-done.4.refs_2_
  41.7 0.1 sum_parts.1.sum_ref
  41.8 8.3 %all-to-all-done.bias_parts = f32[32,8,128]{2,1,0:T(8,128)S(1)} async-done(((f32[32,8,128]{2,1,0:T(8,128)}), f32[32,8,128]{2,1,0:T(8,128)S(1)}, u32[]{:S(2)}, u32[]{:S(2)}) %all-to-all-start) | async-done | bytes 131104 | tf_op jit(solution)/shard_map/all_to_all | solution.py:501
  50.0 0.0 collective-permute-done.5.part_ref
  50.0 0.7 %combine.1 = (bf16[128,512]{1,0:T(8,128)(2,1)}, bf16[128,512]{1,0:T(8,128)(2,1)}, f32[2,8]{1,0:T(2,128)}) custom-call(f32[1024,128]{1,0:T(8,128)S(1)} %sum_parts.1.sum_ref, bf16[1024,128]{1,0:T(8,128)(2,1)S(1)} %collective-permute-done.5.part_ref, f32[32,8,128]{2,1,0:T(8,128)S(1)} %all-to-all-done.bias_parts), custom_call_target="tpu_custom_call" | custom-call | tf_op jit(solution)/shard_map/combine/pallas_call | solution.py:517
Async XLA Ops:
  1.6 14.6 %collective-permute-start.2 = (bf16[1040,128]{1,0:T(8,128)(2,1)S(1)}, bf16[1040,128]{1,0:T(8,128)(2,1)S(1)}, u32[]{:S(2)}, u32[]{:S(2)}) collective-permute-start(bf16[1040,128]{1,0:T(8,128)(2,1)S(1)} %pack.1), channel_id=1, source_target_pairs={{0,3},{1,2},{4,7},{5,6},{8,11},{9,10},{12,15},{13,14},{16,19},{17,... | collective-permute-start | bytes 798728 | tf_op jit(solution)/shard_map/ppermute | solution.py:416
  6.6 12.2 %collective-permute-start.1 = (bf16[1040,128]{1,0:T(8,128)(2,1)S(1)}, bf16[1040,128]{1,0:T(8,128)(2,1)S(1)}, u32[]{:S(2)}, u32[]{:S(2)}) collective-permute-start(bf16[1040,128]{1,0:T(8,128)(2,1)S(1)} %pack.1), channel_id=1, source_target_pairs={{0,2},{1,3},{4,6},{5,7},{8,10},{9,11},{12,14},{13,15},{16,18},{17,... | collective-permute-start | bytes 798728 | tf_op jit(solution)/shard_map/ppermute | solution.py:416
  7.9 10.9 %collective-permute-start = (bf16[1040,128]{1,0:T(8,128)(2,1)S(1)}, bf16[1040,128]{1,0:T(8,128)(2,1)S(1)}, u32[]{:S(2)}, u32[]{:S(2)}) collective-permute-start(bf16[1040,128]{1,0:T(8,128)(2,1)S(1)} %pack.1), channel_id=1, source_target_pairs={{0,1},{2,3},{4,5},{6,7},{8,9},{10,11},{12,13},{14,15},{16,17},{18,... | collective-permute-start | bytes 798728 | tf_op jit(solution)/shard_map/ppermute | solution.py:416
  29.6 12.1 %collective-permute-start.3 = (bf16[1024,128]{1,0:T(8,128)(2,1)S(1)}, bf16[1024,128]{1,0:T(8,128)(2,1)S(1)}, u32[]{:S(2)}, u32[]{:S(2)}) collective-permute-start(bf16[1024,128]{1,0:T(8,128)(2,1)S(1)} %get-tuple-element.27), channel_id=1, source_target_pairs={{2,0},{3,1},{6,4},{7,5},{10,8},{11,9},{14,12},{15,13},{18,16},{19,... | collective-permute-start | bytes 786440 | tf_op jit(solution)/shard_map/ppermute | solution.py:500
  30.9 10.8 %collective-permute-start.4 = (bf16[1024,128]{1,0:T(8,128)(2,1)S(1)}, bf16[1024,128]{1,0:T(8,128)(2,1)S(1)}, u32[]{:S(2)}, u32[]{:S(2)}) collective-permute-start(bf16[1024,128]{1,0:T(8,128)(2,1)S(1)} %get-tuple-element.28), channel_id=1, source_target_pairs={{1,0},{3,2},{5,4},{7,6},{9,8},{11,10},{13,12},{15,14},{17,16},{19,... | collective-permute-start | bytes 786440 | tf_op jit(solution)/shard_map/ppermute | solution.py:500
  32.2 17.9 %collective-permute-start.5 = (bf16[1024,128]{1,0:T(8,128)(2,1)S(1)}, bf16[1024,128]{1,0:T(8,128)(2,1)S(1)}, u32[]{:S(2)}, u32[]{:S(2)}) collective-permute-start(bf16[1024,128]{1,0:T(8,128)(2,1)S(1)} %get-tuple-element.29), channel_id=1, source_target_pairs={{2,1},{3,0},{6,5},{7,4},{10,9},{11,8},{14,13},{15,12},{18,17},{19,... | collective-permute-start | bytes 786440 | tf_op jit(solution)/shard_map/ppermute | solution.py:500
  33.5 16.6 %all-to-all-start = ((f32[32,8,128]{2,1,0:T(8,128)}), f32[32,8,128]{2,1,0:T(8,128)S(1)}, u32[]{:S(2)}, u32[]{:S(2)}) async-start(f32[32,8,128]{2,1,0:T(8,128)} %bitcast.6), calls=%async_computation | async-start | bytes 262144 | tf_op jit(solution)/shard_map/all_to_all | solution.py:501

commit v16 on v15

--- a/solution.py
+++ b/solution.py
@@ -302,25 +302,29 @@
         own_key = key_ref[:, pl.ds(pl.multiple_of(group * WIDTH, WIDTH), WIDTH)]
         keys_across = jnp.transpose(jnp.concatenate([own_key, keys], axis=0))
         half_heads = heads_per_group // 2
+        raws = [dot_nt(keys, stacked(query_ref, group, 0, 2))]
         for pair in range(pairs):
-            query_pair = stacked(query_ref, group, 2 * pair, 2)
             grad_pair = stacked(grad_ref, group, 2 * pair, 2)
             product_pair = stacked(product_ref, group, 2 * pair, 2)
             grad_ext = jnp.concatenate([grad_pair, product_pair], axis=1)
-            raw = dot_nt(keys, query_pair)
-            if pair == pairs // 2:
-                key_acc[...] = key_part(group, 0, half_heads)
+            raw = raws.pop(0)
+            if pair + 1 < pairs:
+                raws.append(dot_nt(keys, stacked(query_ref, group, 2 * pair + 2, 2)))
+            if pair:
+                part = key_part(group, 2 * pair - 2, 2)
+                key_acc[...] = part if pair == 1 else key_acc[...] + part
             scales = [weigh(group, pair, raw, half) for half in range(2)]
-            if pair == pairs // 2:
-                value_acc[...] = value_part(group, 0, half_heads)
+            if pair:
+                part = value_part(group, 2 * pair - 2, 2)
+                value_acc[...] = part if pair == 1 else value_acc[...] + part
             if pair:
                 query_part(keys_across, group, pair - 1)
             centred = dot_nt(value_ext, grad_ext)
             for half in range(2):
                 differentiate(group, pair, centred, scales[half], half)
-        key_whole = key_acc[...] + key_part(group, half_heads, half_heads)
+        key_whole = key_acc[...] + key_part(group, heads_per_group - 2, 2)
         put_part(group, 0, key_whole * factor)
-        put_part(group, 1, value_acc[...] + value_part(group, half_heads, half_heads))
+        put_part(group, 1, value_acc[...] + value_part(group, heads_per_group - 2, 2))
         query_part(keys_across, group, pairs - 1)
         store(group).start()
 

time: 51.2 us -> 50.5 us (0.986)
  Pallas kernels: 17.6 us -> 16.9 us
    pallas_call x1, Pallas kernels: 10.8 us -> 10.1 us  [body(): pl.pallas_call(functools.partial(main_kernel, blocks, heads_per_group, gr...]
where the time goes in v16:
time: 50.5 us; the launch traced here: 50.1 us
  starting transfers between devices  21.6 us (43%)
  Pallas kernels  16.9 us (33%)
  waiting for transfers between devices  10.8 us (21%)
  between operations  0.73 us (1%)
    pallas_call x1, Pallas kernels, body(): pl.pallas_call(functools.partial(main_kernel, blocks, heads_per_group, gr...  10.1 us
    ppermute x3, starting transfers between devices, body(): lax.ppermute(message, 'ctx', [(i, i ^ s) for i in range(blocks) if i < i...  9.58 us
    all_to_all x1, waiting for transfers between devices, body(): lax.all_to_all(bias_parts, ('dp', 'ctx'), split_axis=0, concat_axis=0, ti...  8.29 us
    all_to_all x1, starting transfers between devices, body(): lax.all_to_all(bias_parts, ('dp', 'ctx'), split_axis=0, concat_axis=0, ti...  8.17 us
    pallas_call x1, Pallas kernels, body(): pl.pallas_call(functools.partial(prepare_kernel, heads_per_group, groups)...  4.98 us
    ppermute x3, starting transfers between devices, body(): parts[s] = lax.ppermute(parts[s], 'ctx', back)  3.88 us
    ppermute x3, waiting for transfers between devices, body(): lax.ppermute(message, 'ctx', [(i, i ^ s) for i in range(blocks) if i < i...  2.53 us
  transfers between devices with their start and end apart: 7, of which 2 were waited for; matrix products, arithmetic and copies ran while one was open for 0% of the time, Pallas kernels for 10%

profile of v16, /device:TPU:0, one launch (start us, length us, event | category | flops | bytes accessed | tf_op | source)
XLA Modules:
  0.0 50.1 jit_solution(12520894177114187949)
XLA Ops:
  0.6 1.0 %pack.1 = bf16[1040,128]{1,0:T(8,128)(2,1)S(1)} custom-call(bf16[128,512]{1,0:T(8,128)(2,1)} %bitcast.15, bf16[128,512]{1,0:T(8,128)(2,1)} %bitcast.13, s32[1,128]{1,0:T(1,128)} %depth_ref.3, s32[1,128]{1,0:T(1,128)} %end_hbm.1), custom_call_target="tpu_custom_call" | custom-call | tf_op jit(solution)/shard_map/pack/pallas_call | solution.py:405
  1.6 4.9 %collective-permute-start.2 = (bf16[1040,128]{1,0:T(8,128)(2,1)S(1)}, bf16[1040,128]{1,0:T(8,128)(2,1)S(1)}, u32[]{:S(2)}, u32[]{:S(2)}) collective-permute-start(bf16[1040,128]{1,0:T(8,128)(2,1)S(1)} %pack.1), channel_id=1, source_target_pairs={{0,3},{1,2},{4,7},{5,6},{8,11},{9,10},{12,15},{13,14},{16,19},{17,... | collective-permute-start | bytes 798728 | tf_op jit(solution)/shard_map/ppermute | solution.py:420
  6.6 1.3 %collective-permute-start.1 = (bf16[1040,128]{1,0:T(8,128)(2,1)S(1)}, bf16[1040,128]{1,0:T(8,128)(2,1)S(1)}, u32[]{:S(2)}, u32[]{:S(2)}) collective-permute-start(bf16[1040,128]{1,0:T(8,128)(2,1)S(1)} %pack.1), channel_id=1, source_target_pairs={{0,2},{1,3},{4,6},{5,7},{8,10},{9,11},{12,14},{13,15},{16,18},{17,... | collective-permute-start | bytes 798728 | tf_op jit(solution)/shard_map/ppermute | solution.py:420
  7.9 3.4 %collective-permute-start = (bf16[1040,128]{1,0:T(8,128)(2,1)S(1)}, bf16[1040,128]{1,0:T(8,128)(2,1)S(1)}, u32[]{:S(2)}, u32[]{:S(2)}) collective-permute-start(bf16[1040,128]{1,0:T(8,128)(2,1)S(1)} %pack.1), channel_id=1, source_target_pairs={{0,1},{2,3},{4,5},{6,7},{8,9},{10,11},{12,13},{14,15},{16,17},{18,... | collective-permute-start | bytes 798728 | tf_op jit(solution)/shard_map/ppermute | solution.py:420
  11.2 5.0 %prepare.1 = (bf16[128,4096]{1,0:T(8,128)(2,1)S(1)}, bf16[128,4096]{1,0:T(8,128)(2,1)S(1)}, bf16[128,4096]{1,0:T(8,128)(2,1)S(1)}, f32[128,128]{1,0:T(8,128)}, f...) custom-call(s32[1,8]{1,0:T(1,128)} %lengths_ref.3, ...), custom_call_target="tpu_custom_call" | custom-call | flops 268435456 | bytes 6291456 | tf_op jit(solution)/shard_map/prepare/pallas_call | solution.py:427
  16.2 0.0 collective-permute-done.2.refs_2_
  16.2 2.5 %collective-permute-done.1.refs_1_ = bf16[1040,128]{1,0:T(8,128)(2,1)S(1)} collective-permute-done((bf16[1040,128]{1,0:T(8,128)(2,1)S(1)}, bf16[1040,128]{1,0:T(8,128)(2,1)S(1)}, u32[]{:S(2)}, u32[]{:S(2)}) %collective-permute-start.1) | collective-permute-done | bytes 266272 | tf_op jit(solution)/shard_map/ppermute | solution.py:420
  18.8 0.0 collective-permute-done.refs_0_
  18.8 10.1 %attend.1 = (bf16[128,4096]{1,0:T(8,128)(2,1)}, bf16[1024,128]{1,0:T(8,128)(2,1)S(1)}, bf16[1024,128]{1,0:T(8,128)(2,1)S(1)}, bf16[1024,128]{1,0:T(8,128)(2,1)S(...) custom-call(s32[1,8]{1,0:T(1,128)} %lengths_ref.3, f32[32]{0:T(128)} %slope_ref.3, f32[32]{0:T(128)} %gain_ref.3, ...), custom_call_target="tpu_custom_call" | custom-call | flops 2684354560 | bytes 5242880 | tf_op jit(solution)/shard_map/attend/pallas_call | solution.py:456
  28.9 1.3 %collective-permute-start.3 = (bf16[1024,128]{1,0:T(8,128)(2,1)S(1)}, bf16[1024,128]{1,0:T(8,128)(2,1)S(1)}, u32[]{:S(2)}, u32[]{:S(2)}) collective-permute-start(bf16[1024,128]{1,0:T(8,128)(2,1)S(1)} %get-tuple-element.27), channel_id=1, source_target_pairs={{2,0},{3,1},{6,4},{7,5},{10,8},{11,9},{14,12},{15,13},{18,16},{19,... | collective-permute-start | bytes 786440 | tf_op jit(solution)/shard_map/ppermute | solution.py:504
  30.2 1.3 %collective-permute-start.4 = (bf16[1024,128]{1,0:T(8,128)(2,1)S(1)}, bf16[1024,128]{1,0:T(8,128)(2,1)S(1)}, u32[]{:S(2)}, u32[]{:S(2)}) collective-permute-start(bf16[1024,128]{1,0:T(8,128)(2,1)S(1)} %get-tuple-element.28), channel_id=1, source_target_pairs={{1,0},{3,2},{5,4},{7,6},{9,8},{11,10},{13,12},{15,14},{17,16},{19,... | collective-permute-start | bytes 786440 | tf_op jit(solution)/shard_map/ppermute | solution.py:504
  31.5 1.3 %collective-permute-start.5 = (bf16[1024,128]{1,0:T(8,128)(2,1)S(1)}, bf16[1024,128]{1,0:T(8,128)(2,1)S(1)}, u32[]{:S(2)}, u32[]{:S(2)}) collective-permute-start(bf16[1024,128]{1,0:T(8,128)(2,1)S(1)} %get-tuple-element.29), channel_id=1, source_target_pairs={{2,1},{3,0},{6,5},{7,4},{10,9},{11,8},{14,13},{15,12},{18,17},{19,... | collective-permute-start | bytes 786440 | tf_op jit(solution)/shard_map/ppermute | solution.py:504
  32.8 8.2 %all-to-all-start = ((f32[32,8,128]{2,1,0:T(8,128)}), f32[32,8,128]{2,1,0:T(8,128)S(1)}, u32[]{:S(2)}, u32[]{:S(2)}) async-start(f32[32,8,128]{2,1,0:T(8,128)} %bitcast.6), calls=%async_computation | async-start | bytes 262144 | tf_op jit(solution)/shard_map/all_to_all | solution.py:505
  41.0 0.0 collective-permute-done.3.refs_1_
  41.0 0.0 collective-permute-done.4.refs_2_
  41.0 0.1 sum_parts.1.sum_ref
  41.1 8.3 %all-to-all-done.bias_parts = f32[32,8,128]{2,1,0:T(8,128)S(1)} async-done(((f32[32,8,128]{2,1,0:T(8,128)}), f32[32,8,128]{2,1,0:T(8,128)S(1)}, u32[]{:S(2)}, u32[]{:S(2)}) %all-to-all-start) | async-done | bytes 131104 | tf_op jit(solution)/shard_map/all_to_all | solution.py:505
  49.4 0.0 collective-permute-done.5.part_ref
  49.4 0.7 %combine.1 = (bf16[128,512]{1,0:T(8,128)(2,1)}, bf16[128,512]{1,0:T(8,128)(2,1)}, f32[2,8]{1,0:T(2,128)}) custom-call(f32[1024,128]{1,0:T(8,128)S(1)} %sum_parts.1.sum_ref, bf16[1024,128]{1,0:T(8,128)(2,1)S(1)} %collective-permute-done.5.part_ref, f32[32,8,128]{2,1,0:T(8,128)S(1)} %all-to-all-done.bias_parts), custom_call_target="tpu_custom_call" | custom-call | tf_op jit(solution)/shard_map/combine/pallas_call | solution.py:521
Async XLA Ops:
  1.6 14.6 %collective-permute-start.2 = (bf16[1040,128]{1,0:T(8,128)(2,1)S(1)}, bf16[1040,128]{1,0:T(8,128)(2,1)S(1)}, u32[]{:S(2)}, u32[]{:S(2)}) collective-permute-start(bf16[1040,128]{1,0:T(8,128)(2,1)S(1)} %pack.1), channel_id=1, source_target_pairs={{0,3},{1,2},{4,7},{5,6},{8,11},{9,10},{12,15},{13,14},{16,19},{17,... | collective-permute-start | bytes 798728 | tf_op jit(solution)/shard_map/ppermute | solution.py:420
  6.6 12.2 %collective-permute-start.1 = (bf16[1040,128]{1,0:T(8,128)(2,1)S(1)}, bf16[1040,128]{1,0:T(8,128)(2,1)S(1)}, u32[]{:S(2)}, u32[]{:S(2)}) collective-permute-start(bf16[1040,128]{1,0:T(8,128)(2,1)S(1)} %pack.1), channel_id=1, source_target_pairs={{0,2},{1,3},{4,6},{5,7},{8,10},{9,11},{12,14},{13,15},{16,18},{17,... | collective-permute-start | bytes 798728 | tf_op jit(solution)/shard_map/ppermute | solution.py:420
  7.9 10.9 %collective-permute-start = (bf16[1040,128]{1,0:T(8,128)(2,1)S(1)}, bf16[1040,128]{1,0:T(8,128)(2,1)S(1)}, u32[]{:S(2)}, u32[]{:S(2)}) collective-permute-start(bf16[1040,128]{1,0:T(8,128)(2,1)S(1)} %pack.1), channel_id=1, source_target_pairs={{0,1},{2,3},{4,5},{6,7},{8,9},{10,11},{12,13},{14,15},{16,17},{18,... | collective-permute-start | bytes 798728 | tf_op jit(solution)/shard_map/ppermute | solution.py:420
  28.9 12.1 %collective-permute-start.3 = (bf16[1024,128]{1,0:T(8,128)(2,1)S(1)}, bf16[1024,128]{1,0:T(8,128)(2,1)S(1)}, u32[]{:S(2)}, u32[]{:S(2)}) collective-permute-start(bf16[1024,128]{1,0:T(8,128)(2,1)S(1)} %get-tuple-element.27), channel_id=1, source_target_pairs={{2,0},{3,1},{6,4},{7,5},{10,8},{11,9},{14,12},{15,13},{18,16},{19,... | collective-permute-start | bytes 786440 | tf_op jit(solution)/shard_map/ppermute | solution.py:504
  30.2 10.8 %collective-permute-start.4 = (bf16[1024,128]{1,0:T(8,128)(2,1)S(1)}, bf16[1024,128]{1,0:T(8,128)(2,1)S(1)}, u32[]{:S(2)}, u32[]{:S(2)}) collective-permute-start(bf16[1024,128]{1,0:T(8,128)(2,1)S(1)} %get-tuple-element.28), channel_id=1, source_target_pairs={{1,0},{3,2},{5,4},{7,6},{9,8},{11,10},{13,12},{15,14},{17,16},{19,... | collective-permute-start | bytes 786440 | tf_op jit(solution)/shard_map/ppermute | solution.py:504
  31.5 17.9 %collective-permute-start.5 = (bf16[1024,128]{1,0:T(8,128)(2,1)S(1)}, bf16[1024,128]{1,0:T(8,128)(2,1)S(1)}, u32[]{:S(2)}, u32[]{:S(2)}) collective-permute-start(bf16[1024,128]{1,0:T(8,128)(2,1)S(1)} %get-tuple-element.29), channel_id=1, source_target_pairs={{2,1},{3,0},{6,5},{7,4},{10,9},{11,8},{14,13},{15,12},{18,17},{19,... | collective-permute-start | bytes 786440 | tf_op jit(solution)/shard_map/ppermute | solution.py:504
  32.8 16.6 %all-to-all-start = ((f32[32,8,128]{2,1,0:T(8,128)}), f32[32,8,128]{2,1,0:T(8,128)S(1)}, u32[]{:S(2)}, u32[]{:S(2)}) async-start(f32[32,8,128]{2,1,0:T(8,128)} %bitcast.6), calls=%async_computation | async-start | bytes 262144 | tf_op jit(solution)/shard_map/all_to_all | solution.py:505

commit v17 on v16

--- a/solution.py
+++ b/solution.py
@@ -177,7 +177,7 @@
     remote = [refs[shifts.index(s)] for s in range(1, blocks)]
     query_grad_hbm = refs[blocks - 1]
     part_refs = refs[blocks : 2 * blocks]
-    bias_hbm = refs[2 * blocks]
+    bias_ref = refs[2 * blocks]
     (
         query_grad_ref,
         distance_ref,
@@ -189,18 +189,20 @@
         weight_ref,
         probs_ref,
         dscore_ref,
-        bias_ref,
         store_sems,
-        bias_sem,
     ) = refs[2 * blocks + 1 :]
     factor = WIDTH**-0.5
     group_columns = heads_per_group * WIDTH
     pairs = heads_per_group // 2
 
-    def store(group):
-        wide = pl.ds(pl.multiple_of(group * group_columns, group_columns), group_columns)
+    def store(group, pair):
+        inside = slice(2 * pair * WIDTH, (2 * pair + 2) * WIDTH)
+        at = pl.multiple_of(group * group_columns, group_columns) + 2 * pair * WIDTH
+        wide = pl.ds(pl.multiple_of(at, 2 * WIDTH), 2 * WIDTH)
         return pltpu.make_async_copy(
-            query_grad_ref.at[group], query_grad_hbm.at[:, wide], store_sems.at[group]
+            query_grad_ref.at[group, :, inside],
+            query_grad_hbm.at[:, wide],
+            store_sems.at[group, pair],
         )
 
     block_rows = [slice(s * tokens, (s + 1) * tokens) for s in range(blocks)]
@@ -293,6 +295,7 @@
         for half in range(2):
             at = (2 * pair + half) * WIDTH
             query_grad_ref[group, :, at : at + WIDTH] = rows[half * tokens : (half + 1) * tokens]
+        store(group, pair).start()
 
     @pl.loop(0, groups)
     def _(group):
@@ -326,7 +329,6 @@
         put_part(group, 0, key_whole * factor)
         put_part(group, 1, value_acc[...] + value_part(group, heads_per_group - 2, 2))
         query_part(keys_across, group, pairs - 1)
-        store(group).start()
 
     slope_sum = jnp.sum(slope_rows[...], axis=1, keepdims=True)
     gain_sum = jnp.sum(gain_rows[...], axis=1, keepdims=True)
@@ -342,11 +344,9 @@
         gain_line = jnp.sum(jnp.where(mine, gain_sum, 0.0), axis=0, keepdims=True)
         tile = jnp.where(kind == 0, slope_line, jnp.where(kind == 1, gain_line, 0.0))
         bias_ref[:, part] = jnp.broadcast_to(tile[None], (replicas, rows_here, local))
-    bias_copy = pltpu.make_async_copy(bias_ref, bias_hbm, bias_sem)
-    bias_copy.start()
     for group in range(groups):
-        store(group).wait()
-    bias_copy.wait()
+        for pair in range(pairs):
+            store(group, pair).wait()
 
 
 def gather_parts_kernel(*refs):
@@ -459,7 +459,7 @@
         + [jax.ShapeDtypeStruct((message_rows, WIDTH), bf16)] * blocks
         + [jax.ShapeDtypeStruct(bias_shape, f32)],
         in_specs=[smem] * 3 + [vmem] * (7 + blocks),
-        out_specs=[hbm] + [vmem] * blocks + [hbm],
+        out_specs=[hbm] + [vmem] * (blocks + 1),
         scratch_shapes=[
             pltpu.VMEM((groups, tokens, group_columns), bf16),
             pltpu.VMEM((keys_seen - tokens, tokens), f32),
@@ -471,9 +471,7 @@
             pltpu.VMEM((2, keys_seen - tokens, 2 * tokens), f32),
             pltpu.VMEM((keys_seen, group_columns), bf16),
             pltpu.VMEM((keys_seen, group_columns), bf16),
-            pltpu.VMEM(bias_shape, f32),
-            pltpu.SemaphoreType.DMA((groups,)),
-            pltpu.SemaphoreType.DMA,
+            pltpu.SemaphoreType.DMA((groups, heads_per_group // 2)),
         ],
         compiler_params=params,
         cost_estimate=pl.CostEstimate(

time: 50.5 us -> 51.1 us (1.012)
  Pallas kernels: 16.9 us -> 17.6 us
    pallas_call x1, Pallas kernels: 10.1 us -> 10.8 us  [body(): pl.pallas_call(functools.partial(main_kernel, blocks, heads_per_group, gr...]
where the time goes in v17:
time: 51.1 us; the launch traced here: 50.8 us
  starting transfers between devices  21.6 us (42%)
  Pallas kernels  17.6 us (34%)
  waiting for transfers between devices  10.8 us (21%)
  between operations  0.73 us (1%)
    pallas_call x1, Pallas kernels, body(): pl.pallas_call(functools.partial(main_kernel, blocks, heads_per_group, gr...  10.8 us
    ppermute x3, starting transfers between devices, body(): lax.ppermute(message, 'ctx', [(i, i ^ s) for i in range(blocks) if i < i...  9.58 us
    all_to_all x1, waiting for transfers between devices, body(): lax.all_to_all(bias_parts, ('dp', 'ctx'), split_axis=0, concat_axis=0, ti...  8.29 us
    all_to_all x1, starting transfers between devices, body(): lax.all_to_all(bias_parts, ('dp', 'ctx'), split_axis=0, concat_axis=0, ti...  8.16 us
    pallas_call x1, Pallas kernels, body(): pl.pallas_call(functools.partial(prepare_kernel, heads_per_group, groups)...  4.98 us
    ppermute x3, starting transfers between devices, body(): parts[s] = lax.ppermute(parts[s], 'ctx', back)  3.88 us
    ppermute x3, waiting for transfers between devices, body(): lax.ppermute(message, 'ctx', [(i, i ^ s) for i in range(blocks) if i < i...  2.53 us
  transfers between devices with their start and end apart: 7, of which 2 were waited for; matrix products, arithmetic and copies ran while one was open for 0% of the time, Pallas kernels for 10%

profile of v17, /device:TPU:0, one launch (start us, length us, event | category | flops | bytes accessed | tf_op | source)
XLA Modules:
  0.0 50.8 jit_solution(9682807626093280975)
XLA Ops:
  0.6 1.0 %pack.1 = bf16[1040,128]{1,0:T(8,128)(2,1)S(1)} custom-call(bf16[128,512]{1,0:T(8,128)(2,1)} %bitcast.15, bf16[128,512]{1,0:T(8,128)(2,1)} %bitcast.13, s32[1,128]{1,0:T(1,128)} %depth_ref.3, s32[1,128]{1,0:T(1,128)} %end_hbm.1), custom_call_target="tpu_custom_call" | custom-call | tf_op jit(solution)/shard_map/pack/pallas_call | solution.py:405
  1.6 4.9 %collective-permute-start.2 = (bf16[1040,128]{1,0:T(8,128)(2,1)S(1)}, bf16[1040,128]{1,0:T(8,128)(2,1)S(1)}, u32[]{:S(2)}, u32[]{:S(2)}) collective-permute-start(bf16[1040,128]{1,0:T(8,128)(2,1)S(1)} %pack.1), channel_id=1, source_target_pairs={{0,3},{1,2},{4,7},{5,6},{8,11},{9,10},{12,15},{13,14},{16,19},{17,... | collective-permute-start | bytes 798728 | tf_op jit(solution)/shard_map/ppermute | solution.py:420
  6.6 1.3 %collective-permute-start.1 = (bf16[1040,128]{1,0:T(8,128)(2,1)S(1)}, bf16[1040,128]{1,0:T(8,128)(2,1)S(1)}, u32[]{:S(2)}, u32[]{:S(2)}) collective-permute-start(bf16[1040,128]{1,0:T(8,128)(2,1)S(1)} %pack.1), channel_id=1, source_target_pairs={{0,2},{1,3},{4,6},{5,7},{8,10},{9,11},{12,14},{13,15},{16,18},{17,... | collective-permute-start | bytes 798728 | tf_op jit(solution)/shard_map/ppermute | solution.py:420
  7.9 3.4 %collective-permute-start = (bf16[1040,128]{1,0:T(8,128)(2,1)S(1)}, bf16[1040,128]{1,0:T(8,128)(2,1)S(1)}, u32[]{:S(2)}, u32[]{:S(2)}) collective-permute-start(bf16[1040,128]{1,0:T(8,128)(2,1)S(1)} %pack.1), channel_id=1, source_target_pairs={{0,1},{2,3},{4,5},{6,7},{8,9},{10,11},{12,13},{14,15},{16,17},{18,... | collective-permute-start | bytes 798728 | tf_op jit(solution)/shard_map/ppermute | solution.py:420
  11.2 5.0 %prepare.1 = (bf16[128,4096]{1,0:T(8,128)(2,1)S(1)}, bf16[128,4096]{1,0:T(8,128)(2,1)S(1)}, bf16[128,4096]{1,0:T(8,128)(2,1)S(1)}, f32[128,128]{1,0:T(8,128)}, f...) custom-call(s32[1,8]{1,0:T(1,128)} %lengths_ref.3, ...), custom_call_target="tpu_custom_call" | custom-call | flops 268435456 | bytes 6291456 | tf_op jit(solution)/shard_map/prepare/pallas_call | solution.py:427
  16.2 0.0 collective-permute-done.2.refs_2_
  16.2 2.5 %collective-permute-done.1.refs_1_ = bf16[1040,128]{1,0:T(8,128)(2,1)S(1)} collective-permute-done((bf16[1040,128]{1,0:T(8,128)(2,1)S(1)}, bf16[1040,128]{1,0:T(8,128)(2,1)S(1)}, u32[]{:S(2)}, u32[]{:S(2)}) %collective-permute-start.1) | collective-permute-done | bytes 266272 | tf_op jit(solution)/shard_map/ppermute | solution.py:420
  18.8 0.0 collective-permute-done.refs_0_
  18.8 10.8 %attend.1 = (bf16[128,4096]{1,0:T(8,128)(2,1)}, bf16[1024,128]{1,0:T(8,128)(2,1)S(1)}, bf16[1024,128]{1,0:T(8,128)(2,1)S(1)}, bf16[1024,128]{1,0:T(8,128)(2,1)S(...) custom-call(s32[1,8]{1,0:T(1,128)} %lengths_ref.3, f32[32]{0:T(128)} %slope_ref.3, f32[32]{0:T(128)} %gain_ref.3, ...), custom_call_target="tpu_custom_call" | custom-call | flops 2684354560 | bytes 5242880 | tf_op jit(solution)/shard_map/attend/pallas_call | solution.py:456
  29.5 1.3 %collective-permute-start.3 = (bf16[1024,128]{1,0:T(8,128)(2,1)S(1)}, bf16[1024,128]{1,0:T(8,128)(2,1)S(1)}, u32[]{:S(2)}, u32[]{:S(2)}) collective-permute-start(bf16[1024,128]{1,0:T(8,128)(2,1)S(1)} %get-tuple-element.27), channel_id=1, source_target_pairs={{2,0},{3,1},{6,4},{7,5},{10,8},{11,9},{14,12},{15,13},{18,16},{19,... | collective-permute-start | bytes 786440 | tf_op jit(solution)/shard_map/ppermute | solution.py:502
  30.8 1.3 %collective-permute-start.4 = (bf16[1024,128]{1,0:T(8,128)(2,1)S(1)}, bf16[1024,128]{1,0:T(8,128)(2,1)S(1)}, u32[]{:S(2)}, u32[]{:S(2)}) collective-permute-start(bf16[1024,128]{1,0:T(8,128)(2,1)S(1)} %get-tuple-element.28), channel_id=1, source_target_pairs={{1,0},{3,2},{5,4},{7,6},{9,8},{11,10},{13,12},{15,14},{17,16},{19,... | collective-permute-start | bytes 786440 | tf_op jit(solution)/shard_map/ppermute | solution.py:502
  32.1 1.3 %collective-permute-start.5 = (bf16[1024,128]{1,0:T(8,128)(2,1)S(1)}, bf16[1024,128]{1,0:T(8,128)(2,1)S(1)}, u32[]{:S(2)}, u32[]{:S(2)}) collective-permute-start(bf16[1024,128]{1,0:T(8,128)(2,1)S(1)} %get-tuple-element.29), channel_id=1, source_target_pairs={{2,1},{3,0},{6,5},{7,4},{10,9},{11,8},{14,13},{15,12},{18,17},{19,... | collective-permute-start | bytes 786440 | tf_op jit(solution)/shard_map/ppermute | solution.py:502
  33.4 8.2 %all-to-all-start = ((f32[32,8,128]{2,1,0:T(8,128)}), f32[32,8,128]{2,1,0:T(8,128)S(1)}, u32[]{:S(2)}, u32[]{:S(2)}) async-start(f32[32,8,128]{2,1,0:T(8,128)} %bitcast.6), calls=%async_computation | async-start | bytes 262144 | tf_op jit(solution)/shard_map/all_to_all | solution.py:503
  41.6 0.0 collective-permute-done.3.refs_1_
  41.6 0.0 collective-permute-done.4.refs_2_
  41.6 0.1 sum_parts.1.sum_ref
  41.7 8.3 %all-to-all-done.bias_parts = f32[32,8,128]{2,1,0:T(8,128)S(1)} async-done(((f32[32,8,128]{2,1,0:T(8,128)}), f32[32,8,128]{2,1,0:T(8,128)S(1)}, u32[]{:S(2)}, u32[]{:S(2)}) %all-to-all-start) | async-done | bytes 131104 | tf_op jit(solution)/shard_map/all_to_all | solution.py:503
  50.0 0.0 collective-permute-done.5.part_ref
  50.0 0.7 %combine.1 = (bf16[128,512]{1,0:T(8,128)(2,1)}, bf16[128,512]{1,0:T(8,128)(2,1)}, f32[2,8]{1,0:T(2,128)}) custom-call(f32[1024,128]{1,0:T(8,128)S(1)} %sum_parts.1.sum_ref, bf16[1024,128]{1,0:T(8,128)(2,1)S(1)} %collective-permute-done.5.part_ref, f32[32,8,128]{2,1,0:T(8,128)S(1)} %all-to-all-done.bias_parts), custom_call_target="tpu_custom_call" | custom-call | tf_op jit(solution)/shard_map/combine/pallas_call | solution.py:519
Async XLA Ops:
  1.6 14.6 %collective-permute-start.2 = (bf16[1040,128]{1,0:T(8,128)(2,1)S(1)}, bf16[1040,128]{1,0:T(8,128)(2,1)S(1)}, u32[]{:S(2)}, u32[]{:S(2)}) collective-permute-start(bf16[1040,128]{1,0:T(8,128)(2,1)S(1)} %pack.1), channel_id=1, source_target_pairs={{0,3},{1,2},{4,7},{5,6},{8,11},{9,10},{12,15},{13,14},{16,19},{17,... | collective-permute-start | bytes 798728 | tf_op jit(solution)/shard_map/ppermute | solution.py:420
  6.6 12.2 %collective-permute-start.1 = (bf16[1040,128]{1,0:T(8,128)(2,1)S(1)}, bf16[1040,128]{1,0:T(8,128)(2,1)S(1)}, u32[]{:S(2)}, u32[]{:S(2)}) collective-permute-start(bf16[1040,128]{1,0:T(8,128)(2,1)S(1)} %pack.1), channel_id=1, source_target_pairs={{0,2},{1,3},{4,6},{5,7},{8,10},{9,11},{12,14},{13,15},{16,18},{17,... | collective-permute-start | bytes 798728 | tf_op jit(solution)/shard_map/ppermute | solution.py:420
  7.9 10.9 %collective-permute-start = (bf16[1040,128]{1,0:T(8,128)(2,1)S(1)}, bf16[1040,128]{1,0:T(8,128)(2,1)S(1)}, u32[]{:S(2)}, u32[]{:S(2)}) collective-permute-start(bf16[1040,128]{1,0:T(8,128)(2,1)S(1)} %pack.1), channel_id=1, source_target_pairs={{0,1},{2,3},{4,5},{6,7},{8,9},{10,11},{12,13},{14,15},{16,17},{18,... | collective-permute-start | bytes 798728 | tf_op jit(solution)/shard_map/ppermute | solution.py:420
  29.5 12.1 %collective-permute-start.3 = (bf16[1024,128]{1,0:T(8,128)(2,1)S(1)}, bf16[1024,128]{1,0:T(8,128)(2,1)S(1)}, u32[]{:S(2)}, u32[]{:S(2)}) collective-permute-start(bf16[1024,128]{1,0:T(8,128)(2,1)S(1)} %get-tuple-element.27), channel_id=1, source_target_pairs={{2,0},{3,1},{6,4},{7,5},{10,8},{11,9},{14,12},{15,13},{18,16},{19,... | collective-permute-start | bytes 786440 | tf_op jit(solution)/shard_map/ppermute | solution.py:502
  30.8 10.8 %collective-permute-start.4 = (bf16[1024,128]{1,0:T(8,128)(2,1)S(1)}, bf16[1024,128]{1,0:T(8,128)(2,1)S(1)}, u32[]{:S(2)}, u32[]{:S(2)}) collective-permute-start(bf16[1024,128]{1,0:T(8,128)(2,1)S(1)} %get-tuple-element.28), channel_id=1, source_target_pairs={{1,0},{3,2},{5,4},{7,6},{9,8},{11,10},{13,12},{15,14},{17,16},{19,... | collective-permute-start | bytes 786440 | tf_op jit(solution)/shard_map/ppermute | solution.py:502
  32.1 17.9 %collective-permute-start.5 = (bf16[1024,128]{1,0:T(8,128)(2,1)S(1)}, bf16[1024,128]{1,0:T(8,128)(2,1)S(1)}, u32[]{:S(2)}, u32[]{:S(2)}) collective-permute-start(bf16[1024,128]{1,0:T(8,128)(2,1)S(1)} %get-tuple-element.29), channel_id=1, source_target_pairs={{2,1},{3,0},{6,5},{7,4},{10,9},{11,8},{14,13},{15,12},{18,17},{19,... | collective-permute-start | bytes 786440 | tf_op jit(solution)/shard_map/ppermute | solution.py:502
  33.4 16.6 %all-to-all-start = ((f32[32,8,128]{2,1,0:T(8,128)}), f32[32,8,128]{2,1,0:T(8,128)S(1)}, u32[]{:S(2)}, u32[]{:S(2)}) async-start(f32[32,8,128]{2,1,0:T(8,128)} %bitcast.6), calls=%async_computation | async-start | bytes 262144 | tf_op jit(solution)/shard_map/all_to_all | solution.py:503

commit v18 on v16

--- a/solution.py
+++ b/solution.py
@@ -177,7 +177,7 @@
     remote = [refs[shifts.index(s)] for s in range(1, blocks)]
     query_grad_hbm = refs[blocks - 1]
     part_refs = refs[blocks : 2 * blocks]
-    bias_hbm = refs[2 * blocks]
+    bias_ref = refs[2 * blocks]
     (
         query_grad_ref,
         distance_ref,
@@ -189,9 +189,7 @@
         weight_ref,
         probs_ref,
         dscore_ref,
-        bias_ref,
         store_sems,
-        bias_sem,
     ) = refs[2 * blocks + 1 :]
     factor = WIDTH**-0.5
     group_columns = heads_per_group * WIDTH
@@ -342,11 +340,8 @@
         gain_line = jnp.sum(jnp.where(mine, gain_sum, 0.0), axis=0, keepdims=True)
         tile = jnp.where(kind == 0, slope_line, jnp.where(kind == 1, gain_line, 0.0))
         bias_ref[:, part] = jnp.broadcast_to(tile[None], (replicas, rows_here, local))
-    bias_copy = pltpu.make_async_copy(bias_ref, bias_hbm, bias_sem)
-    bias_copy.start()
     for group in range(groups):
         store(group).wait()
-    bias_copy.wait()
 
 
 def gather_parts_kernel(*refs):
@@ -459,7 +454,7 @@
         + [jax.ShapeDtypeStruct((message_rows, WIDTH), bf16)] * blocks
         + [jax.ShapeDtypeStruct(bias_shape, f32)],
         in_specs=[smem] * 3 + [vmem] * (7 + blocks),
-        out_specs=[hbm] + [vmem] * blocks + [hbm],
+        out_specs=[hbm] + [vmem] * (blocks + 1),
         scratch_shapes=[
             pltpu.VMEM((groups, tokens, group_columns), bf16),
             pltpu.VMEM((keys_seen - tokens, tokens), f32),
@@ -471,9 +466,7 @@
             pltpu.VMEM((2, keys_seen - tokens, 2 * tokens), f32),
             pltpu.VMEM((keys_seen, group_columns), bf16),
             pltpu.VMEM((keys_seen, group_columns), bf16),
-            pltpu.VMEM(bias_shape, f32),
             pltpu.SemaphoreType.DMA((groups,)),
-            pltpu.SemaphoreType.DMA,
         ],
         compiler_params=params,
         cost_estimate=pl.CostEstimate(

time: 50.5 us -> 51.1 us (1.012)
  Pallas kernels: 16.9 us -> 17.5 us
    pallas_call x1, Pallas kernels: 10.1 us -> 10.7 us  [body(): pl.pallas_call(functools.partial(main_kernel, blocks, heads_per_group, gr...]
where the time goes in v18:
time: 51.1 us; the launch traced here: 50.7 us
  starting transfers between devices  21.6 us (42%)
  Pallas kernels  17.5 us (34%)
  waiting for transfers between devices  10.8 us (21%)
  between operations  0.73 us (1%)
    pallas_call x1, Pallas kernels, body(): pl.pallas_call(functools.partial(main_kernel, blocks, heads_per_group, gr...  10.7 us
    ppermute x3, starting transfers between devices, body(): lax.ppermute(message, 'ctx', [(i, i ^ s) for i in range(blocks) if i < i...  9.58 us
    all_to_all x1, waiting for transfers between devices, body(): lax.all_to_all(bias_parts, ('dp', 'ctx'), split_axis=0, concat_axis=0, ti...  8.29 us
    all_to_all x1, starting transfers between devices, body(): lax.all_to_all(bias_parts, ('dp', 'ctx'), split_axis=0, concat_axis=0, ti...  8.16 us
    pallas_call x1, Pallas kernels, body(): pl.pallas_call(functools.partial(prepare_kernel, heads_per_group, groups)...  4.98 us
    ppermute x3, starting transfers between devices, body(): parts[s] = lax.ppermute(parts[s], 'ctx', back)  3.88 us
    ppermute x3, waiting for transfers between devices, body(): lax.ppermute(message, 'ctx', [(i, i ^ s) for i in range(blocks) if i < i...  2.53 us
  transfers between devices with their start and end apart: 7, of which 2 were waited for; matrix products, arithmetic and copies ran while one was open for 0% of the time, Pallas kernels for 10%

profile of v18, /device:TPU:0, one launch (start us, length us, event | category | flops | bytes accessed | tf_op | source)
XLA Modules:
  0.0 50.7 jit_solution(3786413483625418677)
XLA Ops:
  0.6 1.0 %pack.1 = bf16[1040,128]{1,0:T(8,128)(2,1)S(1)} custom-call(bf16[128,512]{1,0:T(8,128)(2,1)} %bitcast.15, bf16[128,512]{1,0:T(8,128)(2,1)} %bitcast.13, s32[1,128]{1,0:T(1,128)} %depth_ref.3, s32[1,128]{1,0:T(1,128)} %end_hbm.1), custom_call_target="tpu_custom_call" | custom-call | tf_op jit(solution)/shard_map/pack/pallas_call | solution.py:400
  1.6 4.9 %collective-permute-start.2 = (bf16[1040,128]{1,0:T(8,128)(2,1)S(1)}, bf16[1040,128]{1,0:T(8,128)(2,1)S(1)}, u32[]{:S(2)}, u32[]{:S(2)}) collective-permute-start(bf16[1040,128]{1,0:T(8,128)(2,1)S(1)} %pack.1), channel_id=1, source_target_pairs={{0,3},{1,2},{4,7},{5,6},{8,11},{9,10},{12,15},{13,14},{16,19},{17,... | collective-permute-start | bytes 798728 | tf_op jit(solution)/shard_map/ppermute | solution.py:415
  6.6 1.3 %collective-permute-start.1 = (bf16[1040,128]{1,0:T(8,128)(2,1)S(1)}, bf16[1040,128]{1,0:T(8,128)(2,1)S(1)}, u32[]{:S(2)}, u32[]{:S(2)}) collective-permute-start(bf16[1040,128]{1,0:T(8,128)(2,1)S(1)} %pack.1), channel_id=1, source_target_pairs={{0,2},{1,3},{4,6},{5,7},{8,10},{9,11},{12,14},{13,15},{16,18},{17,... | collective-permute-start | bytes 798728 | tf_op jit(solution)/shard_map/ppermute | solution.py:415
  7.9 3.4 %collective-permute-start = (bf16[1040,128]{1,0:T(8,128)(2,1)S(1)}, bf16[1040,128]{1,0:T(8,128)(2,1)S(1)}, u32[]{:S(2)}, u32[]{:S(2)}) collective-permute-start(bf16[1040,128]{1,0:T(8,128)(2,1)S(1)} %pack.1), channel_id=1, source_target_pairs={{0,1},{2,3},{4,5},{6,7},{8,9},{10,11},{12,13},{14,15},{16,17},{18,... | collective-permute-start | bytes 798728 | tf_op jit(solution)/shard_map/ppermute | solution.py:415
  11.2 5.0 %prepare.1 = (bf16[128,4096]{1,0:T(8,128)(2,1)S(1)}, bf16[128,4096]{1,0:T(8,128)(2,1)S(1)}, bf16[128,4096]{1,0:T(8,128)(2,1)S(1)}, f32[128,128]{1,0:T(8,128)}, f...) custom-call(s32[1,8]{1,0:T(1,128)} %lengths_ref.3, ...), custom_call_target="tpu_custom_call" | custom-call | flops 268435456 | bytes 6291456 | tf_op jit(solution)/shard_map/prepare/pallas_call | solution.py:422
  16.2 0.0 collective-permute-done.2.refs_2_
  16.2 2.5 %collective-permute-done.1.refs_1_ = bf16[1040,128]{1,0:T(8,128)(2,1)S(1)} collective-permute-done((bf16[1040,128]{1,0:T(8,128)(2,1)S(1)}, bf16[1040,128]{1,0:T(8,128)(2,1)S(1)}, u32[]{:S(2)}, u32[]{:S(2)}) %collective-permute-start.1) | collective-permute-done | bytes 266272 | tf_op jit(solution)/shard_map/ppermute | solution.py:415
  18.8 0.0 collective-permute-done.refs_0_
  18.8 10.7 %attend.1 = (bf16[128,4096]{1,0:T(8,128)(2,1)}, bf16[1024,128]{1,0:T(8,128)(2,1)S(1)}, bf16[1024,128]{1,0:T(8,128)(2,1)S(1)}, bf16[1024,128]{1,0:T(8,128)(2,1)S(...) custom-call(s32[1,8]{1,0:T(1,128)} %lengths_ref.3, f32[32]{0:T(128)} %slope_ref.3, f32[32]{0:T(128)} %gain_ref.3, ...), custom_call_target="tpu_custom_call" | custom-call | flops 2684354560 | bytes 5242880 | tf_op jit(solution)/shard_map/attend/pallas_call | solution.py:451
  29.5 1.3 %collective-permute-start.3 = (bf16[1024,128]{1,0:T(8,128)(2,1)S(1)}, bf16[1024,128]{1,0:T(8,128)(2,1)S(1)}, u32[]{:S(2)}, u32[]{:S(2)}) collective-permute-start(bf16[1024,128]{1,0:T(8,128)(2,1)S(1)} %get-tuple-element.27), channel_id=1, source_target_pairs={{2,0},{3,1},{6,4},{7,5},{10,8},{11,9},{14,12},{15,13},{18,16},{19,... | collective-permute-start | bytes 786440 | tf_op jit(solution)/shard_map/ppermute | solution.py:497
  30.8 1.3 %collective-permute-start.4 = (bf16[1024,128]{1,0:T(8,128)(2,1)S(1)}, bf16[1024,128]{1,0:T(8,128)(2,1)S(1)}, u32[]{:S(2)}, u32[]{:S(2)}) collective-permute-start(bf16[1024,128]{1,0:T(8,128)(2,1)S(1)} %get-tuple-element.28), channel_id=1, source_target_pairs={{1,0},{3,2},{5,4},{7,6},{9,8},{11,10},{13,12},{15,14},{17,16},{19,... | collective-permute-start | bytes 786440 | tf_op jit(solution)/shard_map/ppermute | solution.py:497
  32.1 1.3 %collective-permute-start.5 = (bf16[1024,128]{1,0:T(8,128)(2,1)S(1)}, bf16[1024,128]{1,0:T(8,128)(2,1)S(1)}, u32[]{:S(2)}, u32[]{:S(2)}) collective-permute-start(bf16[1024,128]{1,0:T(8,128)(2,1)S(1)} %get-tuple-element.29), channel_id=1, source_target_pairs={{2,1},{3,0},{6,5},{7,4},{10,9},{11,8},{14,13},{15,12},{18,17},{19,... | collective-permute-start | bytes 786440 | tf_op jit(solution)/shard_map/ppermute | solution.py:497
  33.4 8.2 %all-to-all-start = ((f32[32,8,128]{2,1,0:T(8,128)}), f32[32,8,128]{2,1,0:T(8,128)S(1)}, u32[]{:S(2)}, u32[]{:S(2)}) async-start(f32[32,8,128]{2,1,0:T(8,128)} %bitcast.6), calls=%async_computation | async-start | bytes 262144 | tf_op jit(solution)/shard_map/all_to_all | solution.py:498
  41.6 0.0 collective-permute-done.3.refs_1_
  41.6 0.0 collective-permute-done.4.refs_2_
  41.6 0.1 sum_parts.1.sum_ref
  41.7 8.3 %all-to-all-done.bias_parts = f32[32,8,128]{2,1,0:T(8,128)S(1)} async-done(((f32[32,8,128]{2,1,0:T(8,128)}), f32[32,8,128]{2,1,0:T(8,128)S(1)}, u32[]{:S(2)}, u32[]{:S(2)}) %all-to-all-start) | async-done | bytes 131104 | tf_op jit(solution)/shard_map/all_to_all | solution.py:498
  50.0 0.0 collective-permute-done.5.part_ref
  50.0 0.7 %combine.1 = (bf16[128,512]{1,0:T(8,128)(2,1)}, bf16[128,512]{1,0:T(8,128)(2,1)}, f32[2,8]{1,0:T(2,128)}) custom-call(f32[1024,128]{1,0:T(8,128)S(1)} %sum_parts.1.sum_ref, bf16[1024,128]{1,0:T(8,128)(2,1)S(1)} %collective-permute-done.5.part_ref, f32[32,8,128]{2,1,0:T(8,128)S(1)} %all-to-all-done.bias_parts), custom_call_target="tpu_custom_call" | custom-call | tf_op jit(solution)/shard_map/combine/pallas_call | solution.py:514
Async XLA Ops:
  1.6 14.6 %collective-permute-start.2 = (bf16[1040,128]{1,0:T(8,128)(2,1)S(1)}, bf16[1040,128]{1,0:T(8,128)(2,1)S(1)}, u32[]{:S(2)}, u32[]{:S(2)}) collective-permute-start(bf16[1040,128]{1,0:T(8,128)(2,1)S(1)} %pack.1), channel_id=1, source_target_pairs={{0,3},{1,2},{4,7},{5,6},{8,11},{9,10},{12,15},{13,14},{16,19},{17,... | collective-permute-start | bytes 798728 | tf_op jit(solution)/shard_map/ppermute | solution.py:415
  6.6 12.2 %collective-permute-start.1 = (bf16[1040,128]{1,0:T(8,128)(2,1)S(1)}, bf16[1040,128]{1,0:T(8,128)(2,1)S(1)}, u32[]{:S(2)}, u32[]{:S(2)}) collective-permute-start(bf16[1040,128]{1,0:T(8,128)(2,1)S(1)} %pack.1), channel_id=1, source_target_pairs={{0,2},{1,3},{4,6},{5,7},{8,10},{9,11},{12,14},{13,15},{16,18},{17,... | collective-permute-start | bytes 798728 | tf_op jit(solution)/shard_map/ppermute | solution.py:415
  7.9 10.9 %collective-permute-start = (bf16[1040,128]{1,0:T(8,128)(2,1)S(1)}, bf16[1040,128]{1,0:T(8,128)(2,1)S(1)}, u32[]{:S(2)}, u32[]{:S(2)}) collective-permute-start(bf16[1040,128]{1,0:T(8,128)(2,1)S(1)} %pack.1), channel_id=1, source_target_pairs={{0,1},{2,3},{4,5},{6,7},{8,9},{10,11},{12,13},{14,15},{16,17},{18,... | collective-permute-start | bytes 798728 | tf_op jit(solution)/shard_map/ppermute | solution.py:415
  29.5 12.1 %collective-permute-start.3 = (bf16[1024,128]{1,0:T(8,128)(2,1)S(1)}, bf16[1024,128]{1,0:T(8,128)(2,1)S(1)}, u32[]{:S(2)}, u32[]{:S(2)}) collective-permute-start(bf16[1024,128]{1,0:T(8,128)(2,1)S(1)} %get-tuple-element.27), channel_id=1, source_target_pairs={{2,0},{3,1},{6,4},{7,5},{10,8},{11,9},{14,12},{15,13},{18,16},{19,... | collective-permute-start | bytes 786440 | tf_op jit(solution)/shard_map/ppermute | solution.py:497
  30.8 10.8 %collective-permute-start.4 = (bf16[1024,128]{1,0:T(8,128)(2,1)S(1)}, bf16[1024,128]{1,0:T(8,128)(2,1)S(1)}, u32[]{:S(2)}, u32[]{:S(2)}) collective-permute-start(bf16[1024,128]{1,0:T(8,128)(2,1)S(1)} %get-tuple-element.28), channel_id=1, source_target_pairs={{1,0},{3,2},{5,4},{7,6},{9,8},{11,10},{13,12},{15,14},{17,16},{19,... | collective-permute-start | bytes 786440 | tf_op jit(solution)/shard_map/ppermute | solution.py:497
  32.1 17.9 %collective-permute-start.5 = (bf16[1024,128]{1,0:T(8,128)(2,1)S(1)}, bf16[1024,128]{1,0:T(8,128)(2,1)S(1)}, u32[]{:S(2)}, u32[]{:S(2)}) collective-permute-start(bf16[1024,128]{1,0:T(8,128)(2,1)S(1)} %get-tuple-element.29), channel_id=1, source_target_pairs={{2,1},{3,0},{6,5},{7,4},{10,9},{11,8},{14,13},{15,12},{18,17},{19,... | collective-permute-start | bytes 786440 | tf_op jit(solution)/shard_map/ppermute | solution.py:497
  33.4 16.6 %all-to-all-start = ((f32[32,8,128]{2,1,0:T(8,128)}), f32[32,8,128]{2,1,0:T(8,128)S(1)}, u32[]{:S(2)}, u32[]{:S(2)}) async-start(f32[32,8,128]{2,1,0:T(8,128)} %bitcast.6), calls=%async_computation | async-start | bytes 262144 | tf_op jit(solution)/shard_map/all_to_all | solution.py:498
